TPU v7x, 32 devices: a whole 2x2x4 slice. The times are simulated.
32 devices in a mesh: dp: 16 (over z, x, core), mp: 2 (over y).
Axes of the slice: x: 2, y: 2, z: 4, core: 2. Of those that a mesh axis runs over, the one named last changes fastest.
Arguments:
- tokens: bfloat16 [2, 16, 448, 2048], P(None, 'dp'), may hold values from -6 to 6
- cotangent: bfloat16 [2, 16, 448, 2048], P(None, 'dp', None, 'mp'), may hold values from -6 to 6
- lengths: int32 [2, 16], P(None, 'dp'), may hold values from 1 to 448, as said below
- domains: int32 [2, 16, 1], P(None, 'dp'), may hold values from 0 to 7
- lower_bound: float32 [2048], replicated, may hold values from 0 to 1
- mixer_master: float32 [4, 2048, 2048], P(None, ('dp', 'mp')), may hold values from -0.125 to 0.125
- mixer_first: float32 [4, 2048, 2048], P(None, ('dp', 'mp'))
- mixer_second: float32 [4, 2048, 2048], P(None, ('dp', 'mp'))
- glu_in_master: float32 [2, 2048, 5632], P(None, 'dp', 'mp'), may hold values from -0.125 to 0.125
- glu_in_first: float32 [2, 2048, 5632], P(None, 'dp', 'mp')
- glu_in_second: float32 [2, 2048, 5632], P(None, 'dp', 'mp')
- glu_out_master: float32 [5632, 2048], P('mp', 'dp'), may hold values from -0.078125 to 0.078125
- glu_out_first: float32 [5632, 2048], P('mp', 'dp')
- glu_out_second: float32 [5632, 2048], P('mp', 'dp')
- gain_master: float32 [3, 2048], P(None, ('dp', 'mp')), may hold values from 0.5 to 1.5
- gain_first: float32 [3, 2048], P(None, ('dp', 'mp'))
- gain_second: float32 [3, 2048], P(None, ('dp', 'mp'))
Outputs:
- layer_out: bfloat16 [2, 16, 448, 2048], P(None, 'dp', None, 'mp')
- grad_tokens: bfloat16 [2, 16, 448, 2048], P(None, 'dp', None, 'mp')
- mixer_master_new: float32 [4, 2048, 2048], P(None, ('dp', 'mp'))
- mixer_first_new: float32 [4, 2048, 2048], P(None, ('dp', 'mp'))
- mixer_second_new: float32 [4, 2048, 2048], P(None, ('dp', 'mp'))
- glu_in_master_new: float32 [2, 2048, 5632], P(None, 'dp', 'mp')
- glu_in_first_new: float32 [2, 2048, 5632], P(None, 'dp', 'mp')
- glu_in_second_new: float32 [2, 2048, 5632], P(None, 'dp', 'mp')
- glu_out_master_new: float32 [5632, 2048], P('mp', 'dp')
- glu_out_first_new: float32 [5632, 2048], P('mp', 'dp')
- glu_out_second_new: float32 [5632, 2048], P('mp', 'dp')
- gain_master_new: float32 [3, 2048], P(None, ('dp', 'mp'))
- gain_first_new: float32 [3, 2048], P(None, ('dp', 'mp'))
- gain_second_new: float32 [3, 2048], P(None, ('dp', 'mp'))
Inputs may be any that keep to these rules, and one draw needn't show every extreme that they name: lengths rise from about a third of 448 at the first sequence index to 448 at the last; the last sequence of each micro-batch holds all 448 tokens.
All inputs are finite; a program needn't handle non-finite values.
Results may differ from a plain program's by a relative error of at most 0.023.
Values may be sent and summed in bfloat16 or wider, within the bound.
A program may use at most 296 MiB of HBM per device.

v0:
```python
import jax
import jax.numpy as jnp
from jax import lax
from jax.sharding import PartitionSpec as P

NDOM = 8


EPSILON = 1e-06
BETA_ONE = 0.9
BETA_TWO = 0.95
ADAM_EPSILON = 1e-08
DECAY_RATE = 0.1
MATRIX_RATE = 0.06
GAIN_RATE = 0.5
STEP_NUMBER = 3.0


def inverse_rms(values):
    return lax.rsqrt(jnp.mean(values * values, axis=-1, keepdims=True) + EPSILON)


def norm_back(grad_normed, unit_rows, inverse):
    return inverse * (
        grad_normed - unit_rows * jnp.mean(grad_normed * unit_rows, axis=-1, keepdims=True)
    )


def silu_slope(values):
    sigma = jax.nn.sigmoid(values)
    return sigma * (1.0 + values * (1.0 - sigma))


def linear_pair(earlier, later):
    return (earlier[0] * later[0], later[0] * earlier[1] + later[1])


def adamw_update(master, first, second, gradient, count, rate, decay):
    first_new = BETA_ONE * first + (1.0 - BETA_ONE) * gradient
    second_new = BETA_TWO * second + (1.0 - BETA_TWO) * gradient * gradient
    first_hat = first_new / (1.0 - BETA_ONE**count)
    second_hat = second_new / (1.0 - BETA_TWO**count)
    master_new = master - rate * (
        first_hat / (jnp.sqrt(second_hat) + ADAM_EPSILON) + decay * master
    )
    return (master_new, first_new, second_new)


def gather_weights(mixer_master, glu_in_master, glu_out_master, gain_master):
    mixer_full, gain_full = (
        lax.all_gather(mixer_master.astype(jnp.bfloat16), ("dp", "mp"), axis=1, tiled=True),
        lax.all_gather(gain_master.astype(jnp.bfloat16), ("dp", "mp"), axis=1, tiled=True),
    )
    glu_in_full, glu_out_full = (
        lax.all_gather(glu_in_master.astype(jnp.bfloat16), "dp", axis=1, tiled=True),
        lax.all_gather(glu_out_master.astype(jnp.bfloat16), "dp", axis=1, tiled=True),
    )
    return (mixer_full, gain_full.astype(jnp.float32), glu_in_full, glu_out_full)


def reduce_grads(mixer_grad, gain_grad, glu_in_grad, glu_out_grad):
    groups = lax.axis_size("dp")
    narrow = lax.axis_size("mp")
    mp_place = lax.axis_index("mp")
    full_width = mixer_grad.shape[2]
    row_count = full_width // (groups * narrow)
    mixer_pick = lax.dynamic_index_in_dim(
        mixer_grad.reshape(4, groups, narrow, row_count, full_width), mp_place, 2, keepdims=False
    )
    mixer_pick = mixer_pick.reshape(4, groups * row_count, full_width)
    gain_pick = lax.dynamic_index_in_dim(
        gain_grad.reshape(3, groups, narrow, row_count), mp_place, 2, keepdims=False
    )
    gain_pick = gain_pick.reshape(3, groups * row_count)
    mixer_own, gain_own = (
        lax.psum_scatter(
            mixer_pick.astype(jnp.bfloat16), "dp", scatter_dimension=1, tiled=True
        ).astype(jnp.float32),
        lax.psum_scatter(
            gain_pick.astype(jnp.bfloat16), "dp", scatter_dimension=1, tiled=True
        ).astype(jnp.float32),
    )
    glu_in_own, glu_out_own = (
        lax.psum_scatter(
            glu_in_grad.astype(jnp.bfloat16), "dp", scatter_dimension=1, tiled=True
        ).astype(jnp.float32),
        lax.psum_scatter(
            glu_out_grad.astype(jnp.bfloat16), "dp", scatter_dimension=1, tiled=True
        ).astype(jnp.float32),
    )
    return (mixer_own, gain_own, glu_in_own, glu_out_own)


def add_grads(first_set, second_set):
    return jax.tree.map(jnp.add, first_set, second_set)


def micro_batch(seq_in, cot_part, token_weight, lower_bound, weights_now):
    mixer_full, gain_full, glu_in_full, glu_out_full = weights_now
    mp_place = lax.axis_index("mp")
    part_width = cot_part.shape[1]
    inverse_in = inverse_rms(seq_in)
    unit_in = seq_in * inverse_in
    normed_in = (unit_in * gain_full[0]).astype(jnp.bfloat16)
    in_weights = mixer_full[:3]
    out_weight = mixer_full[3]
    state_gain = gain_full[1]
    pre_all = jnp.einsum("td,kde->kte", normed_in, in_weights, preferred_element_type=jnp.float32)
    pre_input = pre_all[0]
    pre_forget = pre_all[1]
    pre_gate = pre_all[2]
    forget_sig = jax.nn.sigmoid(pre_forget)
    forget = lower_bound + (1.0 - lower_bound) * forget_sig
    fresh_input = jax.nn.silu(pre_input)
    states = lax.associative_scan(linear_pair, (forget, (1.0 - forget) * fresh_input), axis=0)[1]
    inverse_state = inverse_rms(states)
    unit_state = states * inverse_state
    gate_act = jax.nn.silu(pre_gate)
    gated_out = (unit_state * state_gain * gate_act).astype(jnp.bfloat16)
    branch_mix = jnp.dot(gated_out, out_weight, preferred_element_type=jnp.float32)
    middle = seq_in + branch_mix
    inverse_mid = inverse_rms(middle)
    unit_mid = middle * inverse_mid
    normed_mid = (unit_mid * gain_full[2]).astype(jnp.bfloat16)
    pre_glu = jnp.einsum("td,kdf->ktf", normed_mid, glu_in_full, preferred_element_type=jnp.float32)
    act_part = jax.nn.silu(pre_glu[0])
    hidden = (act_part * pre_glu[1]).astype(jnp.bfloat16)
    partial_out = jnp.dot(hidden, glu_out_full, preferred_element_type=jnp.float32)
    branch = lax.psum_scatter(
        partial_out.astype(jnp.bfloat16), "mp", scatter_dimension=1, tiled=True
    ).astype(jnp.float32)
    output = (
        lax.dynamic_slice_in_dim(middle, mp_place * part_width, part_width, 1) + branch
    ).astype(jnp.bfloat16)
    cot_full = lax.all_gather(cot_part, "mp", axis=1, tiled=True)
    back = cot_full.astype(jnp.float32) * token_weight[:, None]
    back_low = back.astype(jnp.bfloat16)
    grad_glu_out = jnp.einsum("tf,td->fd", hidden, back_low, preferred_element_type=jnp.float32)
    grad_hidden = jnp.einsum(
        "td,fd->tf", back_low, glu_out_full, preferred_element_type=jnp.float32
    )
    grad_pre_glu = jnp.stack(
        [grad_hidden * pre_glu[1] * silu_slope(pre_glu[0]), grad_hidden * act_part]
    ).astype(jnp.bfloat16)
    grad_glu_in = jnp.einsum(
        "td,ktf->kdf", normed_mid, grad_pre_glu, preferred_element_type=jnp.float32
    )
    grad_normed_part = jnp.einsum(
        "ktf,kdf->td", grad_pre_glu, glu_in_full, preferred_element_type=jnp.float32
    )
    grad_normed_mid = lax.psum(grad_normed_part, "mp")
    gain_mid = jnp.sum(grad_normed_mid * unit_mid, axis=0)
    grad_middle = back + norm_back(grad_normed_mid * gain_full[2], unit_mid, inverse_mid)
    middle_low = grad_middle.astype(jnp.bfloat16)
    grad_mix_out = jnp.einsum(
        "td,te->de", gated_out, middle_low, preferred_element_type=jnp.float32
    )
    grad_gated = jnp.einsum("te,de->td", middle_low, out_weight, preferred_element_type=jnp.float32)
    gain_state = jnp.sum(grad_gated * unit_state * gate_act, axis=0)
    grad_pre_gate = grad_gated * unit_state * state_gain * silu_slope(pre_gate)
    scaled_grad = grad_gated * state_gain * gate_act
    grad_states = norm_back(scaled_grad, unit_state, inverse_state)
    next_forget = jnp.concatenate([forget[1:], jnp.zeros_like(forget[:1])], axis=0)
    carried = lax.associative_scan(linear_pair, (next_forget, grad_states), reverse=True, axis=0)[1]
    earlier_states = jnp.concatenate([jnp.zeros_like(states[:1]), states[:-1]], axis=0)
    grad_forget = carried * (earlier_states - fresh_input)
    grad_fresh = carried * (1.0 - forget)
    grad_pre = jnp.stack(
        [
            grad_fresh * silu_slope(pre_input),
            grad_forget * (1.0 - lower_bound) * forget_sig * (1.0 - forget_sig),
            grad_pre_gate,
        ]
    ).astype(jnp.bfloat16)
    grad_mix_in = jnp.einsum("td,kte->kde", normed_in, grad_pre, preferred_element_type=jnp.float32)
    grad_normed_in = jnp.einsum(
        "kte,kde->td", grad_pre, in_weights, preferred_element_type=jnp.float32
    )
    gain_in = jnp.sum(grad_normed_in * unit_in, axis=0)
    grad_seq = grad_middle + norm_back(grad_normed_in * gain_full[0], unit_in, inverse_in)
    grad_slice = lax.dynamic_slice_in_dim(grad_seq, mp_place * part_width, part_width, 1).astype(
        jnp.bfloat16
    )
    mixer_grad = jnp.concatenate([grad_mix_in, grad_mix_out[None]], axis=0)
    gain_grad = jnp.stack([gain_in, gain_state, gain_mid])
    return (output, grad_slice, (mixer_grad, gain_grad, grad_glu_in, grad_glu_out))


def shards(
    tokens,
    cotangent,
    lengths,
    domains,
    lower_bound,
    mixer_master,
    mixer_first,
    mixer_second,
    glu_in_master,
    glu_in_first,
    glu_in_second,
    glu_out_master,
    glu_out_first,
    glu_out_second,
    gain_master,
    gain_first,
    gain_second,
):
    batches = tokens.shape[0]
    seq_len = tokens.shape[2]
    groups = lax.axis_size("dp")
    domain_ids = jnp.arange(NDOM, dtype=jnp.int32)
    member = (domains[..., 0][..., None] == domain_ids).astype(jnp.float32)
    live_counts = lengths.astype(jnp.float32)
    counts, token_total = lax.psum(
        (jnp.sum(member * live_counts[..., None], axis=(0, 1)), jnp.sum(live_counts)), "dp"
    )
    seq_weight = token_total / (NDOM * jnp.sum(member * counts, axis=-1))
    positions = jnp.arange(seq_len, dtype=jnp.int32)
    outputs = []
    grad_rows = []
    totals = None
    for batch_index in range(batches):
        weights_now = gather_weights(mixer_master, glu_in_master, glu_out_master, gain_master)
        token_weight = seq_weight[batch_index, 0] * (positions < lengths[batch_index, 0]).astype(
            jnp.float32
        )
        output, grad_slice, local_grads = micro_batch(
            tokens[batch_index, 0].astype(jnp.float32),
            cotangent[batch_index, 0],
            token_weight,
            lower_bound,
            weights_now,
        )
        outputs.append(output)
        grad_rows.append(grad_slice)
        totals = local_grads if totals is None else add_grads(totals, local_grads)
    totals = reduce_grads(totals[0], totals[1], totals[2], totals[3])
    scale_factor = 1.0 / (batches * groups * tokens.shape[1])
    count = STEP_NUMBER
    mixer_new = adamw_update(
        mixer_master,
        mixer_first,
        mixer_second,
        totals[0] * scale_factor,
        count,
        MATRIX_RATE,
        DECAY_RATE,
    )
    gain_new = adamw_update(
        gain_master, gain_first, gain_second, totals[1] * scale_factor, count, GAIN_RATE, 0.0
    )
    glu_in_new = adamw_update(
        glu_in_master,
        glu_in_first,
        glu_in_second,
        totals[2] * scale_factor,
        count,
        MATRIX_RATE,
        DECAY_RATE,
    )
    glu_out_new = adamw_update(
        glu_out_master,
        glu_out_first,
        glu_out_second,
        totals[3] * scale_factor,
        count,
        MATRIX_RATE,
        DECAY_RATE,
    )
    layer_out = jnp.stack(outputs)[:, None]
    grad_tokens = jnp.stack(grad_rows)[:, None]
    return (
        layer_out,
        grad_tokens,
        mixer_new[0],
        mixer_new[1],
        mixer_new[2],
        glu_in_new[0],
        glu_in_new[1],
        glu_in_new[2],
        glu_out_new[0],
        glu_out_new[1],
        glu_out_new[2],
        gain_new[0],
        gain_new[1],
        gain_new[2],
    )


def solution(mesh):
    in_specs = (
        P(None, "dp", None, None),
        P(None, "dp", None, "mp"),
        P(None, "dp"),
        P(None, "dp", None),
        P(),
        P(None, ("dp", "mp"), None),
        P(None, ("dp", "mp"), None),
        P(None, ("dp", "mp"), None),
        P(None, "dp", "mp"),
        P(None, "dp", "mp"),
        P(None, "dp", "mp"),
        P("mp", "dp"),
        P("mp", "dp"),
        P("mp", "dp"),
        P(None, ("dp", "mp")),
        P(None, ("dp", "mp")),
        P(None, ("dp", "mp")),
    )
    out_specs = (
        P(None, "dp", None, "mp"),
        P(None, "dp", None, "mp"),
        P(None, ("dp", "mp"), None),
        P(None, ("dp", "mp"), None),
        P(None, ("dp", "mp"), None),
        P(None, "dp", "mp"),
        P(None, "dp", "mp"),
        P(None, "dp", "mp"),
        P("mp", "dp"),
        P("mp", "dp"),
        P("mp", "dp"),
        P(None, ("dp", "mp")),
        P(None, ("dp", "mp")),
        P(None, ("dp", "mp")),
    )
    return jax.shard_map(shards, mesh=mesh, in_specs=in_specs, out_specs=out_specs, check_vma=False)
```

profile of v0, /device:TPU:0, one launch (start us, length us, event | category | flops | bytes accessed | tf_op | source)
XLA Modules:
  0.0 1983.9 jit_solution(1037557350118298409)
XLA Ops:
  17.5 36.6 %all-reduce.68 = (f32[8]{0:T(128)S(1)}, f32[]{:T(128)}) all-reduce(f32[8]{0:T(128)S(1)} %select_reduce_fusion.1, f32[]{:T(128)} %convert_reduce_fusion), channel_id=1, replica_groups=mesh['dp'=16,'mp'=2] {'dp'}, use_global_device_ids=true, to_apply=%region_11.12 | all-reduce | flops 9 | bytes 72 | tf_op jit(solution)/shard_map/psum | solution.py:214
  58.6 66.2 %all-gather.2 = bf16[32,64,3]{1,2,0:T(4,128)(2,1)S(1)} all-gather(bf16[1,64,3]{1,2,0:T(4,128)(2,1)S(1)} %convert_bitcast_fusion), channel_id=1, replica_groups=mesh['dp'=16,'mp'=2] {'dp','mp'}, dimensions={0}, use_global_device_ids=true | all-gather | bytes 12672 | tf_op jit(solution)/shard_map/all_gather | solution.py:52
  129.3 80.2 %all-gather.9.cloned.1.call-done = bf16[4,2048,2048]{2,1,0:T(8,128)(2,1)} async-done(((bf16[4,64,2048]{2,1,0:T(8,128)(2,1)}), bf16[4,2048,2048]{2,1,0:T(8,128)(2,1)}) %all-gather.9.cloned.1.call-update) | async-done | bytes 33554448 | tf_op jit(solution)/shard_map/all_gather | solution.py:51
  209.5 19.6 fusion.22
  229.1 19.6 fusion.19
  573.9 18.9 convolution_bitcast_fusion
  592.8 14.9 fusion.56
  607.7 17.8 fusion.49
  625.4 19.0 convolution_bitcast_fusion.1
  644.5 14.9 fusion.55
  659.4 17.8 fusion.48
  747.8 16.4 slice.1030
  764.1 16.8 slice.1021
  791.5 16.5 slice.1101
  808.0 16.7 slice.1092
  891.7 16.1 multiply_reduce_fusion.3
  945.0 16.4 slice.1025
  1046.4 16.4 slice.1096
  1184.3 32.1 %rev.4 = f32[448,2048]{1,0:T(8,128)} reverse(f32[448,2048]{1,0:T(8,128)} %add.764), dimensions={0} | reverse | bytes 7340032 | tf_op jit(solution)/shard_map/rev | solution.py:164
  1264.6 32.2 %rev.5 = f32[448,2048]{1,0:T(8,128)} reverse(f32[448,2048]{1,0:T(8,128)} %add.793), dimensions={0} | reverse | bytes 7340032 | tf_op jit(solution)/shard_map/rev | solution.py:164
  1305.9 18.9 fusion.7
  1329.9 22.6 %fusion.39 = (f32[2048]{0:T(1024)S(1)}, f32[448]{0:T(512)}, f32[448]{0:T(512)}, f32[2048]{0:T(1024)S(1)}, f32[448,2048]{1,0:T(8,128)}, /*index=5*/f32[448,2048]{1,0:T(8,128)}, f32[448,2048]{1,0:T(8,128)}, f32[448,2048]{1,0:T(8,128)}) fusion(f32[448]{0:T(512)S(1)} %copy-done.132, bf16[2,1,448,2048]{3,2,1,0:T(8,128)(2,1)} %param.17, f32[448]{0:T(512)S(1)} %copy-done.129, ...), kind=kOutput, calls=%fused_computation.81 | convolution fusion | flops 11292635136 | bytes 52722688 | tf_op jit(solution)/shard_map/kte,kde->td/dot_general | solution.py:176
  1368.4 15.5 copy.92
  1405.6 25.0 %fusion.58 = f32[3,2048,2048]{1,2,0:T(8,128)} fusion(bf16[1,448,2048]{2,1,0:T(8,128)(2,1)S(1)} %copy-done.53, bf16[1,448,2048]{2,1,0:T(8,128)(2,1)S(1)} %copy-done.39, bf16[1,448,2048]{2,1,0:T(8,128)(2,1)S(1)} %copy-done.38, f32[2048]{0:T(1024)S(1)} %bitcast.323, f32[448]{0:T(512)S(1)} %copy-done.129, bf16[2,1,448,2048]{3,2,1,0:T(8,128)(2,1)S(1)} %copy-done.31), kind=kOutput, calls=%fused_computation.148 | convolution fusion | flops 11283464192 | bytes 57681920 | tf_op jit(solution)/shard_map/td,kte->kde/dot_general | solution.py:175
  1430.6 21.7 %fusion.57 = f32[3,2048,2048]{1,2,0:T(8,128)} fusion(bf16[1,448,2048]{2,1,0:T(8,128)(2,1)S(1)} %copy-done.52, bf16[1,448,2048]{2,1,0:T(8,128)(2,1)S(1)} %copy-done.41, bf16[1,448,2048]{2,1,0:T(8,128)(2,1)S(1)} %copy-done.40, f32[448]{0:T(512)S(1)} %copy-done.132, f32[2048]{0:T(1024)S(1)} %bitcast.324, bf16[2,1,448,2048]{3,2,1,0:T(8,128)(2,1)S(1)} %copy-done.31), kind=kOutput, calls=%fused_computation.147 | convolution fusion | flops 11283464192 | bytes 57681920 | tf_op jit(solution)/shard_map/td,kte->kde/dot_general | solution.py:175
  1452.3 28.1 %fusion.2 = bf16[4,16,1,64,2048]{4,3,2,1,0:T(8,128)(2,1)} fusion(s32[]{:T(128)S(6)} %select_n.13, f32[3,16,2,64,2048]{4,3,2,1,0:T(8,128)} %bitcast.297, f32[1,16,2,64,2048]{4,3,2,1,0:T(8,128)} %bitcast.304, f32[3,16,2,64,2048]{4,3,2,1,0:T(8,128)} %bitcast.296, f32[1,16,2,64,2048]{4,3,2,1,0:T(8,128)} %bitcast.303), kind=kLoop, calls=%fused_computation.7 | loop fusion | flops 33554432 | bytes 150994944 | tf_op jit(solution)/shard_map/convert_element_type | solution.py:77
  1481.0 24.5 %fusion.46 = f32[2,2816,2048]{2,1,0:T(8,128)} fusion(bf16[1,448,2816]{2,1,0:T(8,128)(2,1)} %get-tuple-element.161, bf16[1,448,2816]{2,1,0:T(8,128)(2,1)} %get-tuple-element.160, f32[448,2048]{1,0:T(8,128)} %get-tuple-element.253, f32[2048]{0:T(1024)S(1)} %bitcast.313, f32[448]{0:T(512)S(1)} %copy-done.119), kind=kOutput, calls=%fused_computation.128 | convolution fusion | flops 10340040704 | bytes 54863616 | tf_op jit(solution)/shard_map/td,ktf->kdf/dot_general | solution.py:145
  1505.6 27.1 %fusion.4 = bf16[2,2048,2816]{1,2,0:T(8,128)(2,1)} fusion(f32[2,2816,2048]{2,1,0:T(8,128)} %fusion.46, bf16[1,448,2816]{2,1,0:T(8,128)(2,1)} %get-tuple-element.163, bf16[1,448,2816]{2,1,0:T(8,128)(2,1)S(1)} %copy-done.149, f32[448,2048]{1,0:T(8,128)} %get-tuple-element.251, f32[448]{0:T(512)S(1)} %copy-done.126, f32[2048]{0:T(1024)S(1)} %bitcast.314), kind=kOutput, calls=%fused_computation.9 | convolution fusion | flops 10363109376 | bytes 77932288 | tf_op jit(solution)/shard_map/td,ktf->kdf/dot_general | solution.py:145
  1532.6 57.8 %copy.90 = bf16[2,2048,2816]{2,0,1:T(2,128)(2,1)} copy(bf16[2,2048,2816]{1,2,0:T(8,128)(2,1)} %fusion.4) | data formatting | bytes 46137344
  1590.4 24.4 %copy.97 = bf16[256,8,2,2816]{3,1,2,0:T(8,128)(2,1)} copy(bf16[256,8,2,2816]{3,2,1,0:T(2,128)(2,1)} %bitcast.294) | data formatting | bytes 46137344
  1647.8 72.6 %reduce-scatter.17.cloned.1.call-done = bf16[4,64,2048]{2,1,0:T(8,128)(2,1)} async-done(((bf16[4,1024,2048]{2,1,0:T(8,128)(2,1)}), bf16[4,64,2048]{2,1,0:T(8,128)(2,1)}) %reduce-scatter.17.cloned.1.call-update) | async-done | bytes 1048592 | tf_op jit(solution)/shard_map/reduce_scatter | solution.py:76
  1727.5 222.8 %reduce-scatter.19.cloned.1.call-done = bf16[128,5632]{1,0:T(8,128)(2,1)} async-done(((bf16[2048,5632]{1,0:T(8,128)(2,1)}), bf16[128,5632]{1,0:T(8,128)(2,1)}) %reduce-scatter.19.cloned.1.call-update) | async-done | bytes 1441808
  (810 shorter events, 900.3 us)
Async XLA Ops:
  7.2 202.3 %all-gather.9.cloned.1.call-start = ((), (), s32[]{:S(2)}) async-start(), calls=%async_computation.6 | async-start | bytes 34603008 | tf_op jit(solution)/shard_map/all_gather | solution.py:51
  10.1 563.7 %all-gather.11.cloned.1.call-start = ((), (), s32[]{:S(2)}) async-start(), calls=%async_computation.7 | async-start | bytes 24510464 | tf_op jit(solution)/shard_map/all_gather | solution.py:55
  11.5 44.0 %copy-start.135 = (f32[3,64]{1,0:T(4,128)S(1)}, f32[3,64]{1,0:T(4,128)}, u32[]{:S(2)}) copy-start(f32[3,64]{1,0:T(4,128)} %param.31) | copy-start | bytes 2308
  11.5 581.2 %all-gather.17.cloned.1.call-start = ((), (), s32[]{:S(2)}) async-start(), calls=%async_computation.13 | async-start | bytes 2752512 | tf_op jit(solution)/shard_map/all_gather | solution.py:135
  14.5 44.0 %copy-start.97 = (f32[2048]{0:T(1024)S(1)}, f32[2048]{0:T(1024)}, u32[]{:S(2)}) copy-start(f32[2048]{0:T(1024)} %param.21) | copy-start | bytes 24580
  14.5 578.2 %all-gather.13.cloned.1.call-start = ((), (), s32[]{:S(2)}) async-start(), calls=%async_computation.8 | async-start | bytes 12255232 | tf_op jit(solution)/shard_map/all_gather | solution.py:56
  15.6 628.9 %all-gather.15.cloned.1.call-start = ((), (), s32[]{:S(2)}) async-start(), calls=%async_computation.12 | async-start | bytes 2752512 | tf_op jit(solution)/shard_map/all_gather | solution.py:135
  16.2 851.8 %all-reduce.72.cloned.1.call-start = ((), (), s32[]{:S(2)}) async-start(), calls=%async_computation.17 | async-start | bytes 14680064 | tf_op jit(solution)/shard_map/psum | solution.py:151
  58.6 190.2 %copy-start.71 = (f32[2048]{0:T(1024)}, f32[2048]{0:T(1024)S(1)}, u32[]{:S(2)}) copy-start(f32[2048]{0:T(1024)S(1)} %broadcast_subtract_fusion) | copy-start | bytes 24580
  125.5 103.6 %copy-start.137 = (f32[1,2048]{1,0:T(1,128)}, f32[1,2048]{1,0:T(1,128)S(1)}, u32[]{:S(2)}) copy-start(f32[1,2048]{1,0:T(1,128)S(1)} %get-tuple-element.233) | copy-start | bytes 24580
  125.5 422.4 %copy-start.93 = (f32[1,2048]{1,0:T(1,128)}, f32[1,2048]{1,0:T(1,128)S(1)}, u32[]{:S(2)}) copy-start(f32[1,2048]{1,0:T(1,128)S(1)} %get-tuple-element.232) | copy-start | bytes 24580
  129.3 99.8 %copy-start.131 = (f32[448]{0:T(512)}, f32[448]{0:T(512)S(1)}, u32[]{:S(2)}) copy-start(f32[448]{0:T(512)S(1)} %get-tuple-element.255) | copy-start | bytes 5380
  129.3 99.8 %copy-start.128 = (f32[448]{0:T(512)}, f32[448]{0:T(512)S(1)}, u32[]{:S(2)}) copy-start(f32[448]{0:T(512)S(1)} %get-tuple-element.256) | copy-start | bytes 5380
  564.4 308.5 %copy-start.118 = (f32[448]{0:T(512)}, f32[448]{0:T(512)S(1)}, u32[]{:S(2)}) copy-start(f32[448]{0:T(512)S(1)} %add_rsqrt_fusion.3) | copy-start | bytes 5380
  625.4 19.0 copy-start.127
  677.2 946.9 %reduce-scatter.15.cloned.1.call-start = ((), (), s32[]{:S(2)}) async-start(), calls=%async_computation.10 | async-start | bytes 2752512 | tf_op jit(solution)/shard_map/reduce_scatter | solution.py:129
  687.2 940.0 %reduce-scatter.13.cloned.1.call-start = ((), (), s32[]{:S(2)}) async-start(), calls=%async_computation.9 | async-start | bytes 2752512 | tf_op jit(solution)/shard_map/reduce_scatter | solution.py:129
  791.5 33.3 %copy-start.24 = (f32[224,2048]{1,0:T(8,128)S(1)}, f32[224,2048]{1,0:T(8,128)}, u32[]{:S(2)}) copy-start(f32[224,2048]{1,0:T(8,128)} %slice.1093) | copy-start | bytes 5505028
  855.0 783.9 %reduce-scatter.23.cloned.1.call-start = ((), (), s32[]{:S(2)}) async-start(), calls=%async_computation.16 | async-start | bytes 278528
  1184.3 32.1 %copy-start.22 = (f32[223,2048]{1,0:T(8,128)S(1)}, f32[223,2048]{1,0:T(8,128)}, u32[]{:S(2)}) copy-start(f32[223,2048]{1,0:T(8,128)} %slice.1154) | copy-start | bytes 5480452
  1264.6 32.3 %copy-start.72 = (f32[2048]{0:T(1024)S(1)}, f32[2048]{0:T(1024)}, u32[]{:S(2)}) copy-start(f32[2048]{0:T(1024)} %copy-done.71) | copy-start | bytes 24580
  1296.8 28.0 %slice-start.3 = ((s8[11010048]{0:T(1024)(128)(4,1)}), s8[4194304]{0:T(1024)(128)(4,1)S(1)}, s32[]{:S(2)}) async-start(s8[11010048]{0:T(1024)(128)(4,1)} %bitcast.301), calls=%async_computation.21 | async-start | bytes 8388608
  1329.9 23.9 %copy-start.50 = (bf16[1,1,448,2048]{3,2,1,0:T(8,128)(2,1)S(1)}, bf16[1,1,448,2048]{3,2,1,0:T(8,128)(2,1)}, u32[]{:S(2)}) copy-start(bf16[1,1,448,2048]{3,2,1,0:T(8,128)(2,1)} %all-gather.17.cloned.1.call-done) | copy-start | bytes 5505028
  1329.9 23.9 %copy-start.141 = (f32[448]{0:T(512)S(1)}, f32[448]{0:T(512)}, u32[]{:S(2)}) copy-start(f32[448]{0:T(512)} %fusion.132) | copy-start | bytes 5380
  1353.7 286.6 %reduce-scatter.21.cloned.1.call-start = ((), (), s32[]{:S(2)}) async-start(), calls=%async_computation.15 | async-start | bytes 12255232
  1383.9 336.5 %reduce-scatter.17.cloned.1.call-start = ((), (), s32[]{:S(2)}) async-start(), calls=%async_computation.11 | async-start | bytes 17825792 | tf_op jit(solution)/shard_map/reduce_scatter | solution.py:76
  1405.6 25.0 %copy-start.40 = (bf16[1,448,2048]{2,1,0:T(8,128)(2,1)S(1)}, bf16[1,448,2048]{2,1,0:T(8,128)(2,1)}, u32[]{:S(2)}) copy-start(bf16[1,448,2048]{2,1,0:T(8,128)(2,1)} %get-tuple-element.166) | copy-start | bytes 5505028
  1405.6 25.0 %copy-start.41 = (bf16[1,448,2048]{2,1,0:T(8,128)(2,1)S(1)}, bf16[1,448,2048]{2,1,0:T(8,128)(2,1)}, u32[]{:S(2)}) copy-start(bf16[1,448,2048]{2,1,0:T(8,128)(2,1)} %get-tuple-element.167) | copy-start | bytes 5505028
  1405.6 25.0 %copy-start.52 = (bf16[1,448,2048]{2,1,0:T(8,128)(2,1)S(1)}, bf16[1,448,2048]{2,1,0:T(8,128)(2,1)}, u32[]{:S(2)}) copy-start(bf16[1,448,2048]{2,1,0:T(8,128)(2,1)} %get-tuple-element.239) | copy-start | bytes 5505028
  1480.3 25.2 %copy-start.126 = (f32[448]{0:T(512)S(1)}, f32[448]{0:T(512)}, u32[]{:S(2)}) copy-start(f32[448]{0:T(512)} %copy-done.124) | copy-start | bytes 5380
  1480.4 25.2 %copy-start.149 = (bf16[1,448,2816]{2,1,0:T(8,128)(2,1)S(1)}, bf16[1,448,2816]{2,1,0:T(8,128)(2,1)}, u32[]{:S(2)}) copy-start(bf16[1,448,2816]{2,1,0:T(8,128)(2,1)} %get-tuple-element.162) | copy-start | bytes 7569412
  1480.4 469.9 %reduce-scatter.19.cloned.1.call-start = ((), (), s32[]{:S(2)}) async-start(), calls=%async_computation.14 | async-start | bytes 24510464
  (136 other events, 1074.1 us)
Sparse Core Ops, SparseCore 0:
  11.7 197.7 all-gather.8
  211.6 116.8 all-gather.10
  330.1 30.1 all-gather.16
  362.3 97.3 all-gather.12
  461.1 28.3 all-gather.14
  677.3 174.8 all-reduce.71
  855.1 28.9 reduce-scatter.14
  886.9 28.9 reduce-scatter.12
  1353.8 54.1 reduce-scatter.22
  1412.6 125.2 reduce-scatter.20
  1542.0 178.3 reduce-scatter.16
  1724.4 225.8 reduce-scatter.18
where the time goes:
time: 2010 us; the launch traced here: 1980 us
  local copies, waits for them, and re-layouts  851 us (42%)
  matrix products  399 us (20%)
  waiting for transfers between devices  376 us (19%)
  other arithmetic  236 us (12%)
  blocking collectives  103 us (5%)
    slice x110, local copies, waits for them, and re-layouts, micro_batch(): lax.associative_scan(linear_pair, (next_forget, grad_states), reverse=Tru...  349 us
    unnamed x15, waiting for transfers between devices  223 us
    slice x98, local copies, waits for them, and re-layouts, micro_batch(): lax.associative_scan(linear_pair, (forget, (1.0 - forget) * fresh_input),...  188 us
    unnamed x326, local copies, waits for them, and re-layouts  140 us
    all_gather x1, waiting for transfers between devices, gather_weights(): lax.all_gather(mixer_master.astype(jnp.bfloat16), ('dp', 'mp'), axis=1, t...  80.2 us
    reduce_scatter x1, waiting for transfers between devices, reduce_grads(): lax.psum_scatter(mixer_pick.astype(jnp.bfloat16), 'dp', scatter_dimension...  72.6 us
    all_gather x1, blocking collectives, gather_weights(): lax.all_gather(gain_master.astype(jnp.bfloat16), ('dp', 'mp'), axis=1, ti...  66.2 us
    rev x2, local copies, waits for them, and re-layouts, micro_batch(): lax.associative_scan(linear_pair, (next_forget, grad_states), reverse=Tru...  64.4 us
  transfers between devices with their start and end apart: 12, of which 3 were waited for; matrix products, arithmetic and copies ran while one was open for 71% of the time, Pallas kernels for 0%

commit v1 on v0

v1 whole, which is shorter than its diff:
```python
import functools

import jax
import jax.numpy as jnp
from jax import lax
from jax.experimental import pallas as pl
from jax.experimental.pallas import tpu as pltpu
from jax.sharding import PartitionSpec as P

NDOM = 8

EPSILON = 1e-06
BETA_ONE = 0.9
BETA_TWO = 0.95
ADAM_EPSILON = 1e-08
DECAY_RATE = 0.1
MATRIX_RATE = 0.06
GAIN_RATE = 0.5
STEP_NUMBER = 3.0

BF = jnp.bfloat16
F32 = jnp.float32
VMEM_LIMIT = 56 * 1024 * 1024


def inverse_rms(values):
    return lax.rsqrt(jnp.mean(values * values, axis=-1, keepdims=True) + EPSILON)


def silu_slope(values):
    sigma = jax.nn.sigmoid(values)
    return sigma * (1.0 + values * (1.0 - sigma))


def adamw_update(master, first, second, gradient, count, rate, decay):
    first_new = BETA_ONE * first + (1.0 - BETA_ONE) * gradient
    second_new = BETA_TWO * second + (1.0 - BETA_TWO) * gradient * gradient
    first_hat = first_new / (1.0 - BETA_ONE**count)
    second_hat = second_new / (1.0 - BETA_TWO**count)
    master_new = master - rate * (
        first_hat / (jnp.sqrt(second_hat) + ADAM_EPSILON) + decay * master
    )
    return (master_new, first_new, second_new)


def partner_swap(value):
    return lax.ppermute(value, "mp", [(0, 1), (1, 0)])


def mp_sum(part):
    low = part.astype(BF)
    if lax.axis_size("mp") == 2:
        return low.astype(F32) + partner_swap(low).astype(F32)
    return lax.psum(low.astype(F32), "mp")


def mp_sum_wide(part):
    if lax.axis_size("mp") == 2:
        return part + partner_swap(part)
    return lax.psum(part, "mp")


def mp_scatter(part):
    if lax.axis_size("mp") == 2:
        half = part.shape[1] // 2
        place = lax.axis_index("mp")
        own = lax.dynamic_slice_in_dim(part, place * half, half, 1)
        other = lax.dynamic_slice_in_dim(part, (1 - place) * half, half, 1)
        return own.astype(BF).astype(F32) + partner_swap(other.astype(BF)).astype(F32)
    return lax.psum_scatter(part.astype(BF), "mp", scatter_dimension=1, tiled=True).astype(F32)


def mp_swap(pieces):
    if lax.axis_size("mp") == 2:
        place = lax.axis_index("mp")
        own = lax.dynamic_index_in_dim(pieces, place, 0, keepdims=False)
        came = partner_swap(lax.dynamic_index_in_dim(pieces, 1 - place, 0, keepdims=False))
        first = place == 0
        return jnp.stack([jnp.where(first, own, came), jnp.where(first, came, own)])
    return lax.all_to_all(pieces, "mp", 0, 0, tiled=False)


def mp_gather(part):
    if lax.axis_size("mp") == 2:
        place = lax.axis_index("mp")
        came = partner_swap(part)
        first = place == 0
        return jnp.concatenate([jnp.where(first, part, came), jnp.where(first, came, part)], axis=1)
    return lax.all_gather(part, "mp", axis=1, tiled=True)


SUB_ROWS = 8
TILE_ROWS = 16


def channel_block(width):
    return 256 if width % 256 == 0 else width


def scan_rows(total, decay, carry):
    row = lax.broadcasted_iota(jnp.int32, total.shape, 0)
    shift = 1
    while shift < SUB_ROWS:
        keep = row >= shift
        total = total + decay * jnp.where(keep, pltpu.roll(total, shift, 0), 0.0)
        decay = decay * jnp.where(keep, pltpu.roll(decay, shift, 0), 1.0)
        shift *= 2
    return total + decay * carry


def scan_rows_back(total, decay, carry):
    row = lax.broadcasted_iota(jnp.int32, total.shape, 0)
    shift = 1
    while shift < SUB_ROWS:
        keep = row < SUB_ROWS - shift
        total = total + decay * jnp.where(keep, pltpu.roll(total, SUB_ROWS - shift, 0), 0.0)
        decay = decay * jnp.where(keep, pltpu.roll(decay, SUB_ROWS - shift, 0), 1.0)
        shift *= 2
    return total + decay * carry


def scan_forward_kernel(pre_ref, bound_ref, gain_ref, states_ref, raw_ref, square_ref):
    length, width = states_ref.shape[1], states_ref.shape[2]
    bound = bound_ref[...]
    gain = gain_ref[...]
    first_block = pl.program_id(1) == 0

    def step(index, carry):
        rows = pl.ds(pl.multiple_of(index * TILE_ROWS, TILE_ROWS), TILE_ROWS)
        forget = bound + (1.0 - bound) * jax.nn.sigmoid(pre_ref[1, 0, rows, :])
        total = (1.0 - forget) * jax.nn.silu(pre_ref[0, 0, rows, :])
        parts = []
        for low in range(0, TILE_ROWS, SUB_ROWS):
            part = scan_rows(total[low : low + SUB_ROWS], forget[low : low + SUB_ROWS], carry)
            carry = part[SUB_ROWS - 1 : SUB_ROWS]
            parts.append(part)
        states = jnp.concatenate(parts)
        states_ref[0, rows, :] = states
        raw = states * gain * jax.nn.silu(pre_ref[2, 0, rows, :])
        raw_ref[0, rows, :] = raw.astype(raw_ref.dtype)
        square = jnp.sum(states * states, axis=-1, keepdims=True)
        square_ref[0, rows, :] = square + jnp.where(first_block, 0.0, square_ref[0, rows, :])
        return carry

    lax.fori_loop(0, length // TILE_ROWS, step, jnp.zeros((1, width), F32))


def scan_forward(pre, bound, gain):
    _, batches, length, width = pre.shape
    block = channel_block(width)
    return pl.pallas_call(
        scan_forward_kernel,
        grid=(batches, width // block),
        in_specs=[
            pl.BlockSpec((3, 1, length, block), lambda b, c: (0, b, 0, c)),
            pl.BlockSpec((1, block), lambda b, c: (0, c)),
            pl.BlockSpec((1, block), lambda b, c: (0, c)),
        ],
        out_specs=[
            pl.BlockSpec((1, length, block), lambda b, c: (b, 0, c)),
            pl.BlockSpec((1, length, block), lambda b, c: (b, 0, c)),
            pl.BlockSpec((1, length, 1), lambda b, c: (b, 0, 0)),
        ],
        out_shape=[
            jax.ShapeDtypeStruct((batches, length, width), F32),
            jax.ShapeDtypeStruct((batches, length, width), BF),
            jax.ShapeDtypeStruct((batches, length, 1), F32),
        ],
        compiler_params=pltpu.CompilerParams(vmem_limit_bytes=VMEM_LIMIT),
        cost_estimate=pl.CostEstimate(
            flops=batches * length * width * 40,
            bytes_accessed=batches * length * width * 18,
            transcendentals=batches * length * width * 3,
        ),
    )(pre, bound[None], gain[None])


def scan_backward_kernel(
    pre_ref, states_ref, gated_ref, inverse_ref, mean_ref, bound_ref, gain_ref,
    grad_ref, out_ref, gain_grad_ref, dot_ref,
):
    length, width = states_ref.shape[1], states_ref.shape[2]
    bound = bound_ref[...]
    gain = gain_ref[...]
    first_block = pl.program_id(1) == 0
    row = lax.broadcasted_iota(jnp.int32, (TILE_ROWS, width), 0)
    tiles = length // TILE_ROWS

    def step(index, carry):
        carried_next, forget_next, gain_sum = carry
        place = tiles - 1 - index
        rows = pl.ds(pl.multiple_of(place * TILE_ROWS, TILE_ROWS), TILE_ROWS)
        pre_input = pre_ref[0, 0, rows, :]
        pre_forget = pre_ref[1, 0, rows, :]
        pre_gate = pre_ref[2, 0, rows, :]
        states = states_ref[0, rows, :]
        inverse = inverse_ref[0, rows, :]
        grad_gated = gated_ref[0, rows, :]
        unit = states * inverse
        gate_sig = jax.nn.sigmoid(pre_gate)
        gate = pre_gate * gate_sig
        out_ref[0, rows, :] = (unit * gain * gate).astype(out_ref.dtype)
        gain_sum = gain_sum + grad_gated * unit * gate
        scaled = grad_gated * gain
        grad_gate = (scaled * unit * (gate_sig * (1.0 + pre_gate * (1.0 - gate_sig)))).astype(BF)
        grad_ref[2, 0, rows, :] = grad_gate
        total = inverse * (scaled * gate - unit * mean_ref[0, rows, :])
        sigma = jax.nn.sigmoid(pre_forget)
        forget = bound + (1.0 - bound) * sigma
        decay = jnp.where(row == TILE_ROWS - 1, forget_next, pltpu.roll(forget, TILE_ROWS - 1, 0))
        parts = []
        for low in range(TILE_ROWS - SUB_ROWS, -1, -SUB_ROWS):
            part = scan_rows_back(
                total[low : low + SUB_ROWS], decay[low : low + SUB_ROWS], carried_next
            )
            carried_next = part[0:1]
            parts.insert(0, part)
        carried = jnp.concatenate(parts)
        before_rows = pl.ds(
            pl.multiple_of(jnp.maximum(place - 1, 0) * TILE_ROWS, TILE_ROWS), TILE_ROWS
        )
        before = states_ref[0, before_rows, :][TILE_ROWS - 1 : TILE_ROWS, :]
        before = jnp.where(place == 0, 0.0, before)
        earlier = jnp.where(row == 0, before, pltpu.roll(states, 1, 0))
        input_sig = jax.nn.sigmoid(pre_input)
        fresh = pre_input * input_sig
        slope = input_sig * (1.0 + pre_input * (1.0 - input_sig))
        grad_input = (carried * (1.0 - forget) * slope).astype(BF)
        grad_forget = (
            carried * (earlier - fresh) * (1.0 - bound) * sigma * (1.0 - sigma)
        ).astype(BF)
        grad_ref[0, 0, rows, :] = grad_input
        grad_ref[1, 0, rows, :] = grad_forget
        dots = (
            grad_input.astype(F32) * pre_input
            + grad_forget.astype(F32) * pre_forget
            + grad_gate.astype(F32) * pre_gate
        )
        dot = jnp.sum(dots, axis=-1, keepdims=True)
        dot_ref[0, rows, :] = dot + jnp.where(first_block, 0.0, dot_ref[0, rows, :])
        return carried_next, forget[0:1, :], gain_sum

    zero = jnp.zeros((1, width), F32)
    _, _, gain_sum = lax.fori_loop(
        0, tiles, step, (zero, zero, jnp.zeros((TILE_ROWS, width), F32))
    )
    gain_grad_ref[0] = jnp.sum(gain_sum, axis=0, keepdims=True)


def scan_backward(pre, states, grad_gated, inverse, mean, bound, gain):
    _, batches, length, width = pre.shape
    block = channel_block(width)
    whole = pl.BlockSpec((1, length, block), lambda b, c: (b, 0, c))
    column = pl.BlockSpec((1, length, 1), lambda b, c: (b, 0, 0))
    line = pl.BlockSpec((1, block), lambda b, c: (0, c))
    three = pl.BlockSpec((3, 1, length, block), lambda b, c: (0, b, 0, c))
    return pl.pallas_call(
        scan_backward_kernel,
        grid=(batches, width // block),
        in_specs=[three, whole, whole, column, column, line, line],
        out_specs=[
            three,
            whole,
            pl.BlockSpec((1, 1, block), lambda b, c: (b, 0, c)),
            column,
        ],
        out_shape=[
            jax.ShapeDtypeStruct((3, batches, length, width), BF),
            jax.ShapeDtypeStruct((batches, length, width), BF),
            jax.ShapeDtypeStruct((batches, 1, width), F32),
            jax.ShapeDtypeStruct((batches, length, 1), F32),
        ],
        compiler_params=pltpu.CompilerParams(vmem_limit_bytes=VMEM_LIMIT),
        cost_estimate=pl.CostEstimate(
            flops=batches * length * width * 80,
            bytes_accessed=batches * length * width * 28,
            transcendentals=batches * length * width * 3,
        ),
    )(pre, states, grad_gated, inverse, mean, bound[None], gain[None])


def shards(
    tokens,
    cotangent,
    lengths,
    domains,
    lower_bound,
    mixer_master,
    mixer_first,
    mixer_second,
    glu_in_master,
    glu_in_first,
    glu_in_second,
    glu_out_master,
    glu_out_first,
    glu_out_second,
    gain_master,
    gain_first,
    gain_second,
):
    batches, _, length, full = tokens.shape
    rows = batches * length
    groups = lax.axis_size("dp")
    narrow = lax.axis_size("mp")
    place = lax.axis_index("mp")
    own_rows = mixer_master.shape[1]
    channels = groups * own_rows
    part = full // narrow

    domain_ids = jnp.arange(NDOM, dtype=jnp.int32)
    member = (domains[..., 0][..., None] == domain_ids).astype(F32)
    live_counts = lengths.astype(F32)
    counts = lax.psum(jnp.sum(member * live_counts[..., None], axis=(0, 1)), "dp")
    seq_weight = jnp.sum(counts) / (NDOM * jnp.sum(member * counts, axis=-1))
    positions = jnp.arange(length, dtype=jnp.int32)
    token_weight = jnp.where(positions[None, :] < lengths[:, :1], seq_weight[:, :1], 0.0)
    token_weight = token_weight.reshape(rows, 1)

    gain_full = lax.all_gather(gain_master.astype(BF), ("dp", "mp"), axis=1, tiled=True).astype(F32)
    mixer_low = mixer_master.astype(BF)
    in_blocks = mixer_low[:3].reshape(3, own_rows, groups, narrow, own_rows)
    in_blocks = in_blocks.transpose(3, 0, 1, 2, 4).reshape(narrow, 3, own_rows, channels)
    in_rows = mp_swap(in_blocks).transpose(1, 0, 2, 3).reshape(3, narrow * own_rows, channels)
    mixer_in = lax.all_gather(in_rows, "dp", axis=1, tiled=True)
    mixer_out = lax.all_gather(mixer_low[3], "dp", axis=0, tiled=True)
    glu_low = jnp.concatenate([glu_in_master.astype(BF), glu_out_master.astype(BF).T[None]])
    glu_low, _ = lax.optimization_barrier((glu_low, mixer_in))
    glu = lax.all_gather(glu_low, "dp", axis=1, tiled=True)

    own_channels = lambda v: lax.dynamic_index_in_dim(
        v.reshape(groups, narrow, own_rows), place, 1, keepdims=False
    ).reshape(channels)
    bound = own_channels(lower_bound)
    state_gain = own_channels(gain_full[1])

    seq_in = tokens.reshape(rows, full).astype(F32)
    inverse_in = inverse_rms(seq_in)
    unit_in = seq_in * inverse_in
    normed_in = (unit_in * gain_full[0]).astype(BF)
    pre = jnp.einsum("td,kde->kte", normed_in, mixer_in, preferred_element_type=F32)
    pre = pre.reshape(3, batches, length, channels)
    states, raw, square = scan_forward(pre, bound, state_gain)
    square = mp_sum_wide(square.reshape(rows, 1))
    inverse_state = lax.rsqrt(square / full + EPSILON)
    mixed = jnp.dot(raw.reshape(rows, channels), mixer_out, preferred_element_type=F32)
    branch_mix = inverse_state * mp_sum(mixed)
    middle = seq_in + branch_mix
    inverse_mid = inverse_rms(middle)
    unit_mid = middle * inverse_mid
    normed_mid = (unit_mid * gain_full[2]).astype(BF)

    cot_full = mp_gather(cotangent.reshape(rows, part))
    back = cot_full.astype(F32) * token_weight
    back_low = back.astype(BF)
    pre_act = jnp.dot(normed_mid, glu[0], preferred_element_type=F32)
    pre_up = jnp.dot(normed_mid, glu[1], preferred_element_type=F32)
    grad_hidden = jnp.dot(back_low, glu[2], preferred_element_type=F32)
    act_sig = jax.nn.sigmoid(pre_act)
    act_part = pre_act * act_sig
    hidden = (act_part * pre_up).astype(BF)
    grad_act = (grad_hidden * pre_up * silu_slope(pre_act)).astype(BF)
    grad_up = (grad_hidden * act_part).astype(BF)
    across = (((1,), (1,)), ((), ()))
    down = (((0,), (0,)), ((), ()))
    dot = functools.partial(lax.dot_general, preferred_element_type=F32)
    grad_normed_part = dot(grad_act, glu[0], across) + dot(grad_up, glu[1], across)
    grad_normed = mp_sum(grad_normed_part)
    partial_out = dot(hidden, glu[2], across)
    glu_grad = jnp.stack(
        [
            dot(normed_mid, grad_act, down).astype(BF),
            dot(normed_mid, grad_up, down).astype(BF),
            dot(back_low, hidden, down).astype(BF),
        ]
    )
    glu_own = lax.psum_scatter(glu_grad, "dp", scatter_dimension=1, tiled=True).astype(F32)
    middle_own = lax.dynamic_slice_in_dim(middle, place * part, part, 1)
    layer_out = (middle_own + mp_scatter(partial_out)).astype(BF)

    gain_mid = jnp.sum(grad_normed * unit_mid, axis=0)
    scaled_mid = grad_normed * gain_full[2]
    grad_middle = back + inverse_mid * (
        scaled_mid - unit_mid * jnp.mean(scaled_mid * unit_mid, axis=-1, keepdims=True)
    )
    middle_low = grad_middle.astype(BF)
    state_mean = jnp.mean(middle_low.astype(F32) * branch_mix, axis=-1, keepdims=True)
    grad_gated = dot(middle_low, mixer_out, across)
    by_batch = lambda v: v.reshape(batches, length, v.shape[-1])
    grad_pre, gated_out, gain_state, pre_dot = scan_backward(
        pre, states, by_batch(grad_gated), by_batch(inverse_state), by_batch(state_mean), bound, state_gain
    )
    grad_pre = grad_pre.reshape(3, rows, channels)
    grad_mix_out = dot(gated_out.reshape(rows, channels), middle_low, down).astype(BF)
    grad_mix_in = jnp.einsum("td,kte->kde", normed_in, grad_pre, preferred_element_type=F32).astype(BF)
    in_own = lax.psum_scatter(grad_mix_in, "dp", scatter_dimension=1, tiled=True)
    out_own = lax.psum_scatter(grad_mix_out, "dp", scatter_dimension=0, tiled=True)
    in_own = mp_swap(in_own.reshape(3, narrow, own_rows, channels).transpose(1, 0, 2, 3))
    in_own = in_own.reshape(narrow, 3, own_rows, groups, own_rows).transpose(1, 2, 3, 0, 4)
    mixer_own = jnp.concatenate([in_own.reshape(3, own_rows, full), out_own[None]]).astype(F32)

    grad_normed_in = jnp.einsum("kte,kde->td", grad_pre, mixer_in, preferred_element_type=F32)
    grad_normed_in = mp_scatter(grad_normed_in)
    in_mean = mp_sum_wide(pre_dot.reshape(rows, 1)) / full
    own_features = lambda v: lax.dynamic_slice_in_dim(v, place * part, part, v.ndim - 1)
    unit_in_own = own_features(unit_in)
    gain_in = jnp.sum(grad_normed_in * unit_in_own, axis=0)
    grad_seq = own_features(grad_middle) + inverse_in * (
        grad_normed_in * own_features(gain_full[0]) - unit_in_own * in_mean
    )
    grad_tokens = grad_seq.astype(BF)

    zeros = jnp.zeros((full,), F32)
    gain_rows = jnp.stack(
        [
            lax.dynamic_update_slice_in_dim(zeros, gain_in, place * part, 0),
            lax.dynamic_update_slice_in_dim(
                zeros.reshape(groups, narrow, own_rows),
                jnp.sum(gain_state, axis=0).reshape(groups, 1, own_rows),
                place,
                1,
            ).reshape(full),
            lax.dynamic_update_slice_in_dim(zeros, own_features(gain_mid), place * part, 0),
        ]
    )
    gain_total = lax.psum(gain_rows, ("dp", "mp"))
    device = lax.axis_index("dp") * narrow + place
    gain_own = lax.dynamic_slice_in_dim(gain_total, device * own_rows, own_rows, 1)

    scale = 1.0 / (batches * groups * tokens.shape[1])
    count = STEP_NUMBER
    update = functools.partial(adamw_update, count=count)
    mixer_new = update(
        mixer_master, mixer_first, mixer_second, mixer_own * scale, rate=MATRIX_RATE, decay=DECAY_RATE
    )
    gain_new = update(
        gain_master, gain_first, gain_second, gain_own * scale, rate=GAIN_RATE, decay=0.0
    )
    glu_in_new = update(
        glu_in_master, glu_in_first, glu_in_second, glu_own[:2] * scale, rate=MATRIX_RATE, decay=DECAY_RATE
    )
    glu_out_new = update(
        glu_out_master, glu_out_first, glu_out_second, glu_own[2].T * scale, rate=MATRIX_RATE, decay=DECAY_RATE
    )
    return (
        layer_out.reshape(batches, 1, length, part),
        grad_tokens.reshape(batches, 1, length, part),
        *mixer_new,
        *glu_in_new,
        *glu_out_new,
        *gain_new,
    )


def solution(mesh):
    weights = (
        [P(None, ("dp", "mp"), None)] * 3
        + [P(None, "dp", "mp")] * 3
        + [P("mp", "dp")] * 3
        + [P(None, ("dp", "mp"))] * 3
    )
    in_specs = (
        P(None, "dp", None, None),
        P(None, "dp", None, "mp"),
        P(None, "dp"),
        P(None, "dp", None),
        P(),
        *weights,
    )
    out_specs = (P(None, "dp", None, "mp"), P(None, "dp", None, "mp"), *weights)
    return jax.shard_map(shards, mesh=mesh, in_specs=in_specs, out_specs=out_specs, check_vma=False)
```

time: 2010 us -> 1290 us (0.64)
  local copies, waits for them, and re-layouts: 851 us -> 95.6 us
  waiting for transfers between devices: 376 us -> 596 us
  matrix products: 399 us -> 241 us
  other arithmetic: 236 us -> 109 us
  Pallas kernels: 0 us -> 70.2 us
  blocking collectives: 103 us -> 141 us
    slice x214 -> x3, local copies, waits for them, and re-layouts: 547 us -> 1.89 us  [the longest x1 1.79 us: shards(): mixer_out = lax.all_gather(mixer_low[3], 'dp', axis=0, tiled=True)]
    unnamed x15 -> x7, waiting for transfers between devices: 223 us -> 0.12 us
    reduce_scatter x3 -> x2, waiting for transfers between devices: 72.7 us -> 290 us  [the longest x1 290 us: shards(): lax.psum_scatter(glu_grad, 'dp', scatter_dimension=1, tiled=True)]
    ppermute x0 -> x9, waiting for transfers between devices: none -> 212 us  [partner_swap(): return lax.ppermute(value, 'mp', [(0, 1), (1, 0)])]
    dot_general x24 -> x15, matrix products: 399 us -> 241 us  [the longest x1 23.1 us: shards(): grad_hidden = jnp.dot(back_low, glu[2], preferred_element_type=F32)]
    pad x60 -> x0, local copies, waits for them, and re-layouts: 94.9 us -> none  [the longest x30 48.9 us: micro_batch(): lax.associative_scan(linear_pair, (forget, (1.0 - forget) * fresh_input),...]
    pallas_call x0 -> x2, Pallas kernels: none -> 70.2 us  [the longest x1 43.6 us: scan_backward(): pl.pallas_call(scan_backward_kernel, grid=(batches, width // block), in_s...]
    unnamed x326 -> x101, local copies, waits for them, and re-layouts: 140 us -> 70.1 us
  transfers between devices with their start and end apart: 12 -> 15, of which waited for: 3 -> 7; matrix products, arithmetic and copies ran while one was open for 71% -> 18% of each run, Pallas kernels for 0% -> 2%
where the time goes in v1:
time: 1290 us; the launch traced here: 1280 us
  waiting for transfers between devices  596 us (46%)
  matrix products  241 us (19%)
  blocking collectives  141 us (11%)
  other arithmetic  109 us (8%)
  local copies, waits for them, and re-layouts  95.6 us (7%)
  Pallas kernels  70.2 us (5%)
  between operations  15.2 us (1%)
    reduce_scatter x1, waiting for transfers between devices, shards(): lax.psum_scatter(glu_grad, 'dp', scatter_dimension=1, tiled=True)  290 us
    ppermute x9, waiting for transfers between devices, partner_swap(): return lax.ppermute(value, 'mp', [(0, 1), (1, 0)])  212 us
    all_gather x1, waiting for transfers between devices, shards(): mixer_in = lax.all_gather(in_rows, 'dp', axis=1, tiled=True)  93.3 us
    unnamed x101, local copies, waits for them, and re-layouts  70.1 us
    all_gather x1, blocking collectives, shards(): lax.all_gather(gain_master.astype(BF), ('dp', 'mp'), axis=1, tiled=True)  65.9 us
    psum x1, blocking collectives, shards(): gain_total = lax.psum(gain_rows, ('dp', 'mp'))  44.6 us
    pallas_call x1, Pallas kernels, scan_backward(): pl.pallas_call(scan_backward_kernel, grid=(batches, width // block), in_s...  43.6 us
    psum x1, blocking collectives, shards(): lax.psum(jnp.sum(member * live_counts[..., None], axis=(0, 1)), 'dp')  30.8 us
  transfers between devices with their start and end apart: 15, of which 7 were waited for; matrix products, arithmetic and copies ran while one was open for 18% of the time, Pallas kernels for 2%

profile of v1, /device:TPU:0, one launch (start us, length us, event | category | flops | bytes accessed | tf_op | source)
XLA Modules:
  0.0 1276.9 jit_solution(3026931273783919777)
XLA Ops:
  16.1 9.1 collective-permute-done
  35.3 93.3 %all-gather.6.cloned.1.call-done = bf16[3,2048,1024]{2,1,0:T(8,128)(2,1)} async-done(((bf16[3,128,1024]{2,1,0:T(8,128)(2,1)}), bf16[3,2048,1024]{2,1,0:T(8,128)(2,1)}) %all-gather.6.cloned.1.call-update) | async-done | bytes 12582928 | tf_op jit(solution)/shard_map/all_gather | solution.py:324
  132.2 65.9 %all-gather.1 = bf16[32,64,3]{1,2,0:T(4,128)(2,1)S(1)} all-gather(bf16[1,64,3]{1,2,0:T(4,128)(2,1)S(1)} %convert_bitcast_fusion.5), channel_id=1, replica_groups=mesh['dp'=16,'mp'=2] {'dp','mp'}, dimensions={0}, use_global_device_ids=true | all-gather | bytes 12672 | tf_op jit(solution)/shard_map/all_gather | solution.py:319
  202.4 18.7 %fusion.17 = f32[3,1024,896]{1,2,0:T(8,128)} fusion(bf16[3,2048,1024]{2,1,0:T(8,128)(2,1)} %all-gather.6.cloned.1.call-done, f32[896,2048]{1,0:T(8,128)S(1)} %bitcast_multiply_fusion, f32[2048]{0:T(1024)S(1)} %bitcast.164), kind=kOutput, calls=%fused_computation.46 | convolution fusion | flops 11277959168 | bytes 30941184 | tf_op jit(solution)/shard_map/td,kde->kte/dot_general | solution.py:340
  221.1 26.6 %shard_map.272 = (f32[2,448,1024]{2,1,0:T(8,128)}, bf16[2,448,1024]{2,1,0:T(8,128)(2,1)}, f32[2,448,1]{2,1,0:T(8,128)}) custom-call(f32[3,2,448,1024]{3,2,1,0:T(8,128)} %bitcast.147, f32[1,1024]{1,0:T(1,128)} %broadcast_in_dim_reshape.8.bound_ref, f32[1,1024]{1,0:T(1,128)} %broadcast_in_dim_reshape.9.gain_ref), custom_call_target="tpu_custom_call" | custom-call | flops 36700160 | bytes 16515072 | tf_op jit(solution)/shard_map/pallas_call | solution.py:151
  247.7 8.9 fusion.20
  258.8 30.8 %psum.14 = f32[8]{0:T(128)S(1)} all-reduce(f32[8]{0:T(128)S(1)} %select_reduce_fusion.1), channel_id=1, replica_groups=mesh['dp'=16,'mp'=2] {'dp'}, use_global_device_ids=true, to_apply=%region_3.0 | all-reduce | flops 8 | bytes 64 | tf_op jit(solution)/shard_map/psum | solution.py:313
  291.8 83.3 %collective-permute-done.4 = bf16[896,1024]{1,0:T(8,128)(2,1)} collective-permute-done((bf16[896,1024]{1,0:T(8,128)(2,1)S(1)}, bf16[896,1024]{1,0:T(8,128)(2,1)}, u32[]{:S(2)}, u32[]{:S(2)}) %collective-permute-start.4) | collective-permute-done | bytes 1835040 | tf_op jit(solution)/shard_map/ppermute | solution.py:47
  390.0 19.3 %fusion.1 = f32[896,2816]{1,0:T(8,128)} fusion(bf16[896,2048]{1,0:T(8,128)(2,1)} %multiply_convert_fusion.3, bf16[3,2048,2816]{2,1,0:T(8,128)(2,1)} %all-gather.8.cloned.1.call-done), kind=kOutput, calls=%fused_computation.9 | convolution fusion | flops 10334765056 | bytes 25296896 | tf_op jit(solution)/shard_map/dot_general | solution.py:355
  409.2 16.8 %fusion.3 = f32[896,2816]{1,0:T(8,128)} fusion(bf16[896,2048]{1,0:T(8,128)(2,1)S(1)} %copy-done.18, bf16[3,2048,2816]{2,1,0:T(8,128)(2,1)} %all-gather.8.cloned.1.call-done), kind=kOutput, calls=%fused_computation.11 | convolution fusion | flops 10334765056 | bytes 25296896 | tf_op jit(solution)/shard_map/dot_general | solution.py:356
  426.0 23.1 %multiply_convert_fusion = (bf16[896,2816]{1,0:T(8,128)(2,1)}, bf16[896,2816]{1,0:T(8,128)(2,1)}, bf16[896,2816]{1,0:T(8,128)(2,1)}) fusion(f32[896,2816]{1,0:T(8,128)} %fusion.1, f32[896,2816]{1,0:T(8,128)} %fusion.3, bf16[3,2048,2816]{2,1,0:T(8,128)(2,1)} %all-gather.8.cloned.1.call-done, f32[896]{0:T(1024)S(1)} %select_n.85, ...), kind=kOutput, calls=%fused_computation.14 | convolution fusion | flops 10383622144 | bytes 50531840 | tf_op jit(solution)/shard_map/dot_general | solution.py:357
  449.0 14.9 %fusion = f32[896,2048]{1,0:T(8,128)S(1)} fusion(bf16[896,2816]{1,0:T(8,128)(2,1)} %get-tuple-element.119, bf16[3,2048,2816]{2,1,0:T(8,128)(2,1)} %all-gather.8.cloned.1.call-done), kind=kOutput, calls=%fused_computation.8 | convolution fusion | flops 10334765056 | bytes 23920640 | tf_op jit(solution)/shard_map/dot_general | solution.py:366
  464.0 16.4 %add_convert_fusion = bf16[896,2048]{1,0:T(8,128)(2,1)} fusion(f32[896,2048]{1,0:T(8,128)S(1)} %fusion, bf16[896,2816]{1,0:T(8,128)(2,1)} %get-tuple-element.118, bf16[3,2048,2816]{2,1,0:T(8,128)(2,1)} %all-gather.8.cloned.1.call-done), kind=kOutput, calls=%fused_computation.31 | convolution fusion | flops 10338435072 | bytes 27590656 | tf_op jit(solution)/shard_map/dot_general | solution.py:366
  484.5 74.0 %collective-permute-done.5 = bf16[896,2048]{1,0:T(8,128)(2,1)} collective-permute-done((bf16[896,2048]{1,0:T(8,128)(2,1)}, bf16[896,2048]{1,0:T(8,128)(2,1)}, u32[]{:S(2)}, u32[]{:S(2)}) %collective-permute-start.5) | collective-permute-done | bytes 3670048 | tf_op jit(solution)/shard_map/ppermute | solution.py:47
  558.5 7.1 multiply_reduce_fusion
  565.7 10.6 multiply_reduce_fusion.1
  577.3 10.0 fusion.12
  587.4 43.6 %shard_map.273 = (bf16[3,2,448,1024]{3,2,1,0:T(8,128)(2,1)}, bf16[2,448,1024]{2,1,0:T(8,128)(2,1)}, f32[2,1,1024]{2,1,0:T(1,128)}, f32[2,448,1]{2,1,0:T(8,128)}) custom-call(f32[3,2,448,1024]{3,2,1,0:T(8,128)} %bitcast.148, f32[2,448,1024]{2,1,0:T(8,128)} %get-tuple-element.25.states_ref, f32[2,448,1024]{2,1,0:T(8,128)} %bitcast.152, ...), custom_call_target="tpu_custom_call" | custom-call | flops 73400320 | bytes 25690112 | tf_op jit(solution)/shard_map/pallas_call | solution.py:257
  631.0 18.2 %convert_bitcast_fusion = bf16[3,2048,1024]{1,2,0:T(8,128)(2,1)} fusion(bf16[3,896,1024]{2,1,0:T(8,128)(2,1)} %bitcast.170, bf16[896,2048,1]{1,0,2:T(8,128)(2,1)S(1)} %bitcast.151), kind=kOutput, calls=%fused_computation.1 | convolution fusion | flops 11280580608 | bytes 21757952 | tf_op jit(solution)/shard_map/td,kte->kde/dot_general | solution.py:394
  649.2 27.5 %copy.124 = bf16[3,2048,1024]{2,0,1:T(4,128)(2,1)} copy(bf16[3,2048,1024]{1,2,0:T(8,128)(2,1)} %convert_bitcast_fusion) | data formatting | bytes 25165824
  676.7 16.1 %copy.127 = bf16[256,8,3,1024]{3,1,2,0:T(8,128)(2,1)} copy(bf16[256,8,3,1024]{3,2,1,0:T(4,128)(2,1)} %bitcast.145) | data formatting | bytes 25165824
  692.9 18.9 %convert_bitcast_fusion.2 = bf16[1,2048,2816]{2,1,0:T(8,128)(2,1)} fusion(bf16[896,2048]{1,0:T(8,128)(2,1)} %multiply_convert_fusion.3, bf16[896,2816]{1,0:T(8,128)(2,1)} %get-tuple-element.118), kind=kOutput, calls=%fused_computation.6 | convolution fusion | flops 10340532224 | bytes 20250624 | tf_op jit(solution)/shard_map/dot_general | solution.py:372
  711.9 9.9 convolution_convert_fusion
  723.3 19.3 %convert_bitcast_fusion.1 = bf16[1,2048,2816]{2,1,0:T(8,128)(2,1)} fusion(bf16[896,2816]{1,0:T(8,128)(2,1)} %get-tuple-element.120, f32[896]{0:T(1024)S(1)} %select_n.85, bf16[896,1024]{1,0:T(8,128)(2,1)} %get-tuple-element.124, bf16[896,1024]{1,0:T(8,128)(2,1)S(1)} %copy-done.10), kind=kOutput, calls=%fused_computation.5 | convolution fusion | flops 10351542272 | bytes 20254208 | tf_op jit(solution)/shard_map/dot_general | solution.py:373
  742.6 16.9 %convert_bitcast_fusion.3 = bf16[1,2048,2816]{2,1,0:T(8,128)(2,1)} fusion(bf16[896,2048]{1,0:T(8,128)(2,1)S(1)} %copy-done.19, bf16[896,2816]{1,0:T(8,128)(2,1)} %get-tuple-element.119), kind=kOutput, calls=%fused_computation.7 | convolution fusion | flops 10340532224 | bytes 20250624 | tf_op jit(solution)/shard_map/dot_general | solution.py:371
  759.5 23.8 %pad_maximum_fusion = bf16[3,2048,2816]{2,1,0:T(8,128)(2,1)} fusion(bf16[1,2048,2816]{2,1,0:T(8,128)(2,1)} %convert_bitcast_fusion.1, bf16[1,2048,2816]{2,1,0:T(8,128)(2,1)} %convert_bitcast_fusion.2, bf16[1,2048,2816]{2,1,0:T(8,128)(2,1)} %convert_bitcast_fusion.3), kind=kLoop, calls=%fused_computation | loop fusion | flops 34603008 | bytes 69206016 | tf_op jit(solution)/shard_map/stack | solution.py:369
  783.4 15.3 %fusion.5 = bf16[896,2048]{1,0:T(8,128)(2,1)S(1)} fusion(bf16[896,2816]{1,0:T(8,128)(2,1)} %get-tuple-element.120, bf16[3,2048,2816]{2,1,0:T(8,128)(2,1)} %all-gather.8.cloned.1.call-done), kind=kOutput, calls=%fused_computation.13 | convolution fusion | flops 10334765056 | bytes 20250624 | tf_op jit(solution)/shard_map/dot_general | solution.py:368
  801.1 14.6 %convolution_bitcast_fusion = bf16[896,2048]{1,0:T(8,128)(2,1)S(1)} fusion(bf16[3,896,1024]{2,1,0:T(8,128)(2,1)S(1)} %bitcast.173, bf16[3,2048,1024]{2,1,0:T(8,128)(2,1)} %all-gather.6.cloned.1.call-done), kind=kOutput, calls=%fused_computation.43 | convolution fusion | flops 11274289152 | bytes 21757952 | tf_op jit(solution)/shard_map/kte,kde->td/dot_general | solution.py:401
  826.1 18.3 %collective-permute-done.3 = bf16[896,1024]{1,0:T(8,128)(2,1)} collective-permute-done((bf16[896,1024]{1,0:T(8,128)(2,1)}, bf16[896,1024]{1,0:T(8,128)(2,1)}, u32[]{:S(2)}, u32[]{:S(2)}) %collective-permute-start.3) | collective-permute-done | bytes 1835040 | tf_op jit(solution)/shard_map/ppermute | solution.py:47
  850.8 27.0 %collective-permute-done.7 = f32[896,1]{0,1:T(1,128)S(1)} collective-permute-done((f32[896,1]{0,1:T(1,128)S(1)}, f32[896,1]{0,1:T(1,128)S(1)}, u32[]{:S(2)}, u32[]{:S(2)}) %collective-permute-start.7) | collective-permute-done | bytes 3616 | tf_op jit(solution)/shard_map/ppermute | solution.py:47
  887.7 44.6 %psum.15 = f32[3,2048]{1,0:T(4,128)S(1)} all-reduce(f32[3,2048]{1,0:T(4,128)S(1)} %pad_maximum_fusion.5), channel_id=1, replica_groups=mesh['dp'=16,'mp'=2] {'dp','mp'}, use_global_device_ids=true, to_apply=%region_14.15 | all-reduce | flops 6144 | bytes 49152 | tf_op jit(solution)/shard_map/psum | solution.py:425
  958.4 290.5 %reduce-scatter.8.cloned.1.call-done = bf16[3,128,2816]{2,1,0:T(8,128)(2,1)} async-done(((bf16[3,2048,2816]{2,1,0:T(8,128)(2,1)}), bf16[3,128,2816]{2,1,0:T(8,128)(2,1)}) %reduce-scatter.8.cloned.1.call-update) | async-done | bytes 2162704 | tf_op jit(solution)/shard_map/reduce_scatter | solution.py:376
  (206 shorter events, 128.3 us)
Async XLA Ops:
  7.2 121.5 %all-gather.6.cloned.1.call-start = ((), (), s32[]{:S(2)}) async-start(), calls=%async_computation.3 | async-start | bytes 13369344 | tf_op jit(solution)/shard_map/all_gather | solution.py:324
  13.1 12.1 collective-permute-start
  26.3 221.4 %all-gather.10.cloned.1.call-start = ((), (), s32[]{:S(2)}) async-start(), calls=%async_computation.7 | async-start | bytes 4456448 | tf_op jit(solution)/shard_map/all_gather | solution.py:325
  28.1 361.8 %all-gather.8.cloned.1.call-start = ((), (), s32[]{:S(2)}) async-start(), calls=%async_computation.4 | async-start | bytes 36765696 | tf_op jit(solution)/shard_map/all_gather | solution.py:328
  35.3 96.3 %copy-start.35 = (f32[3,64]{1,0:T(4,128)S(1)}, f32[3,64]{1,0:T(4,128)}, u32[]{:S(2)}) copy-start(f32[3,64]{1,0:T(4,128)} %param.31) | copy-start | bytes 2308
  35.3 163.0 %copy-start.33 = (f32[2048]{0:T(1024)S(1)}, f32[2048]{0:T(1024)}, u32[]{:S(2)}) copy-start(f32[2048]{0:T(1024)} %param.21) | copy-start | bytes 24580
  128.7 755.5 %reduce-scatter.10.cloned.1.call-start = ((), (), s32[]{:S(2)}) async-start(), calls=%async_computation.8 | async-start | bytes 13369344
  131.7 70.7 %copy-start.28 = (f32[896]{0:T(1024)}, f32[896]{0:T(1024)S(1)}, u32[]{:S(2)}) copy-start(f32[896]{0:T(1024)S(1)} %rsqrt.24) | copy-start | bytes 10756
  198.2 282.5 %copy-start.26 = (f32[1,2048]{1,0:T(1,128)}, f32[1,2048]{1,0:T(1,128)S(1)}, u32[]{:S(2)}) copy-start(f32[1,2048]{1,0:T(1,128)S(1)} %get-tuple-element.131) | copy-start | bytes 24580
  247.7 43.5 %copy-start.25 = (f32[2,448,1]{2,1,0:T(8,128)S(1)}, f32[2,448,1]{2,1,0:T(8,128)}, u32[]{:S(2)}) copy-start(f32[2,448,1]{2,1,0:T(8,128)} %get-tuple-element.22) | copy-start | bytes 10756
  256.7 121.9 %collective-permute-start.2 = (bf16[896,2048]{1,0:T(8,128)(2,1)}, bf16[896,2048]{1,0:T(8,128)(2,1)}, u32[]{:S(2)}, u32[]{:S(2)}) collective-permute-start(bf16[896,2048]{1,0:T(8,128)(2,1)} %fusion.20), channel_id=1, source_target_pairs={{0,1},{1,0},{2,3},{3,2},{4,5},{5,4},{6,7},{7,6},{8,9},{9,8},{10,11... | collective-permute-start | bytes 11010056 | tf_op jit(solution)/shard_map/ppermute | solution.py:47
  257.0 118.1 %collective-permute-start.4 = (bf16[896,1024]{1,0:T(8,128)(2,1)S(1)}, bf16[896,1024]{1,0:T(8,128)(2,1)}, u32[]{:S(2)}, u32[]{:S(2)}) collective-permute-start(bf16[896,1024]{1,0:T(8,128)(2,1)S(1)} %bitcast.158), channel_id=1, source_target_pairs={{0,1},{1,0},{2,3},{3,2},{4,5},{5,4},{6,7},{7,6},{8,9},{9,8},{10,11... | collective-permute-start | bytes 5505032 | tf_op jit(solution)/shard_map/ppermute | solution.py:47
  291.5 87.1 %copy-start.1 = (bf16[2,1,448,2048]{3,2,1,0:T(8,128)(2,1)S(1)}, bf16[2,1,448,2048]{3,2,1,0:T(8,128)(2,1)}, u32[]{:S(2)}) copy-start(bf16[2,1,448,2048]{3,2,1,0:T(8,128)(2,1)} %param.17) | copy-start | bytes 11010052
  291.5 87.1 %collective-permute-start.1 = (f32[896,1]{0,1:T(1,128)S(1)}, f32[896,1]{0,1:T(1,128)S(1)}, u32[]{:S(2)}, u32[]{:S(2)}) collective-permute-start(f32[896,1]{0,1:T(1,128)S(1)} %reshape.336), channel_id=1, source_target_pairs={{0,1},{1,0},{2,3},{3,2},{4,5},{5,4},{6,7},{7,6},{8,9},{9,8},{10,11... | collective-permute-start | bytes 10760 | tf_op jit(solution)/shard_map/ppermute | solution.py:47
  378.6 47.4 %copy-start.8 = (bf16[896,1024]{1,0:T(8,128)(2,1)}, bf16[896,1024]{1,0:T(8,128)(2,1)S(1)}, u32[]{:S(2)}) copy-start(bf16[896,1024]{1,0:T(8,128)(2,1)S(1)} %get-tuple-element.123) | copy-start | bytes 5505028
  480.4 78.1 %collective-permute-start.5 = (bf16[896,2048]{1,0:T(8,128)(2,1)}, bf16[896,2048]{1,0:T(8,128)(2,1)}, u32[]{:S(2)}, u32[]{:S(2)}) collective-permute-start(bf16[896,2048]{1,0:T(8,128)(2,1)} %add_convert_fusion), channel_id=1, source_target_pairs={{0,1},{1,0},{2,3},{3,2},{4,5},{5,4},{6,7},{7,6},{8,9},{9,8},{10,11... | collective-permute-start | bytes 11010056 | tf_op jit(solution)/shard_map/ppermute | solution.py:47
  480.7 84.9 %slice-start = ((s8[7340032]{0:T(1024)(128)(4,1)}), s8[3145728]{0:T(1024)(128)(4,1)S(1)}, s32[]{:S(2)}) async-start(s8[7340032]{0:T(1024)(128)(4,1)} %bitcast.143), calls=%async_computation.9 | async-start | bytes 6291456
  484.5 81.1 %slice-start.1 = ((s8[7340032]{0:T(1024)(128)(4,1)}), s8[4194304]{0:T(1024)(128)(4,1)S(1)}, s32[]{:S(2)}) async-start(s8[7340032]{0:T(1024)(128)(4,1)} %bitcast.143), calls=%async_computation.10 | async-start | bytes 8388608
  484.5 81.1 %copy-start.9 = (bf16[896,1024]{1,0:T(8,128)(2,1)S(1)}, bf16[896,1024]{1,0:T(8,128)(2,1)}, u32[]{:S(2)}) copy-start(bf16[896,1024]{1,0:T(8,128)(2,1)} %copy-done.8) | copy-start | bytes 5505028
  484.5 81.1 %copy-start.11 = (bf16[896,1024]{1,0:T(8,128)(2,1)S(1)}, bf16[896,1024]{1,0:T(8,128)(2,1)}, u32[]{:S(2)}) copy-start(bf16[896,1024]{1,0:T(8,128)(2,1)} %get-tuple-element.124) | copy-start | bytes 5505028
  587.4 43.6 %copy-start.20 = (bf16[2,1,448,2048]{3,2,1,0:T(8,128)(2,1)S(1)}, bf16[2,1,448,2048]{3,2,1,0:T(8,128)(2,1)}, u32[]{:S(2)}) copy-start(bf16[2,1,448,2048]{3,2,1,0:T(8,128)(2,1)} %fusion.9) | copy-start | bytes 11010052
  692.9 258.6 %reduce-scatter.6.cloned.1.call-start = ((), (), s32[]{:S(2)}) async-start(), calls=%async_computation.5 | async-start | bytes 4456448 | tf_op jit(solution)/shard_map/reduce_scatter | solution.py:396
  721.8 527.1 %reduce-scatter.8.cloned.1.call-start = ((), (), s32[]{:S(2)}) async-start(), calls=%async_computation.6 | async-start | bytes 36765696 | tf_op jit(solution)/shard_map/reduce_scatter | solution.py:376
  801.1 43.3 %collective-permute-start.3 = (bf16[896,1024]{1,0:T(8,128)(2,1)}, bf16[896,1024]{1,0:T(8,128)(2,1)}, u32[]{:S(2)}, u32[]{:S(2)}) collective-permute-start(bf16[896,1024]{1,0:T(8,128)(2,1)} %dynamic-slice_convert_fusion.2), channel_id=1, source_target_pairs={{0,1},{1,0},{2,3},{3,2},{4,5},{5,4},{6,7},{7,6},{8,9},{9,8},{10,11... | collective-permute-start | bytes 5505032 | tf_op jit(solution)/shard_map/ppermute | solution.py:47
  819.1 58.7 %collective-permute-start.6 = (bf16[896,1024]{1,0:T(8,128)(2,1)}, bf16[896,1024]{1,0:T(8,128)(2,1)}, u32[]{:S(2)}, u32[]{:S(2)}) collective-permute-start(bf16[896,1024]{1,0:T(8,128)(2,1)} %dynamic-slice_convert_fusion), channel_id=1, source_target_pairs={{0,1},{1,0},{2,3},{3,2},{4,5},{5,4},{6,7},{7,6},{8,9},{9,8},{10,11... | collective-permute-start | bytes 5505032 | tf_op jit(solution)/shard_map/ppermute | solution.py:47
  826.1 51.7 %copy-start.29 = (f32[896]{0:T(1024)S(1)}, f32[896]{0:T(1024)}, u32[]{:S(2)}) copy-start(f32[896]{0:T(1024)} %copy-done.28) | copy-start | bytes 10756
  850.4 27.3 %collective-permute-start.7 = (f32[896,1]{0,1:T(1,128)S(1)}, f32[896,1]{0,1:T(1,128)S(1)}, u32[]{:S(2)}, u32[]{:S(2)}) collective-permute-start(f32[896,1]{0,1:T(1,128)S(1)} %reshape.343), channel_id=1, source_target_pairs={{0,1},{1,0},{2,3},{3,2},{4,5},{5,4},{6,7},{7,6},{8,9},{9,8},{10,11... | collective-permute-start | bytes 10760 | tf_op jit(solution)/shard_map/ppermute | solution.py:47
  884.1 48.1 %copy-start.36 = (f32[3,64]{1,0:T(4,128)S(1)}, f32[3,64]{1,0:T(4,128)}, u32[]{:S(2)}) copy-start(f32[3,64]{1,0:T(4,128)} %param.31) | copy-start | bytes 2308
  884.1 48.1 %copy-start.37 = (f32[3,64]{1,0:T(4,128)S(1)}, f32[3,64]{1,0:T(4,128)}, u32[]{:S(2)}) copy-start(f32[3,64]{1,0:T(4,128)} %param.32) | copy-start | bytes 2308
  884.1 48.1 %copy-start.38 = (f32[3,64]{1,0:T(4,128)S(1)}, f32[3,64]{1,0:T(4,128)}, u32[]{:S(2)}) copy-start(f32[3,64]{1,0:T(4,128)} %param.33) | copy-start | bytes 2308
  887.3 45.7 %collective-permute-start.8 = (bf16[3,64,1024]{2,1,0:T(8,128)(2,1)S(1)}, bf16[3,64,1024]{2,1,0:T(8,128)(2,1)}, u32[]{:S(2)}, u32[]{:S(2)}) collective-permute-start(bf16[3,64,1024]{2,1,0:T(8,128)(2,1)S(1)} %dynamic-slice_bitcast_fusion), channel_id=1, source_target_pairs={{0,1},{1,0},{2,3},{3,2},{4,5},{5,4},{6,7},{7,6},{8,9},{9,8},{10,11... | collective-permute-start | bytes 1179656 | tf_op jit(solution)/shard_map/ppermute | solution.py:47
  958.4 292.6 %copy-start.12 = (f32[2816,128]{0,1:T(8,128)S(1)}, f32[2816,128]{0,1:T(8,128)}, u32[]{:S(2)}) copy-start(f32[2816,128]{0,1:T(8,128)} %copy.114) | copy-start | bytes 4325380
  (29 other events, 306.0 us)
Sparse Core Ops, SparseCore 0:
  26.4 102.2 all-gather.5
  131.4 48.7 all-gather.9
  182.4 171.7 all-gather.7
  693.0 131.7 reduce-scatter.9
  828.5 71.5 reduce-scatter.5
  904.8 344.0 reduce-scatter.7

commit v2 on v1

--- a/solution.py
+++ b/solution.py
@@ -90,11 +90,11 @@
 
 
 SUB_ROWS = 8
-TILE_ROWS = 16
+TILE_ROWS = 64
 
 
 def channel_block(width):
-    return 256 if width % 256 == 0 else width
+    return 512 if width % 512 == 0 else width
 
 
 def scan_rows(total, decay, carry):
@@ -279,6 +279,390 @@
     )(pre, states, grad_gated, inverse, mean, bound[None], gain[None])
 
 
+MESH_ID = pl.DeviceIdType.MESH
+DEPTH = 4
+LANES = 256
+Z_LAG = 4
+
+
+def device_place():
+    dp = lax.axis_index("dp")
+    return dp // 4, lax.rem(dp // 2, 2), lax.rem(dp, 2)
+
+
+def device_at(z, x, core):
+    return (z * 4 + x * 2 + core, lax.axis_index("mp"))
+
+
+def scatter_kernel(compute, chunks, n_in, *refs):
+    ins, out_ref = refs[:n_in], refs[n_in]
+    (own, core_out, core_in, keep, x_out, x_in, sums, mine, z_out, z_in,
+     core_send, core_recv, x_send, x_recv, z_send, z_recv) = refs[n_in + 1 :]
+    z, x, core = device_place()
+    step = pl.program_id(0)
+
+    def core_copy(p):
+        return pltpu.make_async_remote_copy(
+            core_out.at[lax.rem(p, 2)], core_in.at[lax.rem(p, 4)],
+            core_send.at[lax.rem(p, 2)], core_recv.at[lax.rem(p, 4)],
+            device_id=device_at(z, x, 1 - core), device_id_type=MESH_ID)
+
+    def x_copy(p):
+        return pltpu.make_async_remote_copy(
+            x_out.at[lax.rem(p, 2)], x_in.at[lax.rem(p, 4)],
+            x_send.at[lax.rem(p, 2)], x_recv.at[lax.rem(p, 4)],
+            device_id=device_at(z, 1 - x, core), device_id_type=MESH_ID)
+
+    def z_copy(p, hop):
+        return pltpu.make_async_remote_copy(
+            z_out.at[lax.rem(p, 4), hop - 1], z_in.at[lax.rem(p, 8), hop - 1],
+            z_send.at[lax.rem(p, 4), hop - 1], z_recv.at[lax.rem(p, 8), hop - 1],
+            device_id=device_at(lax.rem(z + hop, DEPTH), x, core), device_id_type=MESH_ID)
+
+    @pl.when(step == 0)
+    def _():
+        barrier = pltpu.get_barrier_semaphore()
+        pl.semaphore_signal(barrier, 1, device_id=device_at(z, x, 1 - core), device_id_type=MESH_ID)
+        pl.semaphore_signal(barrier, 1, device_id=device_at(z, 1 - x, core), device_id_type=MESH_ID)
+        for hop in range(1, DEPTH):
+            pl.semaphore_signal(
+                barrier, 1, device_id=device_at(lax.rem(z + hop, DEPTH), x, core), device_id_type=MESH_ID)
+        pl.semaphore_wait(barrier, DEPTH + 1)
+
+    @pl.when(step < chunks)
+    def _():
+        @pl.when(step >= 2)
+        def _():
+            core_copy(step - 2).wait_send()
+
+        core_out[lax.rem(step, 2)] = compute(step, 1 - core, *ins).astype(BF)
+        core_copy(step).start()
+        own[lax.rem(step, 2)] = compute(step, core, *ins)
+
+    @pl.when((step >= 1) & (step < chunks + 1))
+    def _():
+        p = step - 1
+        core_copy(p).wait_recv()
+
+        @pl.when(p >= 2)
+        def _():
+            x_copy(p - 2).wait_send()
+
+        two, four = lax.rem(p, 2), lax.rem(p, 4)
+        x_out[two] = (own[two, :, 1 - x] + core_in[four, :, 1 - x].astype(F32)).astype(BF)
+        x_copy(p).start()
+        keep[two] = own[two, :, x] + core_in[four, :, x].astype(F32)
+
+    @pl.when((step >= 2) & (step < chunks + 2))
+    def _():
+        p = step - 2
+        x_copy(p).wait_recv()
+        two, four = lax.rem(p, 2), lax.rem(p, 4)
+        sums[...] = keep[two] + x_in[four].astype(F32)
+        for hop in range(1, DEPTH):
+            @pl.when(p >= 4)
+            def _():
+                z_copy(p - 4, hop).wait_send()
+
+            z_out[four, hop - 1] = sums[lax.rem(z + hop, DEPTH)].astype(BF)
+            z_copy(p, hop).start()
+        mine[four] = sums[z]
+
+    @pl.when(step >= Z_LAG)
+    def _():
+        p = step - Z_LAG
+        for hop in range(1, DEPTH):
+            z_copy(p, hop).wait_recv()
+        got = z_in.at[lax.rem(p, 8)]
+        total = mine[lax.rem(p, 4)] + got[0].astype(F32) + got[1].astype(F32) + got[2].astype(F32)
+        out_ref[0] = total
+
+    @pl.when(step == chunks + Z_LAG - 1)
+    def _():
+        for p in range(max(chunks - 2, 0), chunks):
+            core_copy(p).wait_send()
+            x_copy(p).wait_send()
+        for p in range(max(chunks - 4, 0), chunks):
+            for hop in range(1, DEPTH):
+                z_copy(p, hop).wait_send()
+
+
+def scatter_call(compute, chunks, block, operands, in_specs, collective, flops):
+    rows, lanes = block
+    quad = (DEPTH, 2, rows, lanes)
+    line = (DEPTH, rows, lanes)
+    return pl.pallas_call(
+        functools.partial(scatter_kernel, compute, chunks, len(operands)),
+        grid=(chunks + Z_LAG,),
+        in_specs=in_specs,
+        out_specs=pl.BlockSpec((1, rows, lanes), lambda q: (jnp.maximum(q - Z_LAG, 0), 0, 0)),
+        out_shape=jax.ShapeDtypeStruct((chunks, rows, lanes), F32),
+        scratch_shapes=[
+            pltpu.VMEM((2, *quad), F32),
+            pltpu.VMEM((2, *quad), BF),
+            pltpu.VMEM((4, *quad), BF),
+            pltpu.VMEM((2, *line), F32),
+            pltpu.VMEM((2, *line), BF),
+            pltpu.VMEM((4, *line), BF),
+            pltpu.VMEM(line, F32),
+            pltpu.VMEM((4, rows, lanes), F32),
+            pltpu.VMEM((4, DEPTH - 1, rows, lanes), BF),
+            pltpu.VMEM((8, DEPTH - 1, rows, lanes), BF),
+            pltpu.SemaphoreType.DMA((2,)),
+            pltpu.SemaphoreType.DMA((4,)),
+            pltpu.SemaphoreType.DMA((2,)),
+            pltpu.SemaphoreType.DMA((4,)),
+            pltpu.SemaphoreType.DMA((4, DEPTH - 1)),
+            pltpu.SemaphoreType.DMA((8, DEPTH - 1)),
+        ],
+        compiler_params=pltpu.CompilerParams(
+            collective_id=collective, has_side_effects=True, vmem_limit_bytes=VMEM_LIMIT),
+        cost_estimate=pl.CostEstimate(flops=flops, bytes_accessed=flops // 500, transcendentals=0),
+    )(*operands)
+
+
+def glu_scatter(left, right, collective):
+    _, full, tokens = left.shape
+    hidden = right.shape[2]
+    across = hidden // LANES
+    rows = full // 16
+
+    def compute(q, core, left_ref, right_ref):
+        side = left_ref[jnp.minimum(q, 3 * across - 1) // (2 * across), :, :, core]
+        product = jnp.dot(side.reshape(full // 2, tokens), right_ref[0], preferred_element_type=F32)
+        return product.reshape(DEPTH, 2, rows, LANES)
+
+    chunks = 3 * across
+    spot = lambda q: jnp.minimum(q, chunks - 1)
+    out = scatter_call(
+        compute, chunks, (rows, LANES),
+        (left.reshape(2, DEPTH, 2, 2, rows, tokens), right),
+        [
+            pl.BlockSpec((2, DEPTH, 2, 2, rows, tokens), lambda q: (0, 0, 0, 0, 0, 0), pipeline_mode=pl.Buffered(1)),
+            pl.BlockSpec((1, tokens, LANES), lambda q: (spot(q) // across, 0, lax.rem(spot(q), across))),
+        ],
+        collective, 2 * 3 * full * tokens * hidden)
+    return out.reshape(3, across, rows, LANES).transpose(0, 2, 1, 3).reshape(3, rows, hidden)
+
+
+def mixer_scatter(left_in, right_in, left_out, right_out, collective):
+    full, tokens = left_in.shape
+    channels = right_in.shape[2]
+    rows = full // 16
+    half = channels // 16
+    across = channels // LANES
+    across_out = full // (2 * LANES)
+    inside = 3 * across
+    chunks = inside + across_out
+
+    def compute(q, core, left_ref, right_ref, left_out_ref, right_out_ref):
+        def first():
+            side = left_ref[:, :, core].reshape(full // 2, tokens)
+            product = jnp.dot(side, right_ref[0], preferred_element_type=F32)
+            return product.reshape(DEPTH, 2, rows, LANES)
+
+        def second():
+            side = left_out_ref[:, :, core].reshape(channels // 2, tokens)
+            parts = [
+                jnp.dot(side, right_out_ref[:, at : at + LANES], preferred_element_type=F32).reshape(
+                    DEPTH, 2, half, LANES)
+                for at in (0, LANES)
+            ]
+            return jnp.concatenate(parts, axis=2)
+
+        return lax.cond(q < inside, first, second)
+
+    spot = lambda q: jnp.minimum(q, inside - 1)
+    spot_out = lambda q: jnp.clip(q - inside, 0, across_out - 1)
+    out = scatter_call(
+        compute, chunks, (rows, LANES),
+        (left_in.reshape(DEPTH, 2, 2, rows, tokens), right_in,
+         left_out.reshape(DEPTH, 2, 2, half, tokens), right_out),
+        [
+            pl.BlockSpec((DEPTH, 2, 2, rows, tokens), lambda q: (0, 0, 0, 0, 0), pipeline_mode=pl.Buffered(1)),
+            pl.BlockSpec((1, tokens, LANES), lambda q: (spot(q) // across, 0, lax.rem(spot(q), across))),
+            pl.BlockSpec((DEPTH, 2, 2, half, tokens), lambda q: (0, 0, 0, 0, 0), pipeline_mode=pl.Buffered(1)),
+            pl.BlockSpec((tokens, 2 * LANES), lambda q: (0, spot_out(q))),
+        ],
+        collective, 2 * tokens * (3 * full * channels + channels * full))
+    first = out[:inside].reshape(3, across, rows, LANES).transpose(0, 2, 1, 3).reshape(3, rows, channels)
+    second = out[inside:].reshape(across_out, 2, half, LANES).transpose(2, 0, 1, 3).reshape(half, full)
+    return first, second
+
+
+ITEMS = 4
+
+
+def gather_kernel(in_ref, out_ref, small_ref, all_in, all_out, all_small, right_send, left_send,
+                  z_recv, x_send, x_recv, core_send, core_recv, y_send, y_recv, local_sem):
+    z, x, core = device_place()
+    mp = lax.axis_index("mp")
+    barrier = pltpu.get_barrier_semaphore()
+    right, left = lax.rem(z + 1, DEPTH), lax.rem(z + DEPTH - 1, DEPTH)
+    dp = lax.axis_index("dp")
+    for target in (
+        device_at(right, x, core), device_at(left, x, core), device_at(z, 1 - x, core),
+        device_at(z, x, 1 - core), (dp, 1 - mp),
+    ):
+        pl.semaphore_signal(barrier, 1, device_id=target, device_id_type=MESH_ID)
+    pl.semaphore_wait(barrier, 5)
+
+    def spot(item, zs, xs, cs, side=None):
+        if item == 0:
+            return all_in.at[:, zs, xs, cs, mp if side is None else side]
+        if item == 1:
+            return all_out.at[zs, xs, cs]
+        if item == 2:
+            return all_in.at[:, zs, xs, cs, 1 - mp]
+        return all_small.at[zs, xs, cs]
+
+    def own(item):
+        if item == 0:
+            return in_ref.at[mp]
+        if item == 1:
+            return out_ref
+        return spot(item, z, x, core)
+
+    def copy(item, zs, xs, target, send, recv, source=None):
+        return pltpu.make_async_remote_copy(
+            spot(item, zs, xs, core) if source is None else source, spot(item, zs, xs, core),
+            send, recv, device_id=target, device_id_type=MESH_ID)
+
+    def right_copy(item, zs, source=None):
+        return copy(item, zs, x, device_at(right, x, core), right_send.at[zs, item], z_recv.at[zs, item], source)
+
+    def left_copy(item, zs, source=None):
+        return copy(item, zs, x, device_at(left, x, core), left_send.at[zs, item], z_recv.at[zs, item], source)
+
+    def x_copy(item, zs, source=None):
+        return copy(item, zs, x, device_at(z, 1 - x, core), x_send.at[zs, item], x_recv.at[zs, item], source)
+
+    def core_copy(item, zs, xs, source=None):
+        return copy(item, zs, xs, device_at(z, x, 1 - core), core_send.at[zs, xs, item], core_recv.at[zs, xs, item], source)
+
+    y_copies = [
+        pltpu.make_async_remote_copy(
+            in_ref.at[1 - mp], all_in.at[:, z, x, core, mp], y_send.at[0], y_recv.at[0],
+            device_id=(dp, 1 - mp), device_id_type=MESH_ID),
+        pltpu.make_async_remote_copy(
+            small_ref, all_small.at[z, x, core, mp], y_send.at[1], y_recv.at[1],
+            device_id=(dp, 1 - mp), device_id_type=MESH_ID),
+    ]
+    locals_ = [
+        pltpu.make_async_copy(in_ref.at[mp], spot(0, z, x, core), local_sem.at[0]),
+        pltpu.make_async_copy(out_ref, spot(1, z, x, core), local_sem.at[1]),
+        pltpu.make_async_copy(small_ref, all_small.at[z, x, core, mp], local_sem.at[2]),
+    ]
+    for one in y_copies:
+        one.start()
+    locals_[2].start()
+
+    for item in range(ITEMS):
+        if item == 2:
+            y_copies[0].wait_recv()
+        if item == 3:
+            y_copies[1].wait_recv()
+            locals_[2].wait()
+        source = own(item)
+
+        @pl.when(z < DEPTH - 1)
+        def _():
+            right_copy(item, z, source).start()
+
+        @pl.when(z > 0)
+        def _():
+            left_copy(item, z, source).start()
+
+        x_copy(item, z, source).start()
+        core_copy(item, z, x, source).start()
+    locals_[0].start()
+    locals_[1].start()
+
+    def from_x(item, zs):
+        pltpu.make_async_remote_copy(
+            spot(item, zs, 1 - x, core), spot(item, zs, 1 - x, core), x_send.at[zs, item],
+            x_recv.at[zs, item], device_id=device_at(z, 1 - x, core), device_id_type=MESH_ID).wait_recv()
+        core_copy(item, zs, 1 - x).start()
+
+    for hop in range(1, DEPTH + 1):
+        for item in range(ITEMS):
+            if hop < DEPTH:
+                @pl.when(z >= hop)
+                def _():
+                    zs = z - hop
+                    right_copy(item, zs).wait_recv()
+
+                    @pl.when(z < DEPTH - 1)
+                    def _():
+                        right_copy(item, zs).start()
+
+                    x_copy(item, zs).start()
+                    core_copy(item, zs, x).start()
+
+                @pl.when(z + hop < DEPTH)
+                def _():
+                    zs = z + hop
+                    left_copy(item, zs).wait_recv()
+
+                    @pl.when(z > 0)
+                    def _():
+                        left_copy(item, zs).start()
+
+                    x_copy(item, zs).start()
+                    core_copy(item, zs, x).start()
+            if hop == 1:
+                from_x(item, z)
+            else:
+                @pl.when(z >= hop - 1)
+                def _():
+                    from_x(item, z - (hop - 1))
+
+                @pl.when(z + hop - 1 < DEPTH)
+                def _():
+                    from_x(item, z + (hop - 1))
+
+    for item in range(ITEMS):
+        for zs in range(DEPTH):
+            @pl.when((z >= zs) & (z < DEPTH - 1))
+            def _():
+                right_copy(item, zs).wait_send()
+
+            @pl.when((z <= zs) & (z > 0))
+            def _():
+                left_copy(item, zs).wait_send()
+
+            x_copy(item, zs).wait_send()
+            for xs in range(2):
+                core_copy(item, zs, xs).wait()
+    for one in y_copies:
+        one.wait_send()
+    locals_[0].wait()
+    locals_[1].wait()
+
+
+def gather_call(in_blocks, out_rows, small, collective):
+    _, three, own_rows, channels = in_blocks.shape
+    full = out_rows.shape[1]
+    dma = pltpu.SemaphoreType.DMA
+    any_space = pl.BlockSpec(memory_space=pl.ANY)
+    return pl.pallas_call(
+        gather_kernel,
+        in_specs=[any_space] * 3,
+        out_specs=[any_space] * 3,
+        out_shape=[
+            jax.ShapeDtypeStruct((three, DEPTH, 2, 2, 2, own_rows, channels), BF),
+            jax.ShapeDtypeStruct((DEPTH, 2, 2, own_rows, full), BF),
+            jax.ShapeDtypeStruct((DEPTH, 2, 2, 2, *small.shape), F32),
+        ],
+        scratch_shapes=[
+            dma((DEPTH, ITEMS)), dma((DEPTH, ITEMS)), dma((DEPTH, ITEMS)), dma((DEPTH, ITEMS)),
+            dma((DEPTH, ITEMS)), dma((DEPTH, 2, ITEMS)), dma((DEPTH, 2, ITEMS)), dma((2,)), dma((2,)), dma((3,)),
+        ],
+        compiler_params=pltpu.CompilerParams(collective_id=collective, has_side_effects=True),
+        cost_estimate=pl.CostEstimate(flops=0, bytes_accessed=300_000_000, transcendentals=0),
+    )(in_blocks, out_rows, small)
+
+
 def shards(
     tokens,
     cotangent,
@@ -306,26 +690,39 @@
     own_rows = mixer_master.shape[1]
     channels = groups * own_rows
     part = full // narrow
+    quick = groups == 16 and narrow == 2
 
     domain_ids = jnp.arange(NDOM, dtype=jnp.int32)
     member = (domains[..., 0][..., None] == domain_ids).astype(F32)
     live_counts = lengths.astype(F32)
-    counts = lax.psum(jnp.sum(member * live_counts[..., None], axis=(0, 1)), "dp")
+    counts = jnp.sum(member * live_counts[..., None], axis=(0, 1))
+    gain_low = gain_master.astype(BF)
+    mixer_low = mixer_master.astype(BF)
+    in_blocks = mixer_low[:3].reshape(3, own_rows, groups, narrow, own_rows)
+    in_blocks = in_blocks.transpose(3, 0, 1, 2, 4).reshape(narrow, 3, own_rows, channels)
+    if quick:
+        small = jnp.zeros((8, 128), F32)
+        small = small.at[:3, :own_rows].set(gain_low.astype(F32)).at[3, :NDOM].set(counts)
+        mixer_in, mixer_out, small = gather_call(in_blocks, mixer_low[3], small, 2)
+        mixer_in = mixer_in.reshape(3, full, channels)
+        mixer_out = mixer_out.reshape(channels, full)
+        small = small.reshape(groups, narrow, 8, 128)
+        gain_full = small[:, :, :3, :own_rows].transpose(2, 0, 1, 3).reshape(3, full)
+        counts = jnp.sum(small[:, 0, 3, :NDOM], axis=0)
+    else:
+        gain_full = lax.all_gather(gain_low, ("dp", "mp"), axis=1, tiled=True).astype(F32)
+        in_rows = mp_swap(in_blocks).transpose(1, 0, 2, 3).reshape(3, narrow * own_rows, channels)
+        mixer_in = lax.all_gather(in_rows, "dp", axis=1, tiled=True)
+        mixer_out = lax.all_gather(mixer_low[3], "dp", axis=0, tiled=True)
+        counts = lax.psum(counts, "dp")
+    glu_low = jnp.concatenate([glu_in_master.astype(BF), glu_out_master.astype(BF).T[None]])
+    glu_low, mixer_in = lax.optimization_barrier((glu_low, mixer_in))
+    glu = lax.all_gather(glu_low, "dp", axis=1, tiled=True)
+
     seq_weight = jnp.sum(counts) / (NDOM * jnp.sum(member * counts, axis=-1))
     positions = jnp.arange(length, dtype=jnp.int32)
     token_weight = jnp.where(positions[None, :] < lengths[:, :1], seq_weight[:, :1], 0.0)
     token_weight = token_weight.reshape(rows, 1)
-
-    gain_full = lax.all_gather(gain_master.astype(BF), ("dp", "mp"), axis=1, tiled=True).astype(F32)
-    mixer_low = mixer_master.astype(BF)
-    in_blocks = mixer_low[:3].reshape(3, own_rows, groups, narrow, own_rows)
-    in_blocks = in_blocks.transpose(3, 0, 1, 2, 4).reshape(narrow, 3, own_rows, channels)
-    in_rows = mp_swap(in_blocks).transpose(1, 0, 2, 3).reshape(3, narrow * own_rows, channels)
-    mixer_in = lax.all_gather(in_rows, "dp", axis=1, tiled=True)
-    mixer_out = lax.all_gather(mixer_low[3], "dp", axis=0, tiled=True)
-    glu_low = jnp.concatenate([glu_in_master.astype(BF), glu_out_master.astype(BF).T[None]])
-    glu_low, _ = lax.optimization_barrier((glu_low, mixer_in))
-    glu = lax.all_gather(glu_low, "dp", axis=1, tiled=True)
 
     own_channels = lambda v: lax.dynamic_index_in_dim(
         v.reshape(groups, narrow, own_rows), place, 1, keepdims=False
@@ -364,16 +761,22 @@
     down = (((0,), (0,)), ((), ()))
     dot = functools.partial(lax.dot_general, preferred_element_type=F32)
     grad_normed_part = dot(grad_act, glu[0], across) + dot(grad_up, glu[1], across)
-    grad_normed = mp_sum(grad_normed_part)
+    grad_normed_low = grad_normed_part.astype(BF)
+    grad_normed_came = partner_swap(grad_normed_low) if quick else None
     partial_out = dot(hidden, glu[2], across)
-    glu_grad = jnp.stack(
-        [
-            dot(normed_mid, grad_act, down).astype(BF),
-            dot(normed_mid, grad_up, down).astype(BF),
-            dot(back_low, hidden, down).astype(BF),
-        ]
-    )
-    glu_own = lax.psum_scatter(glu_grad, "dp", scatter_dimension=1, tiled=True).astype(F32)
+    rights = jnp.stack([grad_act, grad_up, hidden])
+    if quick:
+        lefts = jnp.stack([normed_mid.T, back_low.T])
+        lefts, rights, grad_normed_low = lax.optimization_barrier((lefts, rights, grad_normed_low))
+        glu_own = glu_scatter(lefts, rights, 0)
+        glu_own, grad_normed_came = lax.optimization_barrier((glu_own, grad_normed_came))
+        grad_normed = grad_normed_low.astype(F32) + grad_normed_came.astype(F32)
+    else:
+        grad_normed = mp_sum(grad_normed_part)
+        glu_grad = jnp.stack(
+            [dot(normed_mid, grad_act, down), dot(normed_mid, grad_up, down), dot(back_low, hidden, down)]
+        ).astype(BF)
+        glu_own = lax.psum_scatter(glu_grad, "dp", scatter_dimension=1, tiled=True).astype(F32)
     middle_own = lax.dynamic_slice_in_dim(middle, place * part, part, 1)
     layer_out = (middle_own + mp_scatter(partial_out)).astype(BF)
 
@@ -390,13 +793,20 @@
         pre, states, by_batch(grad_gated), by_batch(inverse_state), by_batch(state_mean), bound, state_gain
     )
     grad_pre = grad_pre.reshape(3, rows, channels)
-    grad_mix_out = dot(gated_out.reshape(rows, channels), middle_low, down).astype(BF)
-    grad_mix_in = jnp.einsum("td,kte->kde", normed_in, grad_pre, preferred_element_type=F32).astype(BF)
-    in_own = lax.psum_scatter(grad_mix_in, "dp", scatter_dimension=1, tiled=True)
-    out_own = lax.psum_scatter(grad_mix_out, "dp", scatter_dimension=0, tiled=True)
+    gated_out = gated_out.reshape(rows, channels)
+    if quick:
+        in_own, out_own = mixer_scatter(normed_in.T, grad_pre, gated_out.T, middle_low, 1)
+        in_own = in_own.astype(BF)
+    else:
+        grad_mix_out = dot(gated_out, middle_low, down).astype(BF)
+        grad_mix_in = jnp.einsum("td,kte->kde", normed_in, grad_pre, preferred_element_type=F32)
+        in_own = lax.psum_scatter(grad_mix_in.astype(BF), "dp", scatter_dimension=1, tiled=True)
+        out_own = lax.psum_scatter(grad_mix_out, "dp", scatter_dimension=0, tiled=True)
     in_own = mp_swap(in_own.reshape(3, narrow, own_rows, channels).transpose(1, 0, 2, 3))
     in_own = in_own.reshape(narrow, 3, own_rows, groups, own_rows).transpose(1, 2, 3, 0, 4)
-    mixer_own = jnp.concatenate([in_own.reshape(3, own_rows, full), out_own[None]]).astype(F32)
+    mixer_own = jnp.concatenate(
+        [in_own.reshape(3, own_rows, full).astype(F32), out_own[None].astype(F32)]
+    )
 
     grad_normed_in = jnp.einsum("kte,kde->td", grad_pre, mixer_in, preferred_element_type=F32)
     grad_normed_in = mp_scatter(grad_normed_in)

time: 1290 us -> 957 us (0.74)
  waiting for transfers between devices: 596 us -> 101 us
  Pallas kernels: 70.2 us -> 443 us
  blocking collectives: 141 us -> 39.2 us
  matrix products: 241 us -> 154 us
  other arithmetic: 109 us -> 85.7 us
    pallas_call x0 -> x3, Pallas kernels: none -> 414 us  [the longest x2 313 us: scatter_call(): pl.pallas_call(functools.partial(scatter_kernel, compute, chunks, len(ope...]
    reduce_scatter x2 -> x0, waiting for transfers between devices: 290 us -> none  [the longest x1 290 us: shards(): lax.psum_scatter(glu_grad, 'dp', scatter_dimension=1, tiled=True)]
    ppermute x9 -> x8, waiting for transfers between devices: 212 us -> 101 us  [partner_swap(): return lax.ppermute(value, 'mp', [(0, 1), (1, 0)])]
    all_gather x2 -> x0, waiting for transfers between devices: 93.3 us -> none  [the longest x1 93.3 us: shards(): mixer_in = lax.all_gather(in_rows, 'dp', axis=1, tiled=True)]
    dot_general x5 -> x0, matrix products: 83.3 us -> none  [the longest x1 19.3 us: shards(): dot(back_low, hidden, down).astype(BF)]
    all_gather x1 -> x0, blocking collectives: 65.9 us -> none  [shards(): lax.all_gather(gain_master.astype(BF), ('dp', 'mp'), axis=1, tiled=True)]
    unnamed x101 -> x108, local copies, waits for them, and re-layouts: 70.1 us -> 33.3 us
    psum x1 -> x0, blocking collectives: 30.8 us -> none  [shards(): lax.psum(jnp.sum(member * live_counts[..., None], axis=(0, 1)), 'dp')]
  transfers between devices with their start and end apart: 15 -> 9, of which waited for: 7 -> 1; matrix products, arithmetic and copies ran while one was open for 18% -> 19% of each run, Pallas kernels for 2% -> 34%
where the time goes in v2:
time: 957 us; the launch traced here: 952 us
  Pallas kernels  443 us (46%)
  matrix products  154 us (16%)
  local copies, waits for them, and re-layouts  106 us (11%)
  waiting for transfers between devices  101 us (11%)
  other arithmetic  85.7 us (9%)
  blocking collectives  39.2 us (4%)
  between operations  14.9 us (2%)
    pallas_call x2, Pallas kernels, scatter_call(): pl.pallas_call(functools.partial(scatter_kernel, compute, chunks, len(ope...  313 us
    ppermute x8, waiting for transfers between devices, partner_swap(): return lax.ppermute(value, 'mp', [(0, 1), (1, 0)])  101 us
    pallas_call x1, Pallas kernels, gather_call(): pl.pallas_call(gather_kernel, in_specs=[any_space] * 3, out_specs=[any_sp...  101 us
    psum x1, blocking collectives, shards(): gain_total = lax.psum(gain_rows, ('dp', 'mp'))  39.2 us
    unnamed x108, local copies, waits for them, and re-layouts  33.3 us
    dot_general x1, matrix products, shards(): pre_act = jnp.dot(normed_mid, glu[0], preferred_element_type=F32)  24.9 us
  transfers between devices with their start and end apart: 9, of which 1 were waited for; matrix products, arithmetic and copies ran while one was open for 19% of the time, Pallas kernels for 34%

profile of v2, /device:TPU:0, one launch (start us, length us, event | category | flops | bytes accessed | tf_op | source)
XLA Modules:
  0.0 951.6 jit_solution(16399520657127164462)
XLA Ops:
  10.6 4.4 reshape.413
  30.2 100.9 %shard_map.272 = (bf16[3,4,2,2,2,64,1024]{6,5,4,3,2,1,0:T(8,128)(2,1)}, bf16[4,2,2,64,2048]{4,3,2,1,0:T(8,128)(2,1)}, f32[4,2,2,2,8,128]{5,4,3,2,1,0:T(8,128)}) custom-call(bf16[2,3,64,1024]{3,2,1,0:T(8,128)(2,1)} %reshape.414.in_ref, bf16[64,2048]{1,0:T(8,128)(2,1)} %slice_bitcast_fusion.11.out_ref, f32[8,128]{1,0:T(8,128)} %copy-done.31), custom_call_target="tpu_custom_call" | custom-call | bytes 300000000 | tf_op jit(solution)/shard_map/pallas_call | solution.py:648
  136.6 5.3 fusion.12
  141.9 4.7 copy-done.39
  146.6 14.0 %fusion.10 = f32[3,1024,896]{1,2,0:T(8,128)} fusion(bf16[3,2048,1024]{2,1,0:T(8,128)(2,1)S(1)} %bitcast.160, f32[896,2048]{1,0:T(8,128)S(1)} %get-tuple-element.155, f32[2048]{0:T(1024)S(1)} %mul.372), kind=kOutput, calls=%fused_computation.35 | convolution fusion | flops 11277959168 | bytes 30941184 | tf_op jit(solution)/shard_map/td,kde->kte/dot_general | solution.py:737
  160.6 10.8 %shard_map.273 = (f32[2,448,1024]{2,1,0:T(8,128)}, bf16[2,448,1024]{2,1,0:T(8,128)(2,1)}, f32[2,448,1]{2,1,0:T(8,128)}) custom-call(f32[3,2,448,1024]{3,2,1,0:T(8,128)} %bitcast.127, f32[1,1024]{1,0:T(1,128)} %broadcast_in_dim_reshape.11.bound_ref, f32[1,1024]{1,0:T(1,128)} %broadcast_in_dim_reshape.12.gain_ref), custom_call_target="tpu_custom_call" | custom-call | flops 36700160 | bytes 16515072 | tf_op jit(solution)/shard_map/pallas_call | solution.py:151
  171.5 7.0 convolution_convert_fusion
  187.2 6.3 copy.111
  199.2 101.0 %collective-permute-done = f32[896,1]{0,1:T(1,128)S(1)} collective-permute-done((f32[896,1]{0,1:T(1,128)S(1)}, f32[896,1]{0,1:T(1,128)S(1)}, u32[]{:S(2)}, u32[]{:S(2)}) %collective-permute-start) | collective-permute-done | bytes 3616 | tf_op jit(solution)/shard_map/ppermute | solution.py:47
  308.2 5.2 multiply_reduce_fusion.3
  322.1 18.3 %fusion.3 = f32[896,2816]{1,0:T(8,128)} fusion(bf16[3,2048,2816]{2,1,0:T(8,128)(2,1)} %all-gather.2.cloned.1.call-done, f32[896,2048]{1,0:T(8,128)} %copy-done, f32[2048]{0:T(1024)S(1)} %mul.382, f32[896]{0:T(1024)S(1)} %add_rsqrt_fusion), kind=kOutput, calls=%fused_computation.7 | convolution fusion | flops 10340270080 | bytes 28978688 | tf_op jit(solution)/shard_map/dot_general | solution.py:753
  340.4 16.8 %fusion.4 = f32[896,2816]{1,0:T(8,128)} fusion(bf16[3,2048,2816]{2,1,0:T(8,128)(2,1)} %all-gather.2.cloned.1.call-done, f32[896]{0:T(1024)S(1)} %select_n.71, bf16[896,1024]{1,0:T(8,128)(2,1)S(1)} %copy-done.6, bf16[896,1024]{1,0:T(8,128)(2,1)S(1)} %get-tuple-element.156), kind=kOutput, calls=%fused_computation.8 | convolution fusion | flops 10345775104 | bytes 25300480 | tf_op jit(solution)/shard_map/dot_general | solution.py:754
  357.2 24.9 %multiply_convert_fusion.1 = (bf16[896,2816]{1,0:T(8,128)(2,1)}, bf16[896,2816]{1,0:T(8,128)(2,1)}, bf16[896,2816]{1,0:T(8,128)(2,1)}) fusion(f32[896,2816]{1,0:T(8,128)} %fusion.4, f32[896,2816]{1,0:T(8,128)} %fusion.3, bf16[3,2048,2816]{2,1,0:T(8,128)(2,1)} %all-gather.2.cloned.1.call-done, f32[896,2048]{1,0:T(8,128)} %copy-done, f32[2048]{0:T(1024)S(1)} %mul.382, ...), kind=kOutput, calls=%fused_computation.11 | convolution fusion | flops 10378117120 | bytes 54210048 | tf_op jit(solution)/shard_map/dot_general | solution.py:752
  382.1 17.0 %fusion = f32[896,2048]{1,0:T(8,128)} fusion(bf16[896,2816]{1,0:T(8,128)(2,1)} %get-tuple-element.149, bf16[3,2048,2816]{2,1,0:T(8,128)(2,1)} %all-gather.2.cloned.1.call-done), kind=kOutput, calls=%fused_computation.4 | convolution fusion | flops 10334765056 | bytes 23920640 | tf_op jit(solution)/shard_map/dot_general | solution.py:763
  399.1 16.1 %add_convert_fusion = bf16[896,2048]{1,0:T(8,128)(2,1)} fusion(f32[896,2048]{1,0:T(8,128)} %fusion, bf16[896,2816]{1,0:T(8,128)(2,1)S(1)} %copy-done.15, bf16[3,2048,2816]{2,1,0:T(8,128)(2,1)} %all-gather.2.cloned.1.call-done), kind=kOutput, calls=%fused_computation.25 | convolution fusion | flops 10338435072 | bytes 27590656 | tf_op jit(solution)/shard_map/dot_general | solution.py:763
  416.7 15.1 %fusion.5 = bf16[896,2048]{1,0:T(8,128)(2,1)} fusion(bf16[896,2816]{1,0:T(8,128)(2,1)S(1)} %copy-done.16, bf16[3,2048,2816]{2,1,0:T(8,128)(2,1)} %all-gather.2.cloned.1.call-done), kind=kOutput, calls=%fused_computation.9 | convolution fusion | flops 10334765056 | bytes 20250624 | tf_op jit(solution)/shard_map/dot_general | solution.py:766
  431.7 6.5 pad_maximum_fusion.refs_1_
  438.2 11.3 %copy.110 = bf16[2,2048,896]{2,1,0:T(8,128)(2,1)} copy(bf16[2,2048,896]{1,2,0:T(8,128)(2,1)} %pad_maximum_fusion.1) | data formatting | bytes 14680064 | tf_op jit(solution)/shard_map/reshape | solution.py:439
  452.9 204.1 %shard_map.274 = f32[33,128,256]{2,1,0:T(8,128)} custom-call(bf16[2,4,2,2,128,896]{5,4,3,2,1,0:T(8,128)(2,1)} %bitcast.135, bf16[3,896,2816]{2,1,0:T(8,128)(2,1)} %pad_maximum_fusion.refs_1_), custom_call_target="tpu_custom_call" | custom-call | flops 31004295168 | bytes 62008592 | tf_op jit(solution)/shard_map/pallas_call | solution.py:394
  657.0 6.0 copy.93
  663.0 5.5 add_convert_fusion.2
  668.6 4.6 multiply_reduce_fusion
  673.2 11.6 %multiply_reduce_fusion.1 = (f32[896]{0:T(1024)S(1)}, bf16[896,2048]{1,0:T(8,128)(2,1)}, f32[896,2048]{1,0:T(8,128)}) fusion(bf16[896,2048]{1,0:T(8,128)(2,1)} %collective-permute-done.1, bf16[896,2048]{1,0:T(8,128)(2,1)} %convolution_convert_fusion, f32[896]{0:T(1024)S(1)} %copy-done.25, f32[896]{0:T(1024)S(1)} %broadcast_multiply_fusion.1, ...), kind=kLoop, calls=%fused_computation.21 | loop fusion | flops 40369280 | bytes 36726272 | tf_op jit(solution)/shard_map/reduce_sum | solution.py:789
  686.0 9.2 fusion.17.gated_ref
  695.1 17.5 %shard_map.275 = (bf16[3,2,448,1024]{3,2,1,0:T(8,128)(2,1)}, bf16[2,448,1024]{2,1,0:T(8,128)(2,1)}, f32[2,1,1024]{2,1,0:T(1,128)}, f32[2,448,1]{2,1,0:T(8,128)}) custom-call(f32[3,2,448,1024]{3,2,1,0:T(8,128)} %bitcast.128, f32[2,448,1024]{2,1,0:T(8,128)} %get-tuple-element.66.states_ref, f32[2,448,1024]{2,1,0:T(8,128)} %fusion.17.gated_ref, ...), custom_call_target="tpu_custom_call" | custom-call | flops 73400320 | bytes 25690112 | tf_op jit(solution)/shard_map/pallas_call | solution.py:257
  715.4 16.2 %convolution_bitcast_fusion = bf16[896,2048]{1,0:T(8,128)(2,1)S(1)} fusion(bf16[3,896,1024]{2,1,0:T(8,128)(2,1)} %bitcast.161, bf16[3,2048,1024]{2,1,0:T(8,128)(2,1)} %bitcast.159), kind=kOutput, calls=%fused_computation.33 | convolution fusion | flops 11274289152 | bytes 21757952 | tf_op jit(solution)/shard_map/kte,kde->td/dot_general | solution.py:811
  738.1 109.3 %shard_map.276 = f32[16,128,256]{2,1,0:T(8,128)} custom-call(bf16[4,2,2,128,896]{4,3,2,1,0:T(8,128)(2,1)} %bitcast.144, bf16[3,896,1024]{2,1,0:T(8,128)(2,1)} %bitcast.162, bf16[4,2,2,64,896]{4,3,2,1,0:T(8,128)(2,1)} %bitcast.151, bf16[896,2048]{1,0:T(8,128)(2,1)} %get-tuple-element.145.refs_3_), custom_call_target="tpu_custom_call" | custom-call | flops 15032385536 | bytes 30064772 | tf_op jit(solution)/shard_map/pallas_call | solution.py:394
  855.1 6.5 multiply_subtract_fusion
  861.6 4.2 multiply_subtract_fusion.2
  884.5 5.2 reshape.439
  892.5 7.1 multiply_subtract_fusion.1
  904.7 39.2 %psum.7 = f32[3,2048]{1,0:T(4,128)S(1)} all-reduce(f32[3,2048]{1,0:T(4,128)S(1)} %pad_maximum_fusion.4), channel_id=1, replica_groups=mesh['dp'=16,'mp'=2] {'dp','mp'}, use_global_device_ids=true, to_apply=%region_11.12 | all-reduce | flops 6144 | bytes 49152 | tf_op jit(solution)/shard_map/psum | solution.py:835
  (207 shorter events, 105.1 us)
Async XLA Ops:
  7.2 314.9 %all-gather.2.cloned.1.call-start = ((), (), s32[]{:S(2)}) async-start(), calls=%async_computation | async-start | bytes 36765696 | tf_op jit(solution)/shard_map/all_gather | solution.py:720
  10.6 10.6 %copy-start.38 = (s32[2,1]{0,1:T(1,128)S(1)}, s32[2,1]{0,1:T(1,128)}, u32[]{:S(2)}) copy-start(s32[2,1]{0,1:T(1,128)} %param.23) | copy-start | bytes 28
  10.6 10.6 %copy-start.34 = (f32[3,64]{1,0:T(4,128)S(1)}, f32[3,64]{1,0:T(4,128)}, u32[]{:S(2)}) copy-start(f32[3,64]{1,0:T(4,128)} %param.35) | copy-start | bytes 2308
  10.6 10.7 %copy-start.12 = (f32[2,128,2816]{2,1,0:T(8,128)S(1)}, f32[2,128,2816]{2,1,0:T(8,128)}, u32[]{:S(2)}) copy-start(f32[2,128,2816]{2,1,0:T(8,128)} %param.29) | copy-start | bytes 8650756
  29.5 106.3 %copy-start.32 = (f32[2048]{0:T(1024)S(1)}, f32[2048]{0:T(1024)}, u32[]{:S(2)}) copy-start(f32[2048]{0:T(1024)} %param.25) | copy-start | bytes 24580
  132.8 54.4 %copy-start.26 = (f32[2048]{0:T(1024)}, f32[2048]{0:T(1024)S(1)}, u32[]{:S(2)}) copy-start(f32[2048]{0:T(1024)S(1)} %mul.372) | copy-start | bytes 24580
  136.6 10.0 %copy-start.39 = (bf16[3,4,2,2,2,64,1024]{6,5,4,3,2,1,0:T(8,128)(2,1)S(1)}, bf16[3,4,2,2,2,64,1024]{6,5,4,3,2,1,0:T(8,128)(2,1)}, u32[]{:S(2)}) copy-start(bf16[3,4,2,2,2,64,1024]{6,5,4,3,2,1,0:T(8,128)(2,1)} %get-tuple-element.55) | copy-start | bytes 37748740
  141.9 18.7 %copy-start.2 = (f32[896,2048]{1,0:T(8,128)}, f32[896,2048]{1,0:T(8,128)S(1)}, u32[]{:S(2)}) copy-start(f32[896,2048]{1,0:T(8,128)S(1)} %get-tuple-element.155) | copy-start | bytes 22020100
  160.6 10.8 %copy-start.40 = (bf16[4,2,2,64,2048]{4,3,2,1,0:T(8,128)(2,1)S(1)}, bf16[4,2,2,64,2048]{4,3,2,1,0:T(8,128)(2,1)}, u32[]{:S(2)}) copy-start(bf16[4,2,2,64,2048]{4,3,2,1,0:T(8,128)(2,1)} %get-tuple-element.60) | copy-start | bytes 12582916
  171.5 9.1 copy-start.23
  178.5 127.8 %collective-permute-start.1 = (bf16[896,2048]{1,0:T(8,128)(2,1)}, bf16[896,2048]{1,0:T(8,128)(2,1)}, u32[]{:S(2)}, u32[]{:S(2)}) collective-permute-start(bf16[896,2048]{1,0:T(8,128)(2,1)} %convolution_convert_fusion), channel_id=1, source_target_pairs={{0,1},{1,0},{2,3},{3,2},{4,5},{5,4},{6,7},{7,6},{8,9},{9,8},{10,11... | collective-permute-start | bytes 11010056 | tf_op jit(solution)/shard_map/ppermute | solution.py:47
  180.1 121.1 %collective-permute-start.3 = (bf16[896,1024]{1,0:T(8,128)(2,1)}, bf16[896,1024]{1,0:T(8,128)(2,1)}, u32[]{:S(2)}, u32[]{:S(2)}) collective-permute-start(bf16[896,1024]{1,0:T(8,128)(2,1)} %bitcast.21), channel_id=1, source_target_pairs={{0,1},{1,0},{2,3},{3,2},{4,5},{5,4},{6,7},{7,6},{8,9},{9,8},{10,11... | collective-permute-start | bytes 5505032 | tf_op jit(solution)/shard_map/ppermute | solution.py:47
  180.8 119.3 %collective-permute-start = (f32[896,1]{0,1:T(1,128)S(1)}, f32[896,1]{0,1:T(1,128)S(1)}, u32[]{:S(2)}, u32[]{:S(2)}) collective-permute-start(f32[896,1]{0,1:T(1,128)S(1)} %reshape.420), channel_id=1, source_target_pairs={{0,1},{1,0},{2,3},{3,2},{4,5},{5,4},{6,7},{7,6},{8,9},{9,8},{10,11... | collective-permute-start | bytes 10760 | tf_op jit(solution)/shard_map/ppermute | solution.py:47
  187.2 153.2 %copy-start.27 = (f32[896]{0:T(1024)}, f32[896]{0:T(1024)S(1)}, u32[]{:S(2)}) copy-start(f32[896]{0:T(1024)S(1)} %select_n.71) | copy-start | bytes 10756
  303.6 36.8 %copy-start.3 = (bf16[896,1024]{1,0:T(8,128)(2,1)}, bf16[896,1024]{1,0:T(8,128)(2,1)S(1)}, u32[]{:S(2)}) copy-start(bf16[896,1024]{1,0:T(8,128)(2,1)S(1)} %get-tuple-element.156) | copy-start | bytes 5505028
  322.1 18.3 %copy-start.6 = (bf16[896,1024]{1,0:T(8,128)(2,1)S(1)}, bf16[896,1024]{1,0:T(8,128)(2,1)}, u32[]{:S(2)}) copy-start(bf16[896,1024]{1,0:T(8,128)(2,1)} %copy-done.5) | copy-start | bytes 5505028
  382.1 17.0 %copy-start.15 = (bf16[896,2816]{1,0:T(8,128)(2,1)S(1)}, bf16[896,2816]{1,0:T(8,128)(2,1)}, u32[]{:S(2)}) copy-start(bf16[896,2816]{1,0:T(8,128)(2,1)} %get-tuple-element.150) | copy-start | bytes 15138820
  399.1 17.6 %copy-start.16 = (bf16[896,2816]{1,0:T(8,128)(2,1)S(1)}, bf16[896,2816]{1,0:T(8,128)(2,1)}, u32[]{:S(2)}) copy-start(bf16[896,2816]{1,0:T(8,128)(2,1)} %get-tuple-element.151) | copy-start | bytes 15138820
  399.1 32.6 %slice-start.6 = ((s8[5046272]{0:T(1024)(128)(4,1)}), s8[851968]{0:T(1024)(128)(4,1)S(1)}, s32[]{:S(2)}) async-start(s8[5046272]{0:T(1024)(128)(4,1)} %bitcast.137), calls=%async_computation.7 | async-start | bytes 1703936
  415.2 253.4 %collective-permute-start.4 = (bf16[896,2048]{1,0:T(8,128)(2,1)}, bf16[896,2048]{1,0:T(8,128)(2,1)}, u32[]{:S(2)}, u32[]{:S(2)}) collective-permute-start(bf16[896,2048]{1,0:T(8,128)(2,1)} %add_convert_fusion), channel_id=1, source_target_pairs={{0,1},{1,0},{2,3},{3,2},{4,5},{5,4},{6,7},{7,6},{8,9},{9,8},{10,11... | collective-permute-start | bytes 11010056 | tf_op jit(solution)/shard_map/ppermute | solution.py:47
  416.7 15.1 %slice-start.7 = ((s8[5046272]{0:T(1024)(128)(4,1)}), s8[4194304]{0:T(1024)(128)(4,1)S(1)}, s32[]{:S(2)}) async-start(s8[5046272]{0:T(1024)(128)(4,1)} %bitcast.137), calls=%async_computation.8 | async-start | bytes 8388608
  452.4 210.6 %collective-permute-start.2 = (bf16[896,1024]{1,0:T(8,128)(2,1)}, bf16[896,1024]{1,0:T(8,128)(2,1)}, u32[]{:S(2)}, u32[]{:S(2)}) collective-permute-start(bf16[896,1024]{1,0:T(8,128)(2,1)} %dynamic-slice_convert_fusion.2), channel_id=1, source_target_pairs={{0,1},{1,0},{2,3},{3,2},{4,5},{5,4},{6,7},{7,6},{8,9},{9,8},{10,11... | collective-permute-start | bytes 5505032 | tf_op jit(solution)/shard_map/ppermute | solution.py:47
  657.0 11.5 %slice-start = ((s8[7340032]{0:T(1024)(128)(4,1)}), s8[3145728]{0:T(1024)(128)(4,1)S(1)}, s32[]{:S(2)}) async-start(s8[7340032]{0:T(1024)(128)(4,1)} %bitcast.125), calls=%async_computation.1 | async-start | bytes 6291456
  714.0 163.8 %collective-permute-start.6 = (f32[896,1]{0,1:T(1,128)S(1)}, f32[896,1]{0,1:T(1,128)S(1)}, u32[]{:S(2)}, u32[]{:S(2)}) collective-permute-start(f32[896,1]{0,1:T(1,128)S(1)} %reshape.430), channel_id=1, source_target_pairs={{0,1},{1,0},{2,3},{3,2},{4,5},{5,4},{6,7},{7,6},{8,9},{9,8},{10,11... | collective-permute-start | bytes 10760 | tf_op jit(solution)/shard_map/ppermute | solution.py:47
  734.9 164.7 %collective-permute-start.5 = (bf16[896,1024]{1,0:T(8,128)(2,1)}, bf16[896,1024]{1,0:T(8,128)(2,1)}, u32[]{:S(2)}, u32[]{:S(2)}) collective-permute-start(bf16[896,1024]{1,0:T(8,128)(2,1)} %dynamic-slice_convert_fusion), channel_id=1, source_target_pairs={{0,1},{1,0},{2,3},{3,2},{4,5},{5,4},{6,7},{7,6},{8,9},{9,8},{10,11... | collective-permute-start | bytes 5505032 | tf_op jit(solution)/shard_map/ppermute | solution.py:47
  854.8 22.9 %collective-permute-start.7 = (bf16[3,64,1024]{2,1,0:T(8,128)(2,1)}, bf16[3,64,1024]{2,1,0:T(8,128)(2,1)}, u32[]{:S(2)}, u32[]{:S(2)}) collective-permute-start(bf16[3,64,1024]{2,1,0:T(8,128)(2,1)} %dynamic-slice_bitcast_fusion), channel_id=1, source_target_pairs={{0,1},{1,0},{2,3},{3,2},{4,5},{5,4},{6,7},{7,6},{8,9},{9,8},{10,11... | collective-permute-start | bytes 1179656 | tf_op jit(solution)/shard_map/ppermute | solution.py:47
  884.5 15.1 %slice-start.4 = ((s8[7340032]{0:T(1024)(128)(4,1)}), s8[3145728]{0:T(1024)(128)(4,1)S(1)}, s32[]{:S(2)}) async-start(s8[7340032]{0:T(1024)(128)(4,1)} %bitcast.133), calls=%async_computation.5 | async-start | bytes 6291456
  889.7 10.0 %slice-start.2 = ((s8[7340032]{0:T(1024)(128)(4,1)}), s8[4194304]{0:T(1024)(128)(4,1)S(1)}, s32[]{:S(2)}) async-start(s8[7340032]{0:T(1024)(128)(4,1)} %bitcast.131), calls=%async_computation.3 | async-start | bytes 8388608
  892.5 8.3 copy-start.18
  900.8 43.1 %copy-start.35 = (f32[3,64]{1,0:T(4,128)S(1)}, f32[3,64]{1,0:T(4,128)}, u32[]{:S(2)}) copy-start(f32[3,64]{1,0:T(4,128)} %param.35) | copy-start | bytes 2308
  900.8 43.1 %copy-start.36 = (f32[3,64]{1,0:T(4,128)S(1)}, f32[3,64]{1,0:T(4,128)}, u32[]{:S(2)}) copy-start(f32[3,64]{1,0:T(4,128)} %param.36) | copy-start | bytes 2308
  900.8 43.1 %copy-start.37 = (f32[3,64]{1,0:T(4,128)S(1)}, f32[3,64]{1,0:T(4,128)}, u32[]{:S(2)}) copy-start(f32[3,64]{1,0:T(4,128)} %param.37) | copy-start | bytes 2308
  (29 other events, 141.8 us)
Sparse Core Ops, SparseCore 0:
  131.2 171.2 all-gather.1

commit v3 on v2

--- a/solution.py
+++ b/solution.py
@@ -294,12 +294,21 @@
     return (z * 4 + x * 2 + core, lax.axis_index("mp"))
 
 
-def scatter_kernel(compute, chunks, n_in, *refs):
-    ins, out_ref = refs[:n_in], refs[n_in]
+def scatter_barrier(z, x, core, with_mp=False):
+    barrier = pltpu.get_barrier_semaphore()
+    targets = [device_at(z, x, 1 - core), device_at(z, 1 - x, core)]
+    targets += [device_at(lax.rem(z + hop, DEPTH), x, core) for hop in range(1, DEPTH)]
+    if with_mp:
+        targets.append((lax.axis_index("dp"), 1 - lax.axis_index("mp")))
+    for target in targets:
+        pl.semaphore_signal(barrier, 1, device_id=target, device_id_type=MESH_ID)
+    pl.semaphore_wait(barrier, len(targets))
+
+
+def scatter_step(step, chunks, compute, out_ref, scratch):
     (own, core_out, core_in, keep, x_out, x_in, sums, mine, z_out, z_in,
-     core_send, core_recv, x_send, x_recv, z_send, z_recv) = refs[n_in + 1 :]
+     core_send, core_recv, x_send, x_recv, z_send, z_recv) = scratch
     z, x, core = device_place()
-    step = pl.program_id(0)
 
     def core_copy(p):
         return pltpu.make_async_remote_copy(
@@ -319,25 +328,15 @@
             z_send.at[lax.rem(p, 4), hop - 1], z_recv.at[lax.rem(p, 8), hop - 1],
             device_id=device_at(lax.rem(z + hop, DEPTH), x, core), device_id_type=MESH_ID)
 
-    @pl.when(step == 0)
-    def _():
-        barrier = pltpu.get_barrier_semaphore()
-        pl.semaphore_signal(barrier, 1, device_id=device_at(z, x, 1 - core), device_id_type=MESH_ID)
-        pl.semaphore_signal(barrier, 1, device_id=device_at(z, 1 - x, core), device_id_type=MESH_ID)
-        for hop in range(1, DEPTH):
-            pl.semaphore_signal(
-                barrier, 1, device_id=device_at(lax.rem(z + hop, DEPTH), x, core), device_id_type=MESH_ID)
-        pl.semaphore_wait(barrier, DEPTH + 1)
-
     @pl.when(step < chunks)
     def _():
         @pl.when(step >= 2)
         def _():
             core_copy(step - 2).wait_send()
 
-        core_out[lax.rem(step, 2)] = compute(step, 1 - core, *ins).astype(BF)
+        core_out[lax.rem(step, 2)] = compute(step, 1 - core).astype(BF)
         core_copy(step).start()
-        own[lax.rem(step, 2)] = compute(step, core, *ins)
+        own[lax.rem(step, 2)] = compute(step, core)
 
     @pl.when((step >= 1) & (step < chunks + 1))
     def _():
@@ -387,107 +386,491 @@
                 z_copy(p, hop).wait_send()
 
 
-def scatter_call(compute, chunks, block, operands, in_specs, collective, flops):
-    rows, lanes = block
+def scatter_scratch(rows, lanes):
     quad = (DEPTH, 2, rows, lanes)
     line = (DEPTH, rows, lanes)
-    return pl.pallas_call(
-        functools.partial(scatter_kernel, compute, chunks, len(operands)),
+    dma = pltpu.SemaphoreType.DMA
+    return [
+        pltpu.VMEM((2, *quad), F32),
+        pltpu.VMEM((2, *quad), BF),
+        pltpu.VMEM((4, *quad), BF),
+        pltpu.VMEM((2, *line), F32),
+        pltpu.VMEM((2, *line), BF),
+        pltpu.VMEM((4, *line), BF),
+        pltpu.VMEM(line, F32),
+        pltpu.VMEM((4, rows, lanes), F32),
+        pltpu.VMEM((4, DEPTH - 1, rows, lanes), BF),
+        pltpu.VMEM((8, DEPTH - 1, rows, lanes), BF),
+        dma((2,)), dma((4,)), dma((2,)), dma((4,)), dma((4, DEPTH - 1)), dma((8, DEPTH - 1)),
+    ]
+
+
+def scatter_out(chunks, rows, lanes):
+    spec = pl.BlockSpec((1, rows, lanes), lambda q: (jnp.maximum(q - Z_LAG, 0), 0, 0))
+    return spec, jax.ShapeDtypeStruct((chunks, rows, lanes), F32)
+
+
+def fixed(shape):
+    return pl.BlockSpec(shape, lambda q: (0,) * len(shape), pipeline_mode=pl.Buffered(1))
+
+
+def glu_kernel(
+    hidden_blocks, full_blocks, normed_ref, back_ref, left_ref, glu_ref,
+    out_ref, sum_own, sum_came, half_own, half_send, half_came,
+    acts, weights_in, weights_back, sum_stage, half_stage,
+    in_sem, back_sem, stage_sem, sum_send, sum_recv, half_send_sem, half_recv, *scratch,
+):
+    z, x, core = device_place()
+    dp, mp = lax.axis_index("dp"), lax.axis_index("mp")
+    step = pl.program_id(0)
+    chunks = 3 * hidden_blocks
+    rows = normed_ref.shape[0]
+    row_block = rows // 2
+    half_blocks = full_blocks // 2
+    across = (((1,), (1,)), ((), ()))
+
+    def lane_block(index):
+        return pl.ds(pl.multiple_of(index * LANES, LANES), LANES)
+
+    def load_in(index):
+        return pltpu.make_async_copy(glu_ref.at[:, :, lane_block(index)], weights_in, in_sem)
+
+    def load_back(index):
+        return pltpu.make_async_copy(glu_ref.at[:, lane_block(index), :], weights_back, back_sem)
+
+    def stage(index, kind, target):
+        source = (sum_stage, half_stage)[kind].at[lax.rem(index, 2)]
+        return pltpu.make_async_copy(source, target, stage_sem.at[lax.rem(index, 2), kind])
+
+    def half_spot(index):
+        return lax.rem(index, half_blocks)
+
+    def sum_copy(index):
+        return pltpu.make_async_remote_copy(
+            sum_own.at[:, lane_block(index)], sum_came.at[:, lane_block(index)],
+            sum_send.at[index], sum_recv.at[index], device_id=(dp, 1 - mp), device_id_type=MESH_ID)
+
+    def half_copy(spot):
+        return pltpu.make_async_remote_copy(
+            half_send.at[:, lane_block(spot)], half_came.at[:, lane_block(spot)],
+            half_send_sem.at[spot], half_recv.at[spot], device_id=(dp, 1 - mp), device_id_type=MESH_ID)
+
+    @pl.when(step == 0)
+    def _():
+        load_in(0).start()
+        load_back(0).start()
+        scatter_barrier(z, x, core, with_mp=True)
+
+    @pl.when(step < hidden_blocks)
+    def _():
+        load_in(step).wait()
+        lanes = lane_block(step)
+
+        def part(index, _):
+            part_rows = pl.ds(pl.multiple_of(index * row_block, row_block), row_block)
+            normed = normed_ref[part_rows, :]
+            pre_act = jnp.dot(normed, weights_in[0], preferred_element_type=F32)
+            pre_up = jnp.dot(normed, weights_in[1], preferred_element_type=F32)
+            grad_hidden = jnp.dot(back_ref[part_rows, :], weights_in[2], preferred_element_type=F32)
+            sigma = jax.nn.sigmoid(pre_act)
+            act_part = pre_act * sigma
+            acts[0, part_rows, lanes] = (
+                grad_hidden * pre_up * (sigma * (1.0 + pre_act * (1.0 - sigma)))).astype(BF)
+            acts[1, part_rows, lanes] = (grad_hidden * act_part).astype(BF)
+            acts[2, part_rows, lanes] = (act_part * pre_up).astype(BF)
+            return 0
+
+        lax.fori_loop(0, rows // row_block, part, 0)
+
+        @pl.when(step + 1 < hidden_blocks)
+        def _():
+            load_in(step + 1).start()
+
+    @pl.when((step > hidden_blocks) & (step <= hidden_blocks + full_blocks))
+    def _():
+        index = step - hidden_blocks - 1
+        stage(index, 0, sum_own.at[:, lane_block(index)]).wait()
+        sum_copy(index).start()
+        spot = half_spot(index)
+        stage(index, 1, half_own.at[:, lane_block(spot)]).wait()
+
+        @pl.when(index // half_blocks != mp)
+        def _():
+            half_copy(spot).start()
+
+    @pl.when((step >= hidden_blocks) & (step < hidden_blocks + full_blocks))
+    def _():
+        index = step - hidden_blocks
+        load_back(index).wait()
+        slot = lax.rem(index, 2)
+
+        def part(at, _):
+            part_rows = pl.ds(pl.multiple_of(at * row_block, row_block), row_block)
+            dot = functools.partial(
+                lax.dot_general, dimension_numbers=across, preferred_element_type=F32)
+            grad_normed = dot(acts[0, part_rows, :], weights_back[0])
+            grad_normed += dot(acts[1, part_rows, :], weights_back[1])
+            sum_stage[slot, part_rows, :] = grad_normed.astype(BF)
+            half_stage[slot, part_rows, :] = dot(acts[2, part_rows, :], weights_back[2]).astype(BF)
+            return 0
+
+        lax.fori_loop(0, rows // row_block, part, 0)
+
+        @pl.when(index + 1 < full_blocks)
+        def _():
+            load_back(index + 1).start()
+
+        stage(index, 0, sum_own.at[:, lane_block(index)]).start()
+        spot = half_spot(index)
+
+        @pl.when(index // half_blocks == mp)
+        def _():
+            stage(index, 1, half_own.at[:, lane_block(spot)]).start()
+
+        @pl.when(index // half_blocks != mp)
+        def _():
+            stage(index, 1, half_send.at[:, lane_block(spot)]).start()
+
+    def compute(q, core_side):
+        kind = lax.rem(q, 3)
+        side = left_ref[kind // 2, :, :, core_side]
+        side_rows = side.shape[2]
+        product = jnp.dot(
+            side.reshape(DEPTH * 2 * side_rows, rows), acts[kind, :, lane_block(q // 3)],
+            preferred_element_type=F32)
+        return product.reshape(DEPTH, 2, side_rows, LANES)
+
+    scatter_step(step, chunks, compute, out_ref, scratch)
+
+    @pl.when(step == chunks + Z_LAG - 1)
+    def _():
+        for index in range(full_blocks):
+            sum_copy(index).wait()
+        for spot in range(half_blocks):
+            half_copy(spot).wait()
+
+
+def glu_call(normed, back_low, glu, collective):
+    rows, full = normed.shape
+    hidden = glu.shape[2]
+    hidden_blocks, full_blocks = hidden // LANES, full // LANES
+    block = full // 16
+    chunks = 3 * hidden_blocks
+    left = jnp.stack([normed.T, back_low.T]).reshape(2, DEPTH, 2, 2, block, rows)
+    any_space = pl.BlockSpec(memory_space=pl.ANY)
+    out_spec, out_shape = scatter_out(chunks, block, LANES)
+    dma = pltpu.SemaphoreType.DMA
+    wide = jax.ShapeDtypeStruct((rows, full), BF)
+    half = jax.ShapeDtypeStruct((rows, full // 2), BF)
+    out, sum_own, sum_came, half_own, _, half_came = pl.pallas_call(
+        functools.partial(glu_kernel, hidden_blocks, full_blocks),
         grid=(chunks + Z_LAG,),
-        in_specs=in_specs,
-        out_specs=pl.BlockSpec((1, rows, lanes), lambda q: (jnp.maximum(q - Z_LAG, 0), 0, 0)),
-        out_shape=jax.ShapeDtypeStruct((chunks, rows, lanes), F32),
+        in_specs=[fixed(normed.shape), fixed(back_low.shape), fixed(left.shape), any_space],
+        out_specs=[out_spec] + [any_space] * 5,
+        out_shape=[out_shape, wide, wide, half, half, half],
         scratch_shapes=[
-            pltpu.VMEM((2, *quad), F32),
-            pltpu.VMEM((2, *quad), BF),
-            pltpu.VMEM((4, *quad), BF),
-            pltpu.VMEM((2, *line), F32),
-            pltpu.VMEM((2, *line), BF),
-            pltpu.VMEM((4, *line), BF),
-            pltpu.VMEM(line, F32),
-            pltpu.VMEM((4, rows, lanes), F32),
-            pltpu.VMEM((4, DEPTH - 1, rows, lanes), BF),
-            pltpu.VMEM((8, DEPTH - 1, rows, lanes), BF),
-            pltpu.SemaphoreType.DMA((2,)),
-            pltpu.SemaphoreType.DMA((4,)),
-            pltpu.SemaphoreType.DMA((2,)),
-            pltpu.SemaphoreType.DMA((4,)),
-            pltpu.SemaphoreType.DMA((4, DEPTH - 1)),
-            pltpu.SemaphoreType.DMA((8, DEPTH - 1)),
+            pltpu.VMEM((3, rows, hidden), BF),
+            pltpu.VMEM((3, full, LANES), BF),
+            pltpu.VMEM((3, LANES, hidden), BF),
+            pltpu.VMEM((2, rows, LANES), BF),
+            pltpu.VMEM((2, rows, LANES), BF),
+            dma(()), dma(()), dma((2, 2)),
+            dma((full_blocks,)), dma((full_blocks,)), dma((full_blocks // 2,)), dma((full_blocks // 2,)),
+            *scatter_scratch(block, LANES),
+        ],
+        compiler_params=pltpu.CompilerParams(
+            collective_id=collective, has_side_effects=True, vmem_limit_bytes=62 * 1024 * 1024),
+        cost_estimate=pl.CostEstimate(
+            flops=18 * rows * full * hidden, bytes_accessed=6 * full * hidden * 2,
+            transcendentals=rows * hidden),
+    )(normed, back_low, left, glu)
+    return out, sum_own, sum_came, half_own, half_came
+
+
+def mixer_kernel(
+    full_blocks, left_ref, grad_ref, left_out_ref, right_out_ref, gain_ref, tokens_ref, inverse_ref,
+    weights_ref, out_ref, half_own, half_send, half_came, swap_came,
+    weights, token_block, gain_sum, gain_chunk, total, swap_out, half_stage,
+    load_sem, stage_sem, half_send_sem, half_recv, swap_send, swap_recv, *scratch,
+):
+    z, x, core = device_place()
+    dp, mp = lax.axis_index("dp"), lax.axis_index("mp")
+    step = pl.program_id(0)
+    tokens, channels = grad_ref.shape[1], grad_ref.shape[2]
+    block, half = left_ref.shape[3], left_out_ref.shape[3]
+    outer = full_blocks // 2
+    across = channels // LANES
+    gains = outer + 3 * across
+    chunks = gains + 1
+    half_blocks = full_blocks // 2
+    row_block = tokens // 2
+    partner = (dp, 1 - mp)
+
+    def lane_block(index):
+        return pl.ds(pl.multiple_of(index * LANES, LANES), LANES)
+
+    def loads(index):
+        return (
+            pltpu.make_async_copy(weights_ref.at[:, lane_block(index), :], weights, load_sem.at[0]),
+            pltpu.make_async_copy(tokens_ref.at[:, lane_block(index)], token_block, load_sem.at[1]),
+        )
+
+    def stage(index, target):
+        return pltpu.make_async_copy(
+            half_stage.at[lax.rem(index, 2)], target, stage_sem.at[lax.rem(index, 2)])
+
+    def half_copy(spot):
+        return pltpu.make_async_remote_copy(
+            half_send.at[:, lane_block(spot)], half_came.at[:, lane_block(spot)],
+            half_send_sem.at[spot], half_recv.at[spot], device_id=partner, device_id_type=MESH_ID)
+
+    def swap_copy(index):
+        return pltpu.make_async_remote_copy(
+            swap_out.at[lax.rem(index, 2)], swap_came.at[index],
+            swap_send.at[lax.rem(index, 2)], swap_recv.at[index],
+            device_id=partner, device_id_type=MESH_ID)
+
+    @pl.when(step == 0)
+    def _():
+        for one in loads(0):
+            one.start()
+        gain_chunk[...] = jnp.zeros_like(gain_chunk)
+        gain_sum[...] = jnp.zeros_like(gain_sum)
+        scatter_barrier(z, x, core, with_mp=True)
+
+    @pl.when((step > 0) & (step <= full_blocks))
+    def _():
+        index = step - 1
+        spot = lax.rem(index, half_blocks)
+        stage(index, half_own.at[:, lane_block(spot)]).wait()
+
+        @pl.when(index // half_blocks != mp)
+        def _():
+            half_copy(spot).start()
+
+    @pl.when(step < full_blocks)
+    def _():
+        for one in loads(step):
+            one.wait()
+        slot = lax.rem(step, 2)
+        spot = lax.rem(step, half_blocks)
+
+        def part(at, gain_in):
+            part_rows = pl.ds(pl.multiple_of(at * row_block, row_block), row_block)
+            dot = functools.partial(
+                lax.dot_general, dimension_numbers=(((1,), (1,)), ((), ())), preferred_element_type=F32)
+            grad = dot(grad_ref[0, part_rows, :], weights[0])
+            grad += dot(grad_ref[1, part_rows, :], weights[1])
+            grad += dot(grad_ref[2, part_rows, :], weights[2])
+            half_stage[slot, part_rows, :] = grad.astype(BF)
+            unit = token_block[part_rows, :].astype(F32) * inverse_ref[part_rows, :]
+            return gain_in + jnp.sum(grad * unit, axis=0, keepdims=True)
+
+        gain_in = lax.fori_loop(0, tokens // row_block, part, jnp.zeros((1, LANES), F32))
+        gain_sum[2 * step, 0:1, :] = gain_in[:, :128]
+        gain_sum[2 * step + 1, 0:1, :] = gain_in[:, 128:]
+
+        @pl.when(step + 1 < full_blocks)
+        def _():
+            for one in loads(step + 1):
+                one.start()
+
+        @pl.when(step // half_blocks == mp)
+        def _():
+            stage(step, half_own.at[:, lane_block(spot)]).start()
+
+        @pl.when(step // half_blocks != mp)
+        def _():
+            stage(step, half_send.at[:, lane_block(spot)]).start()
+
+    def compute(q, core_side):
+        def outer_chunk():
+            side = left_out_ref[:, :, core_side].reshape(channels // 2, tokens)
+            parts = [
+                jnp.dot(side, right_out_ref[:, lane_block(2 * q + at)], preferred_element_type=F32)
+                for at in (0, 1)
+            ]
+            parts = [part.reshape(DEPTH, 2, half, LANES) for part in parts]
+            return jnp.concatenate(parts, axis=2)
+
+        def inner_chunk():
+            at = q - outer
+            side = left_ref[:, :, core_side].reshape(DEPTH * 2 * block, tokens)
+            right = grad_ref[at // across, :, lane_block(lax.rem(at, across))]
+            return jnp.dot(side, right, preferred_element_type=F32).reshape(DEPTH, 2, block, LANES)
+
+        def gain_block():
+            for owner in range(2 * DEPTH):
+                line = 2 * owner + core_side
+                gain_chunk[owner // 2, owner % 2, 0:8, 0:128] = gain_ref[line] + gain_sum[line]
+            return gain_chunk[...]
+
+        return lax.cond(
+            q < outer, outer_chunk, lambda: lax.cond(q < gains, inner_chunk, gain_block))
+
+    scatter_step(step, chunks, compute, out_ref, scratch)
+
+    @pl.when(step >= Z_LAG + outer)
+    def _():
+        index = step - Z_LAG - outer
+
+        @pl.when(index >= 2)
+        def _():
+            swap_copy(index - 2).wait_send()
+
+        total[...] = out_ref[0]
+        first = jnp.where(index == gains - outer, 0, 1 - mp) * half
+        swap_out[lax.rem(index, 2)] = total[pl.ds(pl.multiple_of(first, half), half), :].astype(BF)
+        swap_copy(index).start()
+
+    @pl.when(step == chunks + Z_LAG - 1)
+    def _():
+        for spot in range(half_blocks):
+            half_copy(spot).wait()
+        for index in range(gains - outer + 1):
+            swap_copy(index).wait_recv()
+        for index in range(gains - outer - 1, gains - outer + 1):
+            swap_copy(index).wait_send()
+
+
+def mixer_call(left_in, grad_pre, left_out, right_out, gain_parts, tokens, inverse, weights, collective):
+    _, rows, channels = grad_pre.shape
+    full = left_in.shape[0]
+    block, half = full // 16, channels // 16
+    full_blocks, across = full // LANES, channels // LANES
+    outer, inner = full_blocks // 2, 3 * across
+    chunks = outer + inner + 1
+    any_space = pl.BlockSpec(memory_space=pl.ANY)
+    dma = pltpu.SemaphoreType.DMA
+    out_spec, out_shape = scatter_out(chunks, block, LANES)
+    part = jax.ShapeDtypeStruct((rows, full // 2), BF)
+    out, half_own, _, half_came, swap_came = pl.pallas_call(
+        functools.partial(mixer_kernel, full_blocks),
+        grid=(chunks + Z_LAG,),
+        in_specs=[
+            fixed((DEPTH, 2, 2, block, rows)), fixed(grad_pre.shape),
+            fixed((DEPTH, 2, 2, half, rows)), fixed(right_out.shape), fixed(gain_parts.shape),
+            any_space, fixed(inverse.shape), any_space,
+        ],
+        out_specs=[out_spec] + [any_space] * 4,
+        out_shape=[
+            out_shape, part, part, part, jax.ShapeDtypeStruct((inner + 1, half, LANES), BF),
+        ],
+        scratch_shapes=[
+            pltpu.VMEM((3, LANES, channels), BF),
+            pltpu.VMEM((rows, LANES), BF),
+            pltpu.VMEM((16, 8, 128), F32),
+            pltpu.VMEM((DEPTH, 2, block, LANES), F32),
+            pltpu.VMEM((block, LANES), F32),
+            pltpu.VMEM((2, half, LANES), BF),
+            pltpu.VMEM((2, rows, LANES), BF),
+            dma((2,)), dma((2,)), dma((full_blocks // 2,)), dma((full_blocks // 2,)),
+            dma((2,)), dma((inner + 1,)),
+            *scatter_scratch(block, LANES),
         ],
         compiler_params=pltpu.CompilerParams(
             collective_id=collective, has_side_effects=True, vmem_limit_bytes=VMEM_LIMIT),
-        cost_estimate=pl.CostEstimate(flops=flops, bytes_accessed=flops // 500, transcendentals=0),
-    )(*operands)
-
-
-def glu_scatter(left, right, collective):
-    _, full, tokens = left.shape
-    hidden = right.shape[2]
-    across = hidden // LANES
-    rows = full // 16
-
-    def compute(q, core, left_ref, right_ref):
-        side = left_ref[jnp.minimum(q, 3 * across - 1) // (2 * across), :, :, core]
-        product = jnp.dot(side.reshape(full // 2, tokens), right_ref[0], preferred_element_type=F32)
-        return product.reshape(DEPTH, 2, rows, LANES)
-
-    chunks = 3 * across
-    spot = lambda q: jnp.minimum(q, chunks - 1)
-    out = scatter_call(
-        compute, chunks, (rows, LANES),
-        (left.reshape(2, DEPTH, 2, 2, rows, tokens), right),
-        [
-            pl.BlockSpec((2, DEPTH, 2, 2, rows, tokens), lambda q: (0, 0, 0, 0, 0, 0), pipeline_mode=pl.Buffered(1)),
-            pl.BlockSpec((1, tokens, LANES), lambda q: (spot(q) // across, 0, lax.rem(spot(q), across))),
+        cost_estimate=pl.CostEstimate(
+            flops=14 * full * rows * channels, bytes_accessed=16 * full * channels, transcendentals=0),
+    )(
+        left_in.reshape(DEPTH, 2, 2, block, rows), grad_pre,
+        left_out.reshape(DEPTH, 2, 2, half, rows), right_out, gain_parts, tokens, inverse, weights,
+    )
+    place = lax.axis_index("mp")
+    out_own = out[:outer].reshape(outer, 2, half, LANES).transpose(2, 0, 1, 3).reshape(half, full)
+    own = lax.dynamic_slice_in_dim(out[outer : outer + inner], place * half, half, 1)
+    came = swap_came[:inner].astype(F32)
+    first = place == 0
+    in_own = jnp.stack([jnp.where(first, own, came), jnp.where(first, came, own)])
+    in_own = in_own.reshape(2, 3, across, half, LANES).transpose(1, 3, 0, 2, 4)
+    in_own = in_own.reshape(3, half, 2, channels)
+    gains = out[chunks - 1, :3, :128] + swap_came[inner, :3, :128].astype(F32)
+    return in_own, out_own, gains, half_own.astype(F32) + half_came.astype(F32)
+
+
+def middle_back_kernel(
+    sum_own_ref, sum_came_ref, middle_ref, cot_ref, tokens_ref, weight_ref, gain_ref, mixer_ref,
+    grad_own_ref, low_ref, mean_ref, gated_ref, gain_grad_ref,
+):
+    rows, full = middle_ref.shape
+    part = full // 2
+    middle = middle_ref[...]
+    inverse = lax.rsqrt(jnp.mean(middle * middle, axis=-1, keepdims=True) + EPSILON)
+    unit = middle * inverse
+    grad_normed = sum_own_ref[...].astype(F32) + sum_came_ref[...].astype(F32)
+    gain_grad = jnp.sum(grad_normed * unit, axis=0, keepdims=True)
+    before = jnp.where(pl.program_id(0) == 0, 0.0, gain_grad_ref[...])
+    gain_grad_ref[...] = before + gain_grad
+    scaled = grad_normed * gain_ref[...]
+    dots = jnp.mean(scaled * unit, axis=-1, keepdims=True)
+    back = cot_ref[...].astype(F32) * weight_ref[...]
+    grad = back + inverse * (scaled - unit * dots)
+    first = lax.axis_index("mp") == 0
+    grad_own_ref[...] = jnp.where(first, grad[:, :part], grad[:, part:])
+    low = grad.astype(BF)
+    low_ref[...] = low
+    branch = middle - tokens_ref[...].astype(F32)
+    mean_ref[...] = jnp.mean(low.astype(F32) * branch, axis=-1, keepdims=True)
+    gated_ref[...] = lax.dot_general(
+        low, mixer_ref[...], (((1,), (1,)), ((), ())), preferred_element_type=F32)
+
+
+def middle_back(sum_own, sum_came, middle, cot, tokens, weight, gain, mixer_out):
+    rows, full = middle.shape
+    channels = mixer_out.shape[0]
+    step = 128 if rows % 128 == 0 else rows
+    line = lambda width: pl.BlockSpec((step, width), lambda r: (r, 0))
+    shape = jax.ShapeDtypeStruct
+    return pl.pallas_call(
+        middle_back_kernel,
+        grid=(rows // step,),
+        in_specs=[line(full)] * 5 + [line(1), fixed((1, full)), fixed(mixer_out.shape)],
+        out_specs=[
+            line(full // 2), line(full), line(1), line(channels),
+            pl.BlockSpec((1, full), lambda r: (0, 0)),
         ],
-        collective, 2 * 3 * full * tokens * hidden)
-    return out.reshape(3, across, rows, LANES).transpose(0, 2, 1, 3).reshape(3, rows, hidden)
-
-
-def mixer_scatter(left_in, right_in, left_out, right_out, collective):
-    full, tokens = left_in.shape
-    channels = right_in.shape[2]
-    rows = full // 16
-    half = channels // 16
-    across = channels // LANES
-    across_out = full // (2 * LANES)
-    inside = 3 * across
-    chunks = inside + across_out
-
-    def compute(q, core, left_ref, right_ref, left_out_ref, right_out_ref):
-        def first():
-            side = left_ref[:, :, core].reshape(full // 2, tokens)
-            product = jnp.dot(side, right_ref[0], preferred_element_type=F32)
-            return product.reshape(DEPTH, 2, rows, LANES)
-
-        def second():
-            side = left_out_ref[:, :, core].reshape(channels // 2, tokens)
-            parts = [
-                jnp.dot(side, right_out_ref[:, at : at + LANES], preferred_element_type=F32).reshape(
-                    DEPTH, 2, half, LANES)
-                for at in (0, LANES)
-            ]
-            return jnp.concatenate(parts, axis=2)
-
-        return lax.cond(q < inside, first, second)
-
-    spot = lambda q: jnp.minimum(q, inside - 1)
-    spot_out = lambda q: jnp.clip(q - inside, 0, across_out - 1)
-    out = scatter_call(
-        compute, chunks, (rows, LANES),
-        (left_in.reshape(DEPTH, 2, 2, rows, tokens), right_in,
-         left_out.reshape(DEPTH, 2, 2, half, tokens), right_out),
-        [
-            pl.BlockSpec((DEPTH, 2, 2, rows, tokens), lambda q: (0, 0, 0, 0, 0), pipeline_mode=pl.Buffered(1)),
-            pl.BlockSpec((1, tokens, LANES), lambda q: (spot(q) // across, 0, lax.rem(spot(q), across))),
-            pl.BlockSpec((DEPTH, 2, 2, half, tokens), lambda q: (0, 0, 0, 0, 0), pipeline_mode=pl.Buffered(1)),
-            pl.BlockSpec((tokens, 2 * LANES), lambda q: (0, spot_out(q))),
+        out_shape=[
+            shape((rows, full // 2), F32), shape((rows, full), BF), shape((rows, 1), F32),
+            shape((rows, channels), F32), shape((1, full), F32),
         ],
-        collective, 2 * tokens * (3 * full * channels + channels * full))
-    first = out[:inside].reshape(3, across, rows, LANES).transpose(0, 2, 1, 3).reshape(3, rows, channels)
-    second = out[inside:].reshape(across_out, 2, half, LANES).transpose(2, 0, 1, 3).reshape(half, full)
-    return first, second
+        compiler_params=pltpu.CompilerParams(vmem_limit_bytes=VMEM_LIMIT),
+        cost_estimate=pl.CostEstimate(
+            flops=2 * rows * full * channels, bytes_accessed=rows * full * 20, transcendentals=0),
+    )(sum_own, sum_came, middle, cot, tokens, weight, gain[None], mixer_out)
+
+
+def glu_update_kernel(scale, act_ref, up_ref, out_ref, *refs):
+    in_refs, down_refs, in_new, down_new = refs[:3], refs[3:6], refs[6:9], refs[9:12]
+    count = STEP_NUMBER
+    for at, grad_ref in ((0, act_ref), (1, up_ref)):
+        new = adamw_update(
+            *(ref[at] for ref in in_refs), grad_ref[0] * scale, count, MATRIX_RATE, DECAY_RATE)
+        for ref, value in zip(in_new, new):
+            ref[at] = value
+    new = adamw_update(
+        *(ref[...] for ref in down_refs), out_ref[0].T * scale, count, MATRIX_RATE, DECAY_RATE)
+    for ref, value in zip(down_new, new):
+        ref[...] = value
+
+
+def glu_update(sums, ins, downs, scale):
+    _, rows, lanes = sums.shape
+    blocks = ins[0].shape[2] // lanes
+    sum_spec = lambda kind: pl.BlockSpec((1, rows, lanes), lambda q: (3 * q + kind, 0, 0))
+    in_spec = pl.BlockSpec((2, rows, lanes), lambda q: (0, 0, q))
+    down_spec = pl.BlockSpec((lanes, rows), lambda q: (q, 0))
+    new = pl.pallas_call(
+        functools.partial(glu_update_kernel, scale),
+        grid=(blocks,),
+        in_specs=[sum_spec(0), sum_spec(1), sum_spec(2)] + [in_spec] * 3 + [down_spec] * 3,
+        out_specs=[in_spec] * 3 + [down_spec] * 3,
+        out_shape=[jax.ShapeDtypeStruct(ins[0].shape, F32)] * 3 + [jax.ShapeDtypeStruct(downs[0].shape, F32)] * 3,
+        compiler_params=pltpu.CompilerParams(vmem_limit_bytes=VMEM_LIMIT),
+        cost_estimate=pl.CostEstimate(
+            flops=60 * rows * lanes * blocks, bytes_accessed=84 * rows * lanes * blocks,
+            transcendentals=6 * rows * lanes * blocks),
+    )(sums, sums, sums, *ins, *downs)
+    return tuple(new[:3]), tuple(new[3:])
 
 
 ITEMS = 4
@@ -692,6 +1075,8 @@
     part = full // narrow
     quick = groups == 16 and narrow == 2
 
+    cot_full = mp_gather(cotangent.reshape(rows, part))
+
     domain_ids = jnp.arange(NDOM, dtype=jnp.int32)
     member = (domains[..., 0][..., None] == domain_ids).astype(F32)
     live_counts = lengths.astype(F32)
@@ -716,7 +1101,7 @@
         mixer_out = lax.all_gather(mixer_low[3], "dp", axis=0, tiled=True)
         counts = lax.psum(counts, "dp")
     glu_low = jnp.concatenate([glu_in_master.astype(BF), glu_out_master.astype(BF).T[None]])
-    glu_low, mixer_in = lax.optimization_barrier((glu_low, mixer_in))
+    glu_low, mixer_in, cot_full = lax.optimization_barrier((glu_low, mixer_in, cot_full))
     glu = lax.all_gather(glu_low, "dp", axis=1, tiled=True)
 
     seq_weight = jnp.sum(counts) / (NDOM * jnp.sum(member * counts, axis=-1))
@@ -730,7 +1115,8 @@
     bound = own_channels(lower_bound)
     state_gain = own_channels(gain_full[1])
 
-    seq_in = tokens.reshape(rows, full).astype(F32)
+    token_rows = tokens.reshape(rows, full)
+    seq_in = token_rows.astype(F32)
     inverse_in = inverse_rms(seq_in)
     unit_in = seq_in * inverse_in
     normed_in = (unit_in * gain_full[0]).astype(BF)
@@ -746,111 +1132,112 @@
     unit_mid = middle * inverse_mid
     normed_mid = (unit_mid * gain_full[2]).astype(BF)
 
-    cot_full = mp_gather(cotangent.reshape(rows, part))
     back = cot_full.astype(F32) * token_weight
     back_low = back.astype(BF)
-    pre_act = jnp.dot(normed_mid, glu[0], preferred_element_type=F32)
-    pre_up = jnp.dot(normed_mid, glu[1], preferred_element_type=F32)
-    grad_hidden = jnp.dot(back_low, glu[2], preferred_element_type=F32)
-    act_sig = jax.nn.sigmoid(pre_act)
-    act_part = pre_act * act_sig
-    hidden = (act_part * pre_up).astype(BF)
-    grad_act = (grad_hidden * pre_up * silu_slope(pre_act)).astype(BF)
-    grad_up = (grad_hidden * act_part).astype(BF)
     across = (((1,), (1,)), ((), ()))
     down = (((0,), (0,)), ((), ()))
     dot = functools.partial(lax.dot_general, preferred_element_type=F32)
-    grad_normed_part = dot(grad_act, glu[0], across) + dot(grad_up, glu[1], across)
-    grad_normed_low = grad_normed_part.astype(BF)
-    grad_normed_came = partner_swap(grad_normed_low) if quick else None
-    partial_out = dot(hidden, glu[2], across)
-    rights = jnp.stack([grad_act, grad_up, hidden])
     if quick:
-        lefts = jnp.stack([normed_mid.T, back_low.T])
-        lefts, rights, grad_normed_low = lax.optimization_barrier((lefts, rights, grad_normed_low))
-        glu_own = glu_scatter(lefts, rights, 0)
-        glu_own, grad_normed_came = lax.optimization_barrier((glu_own, grad_normed_came))
-        grad_normed = grad_normed_low.astype(F32) + grad_normed_came.astype(F32)
+        glu_sums, sum_own, sum_came, half_own, half_came = glu_call(normed_mid, back_low, glu, 0)
+        branch = half_own.astype(F32) + half_came.astype(F32)
     else:
-        grad_normed = mp_sum(grad_normed_part)
+        pre_act = jnp.dot(normed_mid, glu[0], preferred_element_type=F32)
+        pre_up = jnp.dot(normed_mid, glu[1], preferred_element_type=F32)
+        grad_hidden = jnp.dot(back_low, glu[2], preferred_element_type=F32)
+        act_part = jax.nn.silu(pre_act)
+        hidden = (act_part * pre_up).astype(BF)
+        grad_act = (grad_hidden * pre_up * silu_slope(pre_act)).astype(BF)
+        grad_up = (grad_hidden * act_part).astype(BF)
+        grad_normed = mp_sum(dot(grad_act, glu[0], across) + dot(grad_up, glu[1], across))
         glu_grad = jnp.stack(
             [dot(normed_mid, grad_act, down), dot(normed_mid, grad_up, down), dot(back_low, hidden, down)]
         ).astype(BF)
         glu_own = lax.psum_scatter(glu_grad, "dp", scatter_dimension=1, tiled=True).astype(F32)
-    middle_own = lax.dynamic_slice_in_dim(middle, place * part, part, 1)
-    layer_out = (middle_own + mp_scatter(partial_out)).astype(BF)
-
-    gain_mid = jnp.sum(grad_normed * unit_mid, axis=0)
-    scaled_mid = grad_normed * gain_full[2]
-    grad_middle = back + inverse_mid * (
-        scaled_mid - unit_mid * jnp.mean(scaled_mid * unit_mid, axis=-1, keepdims=True)
-    )
-    middle_low = grad_middle.astype(BF)
-    state_mean = jnp.mean(middle_low.astype(F32) * branch_mix, axis=-1, keepdims=True)
-    grad_gated = dot(middle_low, mixer_out, across)
+        branch = mp_scatter(dot(hidden, glu[2], across))
+    own_features = lambda v: lax.dynamic_slice_in_dim(v, place * part, part, v.ndim - 1)
+    layer_out = (own_features(middle) + branch).astype(BF)
+
+    if quick:
+        grad_middle_own, middle_low, state_mean, grad_gated, gain_mid = middle_back(
+            sum_own, sum_came, middle, cot_full, token_rows, token_weight, gain_full[2], mixer_out
+        )
+        gain_mid = gain_mid[0]
+    else:
+        inverse_mid = inverse_rms(middle)
+        unit_mid = middle * inverse_mid
+        gain_mid = jnp.sum(grad_normed * unit_mid, axis=0)
+        scaled_mid = grad_normed * gain_full[2]
+        grad_middle = back + inverse_mid * (
+            scaled_mid - unit_mid * jnp.mean(scaled_mid * unit_mid, axis=-1, keepdims=True)
+        )
+        grad_middle_own = own_features(grad_middle)
+        middle_low = grad_middle.astype(BF)
+        state_mean = jnp.mean(middle_low.astype(F32) * branch_mix, axis=-1, keepdims=True)
+        grad_gated = dot(middle_low, mixer_out, across)
     by_batch = lambda v: v.reshape(batches, length, v.shape[-1])
     grad_pre, gated_out, gain_state, pre_dot = scan_backward(
         pre, states, by_batch(grad_gated), by_batch(inverse_state), by_batch(state_mean), bound, state_gain
     )
     grad_pre = grad_pre.reshape(3, rows, channels)
     gated_out = gated_out.reshape(rows, channels)
+    in_mean = mp_sum_wide(pre_dot.reshape(rows, 1)) / full
+    gain_state = jnp.sum(gain_state, axis=0).reshape(groups, 1, own_rows)
+    gain_state = lax.dynamic_update_slice_in_dim(
+        jnp.zeros((groups, narrow, own_rows), F32), gain_state, place, 1
+    )
+    device = lax.axis_index("dp") * narrow + place
     if quick:
-        in_own, out_own = mixer_scatter(normed_in.T, grad_pre, gated_out.T, middle_low, 1)
-        in_own = in_own.astype(BF)
+        gain_parts = jnp.stack(
+            [
+                jnp.zeros((groups, narrow * own_rows), F32),
+                gain_state.reshape(groups, narrow * own_rows),
+                0.5 * gain_mid.reshape(groups, narrow * own_rows),
+            ],
+            axis=1,
+        )
+        gain_parts = jnp.pad(gain_parts, ((0, 0), (0, 5), (0, 0)))
+        in_own, out_own, gain_own, grad_normed_in = mixer_call(
+            normed_in.T, grad_pre, gated_out.T, middle_low, gain_parts, token_rows, inverse_in, mixer_in, 1
+        )
+        gain_own = lax.dynamic_slice_in_dim(gain_own, place * own_rows, own_rows, 1)
+        in_own = in_own.reshape(3, own_rows, narrow, groups, own_rows).transpose(0, 1, 3, 2, 4)
     else:
         grad_mix_out = dot(gated_out, middle_low, down).astype(BF)
         grad_mix_in = jnp.einsum("td,kte->kde", normed_in, grad_pre, preferred_element_type=F32)
         in_own = lax.psum_scatter(grad_mix_in.astype(BF), "dp", scatter_dimension=1, tiled=True)
         out_own = lax.psum_scatter(grad_mix_out, "dp", scatter_dimension=0, tiled=True)
-    in_own = mp_swap(in_own.reshape(3, narrow, own_rows, channels).transpose(1, 0, 2, 3))
-    in_own = in_own.reshape(narrow, 3, own_rows, groups, own_rows).transpose(1, 2, 3, 0, 4)
-    mixer_own = jnp.concatenate(
-        [in_own.reshape(3, own_rows, full).astype(F32), out_own[None].astype(F32)]
-    )
-
-    grad_normed_in = jnp.einsum("kte,kde->td", grad_pre, mixer_in, preferred_element_type=F32)
-    grad_normed_in = mp_scatter(grad_normed_in)
-    in_mean = mp_sum_wide(pre_dot.reshape(rows, 1)) / full
-    own_features = lambda v: lax.dynamic_slice_in_dim(v, place * part, part, v.ndim - 1)
-    unit_in_own = own_features(unit_in)
-    gain_in = jnp.sum(grad_normed_in * unit_in_own, axis=0)
-    grad_seq = own_features(grad_middle) + inverse_in * (
+        in_own = mp_swap(in_own.reshape(3, narrow, own_rows, channels).transpose(1, 0, 2, 3))
+        in_own = in_own.reshape(narrow, 3, own_rows, groups, own_rows).transpose(1, 2, 3, 0, 4)
+        grad_normed_in = jnp.einsum("kte,kde->td", grad_pre, mixer_in, preferred_element_type=F32)
+        gain_in = jnp.sum(grad_normed_in * unit_in, axis=0)
+        grad_normed_in = mp_scatter(grad_normed_in)
+        gain_rows = jnp.stack([gain_in, gain_state.reshape(full), gain_mid / narrow])
+        gain_total = lax.psum(gain_rows, ("dp", "mp"))
+        gain_own = lax.dynamic_slice_in_dim(gain_total, device * own_rows, own_rows, 1)
+    in_own = in_own.reshape(3, own_rows, full).astype(F32)
+    out_own = out_own.astype(F32)
+    unit_in_own = own_features(token_rows).astype(F32) * inverse_in
+    grad_seq = grad_middle_own + inverse_in * (
         grad_normed_in * own_features(gain_full[0]) - unit_in_own * in_mean
     )
     grad_tokens = grad_seq.astype(BF)
 
-    zeros = jnp.zeros((full,), F32)
-    gain_rows = jnp.stack(
-        [
-            lax.dynamic_update_slice_in_dim(zeros, gain_in, place * part, 0),
-            lax.dynamic_update_slice_in_dim(
-                zeros.reshape(groups, narrow, own_rows),
-                jnp.sum(gain_state, axis=0).reshape(groups, 1, own_rows),
-                place,
-                1,
-            ).reshape(full),
-            lax.dynamic_update_slice_in_dim(zeros, own_features(gain_mid), place * part, 0),
-        ]
-    )
-    gain_total = lax.psum(gain_rows, ("dp", "mp"))
-    device = lax.axis_index("dp") * narrow + place
-    gain_own = lax.dynamic_slice_in_dim(gain_total, device * own_rows, own_rows, 1)
-
     scale = 1.0 / (batches * groups * tokens.shape[1])
-    count = STEP_NUMBER
-    update = functools.partial(adamw_update, count=count)
+    update = functools.partial(adamw_update, count=STEP_NUMBER)
+    mixer_own = jnp.concatenate([in_own, out_own[None]])
     mixer_new = update(
         mixer_master, mixer_first, mixer_second, mixer_own * scale, rate=MATRIX_RATE, decay=DECAY_RATE
     )
     gain_new = update(
         gain_master, gain_first, gain_second, gain_own * scale, rate=GAIN_RATE, decay=0.0
     )
-    glu_in_new = update(
-        glu_in_master, glu_in_first, glu_in_second, glu_own[:2] * scale, rate=MATRIX_RATE, decay=DECAY_RATE
-    )
-    glu_out_new = update(
-        glu_out_master, glu_out_first, glu_out_second, glu_own[2].T * scale, rate=MATRIX_RATE, decay=DECAY_RATE
-    )
+    glu_ins = (glu_in_master, glu_in_first, glu_in_second)
+    glu_downs = (glu_out_master, glu_out_first, glu_out_second)
+    if quick:
+        glu_in_new, glu_out_new = glu_update(glu_sums, glu_ins, glu_downs, scale)
+    else:
+        glu_in_new = update(*glu_ins, glu_own[:2] * scale, rate=MATRIX_RATE, decay=DECAY_RATE)
+        glu_out_new = update(*glu_downs, glu_own[2].T * scale, rate=MATRIX_RATE, decay=DECAY_RATE)
     return (
         layer_out.reshape(batches, 1, length, part),
         grad_tokens.reshape(batches, 1, length, part),

time: 957 us -> 792 us (0.83)
  matrix products: 154 us -> 25.9 us
  Pallas kernels: 443 us -> 539 us
  local copies, waits for them, and re-layouts: 106 us -> 62.2 us
  blocking collectives: 39.2 us -> 0 us
  other arithmetic: 85.7 us -> 50.2 us
  waiting for transfers between devices: 101 us -> 86.3 us
    dot_general x8 -> x0, matrix products: 133 us -> none  [the longest x1 24.9 us: shards(): pre_act = jnp.dot(normed_mid, glu[0], preferred_element_type=F32)]
    pallas_call x2 -> x4, Pallas kernels: 313 us -> 397 us  [the longest x1 234 us: glu_call(): pl.pallas_call(functools.partial(glu_kernel, hidden_blocks, full_blocks),...]
    psum x1 -> x0, blocking collectives: 39.2 us -> none  [shards(): gain_total = lax.psum(gain_rows, ('dp', 'mp'))]
    unnamed x108 -> x57, local copies, waits for them, and re-layouts: 33.3 us -> 5.62 us
    ppermute x8 -> x4, waiting for transfers between devices: 101 us -> 75.1 us  [partner_swap(): return lax.ppermute(value, 'mp', [(0, 1), (1, 0)])]
    reduce_sum x4 -> x1, other arithmetic: 20.1 us -> 0.71 us  [shards(): gain_state = jnp.sum(gain_state, axis=0).reshape(groups, 1, own_rows)]
    convert_element_type x6 -> x0, local copies, waits for them, and re-layouts: 17.6 us -> none  [the longest x2 9.26 us: shards(): in_own.reshape(3, own_rows, full).astype(F32)]
    sub x4 -> x2, other arithmetic: 18.5 us -> 4.53 us  [adamw_update(): master - rate * (first_hat / (jnp.sqrt(second_hat) + ADAM_EPSILON) + deca...]
  transfers between devices with their start and end apart: 9 -> 5, of which waited for: 1 -> 2; matrix products, arithmetic and copies ran while one was open for 19% -> 13% of each run, Pallas kernels for 34% -> 18%
where the time goes in v3:
time: 792 us; the launch traced here: 786 us
  Pallas kernels  539 us (68%)
  waiting for transfers between devices  86.3 us (11%)
  local copies, waits for them, and re-layouts  62.2 us (8%)
  other arithmetic  50.2 us (6%)
  matrix products  25.9 us (3%)
  between operations  14.8 us (2%)
    pallas_call x1, Pallas kernels, glu_call(): pl.pallas_call(functools.partial(glu_kernel, hidden_blocks, full_blocks),...  234 us
    pallas_call x1, Pallas kernels, mixer_call(): pl.pallas_call(functools.partial(mixer_kernel, full_blocks), grid=(chunks...  125 us
    pallas_call x1, Pallas kernels, gather_call(): pl.pallas_call(gather_kernel, in_specs=[any_space] * 3, out_specs=[any_sp...  113 us
    ppermute x4, waiting for transfers between devices, partner_swap(): return lax.ppermute(value, 'mp', [(0, 1), (1, 0)])  75.1 us
    pallas_call x1, Pallas kernels, middle_back(): pl.pallas_call(middle_back_kernel, grid=(rows // step,), in_specs=[line(f...  20.9 us
    dot_general x1, matrix products, shards(): jnp.einsum('td,kde->kte', normed_in, mixer_in, preferred_element_type=F32)  18.8 us
    pallas_call x1, Pallas kernels, scan_backward(): pl.pallas_call(scan_backward_kernel, grid=(batches, width // block), in_s...  17.5 us
    pallas_call x1, Pallas kernels, glu_update(): pl.pallas_call(functools.partial(glu_update_kernel, scale), grid=(blocks,...  16.8 us
  transfers between devices with their start and end apart: 5, of which 2 were waited for; matrix products, arithmetic and copies ran while one was open for 13% of the time, Pallas kernels for 18%

profile of v3, /device:TPU:0, one launch (start us, length us, event | category | flops | bytes accessed | tf_op | source)
XLA Modules:
  0.0 785.9 jit_solution(11343822946026114590)
XLA Ops:
  7.2 3.0 collective-permute-start
  13.0 2.5 reshape.427
  15.6 2.9 copy.74
  18.5 3.5 reshape.428.in_ref
  26.9 113.5 %shard_map.272 = (bf16[3,4,2,2,2,64,1024]{6,5,4,3,2,1,0:T(8,128)(2,1)}, bf16[4,2,2,64,2048]{4,3,2,1,0:T(8,128)(2,1)}, f32[4,2,2,2,8,128]{5,4,3,2,1,0:T(8,128)}) custom-call(bf16[2,3,64,1024]{3,2,1,0:T(8,128)(2,1)} %reshape.428.in_ref, bf16[64,2048]{1,0:T(8,128)(2,1)} %slice_bitcast_fusion.out_ref, f32[8,128]{1,0:T(8,128)} %copy-done.18), custom_call_target="tpu_custom_call" | custom-call | bytes 300000000 | tf_op jit(solution)/shard_map/pallas_call | solution.py:1031
  142.0 2.3 broadcast_select_fusion.1
  144.3 2.1 pad_maximum_fusion.1.cot_ref
  146.6 2.8 multiply_reduce_fusion.1
  151.0 18.8 %fusion.2 = f32[3,1024,896]{1,2,0:T(8,128)} fusion(bf16[3,2048,1024]{2,1,0:T(8,128)(2,1)} %bitcast.86, bf16[896,2048]{1,0:T(8,128)(2,1)} %bitcast.77, f32[2048]{0:T(1024)S(1)} %mul.239, f32[896]{0:T(1024)S(1)} %rsqrt.19), kind=kOutput, calls=%fused_computation.10 | convolution fusion | flops 11281629184 | bytes 27274752 | tf_op jit(solution)/shard_map/td,kde->kte/dot_general | solution.py:1123
  169.9 10.9 %shard_map.273 = (f32[2,448,1024]{2,1,0:T(8,128)}, bf16[2,448,1024]{2,1,0:T(8,128)(2,1)}, f32[2,448,1]{2,1,0:T(8,128)}) custom-call(f32[3,2,448,1024]{3,2,1,0:T(8,128)} %bitcast.75, f32[1,1024]{1,0:T(1,128)} %broadcast_in_dim_reshape.11.bound_ref, f32[1,1024]{1,0:T(1,128)} %broadcast_in_dim_reshape.12.gain_ref), custom_call_target="tpu_custom_call" | custom-call | flops 36700160 | bytes 16515072 | tf_op jit(solution)/shard_map/pallas_call | solution.py:151
  180.8 7.0 convolution_convert_fusion
  194.7 75.1 %collective-permute-done.1 = f32[896,1]{0,1:T(1,128)S(1)} collective-permute-done((f32[896,1]{0,1:T(1,128)S(1)}, f32[896,1]{0,1:T(1,128)S(1)}, u32[]{:S(2)}, u32[]{:S(2)}) %collective-permute-start.1) | collective-permute-done | bytes 3616 | tf_op jit(solution)/shard_map/ppermute | solution.py:47
  270.9 7.4 multiply_reduce_fusion
  278.3 3.9 multiply_convert_fusion
  283.5 6.2 copy.89
  289.7 6.1 copy.90
  295.8 6.1 copy.91
  301.9 6.9 pad_maximum_fusion.left_ref
  308.8 11.2 %all-gather.2.cloned.1.call-done.glu_ref = bf16[3,2048,2816]{2,1,0:T(8,128)(2,1)} async-done(((bf16[3,128,2816]{2,1,0:T(8,128)(2,1)}), bf16[3,2048,2816]{2,1,0:T(8,128)(2,1)}) %all-gather.2.cloned.1.call-update) | async-done | bytes 34603024 | tf_op jit(solution)/shard_map/all_gather | solution.py:1105
  320.0 234.2 %shard_map.274 = (f32[33,128,256]{2,1,0:T(8,128)}, bf16[896,2048]{1,0:T(8,128)(2,1)}, bf16[896,2048]{1,0:T(8,128)(2,1)}, bf16[896,1024]{1,0:T(8,128)(2,1)}, bf16...) custom-call(bf16[896,2048]{1,0:T(8,128)(2,1)} %get-tuple-element.179.normed_ref, ...), custom_call_target="tpu_custom_call" | custom-call | flops 93012885504 | bytes 69206016 | tf_op jit(solution)/shard_map/pallas_call | solution.py:565
  554.2 20.9 %shard_map.275 = (f32[896,1024]{1,0:T(8,128)}, bf16[896,2048]{1,0:T(8,128)(2,1)}, f32[896,1]{1,0:T(8,128)}, f32[896,1024]{1,0:T(8,128)}, f32[1,2048]{1,0:T(1,128)}) custom-call(bf16[896,2048]{1,0:T(8,128)(2,1)} %get-tuple-element.81.sum_own_ref, bf16[896,2048]{1,0:T(8,128)(2,1)} %get-tuple-element.82.sum_came_ref, f32[896,2048]{1,0:T(8,128)} %copy-done, ...), custom_call_target="tpu_custom_call" | custom-call | flops 3758096384 | bytes 36700160 | tf_op jit(solution)/shard_map/pallas_call | solution.py:824
  575.1 17.5 %shard_map.276 = (bf16[3,2,448,1024]{3,2,1,0:T(8,128)(2,1)}, bf16[2,448,1024]{2,1,0:T(8,128)(2,1)}, f32[2,1,1024]{2,1,0:T(1,128)}, f32[2,448,1]{2,1,0:T(8,128)}) custom-call(f32[3,2,448,1024]{3,2,1,0:T(8,128)} %bitcast.76, f32[2,448,1024]{2,1,0:T(8,128)} %get-tuple-element.84.states_ref, f32[2,448,1024]{2,1,0:T(8,128)} %bitcast.92, ...), custom_call_target="tpu_custom_call" | custom-call | flops 73400320 | bytes 25690112 | tf_op jit(solution)/shard_map/pallas_call | solution.py:257
  594.3 4.0 copy.80
  598.3 125.2 %shard_map.277 = (f32[17,128,256]{2,1,0:T(8,128)}, bf16[896,1024]{1,0:T(8,128)(2,1)}, bf16[896,1024]{1,0:T(8,128)(2,1)}, bf16[896,1024]{1,0:T(8,128)(2,1)}, bf16[13,64,256]{2,1,0:T(8,128)(2,1)}) custom-call(bf16[4,2,2,128,896]{4,3,2,1,0:T(8,128)(2,1)} %bitcast.91, bf16[3,896,1024]{2,1,0:T(8,128)(2,1)} %bitcast.108, bf16[4,2,2,64,896]{4,3,2,1,0:T(8,128)(2,1)} %bitcast.99, ...), custom_call_target="tpu_custom_call" | custom-call | flops 26306674688 | bytes 33554432 | tf_op jit(solution)/shard_map/pallas_call | solution.py:747
  730.5 2.6 reshape_reshape.3
  733.1 3.3 copy.85
  736.4 5.3 reshape.449
  745.4 2.4 collective-permute-start.3
  747.9 5.5 add_convert_fusion.1
  753.5 3.9 multiply_subtract_fusion
  758.1 16.8 %shard_map.278 = (f32[2,128,2816]{2,1,0:T(8,128)}, f32[2,128,2816]{2,1,0:T(8,128)}, f32[2,128,2816]{2,1,0:T(8,128)}, f32[2816,128]{1,0:T(8,128)}, f32[2816,128]{1,0:T(8,128)}, /*index=5*/f32[2816,128]{1,0:T(8,128)}) custom-call(f32[33,128,256]{2,1,0:T(8,128)} %get-tuple-element.97.act_ref.up_ref.out_ref, ...), custom_call_target="tpu_custom_call" | custom-call | flops 21626880 | bytes 30277632 | tf_op jit(solution)/shard_map/pallas_call | solution.py:862
  774.9 3.8 add_convert_fusion
  (123 shorter events, 33.2 us)
Async XLA Ops:
  7.2 312.8 %all-gather.2.cloned.1.call-start = ((), (), s32[]{:S(2)}) async-start(), calls=%async_computation | async-start | bytes 36765696 | tf_op jit(solution)/shard_map/all_gather | solution.py:1105
  7.2 134.7 %collective-permute-start = (bf16[896,1024]{1,0:T(8,128)(2,1)}, bf16[896,1024]{1,0:T(8,128)(2,1)}, u32[]{:S(2)}, u32[]{:S(2)}) collective-permute-start(bf16[896,1024]{1,0:T(8,128)(2,1)} %bitcast.100), channel_id=1, source_target_pairs={{0,1},{1,0},{2,3},{3,2},{4,5},{5,4},{6,7},{7,6},{8,9},{9,8},{10,11... | collective-permute-start | bytes 5505032 | tf_op jit(solution)/shard_map/ppermute | solution.py:47
  15.6 6.4 copy-start.21
  15.6 6.4 copy-start.3
  21.9 3.0 copy-start.25
  21.9 3.0 copy-start.26
  23.2 117.2 %copy-start.5 = (bf16[2,128,2816]{2,1,0:T(8,128)(2,1)S(1)}, bf16[2,128,2816]{2,1,0:T(8,128)(2,1)}, u32[]{:S(2)}) copy-start(bf16[2,128,2816]{2,1,0:T(8,128)(2,1)} %convert_element_type.77) | copy-start | bytes 4325380
  25.2 1.7 copy-start.18
  144.3 2.2 copy-start.17
  146.4 3.8 copy-start.19
  146.6 124.2 %copy-start.12 = (f32[2048]{0:T(1024)}, f32[2048]{0:T(1024)S(1)}, u32[]{:S(2)}) copy-start(f32[2048]{0:T(1024)S(1)} %mul.239) | copy-start | bytes 24580
  149.5 121.3 %copy-start.13 = (f32[896]{0:T(1024)}, f32[896]{0:T(1024)S(1)}, u32[]{:S(2)}) copy-start(f32[896]{0:T(1024)S(1)} %rsqrt.19) | copy-start | bytes 10756
  169.9 10.9 %copy-start.7 = (bf16[4,2,2,64,2048]{4,3,2,1,0:T(8,128)(2,1)S(1)}, bf16[4,2,2,64,2048]{4,3,2,1,0:T(8,128)(2,1)}, u32[]{:S(2)}) copy-start(bf16[4,2,2,64,2048]{4,3,2,1,0:T(8,128)(2,1)} %get-tuple-element.76) | copy-start | bytes 12582916
  180.8 9.7 %copy-start.15 = (f32[2,448,1]{2,1,0:T(8,128)S(1)}, f32[2,448,1]{2,1,0:T(8,128)}, u32[]{:S(2)}) copy-start(f32[2,448,1]{2,1,0:T(8,128)} %get-tuple-element.74) | copy-start | bytes 10756
  187.8 83.1 %collective-permute-start.2 = (bf16[896,2048]{1,0:T(8,128)(2,1)}, bf16[896,2048]{1,0:T(8,128)(2,1)}, u32[]{:S(2)}, u32[]{:S(2)}) collective-permute-start(bf16[896,2048]{1,0:T(8,128)(2,1)} %convolution_convert_fusion), channel_id=1, source_target_pairs={{0,1},{1,0},{2,3},{3,2},{4,5},{5,4},{6,7},{7,6},{8,9},{9,8},{10,11... | collective-permute-start | bytes 11010056 | tf_op jit(solution)/shard_map/ppermute | solution.py:47
  190.8 79.0 %collective-permute-start.1 = (f32[896,1]{0,1:T(1,128)S(1)}, f32[896,1]{0,1:T(1,128)S(1)}, u32[]{:S(2)}, u32[]{:S(2)}) collective-permute-start(f32[896,1]{0,1:T(1,128)S(1)} %reshape.435), channel_id=1, source_target_pairs={{0,1},{1,0},{2,3},{3,2},{4,5},{5,4},{6,7},{7,6},{8,9},{9,8},{10,11... | collective-permute-start | bytes 10760 | tf_op jit(solution)/shard_map/ppermute | solution.py:47
  270.8 7.4 copy-start.2
  278.3 5.2 copy-start
  575.1 18.5 %copy-start.20 = (f32[1,2048]{1,0:T(1,128)S(1)}, f32[1,2048]{1,0:T(1,128)}, u32[]{:S(2)}) copy-start(f32[1,2048]{1,0:T(1,128)} %get-tuple-element.91) | copy-start | bytes 24580
  723.6 3.5 copy-start.16
  736.4 6.8 copy-start.11
  745.4 29.4 %collective-permute-start.3 = (f32[896,1]{0,1:T(1,128)S(1)}, f32[896,1]{0,1:T(1,128)S(1)}, u32[]{:S(2)}, u32[]{:S(2)}) collective-permute-start(f32[896,1]{0,1:T(1,128)S(1)} %reshape.447), channel_id=1, source_target_pairs={{0,1},{1,0},{2,3},{3,2},{4,5},{5,4},{6,7},{7,6},{8,9},{9,8},{10,11... | collective-permute-start | bytes 10760 | tf_op jit(solution)/shard_map/ppermute | solution.py:47
  747.9 5.6 copy-start.4
  747.9 5.6 copy-start.9
  747.9 5.6 copy-start.10
  753.5 3.9 copy-start.22
  753.5 3.9 copy-start.23
  753.5 3.9 copy-start.24
  758.1 16.8 %copy-start.1 = (bf16[2,1,448,2048]{3,2,1,0:T(8,128)(2,1)S(1)}, bf16[2,1,448,2048]{3,2,1,0:T(8,128)(2,1)}, u32[]{:S(2)}) copy-start(bf16[2,1,448,2048]{3,2,1,0:T(8,128)(2,1)} %param.21) | copy-start | bytes 11010052
  758.1 16.8 %copy-start.8 = (f32[896,1024]{1,0:T(8,128)S(1)}, f32[896,1024]{1,0:T(8,128)}, u32[]{:S(2)}) copy-start(f32[896,1024]{1,0:T(8,128)} %get-tuple-element.83) | copy-start | bytes 11010052
  758.1 16.8 %dynamic-slice-start = ((f32[2048]{0:T(1024)}, s32[]{:T(128)}), f32[1024]{0:T(1024)S(1)}, s32[]{:S(2)}) async-start(f32[2048]{0:T(1024)} %copy-done.12, s32[]{:T(128)} %select_n.61), calls=%async_computation.1 | async-start | bytes 8704 | tf_op jit(solution)/shard_map/dynamic_slice | solution.py:1157
  758.1 16.8 %copy-start.14 = (f32[896]{0:T(1024)S(1)}, f32[896]{0:T(1024)}, u32[]{:S(2)}) copy-start(f32[896]{0:T(1024)} %copy-done.13) | copy-start | bytes 10756
  (1 other events, 1.0 us)
Sparse Core Ops, SparseCore 0:
  146.6 173.3 all-gather.1

commit v4 on v3

--- a/solution.py
+++ b/solution.py
@@ -282,7 +282,9 @@
 MESH_ID = pl.DeviceIdType.MESH
 DEPTH = 4
 LANES = 256
-Z_LAG = 4
+X_LAG = 4
+Z_LAG = X_LAG + 2
+SWAP_LAG = 2
 
 
 def device_place():
@@ -305,7 +307,7 @@
     pl.semaphore_wait(barrier, len(targets))
 
 
-def scatter_step(step, chunks, compute, out_ref, scratch):
+def scatter_step(step, chunks, compute, finish, scratch):
     (own, core_out, core_in, keep, x_out, x_in, sums, mine, z_out, z_in,
      core_send, core_recv, x_send, x_recv, z_send, z_recv) = scratch
     z, x, core = device_place()
@@ -318,8 +320,8 @@
 
     def x_copy(p):
         return pltpu.make_async_remote_copy(
-            x_out.at[lax.rem(p, 2)], x_in.at[lax.rem(p, 4)],
-            x_send.at[lax.rem(p, 2)], x_recv.at[lax.rem(p, 4)],
+            x_out.at[lax.rem(p, X_LAG)], x_in.at[lax.rem(p, 2 * X_LAG)],
+            x_send.at[lax.rem(p, X_LAG)], x_recv.at[lax.rem(p, 2 * X_LAG)],
             device_id=device_at(z, 1 - x, core), device_id_type=MESH_ID)
 
     def z_copy(p, hop):
@@ -334,30 +336,36 @@
         def _():
             core_copy(step - 2).wait_send()
 
-        core_out[lax.rem(step, 2)] = compute(step, 1 - core).astype(BF)
+        def to_partner(value):
+            core_out[lax.rem(step, 2)] = value.astype(BF)
+
+        def to_own(value):
+            own[lax.rem(step, 2)] = value
+
+        compute(step, 1 - core, to_partner)
         core_copy(step).start()
-        own[lax.rem(step, 2)] = compute(step, core)
+        compute(step, core, to_own)
 
     @pl.when((step >= 1) & (step < chunks + 1))
     def _():
         p = step - 1
         core_copy(p).wait_recv()
 
-        @pl.when(p >= 2)
-        def _():
-            x_copy(p - 2).wait_send()
-
-        two, four = lax.rem(p, 2), lax.rem(p, 4)
-        x_out[two] = (own[two, :, 1 - x] + core_in[four, :, 1 - x].astype(F32)).astype(BF)
+        @pl.when(p >= X_LAG)
+        def _():
+            x_copy(p - X_LAG).wait_send()
+
+        two, four, slot = lax.rem(p, 2), lax.rem(p, 4), lax.rem(p, X_LAG)
+        x_out[slot] = (own[two, :, 1 - x] + core_in[four, :, 1 - x].astype(F32)).astype(BF)
         x_copy(p).start()
-        keep[two] = own[two, :, x] + core_in[four, :, x].astype(F32)
-
-    @pl.when((step >= 2) & (step < chunks + 2))
-    def _():
-        p = step - 2
+        keep[slot] = own[two, :, x] + core_in[four, :, x].astype(F32)
+
+    @pl.when((step >= X_LAG) & (step < chunks + X_LAG))
+    def _():
+        p = step - X_LAG
         x_copy(p).wait_recv()
-        two, four = lax.rem(p, 2), lax.rem(p, 4)
-        sums[...] = keep[two] + x_in[four].astype(F32)
+        four = lax.rem(p, 4)
+        sums[...] = keep[lax.rem(p, X_LAG)] + x_in[lax.rem(p, 2 * X_LAG)].astype(F32)
         for hop in range(1, DEPTH):
             @pl.when(p >= 4)
             def _():
@@ -367,21 +375,21 @@
             z_copy(p, hop).start()
         mine[four] = sums[z]
 
-    @pl.when(step >= Z_LAG)
+    @pl.when((step >= Z_LAG) & (step < chunks + Z_LAG))
     def _():
         p = step - Z_LAG
         for hop in range(1, DEPTH):
             z_copy(p, hop).wait_recv()
         got = z_in.at[lax.rem(p, 8)]
-        total = mine[lax.rem(p, 4)] + got[0].astype(F32) + got[1].astype(F32) + got[2].astype(F32)
-        out_ref[0] = total
+        finish(p, mine[lax.rem(p, 4)] + got[0].astype(F32) + got[1].astype(F32) + got[2].astype(F32))
 
     @pl.when(step == chunks + Z_LAG - 1)
     def _():
-        for p in range(max(chunks - 2, 0), chunks):
+        for p in range(chunks - 2, chunks):
             core_copy(p).wait_send()
+        for p in range(chunks - X_LAG, chunks):
             x_copy(p).wait_send()
-        for p in range(max(chunks - 4, 0), chunks):
+        for p in range(chunks - 4, chunks):
             for hop in range(1, DEPTH):
                 z_copy(p, hop).wait_send()
 
@@ -394,14 +402,14 @@
         pltpu.VMEM((2, *quad), F32),
         pltpu.VMEM((2, *quad), BF),
         pltpu.VMEM((4, *quad), BF),
-        pltpu.VMEM((2, *line), F32),
-        pltpu.VMEM((2, *line), BF),
-        pltpu.VMEM((4, *line), BF),
+        pltpu.VMEM((X_LAG, *line), F32),
+        pltpu.VMEM((X_LAG, *line), BF),
+        pltpu.VMEM((2 * X_LAG, *line), BF),
         pltpu.VMEM(line, F32),
         pltpu.VMEM((4, rows, lanes), F32),
         pltpu.VMEM((4, DEPTH - 1, rows, lanes), BF),
         pltpu.VMEM((8, DEPTH - 1, rows, lanes), BF),
-        dma((2,)), dma((4,)), dma((2,)), dma((4,)), dma((4, DEPTH - 1)), dma((8, DEPTH - 1)),
+        dma((2,)), dma((4,)), dma((X_LAG,)), dma((2 * X_LAG,)), dma((4, DEPTH - 1)), dma((8, DEPTH - 1)),
     ]
 
 
@@ -415,7 +423,7 @@
 
 
 def glu_kernel(
-    hidden_blocks, full_blocks, normed_ref, back_ref, left_ref, glu_ref,
+    hidden_blocks, full_blocks, normed_ref, back_ref, left_ref, left_back_ref, glu_ref,
     out_ref, sum_own, sum_came, half_own, half_send, half_came,
     acts, weights_in, weights_back, sum_stage, half_stage,
     in_sem, back_sem, stage_sem, sum_send, sum_recv, half_send_sem, half_recv, *scratch,
@@ -428,6 +436,14 @@
     row_block = rows // 2
     half_blocks = full_blocks // 2
     across = (((1,), (1,)), ((), ()))
+    spread = min(hidden_blocks + hidden_blocks // 2, 16)
+    second = step - spread
+
+    def first_tasks(at):
+        return at * hidden_blocks // spread
+
+    unit_block = first_tasks(step)
+    in_second = (second >= 0) & (second < 2 * full_blocks)
 
     def lane_block(index):
         return pl.ds(pl.multiple_of(index * LANES, LANES), LANES)
@@ -461,10 +477,10 @@
         load_back(0).start()
         scatter_barrier(z, x, core, with_mp=True)
 
-    @pl.when(step < hidden_blocks)
-    def _():
-        load_in(step).wait()
-        lanes = lane_block(step)
+    @pl.when((step < spread) & ((step == 0) | (unit_block > first_tasks(step - 1))))
+    def _():
+        load_in(unit_block).wait()
+        lanes = lane_block(unit_block)
 
         def part(index, _):
             part_rows = pl.ds(pl.multiple_of(index * row_block, row_block), row_block)
@@ -482,13 +498,13 @@
 
         lax.fori_loop(0, rows // row_block, part, 0)
 
-        @pl.when(step + 1 < hidden_blocks)
-        def _():
-            load_in(step + 1).start()
-
-    @pl.when((step > hidden_blocks) & (step <= hidden_blocks + full_blocks))
-    def _():
-        index = step - hidden_blocks - 1
+        @pl.when(unit_block + 1 < hidden_blocks)
+        def _():
+            load_in(unit_block + 1).start()
+
+    @pl.when(in_second & (lax.rem(second, 2) == 1))
+    def _():
+        index = second // 2
         stage(index, 0, sum_own.at[:, lane_block(index)]).wait()
         sum_copy(index).start()
         spot = half_spot(index)
@@ -498,9 +514,9 @@
         def _():
             half_copy(spot).start()
 
-    @pl.when((step >= hidden_blocks) & (step < hidden_blocks + full_blocks))
-    def _():
-        index = step - hidden_blocks
+    @pl.when(in_second & (lax.rem(second, 2) == 0))
+    def _():
+        index = second // 2
         load_back(index).wait()
         slot = lax.rem(index, 2)
 
@@ -531,16 +547,23 @@
         def _():
             stage(index, 1, half_send.at[:, lane_block(spot)]).start()
 
-    def compute(q, core_side):
+    def compute(q, core_side, store):
         kind = lax.rem(q, 3)
-        side = left_ref[kind // 2, :, :, core_side]
-        side_rows = side.shape[2]
-        product = jnp.dot(
-            side.reshape(DEPTH * 2 * side_rows, rows), acts[kind, :, lane_block(q // 3)],
-            preferred_element_type=F32)
-        return product.reshape(DEPTH, 2, side_rows, LANES)
-
-    scatter_step(step, chunks, compute, out_ref, scratch)
+        side_rows = left_ref.shape[3]
+
+        def product(side_ref):
+            side = side_ref[:, :, core_side].reshape(DEPTH * 2 * side_rows, rows)
+            right = acts[kind, :, lane_block(q // 3)]
+            store(jnp.dot(side, right, preferred_element_type=F32).reshape(
+                DEPTH, 2, side_rows, LANES))
+
+        pl.when(kind < 2)(lambda: product(left_ref))
+        pl.when(kind == 2)(lambda: product(left_back_ref))
+
+    def finish(p, value):
+        out_ref[0] = value
+
+    scatter_step(step, chunks, compute, finish, scratch)
 
     @pl.when(step == chunks + Z_LAG - 1)
     def _():
@@ -550,13 +573,13 @@
             half_copy(spot).wait()
 
 
-def glu_call(normed, back_low, glu, collective):
+def glu_call(normed, back_low, left_back, glu, collective):
     rows, full = normed.shape
     hidden = glu.shape[2]
     hidden_blocks, full_blocks = hidden // LANES, full // LANES
     block = full // 16
     chunks = 3 * hidden_blocks
-    left = jnp.stack([normed.T, back_low.T]).reshape(2, DEPTH, 2, 2, block, rows)
+    left_shape = (DEPTH, 2, 2, block, rows)
     any_space = pl.BlockSpec(memory_space=pl.ANY)
     out_spec, out_shape = scatter_out(chunks, block, LANES)
     dma = pltpu.SemaphoreType.DMA
@@ -565,7 +588,7 @@
     out, sum_own, sum_came, half_own, _, half_came = pl.pallas_call(
         functools.partial(glu_kernel, hidden_blocks, full_blocks),
         grid=(chunks + Z_LAG,),
-        in_specs=[fixed(normed.shape), fixed(back_low.shape), fixed(left.shape), any_space],
+        in_specs=[fixed(normed.shape), fixed(back_low.shape), fixed(left_shape), fixed(left_shape), any_space],
         out_specs=[out_spec] + [any_space] * 5,
         out_shape=[out_shape, wide, wide, half, half, half],
         scratch_shapes=[
@@ -583,15 +606,15 @@
         cost_estimate=pl.CostEstimate(
             flops=18 * rows * full * hidden, bytes_accessed=6 * full * hidden * 2,
             transcendentals=rows * hidden),
-    )(normed, back_low, left, glu)
+    )(normed, back_low, normed.T.reshape(left_shape), left_back.reshape(left_shape), glu)
     return out, sum_own, sum_came, half_own, half_came
 
 
 def mixer_kernel(
     full_blocks, left_ref, grad_ref, left_out_ref, right_out_ref, gain_ref, tokens_ref, inverse_ref,
-    weights_ref, out_ref, half_own, half_send, half_came, swap_came,
-    weights, token_block, gain_sum, gain_chunk, total, swap_out, half_stage,
-    load_sem, stage_sem, half_send_sem, half_recv, swap_send, swap_recv, *scratch,
+    weights_ref, dot_ref, out_ref, gain_out, half_own, half_send, half_came, dot_came,
+    weights, token_block, gain_sum, gain_chunk, total, swap_out, swap_in, half_stage,
+    load_sem, stage_sem, half_send_sem, half_recv, swap_send, swap_recv, dot_sem, *scratch,
 ):
     z, x, core = device_place()
     dp, mp = lax.axis_index("dp"), lax.axis_index("mp")
@@ -626,9 +649,12 @@
 
     def swap_copy(index):
         return pltpu.make_async_remote_copy(
-            swap_out.at[lax.rem(index, 2)], swap_came.at[index],
-            swap_send.at[lax.rem(index, 2)], swap_recv.at[index],
+            swap_out.at[lax.rem(index, 2)], swap_in.at[lax.rem(index, 8)],
+            swap_send.at[lax.rem(index, 2)], swap_recv.at[lax.rem(index, 8)],
             device_id=partner, device_id_type=MESH_ID)
+
+    dot_copy = pltpu.make_async_remote_copy(
+        dot_ref, dot_came, dot_sem.at[0], dot_sem.at[1], device_id=partner, device_id_type=MESH_ID)
 
     @pl.when(step == 0)
     def _():
@@ -637,6 +663,7 @@
         gain_chunk[...] = jnp.zeros_like(gain_chunk)
         gain_sum[...] = jnp.zeros_like(gain_sum)
         scatter_barrier(z, x, core, with_mp=True)
+        dot_copy.start()
 
     @pl.when((step > 0) & (step <= full_blocks))
     def _():
@@ -683,57 +710,91 @@
         def _():
             stage(step, half_send.at[:, lane_block(spot)]).start()
 
-    def compute(q, core_side):
-        def outer_chunk():
+    def compute(q, core_side, store):
+        @pl.when(q < outer)
+        def _():
             side = left_out_ref[:, :, core_side].reshape(channels // 2, tokens)
             parts = [
                 jnp.dot(side, right_out_ref[:, lane_block(2 * q + at)], preferred_element_type=F32)
                 for at in (0, 1)
             ]
             parts = [part.reshape(DEPTH, 2, half, LANES) for part in parts]
-            return jnp.concatenate(parts, axis=2)
-
-        def inner_chunk():
+            store(jnp.concatenate(parts, axis=2))
+
+        @pl.when((q >= outer) & (q < gains))
+        def _():
             at = q - outer
             side = left_ref[:, :, core_side].reshape(DEPTH * 2 * block, tokens)
             right = grad_ref[at // across, :, lane_block(lax.rem(at, across))]
-            return jnp.dot(side, right, preferred_element_type=F32).reshape(DEPTH, 2, block, LANES)
-
-        def gain_block():
+            store(jnp.dot(side, right, preferred_element_type=F32).reshape(DEPTH, 2, block, LANES))
+
+        @pl.when(q == gains)
+        def _():
             for owner in range(2 * DEPTH):
                 line = 2 * owner + core_side
                 gain_chunk[owner // 2, owner % 2, 0:8, 0:128] = gain_ref[line] + gain_sum[line]
-            return gain_chunk[...]
-
-        return lax.cond(
-            q < outer, outer_chunk, lambda: lax.cond(q < gains, inner_chunk, gain_block))
-
-    scatter_step(step, chunks, compute, out_ref, scratch)
-
-    @pl.when(step >= Z_LAG + outer)
-    def _():
-        index = step - Z_LAG - outer
-
-        @pl.when(index >= 2)
-        def _():
-            swap_copy(index - 2).wait_send()
-
-        total[...] = out_ref[0]
-        first = jnp.where(index == gains - outer, 0, 1 - mp) * half
-        swap_out[lax.rem(index, 2)] = total[pl.ds(pl.multiple_of(first, half), half), :].astype(BF)
-        swap_copy(index).start()
-
-    @pl.when(step == chunks + Z_LAG - 1)
+            store(gain_chunk[...])
+
+    def finish(p, value):
+        total[lax.rem(p, 4)] = value
+
+        @pl.when(p >= outer)
+        def _():
+            index = p - outer
+
+            @pl.when(index >= 2)
+            def _():
+                swap_copy(index - 2).wait_send()
+
+            first = jnp.where(p == gains, 0, 1 - mp) * half
+            rows = pl.ds(pl.multiple_of(first, half), half)
+            swap_out[lax.rem(index, 2)] = total[lax.rem(p, 4), rows, :].astype(BF)
+            swap_copy(index).start()
+
+    scatter_step(step, chunks, compute, finish, scratch)
+
+    @pl.when((step >= Z_LAG + SWAP_LAG) & (step < chunks + Z_LAG + SWAP_LAG))
+    def _():
+        p = step - Z_LAG - SWAP_LAG
+        slot = lax.rem(p, 4)
+
+        @pl.when(p < outer)
+        def _():
+            out_ref[0, :, :LANES] = total[slot, :half, :]
+            out_ref[0, :, LANES:] = total[slot, half:, :]
+
+        @pl.when(p >= outer)
+        def _():
+            swap_copy(p - outer).wait_recv()
+            came = swap_in[lax.rem(p - outer, 8)].astype(F32)
+
+            @pl.when(p < gains)
+            def _():
+                own = total[slot, pl.ds(pl.multiple_of(mp * half, half), half), :]
+                first = jnp.where(mp == 0, own, came)
+                second = jnp.where(mp == 0, came, own)
+                for tile in (0, 1):
+                    lanes = slice(128 * tile, 128 * tile + 128)
+                    left, right = split_lanes(first[:, lanes], second[:, lanes])
+                    out_ref[0, :, 256 * tile : 256 * tile + 128] = left
+                    out_ref[0, :, 256 * tile + 128 : 256 * tile + 256] = right
+
+            @pl.when(p == gains)
+            def _():
+                gain_out[...] = total[slot, 0:8, 0:128] + came[0:8, 0:128]
+
+    @pl.when(step == chunks + Z_LAG + SWAP_LAG - 1)
     def _():
         for spot in range(half_blocks):
             half_copy(spot).wait()
-        for index in range(gains - outer + 1):
-            swap_copy(index).wait_recv()
         for index in range(gains - outer - 1, gains - outer + 1):
             swap_copy(index).wait_send()
-
-
-def mixer_call(left_in, grad_pre, left_out, right_out, gain_parts, tokens, inverse, weights, collective):
+        dot_copy.wait()
+
+
+def mixer_call(
+    left_in, grad_pre, left_out, right_out, gain_parts, tokens, inverse, weights, dots, collective
+):
     _, rows, channels = grad_pre.shape
     full = left_in.shape[0]
     block, half = full // 16, channels // 16
@@ -742,30 +803,41 @@
     chunks = outer + inner + 1
     any_space = pl.BlockSpec(memory_space=pl.ANY)
     dma = pltpu.SemaphoreType.DMA
-    out_spec, out_shape = scatter_out(chunks, block, LANES)
     part = jax.ShapeDtypeStruct((rows, full // 2), BF)
-    out, half_own, _, half_came, swap_came = pl.pallas_call(
+
+    def out_place(q):
+        p = jnp.clip(q - Z_LAG - SWAP_LAG, 0, outer + inner - 1)
+        inside = jnp.maximum(p - outer, 0)
+        return (
+            jnp.where(p < outer, 3, inside // across), 0, jnp.where(p < outer, p, lax.rem(inside, across)))
+
+    out, gains, half_own, _, half_came, dot_came = pl.pallas_call(
         functools.partial(mixer_kernel, full_blocks),
-        grid=(chunks + Z_LAG,),
+        grid=(chunks + Z_LAG + SWAP_LAG,),
         in_specs=[
             fixed((DEPTH, 2, 2, block, rows)), fixed(grad_pre.shape),
             fixed((DEPTH, 2, 2, half, rows)), fixed(right_out.shape), fixed(gain_parts.shape),
-            any_space, fixed(inverse.shape), any_space,
+            any_space, fixed(inverse.shape), any_space, any_space,
         ],
-        out_specs=[out_spec] + [any_space] * 4,
+        out_specs=[
+            pl.BlockSpec((1, half, 2 * LANES), out_place),
+            pl.BlockSpec((8, 128), lambda q: (0, 0)),
+        ] + [any_space] * 4,
         out_shape=[
-            out_shape, part, part, part, jax.ShapeDtypeStruct((inner + 1, half, LANES), BF),
+            jax.ShapeDtypeStruct((4, half, full), F32), jax.ShapeDtypeStruct((8, 128), F32),
+            part, part, part, jax.ShapeDtypeStruct(dots.shape, F32),
         ],
         scratch_shapes=[
             pltpu.VMEM((3, LANES, channels), BF),
             pltpu.VMEM((rows, LANES), BF),
             pltpu.VMEM((16, 8, 128), F32),
             pltpu.VMEM((DEPTH, 2, block, LANES), F32),
-            pltpu.VMEM((block, LANES), F32),
+            pltpu.VMEM((4, block, LANES), F32),
             pltpu.VMEM((2, half, LANES), BF),
+            pltpu.VMEM((8, half, LANES), BF),
             pltpu.VMEM((2, rows, LANES), BF),
             dma((2,)), dma((2,)), dma((full_blocks // 2,)), dma((full_blocks // 2,)),
-            dma((2,)), dma((inner + 1,)),
+            dma((2,)), dma((8,)), dma((2,)),
             *scatter_scratch(block, LANES),
         ],
         compiler_params=pltpu.CompilerParams(
@@ -774,18 +846,9 @@
             flops=14 * full * rows * channels, bytes_accessed=16 * full * channels, transcendentals=0),
     )(
         left_in.reshape(DEPTH, 2, 2, block, rows), grad_pre,
-        left_out.reshape(DEPTH, 2, 2, half, rows), right_out, gain_parts, tokens, inverse, weights,
+        left_out.reshape(DEPTH, 2, 2, half, rows), right_out, gain_parts, tokens, inverse, weights, dots,
     )
-    place = lax.axis_index("mp")
-    out_own = out[:outer].reshape(outer, 2, half, LANES).transpose(2, 0, 1, 3).reshape(half, full)
-    own = lax.dynamic_slice_in_dim(out[outer : outer + inner], place * half, half, 1)
-    came = swap_came[:inner].astype(F32)
-    first = place == 0
-    in_own = jnp.stack([jnp.where(first, own, came), jnp.where(first, came, own)])
-    in_own = in_own.reshape(2, 3, across, half, LANES).transpose(1, 3, 0, 2, 4)
-    in_own = in_own.reshape(3, half, 2, channels)
-    gains = out[chunks - 1, :3, :128] + swap_came[inner, :3, :128].astype(F32)
-    return in_own, out_own, gains, half_own.astype(F32) + half_came.astype(F32)
+    return out, gains, half_own.astype(F32) + half_came.astype(F32), dot_came
 
 
 def middle_back_kernel(
@@ -798,13 +861,12 @@
     inverse = lax.rsqrt(jnp.mean(middle * middle, axis=-1, keepdims=True) + EPSILON)
     unit = middle * inverse
     grad_normed = sum_own_ref[...].astype(F32) + sum_came_ref[...].astype(F32)
-    gain_grad = jnp.sum(grad_normed * unit, axis=0, keepdims=True)
+    product = grad_normed * unit
     before = jnp.where(pl.program_id(0) == 0, 0.0, gain_grad_ref[...])
-    gain_grad_ref[...] = before + gain_grad
-    scaled = grad_normed * gain_ref[...]
-    dots = jnp.mean(scaled * unit, axis=-1, keepdims=True)
+    gain_grad_ref[...] = before + jnp.sum(product, axis=0, keepdims=True)
+    dots = jnp.mean(product * gain_ref[...], axis=-1, keepdims=True)
     back = cot_ref[...].astype(F32) * weight_ref[...]
-    grad = back + inverse * (scaled - unit * dots)
+    grad = back + inverse * (grad_normed * gain_ref[...] - unit * dots)
     first = lax.axis_index("mp") == 0
     grad_own_ref[...] = jnp.where(first, grad[:, :part], grad[:, part:])
     low = grad.astype(BF)
@@ -818,7 +880,7 @@
 def middle_back(sum_own, sum_came, middle, cot, tokens, weight, gain, mixer_out):
     rows, full = middle.shape
     channels = mixer_out.shape[0]
-    step = 128 if rows % 128 == 0 else rows
+    step = 224 if rows % 224 == 0 else rows
     line = lambda width: pl.BlockSpec((step, width), lambda r: (r, 0))
     shape = jax.ShapeDtypeStruct
     return pl.pallas_call(
@@ -876,11 +938,36 @@
 ITEMS = 4
 
 
-def gather_kernel(in_ref, out_ref, small_ref, all_in, all_out, all_small, right_send, left_send,
+def split_lanes(first, second):
+    low = lax.broadcasted_iota(jnp.int32, first.shape, 1) < 64
+    return (
+        jnp.where(low, first, pltpu.roll(second, 64, 1)),
+        jnp.where(low, pltpu.roll(first, 64, 1), second),
+    )
+
+
+def gather_kernel(mixer_ref, gain_ref, lengths_ref, domains_ref, glu_in_ref, glu_out_ref, cot_ref,
+                  all_in, all_out, all_small, cot_full, glu_low,
+                  in_ref, out_ref, small_ref, right_send, left_send,
                   z_recv, x_send, x_recv, core_send, core_recv, y_send, y_recv, local_sem):
     z, x, core = device_place()
     mp = lax.axis_index("mp")
     barrier = pltpu.get_barrier_semaphore()
+    for kind in range(3):
+        for tile in range(in_ref.shape[3] // 128):
+            first = mixer_ref[kind, :, 256 * tile : 256 * tile + 128]
+            second = mixer_ref[kind, :, 256 * tile + 128 : 256 * tile + 256]
+            for side, value in enumerate(split_lanes(first, second)):
+                in_ref[side, kind, :, 128 * tile : 128 * tile + 128] = value.astype(BF)
+    out_ref[...] = mixer_ref[3].astype(BF)
+    lane = lax.broadcasted_iota(jnp.int32, (1, 128), 1)
+    live = jnp.zeros((1, 128), F32)
+    for batch in range(lengths_ref.shape[0]):
+        count = lengths_ref[batch : batch + 1, :].astype(F32)
+        live = live + jnp.where(lane == domains_ref[batch : batch + 1, :], count, 0.0)
+    small_ref[...] = jnp.zeros_like(small_ref)
+    small_ref[0:3, 0:64] = gain_ref[...].astype(BF).astype(F32)
+    small_ref[3:4, :] = live
     right, left = lax.rem(z + 1, DEPTH), lax.rem(z + DEPTH - 1, DEPTH)
     dp = lax.axis_index("dp")
     for target in (
@@ -936,6 +1023,11 @@
         pltpu.make_async_copy(out_ref, spot(1, z, x, core), local_sem.at[1]),
         pltpu.make_async_copy(small_ref, all_small.at[z, x, core, mp], local_sem.at[2]),
     ]
+    cot_lanes = pl.ds(pl.multiple_of(mp * cot_ref.shape[1], 128), cot_ref.shape[1])
+    cot_local = pltpu.make_async_copy(cot_ref, cot_full.at[:, cot_lanes], local_sem.at[3])
+    cot_copy = pltpu.make_async_remote_copy(
+        cot_ref, cot_full.at[:, cot_lanes], y_send.at[2], y_recv.at[2],
+        device_id=(dp, 1 - mp), device_id_type=MESH_ID)
     for one in y_copies:
         one.start()
     locals_[2].start()
@@ -960,6 +1052,12 @@
         core_copy(item, z, x, source).start()
     locals_[0].start()
     locals_[1].start()
+    cot_copy.start()
+    cot_local.start()
+    glu_low[0:2] = glu_in_ref[...].astype(BF)
+    for tile in range(glu_out_ref.shape[0] // 128):
+        lanes = slice(128 * tile, 128 * tile + 128)
+        glu_low[2, :, lanes] = glu_out_ref[lanes, :].T.astype(BF)
 
     def from_x(item, zs):
         pltpu.make_async_remote_copy(
@@ -1021,29 +1119,42 @@
         one.wait_send()
     locals_[0].wait()
     locals_[1].wait()
-
-
-def gather_call(in_blocks, out_rows, small, collective):
-    _, three, own_rows, channels = in_blocks.shape
-    full = out_rows.shape[1]
+    cot_local.wait()
+    cot_copy.wait_send()
+    pltpu.make_async_remote_copy(
+        cot_ref, cot_full.at[:, pl.ds(pl.multiple_of((1 - mp) * cot_ref.shape[1], 128), cot_ref.shape[1])],
+        y_send.at[2], y_recv.at[2], device_id=(dp, 1 - mp), device_id_type=MESH_ID).wait_recv()
+
+
+def gather_call(mixer, gain, lengths, domains, glu_in, glu_out, cot, collective):
+    _, own_rows, full = mixer.shape
+    channels = full // 2
     dma = pltpu.SemaphoreType.DMA
     any_space = pl.BlockSpec(memory_space=pl.ANY)
+    in_vmem = pl.BlockSpec(memory_space=pltpu.VMEM)
+    _, glu_rows, hidden = glu_in.shape
     return pl.pallas_call(
         gather_kernel,
-        in_specs=[any_space] * 3,
-        out_specs=[any_space] * 3,
+        in_specs=[in_vmem] * 6 + [any_space],
+        out_specs=[any_space] * 4 + [in_vmem],
         out_shape=[
-            jax.ShapeDtypeStruct((three, DEPTH, 2, 2, 2, own_rows, channels), BF),
+            jax.ShapeDtypeStruct((3, DEPTH, 2, 2, 2, own_rows, channels), BF),
             jax.ShapeDtypeStruct((DEPTH, 2, 2, own_rows, full), BF),
-            jax.ShapeDtypeStruct((DEPTH, 2, 2, 2, *small.shape), F32),
+            jax.ShapeDtypeStruct((DEPTH, 2, 2, 2, 8, 128), F32),
+            jax.ShapeDtypeStruct((cot.shape[0], 2 * cot.shape[1]), BF),
+            jax.ShapeDtypeStruct((3, glu_rows, hidden), BF),
         ],
         scratch_shapes=[
+            pltpu.VMEM((2, 3, own_rows, channels), BF),
+            pltpu.VMEM((own_rows, full), BF),
+            pltpu.VMEM((8, 128), F32),
             dma((DEPTH, ITEMS)), dma((DEPTH, ITEMS)), dma((DEPTH, ITEMS)), dma((DEPTH, ITEMS)),
-            dma((DEPTH, ITEMS)), dma((DEPTH, 2, ITEMS)), dma((DEPTH, 2, ITEMS)), dma((2,)), dma((2,)), dma((3,)),
+            dma((DEPTH, ITEMS)), dma((DEPTH, 2, ITEMS)), dma((DEPTH, 2, ITEMS)), dma((3,)), dma((3,)), dma((4,)),
         ],
-        compiler_params=pltpu.CompilerParams(collective_id=collective, has_side_effects=True),
+        compiler_params=pltpu.CompilerParams(
+            collective_id=collective, has_side_effects=True, vmem_limit_bytes=VMEM_LIMIT),
         cost_estimate=pl.CostEstimate(flops=0, bytes_accessed=300_000_000, transcendentals=0),
-    )(in_blocks, out_rows, small)
+    )(mixer, gain, lengths, domains, glu_in, glu_out, cot)
 
 
 def shards(
@@ -1073,35 +1184,33 @@
     own_rows = mixer_master.shape[1]
     channels = groups * own_rows
     part = full // narrow
-    quick = groups == 16 and narrow == 2
-
-    cot_full = mp_gather(cotangent.reshape(rows, part))
+    quick = groups == 16 and narrow == 2 and own_rows == 64
 
     domain_ids = jnp.arange(NDOM, dtype=jnp.int32)
     member = (domains[..., 0][..., None] == domain_ids).astype(F32)
-    live_counts = lengths.astype(F32)
-    counts = jnp.sum(member * live_counts[..., None], axis=(0, 1))
-    gain_low = gain_master.astype(BF)
-    mixer_low = mixer_master.astype(BF)
-    in_blocks = mixer_low[:3].reshape(3, own_rows, groups, narrow, own_rows)
-    in_blocks = in_blocks.transpose(3, 0, 1, 2, 4).reshape(narrow, 3, own_rows, channels)
+    cot_part = cotangent.reshape(rows, part)
     if quick:
-        small = jnp.zeros((8, 128), F32)
-        small = small.at[:3, :own_rows].set(gain_low.astype(F32)).at[3, :NDOM].set(counts)
-        mixer_in, mixer_out, small = gather_call(in_blocks, mixer_low[3], small, 2)
+        mixer_in, mixer_out, small, cot_full, glu_low = gather_call(
+            mixer_master, gain_master, lengths, domains[..., 0], glu_in_master, glu_out_master, cot_part, 2
+        )
         mixer_in = mixer_in.reshape(3, full, channels)
         mixer_out = mixer_out.reshape(channels, full)
         small = small.reshape(groups, narrow, 8, 128)
         gain_full = small[:, :, :3, :own_rows].transpose(2, 0, 1, 3).reshape(3, full)
         counts = jnp.sum(small[:, 0, 3, :NDOM], axis=0)
     else:
-        gain_full = lax.all_gather(gain_low, ("dp", "mp"), axis=1, tiled=True).astype(F32)
+        gain_full = lax.all_gather(
+            gain_master.astype(BF), ("dp", "mp"), axis=1, tiled=True
+        ).astype(F32)
+        mixer_low = mixer_master.astype(BF)
+        in_blocks = mixer_low[:3].reshape(3, own_rows, groups, narrow, own_rows)
+        in_blocks = in_blocks.transpose(3, 0, 1, 2, 4).reshape(narrow, 3, own_rows, channels)
         in_rows = mp_swap(in_blocks).transpose(1, 0, 2, 3).reshape(3, narrow * own_rows, channels)
         mixer_in = lax.all_gather(in_rows, "dp", axis=1, tiled=True)
         mixer_out = lax.all_gather(mixer_low[3], "dp", axis=0, tiled=True)
-        counts = lax.psum(counts, "dp")
-    glu_low = jnp.concatenate([glu_in_master.astype(BF), glu_out_master.astype(BF).T[None]])
-    glu_low, mixer_in, cot_full = lax.optimization_barrier((glu_low, mixer_in, cot_full))
+        counts = lax.psum(jnp.sum(member * lengths.astype(F32)[..., None], axis=(0, 1)), "dp")
+        cot_full = mp_gather(cot_part)
+        glu_low = jnp.concatenate([glu_in_master.astype(BF), glu_out_master.astype(BF).T[None]])
     glu = lax.all_gather(glu_low, "dp", axis=1, tiled=True)
 
     seq_weight = jnp.sum(counts) / (NDOM * jnp.sum(member * counts, axis=-1))
@@ -1126,19 +1235,26 @@
     square = mp_sum_wide(square.reshape(rows, 1))
     inverse_state = lax.rsqrt(square / full + EPSILON)
     mixed = jnp.dot(raw.reshape(rows, channels), mixer_out, preferred_element_type=F32)
-    branch_mix = inverse_state * mp_sum(mixed)
+    back_low = (cot_full.astype(F32) * token_weight).astype(BF)
+    if quick:
+        mixed = mixed.astype(BF)
+        came, left_back, left_in = lax.optimization_barrier(
+            (partner_swap(mixed), back_low.T, normed_in.T)
+        )
+        mixed = mixed.astype(F32) + came.astype(F32)
+    else:
+        mixed = mp_sum(mixed)
+    branch_mix = inverse_state * mixed
     middle = seq_in + branch_mix
     inverse_mid = inverse_rms(middle)
     unit_mid = middle * inverse_mid
     normed_mid = (unit_mid * gain_full[2]).astype(BF)
 
-    back = cot_full.astype(F32) * token_weight
-    back_low = back.astype(BF)
     across = (((1,), (1,)), ((), ()))
     down = (((0,), (0,)), ((), ()))
     dot = functools.partial(lax.dot_general, preferred_element_type=F32)
     if quick:
-        glu_sums, sum_own, sum_came, half_own, half_came = glu_call(normed_mid, back_low, glu, 0)
+        glu_sums, sum_own, sum_came, half_own, half_came = glu_call(normed_mid, back_low, left_back, glu, 0)
         branch = half_own.astype(F32) + half_came.astype(F32)
     else:
         pre_act = jnp.dot(normed_mid, glu[0], preferred_element_type=F32)
@@ -1167,6 +1283,7 @@
         unit_mid = middle * inverse_mid
         gain_mid = jnp.sum(grad_normed * unit_mid, axis=0)
         scaled_mid = grad_normed * gain_full[2]
+        back = cot_full.astype(F32) * token_weight
         grad_middle = back + inverse_mid * (
             scaled_mid - unit_mid * jnp.mean(scaled_mid * unit_mid, axis=-1, keepdims=True)
         )
@@ -1180,7 +1297,6 @@
     )
     grad_pre = grad_pre.reshape(3, rows, channels)
     gated_out = gated_out.reshape(rows, channels)
-    in_mean = mp_sum_wide(pre_dot.reshape(rows, 1)) / full
     gain_state = jnp.sum(gain_state, axis=0).reshape(groups, 1, own_rows)
     gain_state = lax.dynamic_update_slice_in_dim(
         jnp.zeros((groups, narrow, own_rows), F32), gain_state, place, 1
@@ -1196,11 +1312,12 @@
             axis=1,
         )
         gain_parts = jnp.pad(gain_parts, ((0, 0), (0, 5), (0, 0)))
-        in_own, out_own, gain_own, grad_normed_in = mixer_call(
-            normed_in.T, grad_pre, gated_out.T, middle_low, gain_parts, token_rows, inverse_in, mixer_in, 1
+        pre_dot = pre_dot.reshape(-1, 128)
+        mixer_own, gain_own, grad_normed_in, dot_came = mixer_call(
+            left_in, grad_pre, gated_out.T, middle_low, gain_parts, token_rows, inverse_in, mixer_in, pre_dot, 1
         )
-        gain_own = lax.dynamic_slice_in_dim(gain_own, place * own_rows, own_rows, 1)
-        in_own = in_own.reshape(3, own_rows, narrow, groups, own_rows).transpose(0, 1, 3, 2, 4)
+        in_mean = (pre_dot + dot_came).reshape(rows, 1) / full
+        gain_own = lax.dynamic_slice_in_dim(gain_own[:3], place * own_rows, own_rows, 1)
     else:
         grad_mix_out = dot(gated_out, middle_low, down).astype(BF)
         grad_mix_in = jnp.einsum("td,kte->kde", normed_in, grad_pre, preferred_element_type=F32)
@@ -1214,8 +1331,9 @@
         gain_rows = jnp.stack([gain_in, gain_state.reshape(full), gain_mid / narrow])
         gain_total = lax.psum(gain_rows, ("dp", "mp"))
         gain_own = lax.dynamic_slice_in_dim(gain_total, device * own_rows, own_rows, 1)
-    in_own = in_own.reshape(3, own_rows, full).astype(F32)
-    out_own = out_own.astype(F32)
+        in_mean = mp_sum_wide(pre_dot.reshape(rows, 1)) / full
+        in_own = in_own.reshape(3, own_rows, full)
+        mixer_own = jnp.concatenate([in_own, out_own[None]]).astype(F32)
     unit_in_own = own_features(token_rows).astype(F32) * inverse_in
     grad_seq = grad_middle_own + inverse_in * (
         grad_normed_in * own_features(gain_full[0]) - unit_in_own * in_mean
@@ -1224,7 +1342,6 @@
 
     scale = 1.0 / (batches * groups * tokens.shape[1])
     update = functools.partial(adamw_update, count=STEP_NUMBER)
-    mixer_own = jnp.concatenate([in_own, out_own[None]])
     mixer_new = update(
         mixer_master, mixer_first, mixer_second, mixer_own * scale, rate=MATRIX_RATE, decay=DECAY_RATE
     )

time: 792 us -> 718 us (0.907)
  Pallas kernels: 539 us -> 516 us
  local copies, waits for them, and re-layouts: 62.2 us -> 40 us
  waiting for transfers between devices: 86.3 us -> 75.6 us
    pallas_call x1, Pallas kernels: 234 us -> 216 us  [glu_call(): pl.pallas_call(functools.partial(glu_kernel, hidden_blocks, full_blocks),...]
    another operation x6 -> x0, local copies, waits for them, and re-layouts: 16.4 us -> none  [the longest x2 12.3 us: glu_call(): jnp.stack([normed.T, back_low.T]).reshape(2, DEPTH, 2, 2, block, rows)]
    ppermute x4 -> x2, waiting for transfers between devices: 75.1 us -> 64.7 us  [partner_swap(): return lax.ppermute(value, 'mp', [(0, 1), (1, 0)])]
    transpose x1 -> x3, other arithmetic: 1.49 us -> 9.87 us  [the longest x2 7.41 us: shards(): came, left_back, left_in = lax.optimization_barrier((partner_swap(mixed),...]
    pallas_call x1, Pallas kernels: 113 us -> 105 us  [gather_call(): pl.pallas_call(gather_kernel, in_specs=[in_vmem] * 6 + [any_space], out_s...]
  transfers between devices with their start and end apart: 5 -> 3, of which waited for: 2 -> 2; matrix products, arithmetic and copies ran while one was open for 13% -> 11% of each run, Pallas kernels for 18% -> 2%
where the time goes in v4:
time: 718 us; the launch traced here: 717 us
  Pallas kernels  516 us (72%)
  waiting for transfers between devices  75.6 us (11%)
  other arithmetic  45.1 us (6%)
  local copies, waits for them, and re-layouts  40 us (6%)
  matrix products  23.1 us (3%)
  between operations  14.3 us (2%)
    pallas_call x1, Pallas kernels, glu_call(): pl.pallas_call(functools.partial(glu_kernel, hidden_blocks, full_blocks),...  216 us
    pallas_call x1, Pallas kernels, mixer_call(): pl.pallas_call(functools.partial(mixer_kernel, full_blocks), grid=(chunks...  133 us
    pallas_call x1, Pallas kernels, gather_call(): pl.pallas_call(gather_kernel, in_specs=[in_vmem] * 6 + [any_space], out_s...  105 us
    ppermute x2, waiting for transfers between devices, partner_swap(): return lax.ppermute(value, 'mp', [(0, 1), (1, 0)])  64.7 us
    pallas_call x1, Pallas kernels, middle_back(): pl.pallas_call(middle_back_kernel, grid=(rows // step,), in_specs=[line(f...  18.1 us
    pallas_call x1, Pallas kernels, scan_backward(): pl.pallas_call(scan_backward_kernel, grid=(batches, width // block), in_s...  17.7 us
    dot_general x1, matrix products, shards(): jnp.einsum('td,kde->kte', normed_in, mixer_in, preferred_element_type=F32)  16.1 us
    pallas_call x1, Pallas kernels, glu_update(): pl.pallas_call(functools.partial(glu_update_kernel, scale), grid=(blocks,...  15.8 us
  transfers between devices with their start and end apart: 3, of which 2 were waited for; matrix products, arithmetic and copies ran while one was open for 11% of the time, Pallas kernels for 2%

profile of v4, /device:TPU:0, one launch (start us, length us, event | category | flops | bytes accessed | tf_op | source)
XLA Modules:
  0.0 716.6 jit_solution(18196645296826848474)
XLA Ops:
  7.2 1.3 copy.53.lengths_ref
  8.5 1.3 copy.54.domains_ref
  9.8 105.3 %shard_map.272 = (bf16[3,4,2,2,2,64,1024]{6,5,4,3,2,1,0:T(8,128)(2,1)}, bf16[4,2,2,64,2048]{4,3,2,1,0:T(8,128)(2,1)}, f32[4,2,2,2,8,128]{5,4,3,2,1,0:T(8,128)}, ...) custom-call(f32[4,64,2048]{2,1,0:T(8,128)} %mixer_ref.1, f32[3,64]{1,0:T(4,128)} %gain_ref.1, s32[2,1]{1,0:T(2,128)} %copy.53.lengths_ref, ...), custom_call_target="tpu_custom_call" | custom-call | bytes 300000000 | tf_op jit(solution)/shard_map/pallas_call | solution.py:1136
  117.7 3.0 fusion.2
  122.5 16.1 %fusion.8 = f32[3,1024,896]{1,2,0:T(8,128)} fusion(bf16[896,2048,1]{1,0,2:T(8,128)(2,1)S(1)} %bitcast.64, bf16[3,2048,1024]{2,1,0:T(8,128)(2,1)} %bitcast.76), kind=kOutput, calls=%fused_computation.38 | convolution fusion | flops 11274289152 | bytes 27262976 | tf_op jit(solution)/shard_map/td,kde->kte/dot_general | solution.py:1232
  138.6 10.8 %shard_map.273 = (f32[2,448,1024]{2,1,0:T(8,128)}, bf16[2,448,1024]{2,1,0:T(8,128)(2,1)}, f32[2,448,1]{2,1,0:T(8,128)}) custom-call(f32[3,2,448,1024]{3,2,1,0:T(8,128)} %bitcast.57, f32[1,1024]{1,0:T(1,128)} %broadcast_in_dim_reshape.8.bound_ref, f32[1,1024]{1,0:T(1,128)} %broadcast_in_dim_reshape.9.gain_ref), custom_call_target="tpu_custom_call" | custom-call | flops 36700160 | bytes 16515072 | tf_op jit(solution)/shard_map/pallas_call | solution.py:151
  149.4 7.0 convolution_convert_fusion
  156.4 1.2 collective-permute-start.1
  158.8 1.5 slice_reduce_fusion.1
  161.3 4.7 fusion.14
  165.9 2.7 fusion.5
  168.7 2.5 multiply_convert_fusion.1.back_ref
  171.2 1.1 select_n.38.weight_ref
  174.1 64.7 %collective-permute-done = f32[896,1]{0,1:T(1,128)S(1)} collective-permute-done((f32[896,1]{0,1:T(1,128)S(1)}, f32[896,1]{0,1:T(1,128)S(1)}, u32[]{:S(2)}, u32[]{:S(2)}) %collective-permute-start) | collective-permute-done | bytes 3616 | tf_op jit(solution)/shard_map/ppermute | solution.py:47
  239.9 6.3 multiply_reduce_fusion
  246.2 3.0 copy-done
  249.3 2.5 fusion.13
  251.7 6.1 copy.65
  257.8 6.2 copy.56
  264.0 6.1 copy.66
  270.1 5.6 multiply_convert_fusion.normed_ref
  275.6 10.9 %all-gather.2.cloned.1.call-done.glu_ref = bf16[3,2048,2816]{2,1,0:T(8,128)(2,1)} async-done(((bf16[3,128,2816]{2,1,0:T(8,128)(2,1)}), bf16[3,2048,2816]{2,1,0:T(8,128)(2,1)}) %all-gather.2.cloned.1.call-update) | async-done | bytes 34603024 | tf_op jit(solution)/shard_map/all_gather | solution.py:1214
  286.6 215.7 %shard_map.274 = (f32[33,128,256]{2,1,0:T(8,128)}, bf16[896,2048]{1,0:T(8,128)(2,1)}, bf16[896,2048]{1,0:T(8,128)(2,1)}, bf16[896,1024]{1,0:T(8,128)(2,1)}, bf16...) custom-call(bf16[896,2048]{1,0:T(8,128)(2,1)} %multiply_convert_fusion.normed_ref, ...), custom_call_target="tpu_custom_call" | custom-call | flops 93012885504 | bytes 69206016 | tf_op jit(solution)/shard_map/pallas_call | solution.py:588
  502.3 18.1 %shard_map.275 = (f32[896,1024]{1,0:T(8,128)}, bf16[896,2048]{1,0:T(8,128)(2,1)}, f32[896,1]{1,0:T(8,128)}, f32[896,1024]{1,0:T(8,128)}, f32[1,2048]{1,0:T(1,128)}) custom-call(bf16[896,2048]{1,0:T(8,128)(2,1)} %get-tuple-element.61.sum_own_ref, bf16[896,2048]{1,0:T(8,128)(2,1)} %get-tuple-element.62.sum_came_ref, f32[896,2048]{1,0:T(8,128)} %copy-done, ...), custom_call_target="tpu_custom_call" | custom-call | flops 3758096384 | bytes 36700160 | tf_op jit(solution)/shard_map/pallas_call | solution.py:886
  520.4 17.7 %shard_map.276 = (bf16[3,2,448,1024]{3,2,1,0:T(8,128)(2,1)}, bf16[2,448,1024]{2,1,0:T(8,128)(2,1)}, f32[2,1,1024]{2,1,0:T(1,128)}, f32[2,448,1]{2,1,0:T(8,128)}) custom-call(f32[3,2,448,1024]{3,2,1,0:T(8,128)} %bitcast.58, f32[2,448,1024]{2,1,0:T(8,128)} %get-tuple-element.65.states_ref, f32[2,448,1024]{2,1,0:T(8,128)} %bitcast.65, ...), custom_call_target="tpu_custom_call" | custom-call | flops 73400320 | bytes 25690112 | tf_op jit(solution)/shard_map/pallas_call | solution.py:257
  539.8 3.8 copy.60
  543.6 1.2 reduce.12
  545.5 133.0 %shard_map.277 = (f32[4,64,2048]{2,1,0:T(8,128)}, f32[8,128]{1,0:T(8,128)}, bf16[896,1024]{1,0:T(8,128)(2,1)}, bf16[896,1024]{1,0:T(8,128)(2,1)}, bf16[896,1024]{1,0:T(8,128)(2,1)}, /*index=5*/f32[7,128]{1,0:T(8,128)}) custom-call(bf16[4,2,2,128,896]{4,3,2,1,0:T(8,128)(2,1)} %bitcast.61, bf16[3,896,1024]{2,1,0:T(8,128)(2,1)} %bitcast.78, ...), custom_call_target="tpu_custom_call" | custom-call | flops 26306674688 | bytes 33554432 | tf_op jit(solution)/shard_map/pallas_call | solution.py:814
  679.9 4.5 add_convert_fusion.1
  685.2 4.1 multiply_subtract_fusion
  691.6 2.4 add_convert_fusion
  694.0 15.8 %shard_map.278 = (f32[2,128,2816]{2,1,0:T(8,128)}, f32[2,128,2816]{2,1,0:T(8,128)}, f32[2,128,2816]{2,1,0:T(8,128)}, f32[2816,128]{1,0:T(8,128)}, f32[2816,128]{1,0:T(8,128)}, /*index=5*/f32[2816,128]{1,0:T(8,128)}) custom-call(f32[33,128,256]{2,1,0:T(8,128)} %get-tuple-element.78.act_ref.up_ref.out_ref, ...), custom_call_target="tpu_custom_call" | custom-call | flops 21626880 | bytes 30277632 | tf_op jit(solution)/shard_map/pallas_call | solution.py:924
  (97 shorter events, 16.3 us)
Async XLA Ops:
  7.2 279.4 %all-gather.2.cloned.1.call-start = ((), (), s32[]{:S(2)}) async-start(), calls=%async_computation | async-start | bytes 36765696 | tf_op jit(solution)/shard_map/all_gather | solution.py:1214
  9.8 107.1 %copy-start.19 = (f32[2048]{0:T(1024)S(1)}, f32[2048]{0:T(1024)}, u32[]{:S(2)}) copy-start(f32[2048]{0:T(1024)} %param.21) | copy-start | bytes 24580
  116.9 57.2 %copy-start.14 = (f32[2048]{0:T(1024)}, f32[2048]{0:T(1024)S(1)}, u32[]{:S(2)}) copy-start(f32[2048]{0:T(1024)S(1)} %mul.230) | copy-start | bytes 24580
  117.7 3.8 copy-start.1
  138.6 10.8 %copy-start.6 = (bf16[4,2,2,64,2048]{4,3,2,1,0:T(8,128)(2,1)S(1)}, bf16[4,2,2,64,2048]{4,3,2,1,0:T(8,128)(2,1)}, u32[]{:S(2)}) copy-start(bf16[4,2,2,64,2048]{4,3,2,1,0:T(8,128)(2,1)} %get-tuple-element.54) | copy-start | bytes 12582916
  149.4 8.2 %copy-start.13 = (f32[2,448,1]{2,1,0:T(8,128)S(1)}, f32[2,448,1]{2,1,0:T(8,128)}, u32[]{:S(2)}) copy-start(f32[2,448,1]{2,1,0:T(8,128)} %get-tuple-element.52) | copy-start | bytes 10756
  149.4 10.9 %copy-start.24 = (s32[2,1,1]{0,2,1:T(1,128)S(1)}, s32[2,1,1]{0,2,1:T(1,128)}, u32[]{:S(2)}) copy-start(s32[2,1,1]{0,2,1:T(1,128)} %param.20) | copy-start | bytes 28
  149.4 11.7 %copy-start.23 = (s32[2,1]{0,1:T(1,128)S(1)}, s32[2,1]{0,1:T(1,128)}, u32[]{:S(2)}) copy-start(s32[2,1]{0,1:T(1,128)} %param.19) | copy-start | bytes 28
  156.4 83.5 %collective-permute-start.1 = (bf16[896,2048]{1,0:T(8,128)(2,1)}, bf16[896,2048]{1,0:T(8,128)(2,1)}, u32[]{:S(2)}, u32[]{:S(2)}) collective-permute-start(bf16[896,2048]{1,0:T(8,128)(2,1)} %convolution_convert_fusion), channel_id=1, source_target_pairs={{0,1},{1,0},{2,3},{3,2},{4,5},{5,4},{6,7},{7,6},{8,9},{9,8},{10,11... | collective-permute-start | bytes 11010056 | tf_op jit(solution)/shard_map/ppermute | solution.py:47
  157.9 80.9 %collective-permute-start = (f32[896,1]{0,1:T(1,128)S(1)}, f32[896,1]{0,1:T(1,128)S(1)}, u32[]{:S(2)}, u32[]{:S(2)}) collective-permute-start(f32[896,1]{0,1:T(1,128)S(1)} %reshape.307), channel_id=1, source_target_pairs={{0,1},{1,0},{2,3},{3,2},{4,5},{5,4},{6,7},{7,6},{8,9},{9,8},{10,11... | collective-permute-start | bytes 10760 | tf_op jit(solution)/shard_map/ppermute | solution.py:47
  158.8 7.1 copy-start.15
  161.3 4.7 copy-start.2
  165.9 2.8 copy-start.4
  246.2 3.0 copy-start
  520.4 18.7 %copy-start.20 = (f32[1,2048]{1,0:T(1,128)S(1)}, f32[1,2048]{1,0:T(1,128)}, u32[]{:S(2)}) copy-start(f32[1,2048]{1,0:T(1,128)} %get-tuple-element.72) | copy-start | bytes 24580
  520.4 159.5 %slice-start = ((s8[7340032]{0:T(1024)(128)(4,1)}), s8[3145728]{0:T(1024)(128)(4,1)S(1)}, s32[]{:S(2)}) async-start(s8[7340032]{0:T(1024)(128)(4,1)} %bitcast.52), calls=%async_computation.1 | async-start | bytes 6291456
  545.5 133.0 %copy-start.17 = (f32[7,128]{1,0:T(8,128)S(1)}, f32[7,128]{1,0:T(8,128)}, u32[]{:S(2)}) copy-start(f32[7,128]{1,0:T(8,128)} %reshape.321.dot_ref) | copy-start | bytes 10756
  545.5 134.4 %slice-start.1 = ((s8[7340032]{0:T(1024)(128)(4,1)}), s8[4194304]{0:T(1024)(128)(4,1)S(1)}, s32[]{:S(2)}) async-start(s8[7340032]{0:T(1024)(128)(4,1)} %bitcast.52), calls=%async_computation.2 | async-start | bytes 8388608
  679.9 4.5 copy-start.5
  679.9 4.5 copy-start.8
  679.9 4.5 copy-start.9
  679.9 5.2 copy-start.10
  685.1 4.2 copy-start.18
  685.1 4.2 copy-start.21
  685.1 4.2 copy-start.22
  685.1 4.9 copy-start.3
  685.1 5.4 copy-start.7
  685.2 5.9 copy-start.11
  685.2 6.4 copy-start.12
  685.2 6.4 dynamic-slice-start
  685.2 6.4 copy-start.16
Sparse Core Ops, SparseCore 0:
  115.3 171.2 all-gather.1

commit v5 on v4

--- a/solution.py
+++ b/solution.py
@@ -307,34 +307,56 @@
     pl.semaphore_wait(barrier, len(targets))
 
 
-def scatter_step(step, chunks, compute, finish, scratch):
+def scatter_step(step, chunks, compute, finish, scratch, small_last=False):
     (own, core_out, core_in, keep, x_out, x_in, sums, mine, z_out, z_in,
      core_send, core_recv, x_send, x_recv, z_send, z_recv) = scratch
     z, x, core = device_place()
 
-    def core_copy(p):
+    def core_copy(p, cut=()):
         return pltpu.make_async_remote_copy(
-            core_out.at[lax.rem(p, 2)], core_in.at[lax.rem(p, 4)],
+            core_out.at[(lax.rem(p, 2), *cut)], core_in.at[(lax.rem(p, 4), *cut)],
             core_send.at[lax.rem(p, 2)], core_recv.at[lax.rem(p, 4)],
             device_id=device_at(z, x, 1 - core), device_id_type=MESH_ID)
 
-    def x_copy(p):
+    def x_copy(p, cut=()):
         return pltpu.make_async_remote_copy(
-            x_out.at[lax.rem(p, X_LAG)], x_in.at[lax.rem(p, 2 * X_LAG)],
+            x_out.at[(lax.rem(p, X_LAG), *cut)], x_in.at[(lax.rem(p, 2 * X_LAG), *cut)],
             x_send.at[lax.rem(p, X_LAG)], x_recv.at[lax.rem(p, 2 * X_LAG)],
             device_id=device_at(z, 1 - x, core), device_id_type=MESH_ID)
 
-    def z_copy(p, hop):
+    def z_copy(p, hop, cut=()):
         return pltpu.make_async_remote_copy(
-            z_out.at[lax.rem(p, 4), hop - 1], z_in.at[lax.rem(p, 8), hop - 1],
+            z_out.at[(lax.rem(p, 4), hop - 1, *cut)], z_in.at[(lax.rem(p, 8), hop - 1, *cut)],
             z_send.at[lax.rem(p, 4), hop - 1], z_recv.at[lax.rem(p, 8), hop - 1],
             device_id=device_at(lax.rem(z + hop, DEPTH), x, core), device_id_type=MESH_ID)
 
+    corner = (slice(0, 16), slice(0, 128))
+    every = slice(None)
+
+    def go(copy, lead, p, act):
+        if not small_last:
+            act(copy(p))
+            return
+        pl.when(p < chunks - 1)(lambda: act(copy(p)))
+        pl.when(p == chunks - 1)(lambda: act(copy(p, (*(every,) * lead, *corner))))
+
+    def core_go(p, act):
+        go(core_copy, 2, p, act)
+
+    def x_go(p, act):
+        go(x_copy, 1, p, act)
+
+    def z_go(p, hop, act):
+        go(lambda p, cut=(): z_copy(p, hop, cut), 0, p, act)
+
+    start, wait_recv, wait_send = (
+        lambda copy: copy.start(), lambda copy: copy.wait_recv(), lambda copy: copy.wait_send())
+
     @pl.when(step < chunks)
     def _():
         @pl.when(step >= 2)
         def _():
-            core_copy(step - 2).wait_send()
+            core_go(step - 2, wait_send)
 
         def to_partner(value):
             core_out[lax.rem(step, 2)] = value.astype(BF)
@@ -343,55 +365,55 @@
             own[lax.rem(step, 2)] = value
 
         compute(step, 1 - core, to_partner)
-        core_copy(step).start()
+        core_go(step, start)
         compute(step, core, to_own)
 
     @pl.when((step >= 1) & (step < chunks + 1))
     def _():
         p = step - 1
-        core_copy(p).wait_recv()
+        core_go(p, wait_recv)
 
         @pl.when(p >= X_LAG)
         def _():
-            x_copy(p - X_LAG).wait_send()
+            x_go(p - X_LAG, wait_send)
 
         two, four, slot = lax.rem(p, 2), lax.rem(p, 4), lax.rem(p, X_LAG)
         x_out[slot] = (own[two, :, 1 - x] + core_in[four, :, 1 - x].astype(F32)).astype(BF)
-        x_copy(p).start()
+        x_go(p, start)
         keep[slot] = own[two, :, x] + core_in[four, :, x].astype(F32)
 
     @pl.when((step >= X_LAG) & (step < chunks + X_LAG))
     def _():
         p = step - X_LAG
-        x_copy(p).wait_recv()
+        x_go(p, wait_recv)
         four = lax.rem(p, 4)
         sums[...] = keep[lax.rem(p, X_LAG)] + x_in[lax.rem(p, 2 * X_LAG)].astype(F32)
         for hop in range(1, DEPTH):
             @pl.when(p >= 4)
             def _():
-                z_copy(p - 4, hop).wait_send()
+                z_go(p - 4, hop, wait_send)
 
             z_out[four, hop - 1] = sums[lax.rem(z + hop, DEPTH)].astype(BF)
-            z_copy(p, hop).start()
+            z_go(p, hop, start)
         mine[four] = sums[z]
 
     @pl.when((step >= Z_LAG) & (step < chunks + Z_LAG))
     def _():
         p = step - Z_LAG
         for hop in range(1, DEPTH):
-            z_copy(p, hop).wait_recv()
+            z_go(p, hop, wait_recv)
         got = z_in.at[lax.rem(p, 8)]
         finish(p, mine[lax.rem(p, 4)] + got[0].astype(F32) + got[1].astype(F32) + got[2].astype(F32))
 
     @pl.when(step == chunks + Z_LAG - 1)
     def _():
         for p in range(chunks - 2, chunks):
-            core_copy(p).wait_send()
+            core_go(jnp.int32(p), wait_send)
         for p in range(chunks - X_LAG, chunks):
-            x_copy(p).wait_send()
+            x_go(jnp.int32(p), wait_send)
         for p in range(chunks - 4, chunks):
             for hop in range(1, DEPTH):
-                z_copy(p, hop).wait_send()
+                z_go(jnp.int32(p), hop, wait_send)
 
 
 def scatter_scratch(rows, lanes):
@@ -424,9 +446,9 @@
 
 def glu_kernel(
     hidden_blocks, full_blocks, normed_ref, back_ref, left_ref, left_back_ref, glu_ref,
-    out_ref, sum_own, sum_came, half_own, half_send, half_came,
-    acts, weights_in, weights_back, sum_stage, half_stage,
-    in_sem, back_sem, stage_sem, sum_send, sum_recv, half_send_sem, half_recv, *scratch,
+    out_ref, sum_own, sum_came, half_own, half_send,
+    left, left_back, left_sem, acts, weights_in, weights_back, sum_stage, half_stage,
+    in_sem, back_sem, stage_sem, sum_send, sum_recv, *scratch,
 ):
     z, x, core = device_place()
     dp, mp = lax.axis_index("dp"), lax.axis_index("mp")
@@ -466,15 +488,15 @@
             sum_own.at[:, lane_block(index)], sum_came.at[:, lane_block(index)],
             sum_send.at[index], sum_recv.at[index], device_id=(dp, 1 - mp), device_id_type=MESH_ID)
 
-    def half_copy(spot):
-        return pltpu.make_async_remote_copy(
-            half_send.at[:, lane_block(spot)], half_came.at[:, lane_block(spot)],
-            half_send_sem.at[spot], half_recv.at[spot], device_id=(dp, 1 - mp), device_id_type=MESH_ID)
+    left_loads = (
+        pltpu.make_async_copy(left_ref, left, left_sem.at[0]),
+        pltpu.make_async_copy(left_back_ref, left_back, left_sem.at[1]),
+    )
 
     @pl.when(step == 0)
     def _():
-        load_in(0).start()
-        load_back(0).start()
+        for one in (load_in(0), *left_loads, load_back(0)):
+            one.start()
         scatter_barrier(z, x, core, with_mp=True)
 
     @pl.when((step < spread) & ((step == 0) | (unit_block > first_tasks(step - 1))))
@@ -510,10 +532,6 @@
         spot = half_spot(index)
         stage(index, 1, half_own.at[:, lane_block(spot)]).wait()
 
-        @pl.when(index // half_blocks != mp)
-        def _():
-            half_copy(spot).start()
-
     @pl.when(in_second & (lax.rem(second, 2) == 0))
     def _():
         index = second // 2
@@ -549,7 +567,7 @@
 
     def compute(q, core_side, store):
         kind = lax.rem(q, 3)
-        side_rows = left_ref.shape[3]
+        side_rows = left.shape[3]
 
         def product(side_ref):
             side = side_ref[:, :, core_side].reshape(DEPTH * 2 * side_rows, rows)
@@ -557,8 +575,13 @@
             store(jnp.dot(side, right, preferred_element_type=F32).reshape(
                 DEPTH, 2, side_rows, LANES))
 
-        pl.when(kind < 2)(lambda: product(left_ref))
-        pl.when(kind == 2)(lambda: product(left_back_ref))
+        pl.when(kind < 2)(lambda: product(left))
+        pl.when(kind == 2)(lambda: product(left_back))
+
+    @pl.when(step == 0)
+    def _():
+        for one in left_loads:
+            one.wait()
 
     def finish(p, value):
         out_ref[0] = value
@@ -569,8 +592,6 @@
     def _():
         for index in range(full_blocks):
             sum_copy(index).wait()
-        for spot in range(half_blocks):
-            half_copy(spot).wait()
 
 
 def glu_call(normed, back_low, left_back, glu, collective):
@@ -585,20 +606,23 @@
     dma = pltpu.SemaphoreType.DMA
     wide = jax.ShapeDtypeStruct((rows, full), BF)
     half = jax.ShapeDtypeStruct((rows, full // 2), BF)
-    out, sum_own, sum_came, half_own, _, half_came = pl.pallas_call(
+    out, sum_own, sum_came, half_own, half_send = pl.pallas_call(
         functools.partial(glu_kernel, hidden_blocks, full_blocks),
         grid=(chunks + Z_LAG,),
-        in_specs=[fixed(normed.shape), fixed(back_low.shape), fixed(left_shape), fixed(left_shape), any_space],
-        out_specs=[out_spec] + [any_space] * 5,
-        out_shape=[out_shape, wide, wide, half, half, half],
+        in_specs=[fixed(normed.shape), fixed(back_low.shape)] + [any_space] * 3,
+        out_specs=[out_spec] + [any_space] * 4,
+        out_shape=[out_shape, wide, wide, half, half],
         scratch_shapes=[
+            pltpu.VMEM(left_shape, BF),
+            pltpu.VMEM(left_shape, BF),
+            dma((2,)),
             pltpu.VMEM((3, rows, hidden), BF),
             pltpu.VMEM((3, full, LANES), BF),
             pltpu.VMEM((3, LANES, hidden), BF),
             pltpu.VMEM((2, rows, LANES), BF),
             pltpu.VMEM((2, rows, LANES), BF),
             dma(()), dma(()), dma((2, 2)),
-            dma((full_blocks,)), dma((full_blocks,)), dma((full_blocks // 2,)), dma((full_blocks // 2,)),
+            dma((full_blocks,)), dma((full_blocks,)),
             *scatter_scratch(block, LANES),
         ],
         compiler_params=pltpu.CompilerParams(
@@ -607,13 +631,13 @@
             flops=18 * rows * full * hidden, bytes_accessed=6 * full * hidden * 2,
             transcendentals=rows * hidden),
     )(normed, back_low, normed.T.reshape(left_shape), left_back.reshape(left_shape), glu)
-    return out, sum_own, sum_came, half_own, half_came
+    return out, sum_own, sum_came, half_own, half_send
 
 
 def mixer_kernel(
-    full_blocks, left_ref, grad_ref, left_out_ref, right_out_ref, gain_ref, tokens_ref, inverse_ref,
+    full_blocks, left_hbm, grad_hbm, left_out_ref, right_out_ref, gain_ref, tokens_ref, inverse_ref,
     weights_ref, dot_ref, out_ref, gain_out, half_own, half_send, half_came, dot_came,
-    weights, token_block, gain_sum, gain_chunk, total, swap_out, swap_in, half_stage,
+    left_ref, grad_ref, big_sem, weights, token_block, gain_sum, gain_chunk, total, swap_out, swap_in, half_stage,
     load_sem, stage_sem, half_send_sem, half_recv, swap_send, swap_recv, dot_sem, *scratch,
 ):
     z, x, core = device_place()
@@ -653,21 +677,32 @@
             swap_send.at[lax.rem(index, 2)], swap_recv.at[lax.rem(index, 8)],
             device_id=partner, device_id_type=MESH_ID)
 
+    big_loads = (
+        pltpu.make_async_copy(grad_hbm, grad_ref, big_sem.at[0]),
+        pltpu.make_async_copy(left_hbm, left_ref, big_sem.at[1]),
+    )
     dot_copy = pltpu.make_async_remote_copy(
         dot_ref, dot_came, dot_sem.at[0], dot_sem.at[1], device_id=partner, device_id_type=MESH_ID)
 
     @pl.when(step == 0)
     def _():
-        for one in loads(0):
+        for one in (*big_loads, *loads(0)):
             one.start()
         gain_chunk[...] = jnp.zeros_like(gain_chunk)
         gain_sum[...] = jnp.zeros_like(gain_sum)
         scatter_barrier(z, x, core, with_mp=True)
         dot_copy.start()
 
-    @pl.when((step > 0) & (step <= full_blocks))
-    def _():
-        index = step - 1
+    @pl.when(step == 1)
+    def _():
+        for one in big_loads:
+            one.wait()
+
+    task = (step - 1) // 2
+
+    @pl.when((step >= 2) & (step <= 2 * full_blocks) & (lax.rem(step, 2) == 0))
+    def _():
+        index = task
         spot = lax.rem(index, half_blocks)
         stage(index, half_own.at[:, lane_block(spot)]).wait()
 
@@ -675,12 +710,12 @@
         def _():
             half_copy(spot).start()
 
-    @pl.when(step < full_blocks)
-    def _():
-        for one in loads(step):
+    @pl.when((step < 2 * full_blocks) & (lax.rem(step, 2) == 1))
+    def _():
+        for one in loads(task):
             one.wait()
-        slot = lax.rem(step, 2)
-        spot = lax.rem(step, half_blocks)
+        slot = lax.rem(task, 2)
+        spot = lax.rem(task, half_blocks)
 
         def part(at, gain_in):
             part_rows = pl.ds(pl.multiple_of(at * row_block, row_block), row_block)
@@ -694,21 +729,21 @@
             return gain_in + jnp.sum(grad * unit, axis=0, keepdims=True)
 
         gain_in = lax.fori_loop(0, tokens // row_block, part, jnp.zeros((1, LANES), F32))
-        gain_sum[2 * step, 0:1, :] = gain_in[:, :128]
-        gain_sum[2 * step + 1, 0:1, :] = gain_in[:, 128:]
-
-        @pl.when(step + 1 < full_blocks)
-        def _():
-            for one in loads(step + 1):
+        gain_sum[2 * task, 0:1, :] = gain_in[:, :128]
+        gain_sum[2 * task + 1, 0:1, :] = gain_in[:, 128:]
+
+        @pl.when(task + 1 < full_blocks)
+        def _():
+            for one in loads(task + 1):
                 one.start()
 
-        @pl.when(step // half_blocks == mp)
-        def _():
-            stage(step, half_own.at[:, lane_block(spot)]).start()
-
-        @pl.when(step // half_blocks != mp)
-        def _():
-            stage(step, half_send.at[:, lane_block(spot)]).start()
+        @pl.when(task // half_blocks == mp)
+        def _():
+            stage(task, half_own.at[:, lane_block(spot)]).start()
+
+        @pl.when(task // half_blocks != mp)
+        def _():
+            stage(task, half_send.at[:, lane_block(spot)]).start()
 
     def compute(q, core_side, store):
         @pl.when(q < outer)
@@ -751,7 +786,7 @@
             swap_out[lax.rem(index, 2)] = total[lax.rem(p, 4), rows, :].astype(BF)
             swap_copy(index).start()
 
-    scatter_step(step, chunks, compute, finish, scratch)
+    scatter_step(step, chunks, compute, finish, scratch, small_last=True)
 
     @pl.when((step >= Z_LAG + SWAP_LAG) & (step < chunks + Z_LAG + SWAP_LAG))
     def _():
@@ -815,7 +850,7 @@
         functools.partial(mixer_kernel, full_blocks),
         grid=(chunks + Z_LAG + SWAP_LAG,),
         in_specs=[
-            fixed((DEPTH, 2, 2, block, rows)), fixed(grad_pre.shape),
+            any_space, any_space,
             fixed((DEPTH, 2, 2, half, rows)), fixed(right_out.shape), fixed(gain_parts.shape),
             any_space, fixed(inverse.shape), any_space, any_space,
         ],
@@ -828,6 +863,9 @@
             part, part, part, jax.ShapeDtypeStruct(dots.shape, F32),
         ],
         scratch_shapes=[
+            pltpu.VMEM((DEPTH, 2, 2, block, rows), BF),
+            pltpu.VMEM(grad_pre.shape, BF),
+            dma((2,)),
             pltpu.VMEM((3, LANES, channels), BF),
             pltpu.VMEM((rows, LANES), BF),
             pltpu.VMEM((16, 8, 128), F32),
@@ -1254,8 +1292,8 @@
     down = (((0,), (0,)), ((), ()))
     dot = functools.partial(lax.dot_general, preferred_element_type=F32)
     if quick:
-        glu_sums, sum_own, sum_came, half_own, half_came = glu_call(normed_mid, back_low, left_back, glu, 0)
-        branch = half_own.astype(F32) + half_came.astype(F32)
+        glu_sums, sum_own, sum_came, half_own, half_send = glu_call(normed_mid, back_low, left_back, glu, 0)
+        branch = half_own.astype(F32) + partner_swap(half_send).astype(F32)
     else:
         pre_act = jnp.dot(normed_mid, glu[0], preferred_element_type=F32)
         pre_up = jnp.dot(normed_mid, glu[1], preferred_element_type=F32)
@@ -1271,8 +1309,6 @@
         glu_own = lax.psum_scatter(glu_grad, "dp", scatter_dimension=1, tiled=True).astype(F32)
         branch = mp_scatter(dot(hidden, glu[2], across))
     own_features = lambda v: lax.dynamic_slice_in_dim(v, place * part, part, v.ndim - 1)
-    layer_out = (own_features(middle) + branch).astype(BF)
-
     if quick:
         grad_middle_own, middle_low, state_mean, grad_gated, gain_mid = middle_back(
             sum_own, sum_came, middle, cot_full, token_rows, token_weight, gain_full[2], mixer_out
@@ -1339,6 +1375,7 @@
         grad_normed_in * own_features(gain_full[0]) - unit_in_own * in_mean
     )
     grad_tokens = grad_seq.astype(BF)
+    layer_out = (own_features(middle) + branch).astype(BF)
 
     scale = 1.0 / (batches * groups * tokens.shape[1])
     update = functools.partial(adamw_update, count=STEP_NUMBER)

time: 718 us -> 713 us (level)
    ppermute x2 -> x3, waiting for transfers between devices: 64.7 us -> 64.6 us  [partner_swap(): return lax.ppermute(value, 'mp', [(0, 1), (1, 0)])]
  transfers between devices with their start and end apart: 3 -> 4, of which waited for: 2 -> 2; matrix products, arithmetic and copies ran while one was open for 11% -> 13% of each run, Pallas kernels for 2% -> 22%
where the time goes in v5:
time: 713 us; the launch traced here: 712 us
  Pallas kernels  511 us (72%)
  waiting for transfers between devices  75.5 us (11%)
  other arithmetic  46.1 us (6%)
  local copies, waits for them, and re-layouts  38.4 us (5%)
  matrix products  23.1 us (3%)
  between operations  14.4 us (2%)
    pallas_call x1, Pallas kernels, glu_call(): pl.pallas_call(functools.partial(glu_kernel, hidden_blocks, full_blocks),...  214 us
    pallas_call x1, Pallas kernels, mixer_call(): pl.pallas_call(functools.partial(mixer_kernel, full_blocks), grid=(chunks...  128 us
    pallas_call x1, Pallas kernels, gather_call(): pl.pallas_call(gather_kernel, in_specs=[in_vmem] * 6 + [any_space], out_s...  105 us
    ppermute x3, waiting for transfers between devices, partner_swap(): return lax.ppermute(value, 'mp', [(0, 1), (1, 0)])  64.6 us
    pallas_call x1, Pallas kernels, middle_back(): pl.pallas_call(middle_back_kernel, grid=(rows // step,), in_specs=[line(f...  18.1 us
    pallas_call x1, Pallas kernels, scan_backward(): pl.pallas_call(scan_backward_kernel, grid=(batches, width // block), in_s...  17.5 us
    pallas_call x1, Pallas kernels, glu_update(): pl.pallas_call(functools.partial(glu_update_kernel, scale), grid=(blocks,...  16.8 us
    dot_general x1, matrix products, shards(): jnp.einsum('td,kde->kte', normed_in, mixer_in, preferred_element_type=F32)  16.1 us
  transfers between devices with their start and end apart: 4, of which 2 were waited for; matrix products, arithmetic and copies ran while one was open for 13% of the time, Pallas kernels for 22%

profile of v5, /device:TPU:0, one launch (start us, length us, event | category | flops | bytes accessed | tf_op | source)
XLA Modules:
  0.0 711.7 jit_solution(13593603602446183132)
XLA Ops:
  7.2 1.3 copy.53.lengths_ref
  8.5 1.3 copy.54.domains_ref
  9.8 105.3 %shard_map.272 = (bf16[3,4,2,2,2,64,1024]{6,5,4,3,2,1,0:T(8,128)(2,1)}, bf16[4,2,2,64,2048]{4,3,2,1,0:T(8,128)(2,1)}, f32[4,2,2,2,8,128]{5,4,3,2,1,0:T(8,128)}, ...) custom-call(f32[4,64,2048]{2,1,0:T(8,128)} %mixer_ref.1, f32[3,64]{1,0:T(4,128)} %gain_ref.1, s32[2,1]{1,0:T(2,128)} %copy.53.lengths_ref, ...), custom_call_target="tpu_custom_call" | custom-call | bytes 300000000 | tf_op jit(solution)/shard_map/pallas_call | solution.py:1174
  117.7 3.0 fusion.2
  122.5 16.1 %fusion.8 = f32[3,1024,896]{1,2,0:T(8,128)} fusion(bf16[896,2048,1]{1,0,2:T(8,128)(2,1)S(1)} %bitcast.64, bf16[3,2048,1024]{2,1,0:T(8,128)(2,1)} %bitcast.76), kind=kOutput, calls=%fused_computation.38 | convolution fusion | flops 11274289152 | bytes 27262976 | tf_op jit(solution)/shard_map/td,kde->kte/dot_general | solution.py:1270
  138.6 10.8 %shard_map.273 = (f32[2,448,1024]{2,1,0:T(8,128)}, bf16[2,448,1024]{2,1,0:T(8,128)(2,1)}, f32[2,448,1]{2,1,0:T(8,128)}) custom-call(f32[3,2,448,1024]{3,2,1,0:T(8,128)} %bitcast.57, f32[1,1024]{1,0:T(1,128)} %broadcast_in_dim_reshape.8.bound_ref, f32[1,1024]{1,0:T(1,128)} %broadcast_in_dim_reshape.9.gain_ref), custom_call_target="tpu_custom_call" | custom-call | flops 36700160 | bytes 16515072 | tf_op jit(solution)/shard_map/pallas_call | solution.py:151
  149.4 7.0 convolution_convert_fusion
  156.4 1.2 collective-permute-start.1
  158.8 1.5 slice_reduce_fusion.1
  161.3 4.7 fusion.14
  166.0 2.8 fusion.5
  168.7 2.5 multiply_convert_fusion.1.back_ref
  171.3 1.1 select_n.38.weight_ref
  174.2 64.6 %collective-permute-done = f32[896,1]{0,1:T(1,128)S(1)} collective-permute-done((f32[896,1]{0,1:T(1,128)S(1)}, f32[896,1]{0,1:T(1,128)S(1)}, u32[]{:S(2)}, u32[]{:S(2)}) %collective-permute-start) | collective-permute-done | bytes 3616 | tf_op jit(solution)/shard_map/ppermute | solution.py:47
  239.9 6.3 multiply_reduce_fusion
  246.3 3.0 copy-done
  249.3 2.5 fusion.13
  251.7 6.1 copy.65
  257.8 6.2 copy.56
  264.0 6.2 copy.66
  270.2 5.6 multiply_convert_fusion.normed_ref
  275.7 10.9 %all-gather.2.cloned.1.call-done.glu_ref = bf16[3,2048,2816]{2,1,0:T(8,128)(2,1)} async-done(((bf16[3,128,2816]{2,1,0:T(8,128)(2,1)}), bf16[3,2048,2816]{2,1,0:T(8,128)(2,1)}) %all-gather.2.cloned.1.call-update) | async-done | bytes 34603024 | tf_op jit(solution)/shard_map/all_gather | solution.py:1252
  286.6 214.1 %shard_map.274 = (f32[33,128,256]{2,1,0:T(8,128)}, bf16[896,2048]{1,0:T(8,128)(2,1)}, bf16[896,2048]{1,0:T(8,128)(2,1)}, bf16[896,1024]{1,0:T(8,128)(2,1)}, bf16[896,1024]{1,0:T(8,128)(2,1)}) custom-call(bf16[896,2048]{1,0:T(8,128)(2,1)} %multiply_convert_fusion.normed_ref, bf16[896,2048]{1,0:T(8,128)(2,1)} %multiply_convert_fusion.1.back_ref, ...), custom_call_target="tpu_custom_call" | custom-call | flops 93012885504 | bytes 69206016 | tf_op jit(solution)/shard_map/pallas_call | solution.py:609
  500.7 18.1 %shard_map.275 = (f32[896,1024]{1,0:T(8,128)}, bf16[896,2048]{1,0:T(8,128)(2,1)}, f32[896,1]{1,0:T(8,128)}, f32[896,1024]{1,0:T(8,128)}, f32[1,2048]{1,0:T(1,128)}) custom-call(bf16[896,2048]{1,0:T(8,128)(2,1)} %get-tuple-element.61.sum_own_ref, bf16[896,2048]{1,0:T(8,128)(2,1)} %get-tuple-element.62.sum_came_ref, f32[896,2048]{1,0:T(8,128)} %copy-done, ...), custom_call_target="tpu_custom_call" | custom-call | flops 3758096384 | bytes 36700160 | tf_op jit(solution)/shard_map/pallas_call | solution.py:924
  518.8 17.5 %shard_map.276 = (bf16[3,2,448,1024]{3,2,1,0:T(8,128)(2,1)}, bf16[2,448,1024]{2,1,0:T(8,128)(2,1)}, f32[2,1,1024]{2,1,0:T(1,128)}, f32[2,448,1]{2,1,0:T(8,128)}) custom-call(f32[3,2,448,1024]{3,2,1,0:T(8,128)} %bitcast.58, f32[2,448,1024]{2,1,0:T(8,128)} %get-tuple-element.65.states_ref, f32[2,448,1024]{2,1,0:T(8,128)} %bitcast.65, ...), custom_call_target="tpu_custom_call" | custom-call | flops 73400320 | bytes 25690112 | tf_op jit(solution)/shard_map/pallas_call | solution.py:257
  538.1 3.8 copy.60
  542.8 1.5 collective-permute-start.2
  544.3 128.1 %shard_map.277 = (f32[4,64,2048]{2,1,0:T(8,128)}, f32[8,128]{1,0:T(8,128)}, bf16[896,1024]{1,0:T(8,128)(2,1)}, bf16[896,1024]{1,0:T(8,128)(2,1)}, bf16[896,1024]{1,0:T(8,128)(2,1)}, /*index=5*/f32[7,128]{1,0:T(8,128)}) custom-call(bf16[4,2,2,128,896]{4,3,2,1,0:T(8,128)(2,1)} %bitcast.61, bf16[3,896,1024]{2,1,0:T(8,128)(2,1)} %bitcast.78, ...), custom_call_target="tpu_custom_call" | custom-call | flops 26306674688 | bytes 33554432 | tf_op jit(solution)/shard_map/pallas_call | solution.py:849
  673.1 16.8 %shard_map.278 = (f32[2,128,2816]{2,1,0:T(8,128)}, f32[2,128,2816]{2,1,0:T(8,128)}, f32[2,128,2816]{2,1,0:T(8,128)}, f32[2816,128]{1,0:T(8,128)}, f32[2816,128]{1,0:T(8,128)}, /*index=5*/f32[2816,128]{1,0:T(8,128)}) custom-call(f32[33,128,256]{2,1,0:T(8,128)} %get-tuple-element.78.act_ref.up_ref.out_ref, ...), custom_call_target="tpu_custom_call" | custom-call | flops 21626880 | bytes 30277632 | tf_op jit(solution)/shard_map/pallas_call | solution.py:962
  690.7 4.0 add_convert_fusion
  695.3 5.8 multiply_subtract_fusion
  701.1 3.7 add_convert_fusion.1
  (99 shorter events, 14.1 us)
Async XLA Ops:
  7.2 279.4 %all-gather.2.cloned.1.call-start = ((), (), s32[]{:S(2)}) async-start(), calls=%async_computation | async-start | bytes 36765696 | tf_op jit(solution)/shard_map/all_gather | solution.py:1252
  9.8 107.1 %copy-start.18 = (f32[2048]{0:T(1024)S(1)}, f32[2048]{0:T(1024)}, u32[]{:S(2)}) copy-start(f32[2048]{0:T(1024)} %param.21) | copy-start | bytes 24580
  116.9 57.2 %copy-start.13 = (f32[2048]{0:T(1024)}, f32[2048]{0:T(1024)S(1)}, u32[]{:S(2)}) copy-start(f32[2048]{0:T(1024)S(1)} %mul.230) | copy-start | bytes 24580
  117.7 3.8 copy-start.1
  138.6 10.8 %copy-start.6 = (bf16[4,2,2,64,2048]{4,3,2,1,0:T(8,128)(2,1)S(1)}, bf16[4,2,2,64,2048]{4,3,2,1,0:T(8,128)(2,1)}, u32[]{:S(2)}) copy-start(bf16[4,2,2,64,2048]{4,3,2,1,0:T(8,128)(2,1)} %get-tuple-element.54) | copy-start | bytes 12582916
  149.4 8.2 %copy-start.12 = (f32[2,448,1]{2,1,0:T(8,128)S(1)}, f32[2,448,1]{2,1,0:T(8,128)}, u32[]{:S(2)}) copy-start(f32[2,448,1]{2,1,0:T(8,128)} %get-tuple-element.52) | copy-start | bytes 10756
  149.4 10.9 %copy-start.24 = (s32[2,1,1]{0,2,1:T(1,128)S(1)}, s32[2,1,1]{0,2,1:T(1,128)}, u32[]{:S(2)}) copy-start(s32[2,1,1]{0,2,1:T(1,128)} %param.20) | copy-start | bytes 28
  149.4 11.7 %copy-start.23 = (s32[2,1]{0,1:T(1,128)S(1)}, s32[2,1]{0,1:T(1,128)}, u32[]{:S(2)}) copy-start(s32[2,1]{0,1:T(1,128)} %param.19) | copy-start | bytes 28
  156.4 83.5 %collective-permute-start.1 = (bf16[896,2048]{1,0:T(8,128)(2,1)}, bf16[896,2048]{1,0:T(8,128)(2,1)}, u32[]{:S(2)}, u32[]{:S(2)}) collective-permute-start(bf16[896,2048]{1,0:T(8,128)(2,1)} %convolution_convert_fusion), channel_id=1, source_target_pairs={{0,1},{1,0},{2,3},{3,2},{4,5},{5,4},{6,7},{7,6},{8,9},{9,8},{10,11... | collective-permute-start | bytes 11010056 | tf_op jit(solution)/shard_map/ppermute | solution.py:47
  157.9 80.9 %collective-permute-start = (f32[896,1]{0,1:T(1,128)S(1)}, f32[896,1]{0,1:T(1,128)S(1)}, u32[]{:S(2)}, u32[]{:S(2)}) collective-permute-start(f32[896,1]{0,1:T(1,128)S(1)} %reshape.307), channel_id=1, source_target_pairs={{0,1},{1,0},{2,3},{3,2},{4,5},{5,4},{6,7},{7,6},{8,9},{9,8},{10,11... | collective-permute-start | bytes 10760 | tf_op jit(solution)/shard_map/ppermute | solution.py:47
  158.8 7.2 %copy-start.14 = (f32[896]{0:T(1024)}, f32[896]{0:T(1024)S(1)}, u32[]{:S(2)}) copy-start(f32[896]{0:T(1024)S(1)} %rsqrt.20) | copy-start | bytes 10756
  161.3 4.7 copy-start.2
  166.0 2.8 copy-start.4
  246.2 3.1 copy-start
  518.8 18.6 %copy-start.19 = (f32[1,2048]{1,0:T(1,128)S(1)}, f32[1,2048]{1,0:T(1,128)}, u32[]{:S(2)}) copy-start(f32[1,2048]{1,0:T(1,128)} %get-tuple-element.72) | copy-start | bytes 24580
  536.3 5.5 copy-start.11
  542.8 158.3 %collective-permute-start.2 = (bf16[896,1024]{1,0:T(8,128)(2,1)}, bf16[896,1024]{1,0:T(8,128)(2,1)}, u32[]{:S(2)}, u32[]{:S(2)}) collective-permute-start(bf16[896,1024]{1,0:T(8,128)(2,1)} %get-tuple-element.60), channel_id=1, source_target_pairs={{0,1},{1,0},{2,3},{3,2},{4,5},{5,4},{6,7},{7,6},{8,9},{9,8},{10,11... | collective-permute-start | bytes 5505032 | tf_op jit(solution)/shard_map/ppermute | solution.py:47
  673.0 16.8 %copy-start.16 = (f32[7,128]{1,0:T(8,128)S(1)}, f32[7,128]{1,0:T(8,128)}, u32[]{:S(2)}) copy-start(f32[7,128]{1,0:T(8,128)} %reshape.321.dot_ref) | copy-start | bytes 10756
  673.0 16.8 %copy-start.20 = (f32[7,128]{1,0:T(8,128)S(1)}, f32[7,128]{1,0:T(8,128)}, u32[]{:S(2)}) copy-start(f32[7,128]{1,0:T(8,128)} %get-tuple-element.76) | copy-start | bytes 10756
  673.0 16.9 %copy-start.17 = (f32[3,64]{1,0:T(4,128)S(1)}, f32[3,64]{1,0:T(4,128)}, u32[]{:S(2)}) copy-start(f32[3,64]{1,0:T(4,128)} %gain_ref.1) | copy-start | bytes 2308
  673.0 16.9 %copy-start.21 = (f32[3,64]{1,0:T(4,128)S(1)}, f32[3,64]{1,0:T(4,128)}, u32[]{:S(2)}) copy-start(f32[3,64]{1,0:T(4,128)} %param.32) | copy-start | bytes 2308
  673.0 16.9 %copy-start.22 = (f32[3,64]{1,0:T(4,128)S(1)}, f32[3,64]{1,0:T(4,128)}, u32[]{:S(2)}) copy-start(f32[3,64]{1,0:T(4,128)} %param.33) | copy-start | bytes 2308
  673.0 17.6 %copy-start.3 = (bf16[2,1,448,2048]{3,2,1,0:T(8,128)(2,1)S(1)}, bf16[2,1,448,2048]{3,2,1,0:T(8,128)(2,1)}, u32[]{:S(2)}) copy-start(bf16[2,1,448,2048]{3,2,1,0:T(8,128)(2,1)} %param.17) | copy-start | bytes 11010052
  673.1 17.5 %copy-start.7 = (f32[896,1024]{1,0:T(8,128)S(1)}, f32[896,1024]{1,0:T(8,128)}, u32[]{:S(2)}) copy-start(f32[896,1024]{1,0:T(8,128)} %get-tuple-element.63) | copy-start | bytes 11010052
  673.1 17.5 %dynamic-slice-start = ((f32[2048]{0:T(1024)}, s32[]{:T(128)}), f32[1024]{0:T(1024)S(1)}, s32[]{:S(2)}) async-start(f32[2048]{0:T(1024)} %copy-done.13, s32[]{:T(128)} %select_n.35), calls=%async_computation.3 | async-start | bytes 8704 | tf_op jit(solution)/shard_map/dynamic_slice | solution.py:1311
  673.1 17.5 %copy-start.15 = (f32[896]{0:T(1024)S(1)}, f32[896]{0:T(1024)}, u32[]{:S(2)}) copy-start(f32[896]{0:T(1024)} %copy-done.14) | copy-start | bytes 10756
  690.6 4.0 copy-start.5
  690.6 4.0 copy-start.8
  690.6 4.6 copy-start.9
  690.7 10.4 %slice-start = ((s8[7340032]{0:T(1024)(128)(4,1)}), s8[4194304]{0:T(1024)(128)(4,1)S(1)}, s32[]{:S(2)}) async-start(s8[7340032]{0:T(1024)(128)(4,1)} %bitcast.52), calls=%async_computation.1 | async-start | bytes 8388608
  695.2 5.8 slice-start.1
  695.2 5.8 copy-start.10
Sparse Core Ops, SparseCore 0:
  115.3 171.2 all-gather.1

commit v6 on v5

--- a/solution.py
+++ b/solution.py
@@ -285,6 +285,7 @@
 X_LAG = 4
 Z_LAG = X_LAG + 2
 SWAP_LAG = 2
+TAIL = 2
 
 
 def device_place():
@@ -446,14 +447,15 @@
 
 def glu_kernel(
     hidden_blocks, full_blocks, normed_ref, back_ref, left_ref, left_back_ref, glu_ref,
-    out_ref, sum_own, sum_came, half_own, half_send,
-    left, left_back, left_sem, acts, weights_in, weights_back, sum_stage, half_stage,
+    out_ref, sum_own, sum_came, half_own, half_send, tail_ref,
+    tail_stage, tail_sem, left, left_back, left_sem, acts, weights_in, weights_back, sum_stage, half_stage,
     in_sem, back_sem, stage_sem, sum_send, sum_recv, *scratch,
 ):
     z, x, core = device_place()
     dp, mp = lax.axis_index("dp"), lax.axis_index("mp")
     step = pl.program_id(0)
-    chunks = 3 * hidden_blocks
+    scattered = hidden_blocks - TAIL
+    chunks = 3 * scattered
     rows = normed_ref.shape[0]
     row_block = rows // 2
     half_blocks = full_blocks // 2
@@ -464,8 +466,14 @@
     def first_tasks(at):
         return at * hidden_blocks // spread
 
+    def second_task(at):
+        return 2 * at // 3
+
+    def has_second(at):
+        return (at == 0) | (
+            (at > 0) & (second_task(at) > second_task(at - 1)) & (second_task(at) < full_blocks))
+
     unit_block = first_tasks(step)
-    in_second = (second >= 0) & (second < 2 * full_blocks)
 
     def lane_block(index):
         return pl.ds(pl.multiple_of(index * LANES, LANES), LANES)
@@ -524,17 +532,17 @@
         def _():
             load_in(unit_block + 1).start()
 
-    @pl.when(in_second & (lax.rem(second, 2) == 1))
-    def _():
-        index = second // 2
+    @pl.when(has_second(second - 1))
+    def _():
+        index = second_task(second - 1)
         stage(index, 0, sum_own.at[:, lane_block(index)]).wait()
         sum_copy(index).start()
         spot = half_spot(index)
         stage(index, 1, half_own.at[:, lane_block(spot)]).wait()
 
-    @pl.when(in_second & (lax.rem(second, 2) == 0))
-    def _():
-        index = second // 2
+    @pl.when(has_second(second))
+    def _():
+        index = second_task(second)
         load_back(index).wait()
         slot = lax.rem(index, 2)
 
@@ -588,8 +596,30 @@
 
     scatter_step(step, chunks, compute, finish, scratch)
 
+    def tail_copy(index):
+        spot = tail_ref.at[lax.rem(index, 3), :, :, :, :, lane_block(index // 3)]
+        return pltpu.make_async_copy(
+            tail_stage.at[lax.rem(index, 2)], spot, tail_sem.at[lax.rem(index, 2)])
+
+    @pl.when((step >= chunks) & (step < chunks + 3 * TAIL))
+    def _():
+        index = step - chunks
+
+        @pl.when(index >= 2)
+        def _():
+            tail_copy(index - 2).wait()
+
+        for side in (0, 1):
+            def to_stage(value):
+                tail_stage[lax.rem(index, 2), :, :, side] = value.astype(BF)
+
+            compute(step, side, to_stage)
+        tail_copy(index).start()
+
     @pl.when(step == chunks + Z_LAG - 1)
     def _():
+        for index in range(3 * TAIL - 2, 3 * TAIL):
+            tail_copy(jnp.int32(index)).wait()
         for index in range(full_blocks):
             sum_copy(index).wait()
 
@@ -599,20 +629,25 @@
     hidden = glu.shape[2]
     hidden_blocks, full_blocks = hidden // LANES, full // LANES
     block = full // 16
-    chunks = 3 * hidden_blocks
+    chunks = 3 * (hidden_blocks - TAIL)
     left_shape = (DEPTH, 2, 2, block, rows)
     any_space = pl.BlockSpec(memory_space=pl.ANY)
     out_spec, out_shape = scatter_out(chunks, block, LANES)
     dma = pltpu.SemaphoreType.DMA
     wide = jax.ShapeDtypeStruct((rows, full), BF)
     half = jax.ShapeDtypeStruct((rows, full // 2), BF)
-    out, sum_own, sum_came, half_own, half_send = pl.pallas_call(
+    out, sum_own, sum_came, half_own, half_send, tail = pl.pallas_call(
         functools.partial(glu_kernel, hidden_blocks, full_blocks),
         grid=(chunks + Z_LAG,),
         in_specs=[fixed(normed.shape), fixed(back_low.shape)] + [any_space] * 3,
-        out_specs=[out_spec] + [any_space] * 4,
-        out_shape=[out_shape, wide, wide, half, half],
+        out_specs=[out_spec] + [any_space] * 5,
+        out_shape=[
+            out_shape, wide, wide, half, half,
+            jax.ShapeDtypeStruct((3, DEPTH, 2, 2, block, TAIL * LANES), BF),
+        ],
         scratch_shapes=[
+            pltpu.VMEM((2, DEPTH, 2, 2, block, LANES), BF),
+            dma((2,)),
             pltpu.VMEM(left_shape, BF),
             pltpu.VMEM(left_shape, BF),
             dma((2,)),
@@ -631,7 +666,7 @@
             flops=18 * rows * full * hidden, bytes_accessed=6 * full * hidden * 2,
             transcendentals=rows * hidden),
     )(normed, back_low, normed.T.reshape(left_shape), left_back.reshape(left_shape), glu)
-    return out, sum_own, sum_came, half_own, half_send
+    return out, tail.reshape(3, full, TAIL * LANES), sum_own, sum_came, half_own, half_send
 
 
 def mixer_kernel(
@@ -940,37 +975,38 @@
 
 
 def glu_update_kernel(scale, act_ref, up_ref, out_ref, *refs):
-    in_refs, down_refs, in_new, down_new = refs[:3], refs[3:6], refs[6:9], refs[9:12]
+    in_refs, down_refs, in_new, down_new = refs[:3], refs[3:6], refs[-6:-3], refs[-3:]
     count = STEP_NUMBER
     for at, grad_ref in ((0, act_ref), (1, up_ref)):
         new = adamw_update(
-            *(ref[at] for ref in in_refs), grad_ref[0] * scale, count, MATRIX_RATE, DECAY_RATE)
+            *(ref[at] for ref in in_refs), grad_ref[0].astype(F32) * scale, count, MATRIX_RATE, DECAY_RATE)
         for ref, value in zip(in_new, new):
             ref[at] = value
     new = adamw_update(
-        *(ref[...] for ref in down_refs), out_ref[0].T * scale, count, MATRIX_RATE, DECAY_RATE)
+        *(ref[...] for ref in down_refs), out_ref[0].astype(F32).T * scale, count, MATRIX_RATE, DECAY_RATE)
     for ref, value in zip(down_new, new):
         ref[...] = value
 
 
-def glu_update(sums, ins, downs, scale):
-    _, rows, lanes = sums.shape
-    blocks = ins[0].shape[2] // lanes
-    sum_spec = lambda kind: pl.BlockSpec((1, rows, lanes), lambda q: (3 * q + kind, 0, 0))
-    in_spec = pl.BlockSpec((2, rows, lanes), lambda q: (0, 0, q))
-    down_spec = pl.BlockSpec((lanes, rows), lambda q: (q, 0))
+def glu_update(sums, sum_place, first, blocks, ins, downs, scale, earlier=()):
+    rows, lanes = ins[0].shape[1], LANES
+    sum_spec = lambda kind: pl.BlockSpec((1, rows, lanes), lambda q: sum_place(kind, q))
+    in_spec = pl.BlockSpec((2, rows, lanes), lambda q: (0, 0, q + first))
+    down_spec = pl.BlockSpec((lanes, rows), lambda q: (q + first, 0))
     new = pl.pallas_call(
         functools.partial(glu_update_kernel, scale),
         grid=(blocks,),
-        in_specs=[sum_spec(0), sum_spec(1), sum_spec(2)] + [in_spec] * 3 + [down_spec] * 3,
+        in_specs=[sum_spec(0), sum_spec(1), sum_spec(2)] + [in_spec] * 3 + [down_spec] * 3
+        + [pl.BlockSpec(memory_space=pl.ANY)] * len(earlier),
         out_specs=[in_spec] * 3 + [down_spec] * 3,
         out_shape=[jax.ShapeDtypeStruct(ins[0].shape, F32)] * 3 + [jax.ShapeDtypeStruct(downs[0].shape, F32)] * 3,
+        input_output_aliases={9 + at: at for at in range(len(earlier))},
         compiler_params=pltpu.CompilerParams(vmem_limit_bytes=VMEM_LIMIT),
         cost_estimate=pl.CostEstimate(
             flops=60 * rows * lanes * blocks, bytes_accessed=84 * rows * lanes * blocks,
             transcendentals=6 * rows * lanes * blocks),
-    )(sums, sums, sums, *ins, *downs)
-    return tuple(new[:3]), tuple(new[3:])
+    )(sums, sums, sums, *ins, *downs, *earlier)
+    return tuple(new)
 
 
 ITEMS = 4
@@ -1292,8 +1328,9 @@
     down = (((0,), (0,)), ((), ()))
     dot = functools.partial(lax.dot_general, preferred_element_type=F32)
     if quick:
-        glu_sums, sum_own, sum_came, half_own, half_send = glu_call(normed_mid, back_low, left_back, glu, 0)
-        branch = half_own.astype(F32) + partner_swap(half_send).astype(F32)
+        glu_sums, glu_tail, sum_own, sum_came, half_own, half_send = glu_call(normed_mid, back_low, left_back, glu, 0)
+        half_came = partner_swap(half_send)
+        glu_tail = lax.psum_scatter(glu_tail, "dp", scatter_dimension=1, tiled=True)
     else:
         pre_act = jnp.dot(normed_mid, glu[0], preferred_element_type=F32)
         pre_up = jnp.dot(normed_mid, glu[1], preferred_element_type=F32)
@@ -1308,6 +1345,7 @@
         ).astype(BF)
         glu_own = lax.psum_scatter(glu_grad, "dp", scatter_dimension=1, tiled=True).astype(F32)
         branch = mp_scatter(dot(hidden, glu[2], across))
+    scale = 1.0 / (batches * groups * tokens.shape[1])
     own_features = lambda v: lax.dynamic_slice_in_dim(v, place * part, part, v.ndim - 1)
     if quick:
         grad_middle_own, middle_low, state_mean, grad_gated, gain_mid = middle_back(
@@ -1331,6 +1369,15 @@
     grad_pre, gated_out, gain_state, pre_dot = scan_backward(
         pre, states, by_batch(grad_gated), by_batch(inverse_state), by_batch(state_mean), bound, state_gain
     )
+    if quick:
+        scattered = glu_in_master.shape[2] // LANES - TAIL
+        glu_ins = (glu_in_master, glu_in_first, glu_in_second)
+        glu_downs = (glu_out_master, glu_out_first, glu_out_second)
+        glu_new = glu_update(
+            glu_sums, lambda kind, q: (3 * q + kind, 0, 0), 0, scattered, glu_ins, glu_downs, scale
+        )
+        half_came, grad_pre, glu_new = lax.optimization_barrier((half_came, grad_pre, glu_new))
+        branch = half_own.astype(F32) + half_came.astype(F32)
     grad_pre = grad_pre.reshape(3, rows, channels)
     gated_out = gated_out.reshape(rows, channels)
     gain_state = jnp.sum(gain_state, axis=0).reshape(groups, 1, own_rows)
@@ -1377,7 +1424,6 @@
     grad_tokens = grad_seq.astype(BF)
     layer_out = (own_features(middle) + branch).astype(BF)
 
-    scale = 1.0 / (batches * groups * tokens.shape[1])
     update = functools.partial(adamw_update, count=STEP_NUMBER)
     mixer_new = update(
         mixer_master, mixer_first, mixer_second, mixer_own * scale, rate=MATRIX_RATE, decay=DECAY_RATE
@@ -1385,19 +1431,25 @@
     gain_new = update(
         gain_master, gain_first, gain_second, gain_own * scale, rate=GAIN_RATE, decay=0.0
     )
-    glu_ins = (glu_in_master, glu_in_first, glu_in_second)
-    glu_downs = (glu_out_master, glu_out_first, glu_out_second)
     if quick:
-        glu_in_new, glu_out_new = glu_update(glu_sums, glu_ins, glu_downs, scale)
+        glu_new = glu_update(
+            glu_tail, lambda kind, q: (kind, 0, q), scattered, TAIL, glu_ins, glu_downs, scale, glu_new
+        )
     else:
-        glu_in_new = update(*glu_ins, glu_own[:2] * scale, rate=MATRIX_RATE, decay=DECAY_RATE)
-        glu_out_new = update(*glu_downs, glu_own[2].T * scale, rate=MATRIX_RATE, decay=DECAY_RATE)
+        glu_in_new = update(
+            glu_in_master, glu_in_first, glu_in_second, glu_own[:2] * scale,
+            rate=MATRIX_RATE, decay=DECAY_RATE,
+        )
+        glu_out_new = update(
+            glu_out_master, glu_out_first, glu_out_second, glu_own[2].T * scale,
+            rate=MATRIX_RATE, decay=DECAY_RATE,
+        )
+        glu_new = (*glu_in_new, *glu_out_new)
     return (
         layer_out.reshape(batches, 1, length, part),
         grad_tokens.reshape(batches, 1, length, part),
         *mixer_new,
-        *glu_in_new,
-        *glu_out_new,
+        *glu_new,
         *gain_new,
     )
 

time: 713 us -> 685 us (0.961)
  Pallas kernels: 511 us -> 468 us
  waiting for transfers between devices: 75.5 us -> 85.1 us
    pallas_call x1, Pallas kernels: 214 us -> 183 us  [glu_call(): pl.pallas_call(functools.partial(glu_kernel, hidden_blocks, full_blocks),...]
    pallas_call x1, Pallas kernels: 128 us -> 115 us  [mixer_call(): pl.pallas_call(functools.partial(mixer_kernel, full_blocks), grid=(chunks...]
    pallas_call x1 -> x2, Pallas kernels: 16.8 us -> 16.9 us  [glu_update(): pl.pallas_call(functools.partial(glu_update_kernel, scale), grid=(blocks,...]
  transfers between devices with their start and end apart: 4 -> 5, of which waited for: 2 -> 2; matrix products, arithmetic and copies ran while one was open for 13% -> 15% of each run, Pallas kernels for 22% -> 26%
where the time goes in v6:
time: 685 us; the launch traced here: 680 us
  Pallas kernels  468 us (68%)
  waiting for transfers between devices  85.1 us (12%)
  other arithmetic  46.1 us (7%)
  local copies, waits for them, and re-layouts  39.9 us (6%)
  matrix products  23.1 us (3%)
  between operations  14.8 us (2%)
    pallas_call x1, Pallas kernels, glu_call(): pl.pallas_call(functools.partial(glu_kernel, hidden_blocks, full_blocks),...  183 us
    pallas_call x1, Pallas kernels, mixer_call(): pl.pallas_call(functools.partial(mixer_kernel, full_blocks), grid=(chunks...  115 us
    pallas_call x1, Pallas kernels, gather_call(): pl.pallas_call(gather_kernel, in_specs=[in_vmem] * 6 + [any_space], out_s...  105 us
    ppermute x3, waiting for transfers between devices, partner_swap(): return lax.ppermute(value, 'mp', [(0, 1), (1, 0)])  67.4 us
    pallas_call x1, Pallas kernels, middle_back(): pl.pallas_call(middle_back_kernel, grid=(rows // step,), in_specs=[line(f...  19.1 us
    all_gather x1, waiting for transfers between devices, shards(): glu = lax.all_gather(glu_low, 'dp', axis=1, tiled=True)  17.7 us
    pallas_call x1, Pallas kernels, scan_backward(): pl.pallas_call(scan_backward_kernel, grid=(batches, width // block), in_s...  17.6 us
    pallas_call x2, Pallas kernels, glu_update(): pl.pallas_call(functools.partial(glu_update_kernel, scale), grid=(blocks,...  16.9 us
  transfers between devices with their start and end apart: 5, of which 2 were waited for; matrix products, arithmetic and copies ran while one was open for 15% of the time, Pallas kernels for 26%

profile of v6, /device:TPU:0, one launch (start us, length us, event | category | flops | bytes accessed | tf_op | source)
XLA Modules:
  0.0 680.3 jit_solution(9454120781959495130)
XLA Ops:
  7.2 1.3 copy.59.lengths_ref
  8.5 1.3 copy.60.domains_ref
  9.8 105.3 %shard_map.272 = (bf16[3,4,2,2,2,64,1024]{6,5,4,3,2,1,0:T(8,128)(2,1)}, bf16[4,2,2,64,2048]{4,3,2,1,0:T(8,128)(2,1)}, f32[4,2,2,2,8,128]{5,4,3,2,1,0:T(8,128)}, ...) custom-call(f32[4,64,2048]{2,1,0:T(8,128)} %mixer_ref.1, f32[3,64]{1,0:T(4,128)} %gain_ref.1, s32[2,1]{1,0:T(2,128)} %copy.59.lengths_ref, ...), custom_call_target="tpu_custom_call" | custom-call | bytes 300000000 | tf_op jit(solution)/shard_map/pallas_call | solution.py:1210
  117.7 3.0 fusion.2
  122.5 16.1 %fusion.8 = f32[3,1024,896]{1,2,0:T(8,128)} fusion(bf16[896,2048,1]{1,0,2:T(8,128)(2,1)S(1)} %bitcast.66, bf16[3,2048,1024]{2,1,0:T(8,128)(2,1)} %bitcast.78), kind=kOutput, calls=%fused_computation.38 | convolution fusion | flops 11274289152 | bytes 27262976 | tf_op jit(solution)/shard_map/td,kde->kte/dot_general | solution.py:1306
  138.6 10.8 %shard_map.273 = (f32[2,448,1024]{2,1,0:T(8,128)}, bf16[2,448,1024]{2,1,0:T(8,128)(2,1)}, f32[2,448,1]{2,1,0:T(8,128)}) custom-call(f32[3,2,448,1024]{3,2,1,0:T(8,128)} %bitcast.58, f32[1,1024]{1,0:T(1,128)} %broadcast_in_dim_reshape.8.bound_ref, f32[1,1024]{1,0:T(1,128)} %broadcast_in_dim_reshape.9.gain_ref), custom_call_target="tpu_custom_call" | custom-call | flops 36700160 | bytes 16515072 | tf_op jit(solution)/shard_map/pallas_call | solution.py:151
  149.5 7.0 %convolution_convert_fusion = bf16[896,2048]{1,0:T(8,128)(2,1)} fusion(bf16[896,1024]{1,0:T(8,128)(2,1)} %bitcast.81, bf16[1024,2048]{1,0:T(8,128)(2,1)S(1)} %bitcast.62), kind=kOutput, calls=%fused_computation.15 | convolution fusion | flops 3759931392 | bytes 9699328 | tf_op jit(solution)/shard_map/dot_general | solution.py:1311
  156.4 1.2 collective-permute-start.1
  158.8 1.5 slice_reduce_fusion.1
  161.3 4.7 fusion.14
  166.0 2.8 fusion.5
  168.8 2.6 multiply_convert_fusion.1.back_ref
  171.5 67.4 %collective-permute-done = f32[896,1]{0,1:T(1,128)S(1)} collective-permute-done((f32[896,1]{0,1:T(1,128)S(1)}, f32[896,1]{0,1:T(1,128)S(1)}, u32[]{:S(2)}, u32[]{:S(2)}) %collective-permute-start) | collective-permute-done | bytes 3616 | tf_op jit(solution)/shard_map/ppermute | solution.py:47
  238.9 6.4 multiply_reduce_fusion
  245.3 3.0 copy-done
  248.4 2.6 fusion.13
  250.9 6.1 copy.71
  257.0 6.1 copy.62
  263.1 5.8 multiply_convert_fusion.normed_ref
  268.8 17.7 %all-gather.2.cloned.1.call-done.glu_ref = bf16[3,2048,2816]{2,1,0:T(8,128)(2,1)} async-done(((bf16[3,128,2816]{2,1,0:T(8,128)(2,1)}), bf16[3,2048,2816]{2,1,0:T(8,128)(2,1)}) %all-gather.2.cloned.1.call-update) | async-done | bytes 34603024 | tf_op jit(solution)/shard_map/all_gather | solution.py:1288
  286.6 183.5 %shard_map.274 = (f32[27,128,256]{2,1,0:T(8,128)}, bf16[896,2048]{1,0:T(8,128)(2,1)}, bf16[896,2048]{1,0:T(8,128)(2,1)}, bf16[896,1024]{1,0:T(8,128)(2,1)}, bf16...) custom-call(bf16[896,2048]{1,0:T(8,128)(2,1)} %multiply_convert_fusion.normed_ref, ...), custom_call_target="tpu_custom_call" | custom-call | flops 93012885504 | bytes 69206016 | tf_op jit(solution)/shard_map/pallas_call | solution.py:639
  470.1 1.5 collective-permute-start.2
  475.5 6.3 copy.72
  481.8 19.1 %shard_map.275 = (f32[896,1024]{1,0:T(8,128)}, bf16[896,2048]{1,0:T(8,128)(2,1)}, f32[896,1]{1,0:T(8,128)}, f32[896,1024]{1,0:T(8,128)}, f32[1,2048]{1,0:T(1,128)}) custom-call(bf16[896,2048]{1,0:T(8,128)(2,1)} %get-tuple-element.77.sum_own_ref, bf16[896,2048]{1,0:T(8,128)(2,1)} %get-tuple-element.78.sum_came_ref, f32[896,2048]{1,0:T(8,128)} %copy-done, ...), custom_call_target="tpu_custom_call" | custom-call | flops 3758096384 | bytes 36700160 | tf_op jit(solution)/shard_map/pallas_call | solution.py:959
  500.9 17.6 %shard_map.276 = (bf16[3,2,448,1024]{3,2,1,0:T(8,128)(2,1)}, bf16[2,448,1024]{2,1,0:T(8,128)(2,1)}, f32[2,1,1024]{2,1,0:T(1,128)}, f32[2,448,1]{2,1,0:T(8,128)}) custom-call(f32[3,2,448,1024]{3,2,1,0:T(8,128)} %bitcast.59, f32[2,448,1024]{2,1,0:T(8,128)} %get-tuple-element.76.states_ref, f32[2,448,1024]{2,1,0:T(8,128)} %bitcast.67, ...), custom_call_target="tpu_custom_call" | custom-call | flops 73400320 | bytes 25690112 | tf_op jit(solution)/shard_map/pallas_call | solution.py:257
  520.2 4.1 copy.66
  525.2 13.7 %shard_map.277 = (f32[2,128,2816]{2,1,0:T(8,128)}, f32[2,128,2816]{2,1,0:T(8,128)}, f32[2,128,2816]{2,1,0:T(8,128)}, f32[2816,128]{1,0:T(8,128)}, f32[2816,128]{1,0:T(8,128)}, /*index=5*/f32[2816,128]{1,0:T(8,128)}) custom-call(f32[27,128,256]{2,1,0:T(8,128)} %get-tuple-element.82.act_ref.up_ref.out_ref, ...), custom_call_target="tpu_custom_call" | custom-call | flops 17694720 | bytes 24772608 | tf_op jit(solution)/shard_map/pallas_call | solution.py:996
  539.0 114.6 %shard_map.278 = (f32[4,64,2048]{2,1,0:T(8,128)}, f32[8,128]{1,0:T(8,128)}, bf16[896,1024]{1,0:T(8,128)(2,1)}, bf16[896,1024]{1,0:T(8,128)(2,1)}, bf16[896,1024]{1,0:T(8,128)(2,1)}, /*index=5*/f32[7,128]{1,0:T(8,128)}) custom-call(bf16[4,2,2,128,896]{4,3,2,1,0:T(8,128)(2,1)} %bitcast.63, bf16[3,896,1024]{2,1,0:T(8,128)(2,1)} %bitcast.80, ...), custom_call_target="tpu_custom_call" | custom-call | flops 26306674688 | bytes 33554432 | tf_op jit(solution)/shard_map/pallas_call | solution.py:884
  655.7 4.5 add_convert_fusion.1
  661.2 3.8 add_convert_fusion
  665.8 4.0 multiply_subtract_fusion
  669.8 3.2 shard_map.279
  (103 shorter events, 17.2 us)
Async XLA Ops:
  7.2 279.4 %all-gather.2.cloned.1.call-start = ((), (), s32[]{:S(2)}) async-start(), calls=%async_computation.1 | async-start | bytes 36765696 | tf_op jit(solution)/shard_map/all_gather | solution.py:1288
  9.8 107.1 %copy-start.19 = (f32[2048]{0:T(1024)S(1)}, f32[2048]{0:T(1024)}, u32[]{:S(2)}) copy-start(f32[2048]{0:T(1024)} %param.21) | copy-start | bytes 24580
  115.1 554.7 %reduce-scatter.2.cloned.1.call-start = ((), (), s32[]{:S(2)}) async-start(), calls=%async_computation.2 | async-start | bytes 6684672 | tf_op jit(solution)/shard_map/reduce_scatter | solution.py:1333
  116.9 357.5 %copy-start.14 = (f32[2048]{0:T(1024)}, f32[2048]{0:T(1024)S(1)}, u32[]{:S(2)}) copy-start(f32[2048]{0:T(1024)S(1)} %mul.230) | copy-start | bytes 24580
  117.7 3.9 copy-start.1
  138.6 10.8 %copy-start.6 = (bf16[4,2,2,64,2048]{4,3,2,1,0:T(8,128)(2,1)S(1)}, bf16[4,2,2,64,2048]{4,3,2,1,0:T(8,128)(2,1)}, u32[]{:S(2)}) copy-start(bf16[4,2,2,64,2048]{4,3,2,1,0:T(8,128)(2,1)} %get-tuple-element.69) | copy-start | bytes 12582916
  149.4 8.2 %copy-start.13 = (f32[2,448,1]{2,1,0:T(8,128)S(1)}, f32[2,448,1]{2,1,0:T(8,128)}, u32[]{:S(2)}) copy-start(f32[2,448,1]{2,1,0:T(8,128)} %get-tuple-element.67) | copy-start | bytes 10756
  149.4 10.9 %copy-start.24 = (s32[2,1,1]{0,2,1:T(1,128)S(1)}, s32[2,1,1]{0,2,1:T(1,128)}, u32[]{:S(2)}) copy-start(s32[2,1,1]{0,2,1:T(1,128)} %param.20) | copy-start | bytes 28
  149.5 11.7 %copy-start.23 = (s32[2,1]{0,1:T(1,128)S(1)}, s32[2,1]{0,1:T(1,128)}, u32[]{:S(2)}) copy-start(s32[2,1]{0,1:T(1,128)} %param.19) | copy-start | bytes 28
  156.4 82.5 %collective-permute-start.1 = (bf16[896,2048]{1,0:T(8,128)(2,1)}, bf16[896,2048]{1,0:T(8,128)(2,1)}, u32[]{:S(2)}, u32[]{:S(2)}) collective-permute-start(bf16[896,2048]{1,0:T(8,128)(2,1)} %convolution_convert_fusion), channel_id=1, source_target_pairs={{0,1},{1,0},{2,3},{3,2},{4,5},{5,4},{6,7},{7,6},{8,9},{9,8},{10,11... | collective-permute-start | bytes 11010056 | tf_op jit(solution)/shard_map/ppermute | solution.py:47
  157.9 80.9 %collective-permute-start = (f32[896,1]{0,1:T(1,128)S(1)}, f32[896,1]{0,1:T(1,128)S(1)}, u32[]{:S(2)}, u32[]{:S(2)}) collective-permute-start(f32[896,1]{0,1:T(1,128)S(1)} %reshape.310), channel_id=1, source_target_pairs={{0,1},{1,0},{2,3},{3,2},{4,5},{5,4},{6,7},{7,6},{8,9},{9,8},{10,11... | collective-permute-start | bytes 10760 | tf_op jit(solution)/shard_map/ppermute | solution.py:47
  158.8 7.2 %copy-start.15 = (f32[896]{0:T(1024)}, f32[896]{0:T(1024)S(1)}, u32[]{:S(2)}) copy-start(f32[896]{0:T(1024)S(1)} %rsqrt.20) | copy-start | bytes 10756
  161.3 4.7 copy-start.2
  245.3 3.1 copy-start
  470.1 68.8 %collective-permute-start.2 = (bf16[896,1024]{1,0:T(8,128)(2,1)}, bf16[896,1024]{1,0:T(8,128)(2,1)}, u32[]{:S(2)}, u32[]{:S(2)}) collective-permute-start(bf16[896,1024]{1,0:T(8,128)(2,1)} %get-tuple-element.75), channel_id=1, source_target_pairs={{0,1},{1,0},{2,3},{3,2},{4,5},{5,4},{6,7},{7,6},{8,9},{9,8},{10,11... | collective-permute-start | bytes 5505032 | tf_op jit(solution)/shard_map/ppermute | solution.py:47
  500.9 18.6 %copy-start.20 = (f32[1,2048]{1,0:T(1,128)S(1)}, f32[1,2048]{1,0:T(1,128)}, u32[]{:S(2)}) copy-start(f32[1,2048]{1,0:T(1,128)} %get-tuple-element.96) | copy-start | bytes 24580
  518.4 5.8 copy-start.12
  525.2 130.5 %slice-start = ((s8[7340032]{0:T(1024)(128)(4,1)}), s8[4194304]{0:T(1024)(128)(4,1)S(1)}, s32[]{:S(2)}) async-start(s8[7340032]{0:T(1024)(128)(4,1)} %bitcast.53), calls=%async_computation.3 | async-start | bytes 8388608
  538.9 115.4 %copy-start.17 = (f32[7,128]{1,0:T(8,128)S(1)}, f32[7,128]{1,0:T(8,128)}, u32[]{:S(2)}) copy-start(f32[7,128]{1,0:T(8,128)} %reshape.324.dot_ref) | copy-start | bytes 10756
  538.9 116.1 %copy-start.18 = (f32[3,64]{1,0:T(4,128)S(1)}, f32[3,64]{1,0:T(4,128)}, u32[]{:S(2)}) copy-start(f32[3,64]{1,0:T(4,128)} %gain_ref.1) | copy-start | bytes 2308
  538.9 116.1 %copy-start.21 = (f32[3,64]{1,0:T(4,128)S(1)}, f32[3,64]{1,0:T(4,128)}, u32[]{:S(2)}) copy-start(f32[3,64]{1,0:T(4,128)} %param.32) | copy-start | bytes 2308
  538.9 116.1 %copy-start.22 = (f32[3,64]{1,0:T(4,128)S(1)}, f32[3,64]{1,0:T(4,128)}, u32[]{:S(2)}) copy-start(f32[3,64]{1,0:T(4,128)} %param.33) | copy-start | bytes 2308
  539.0 116.7 %slice-start.1 = ((s8[7340032]{0:T(1024)(128)(4,1)}), s8[3145728]{0:T(1024)(128)(4,1)S(1)}, s32[]{:S(2)}) async-start(s8[7340032]{0:T(1024)(128)(4,1)} %bitcast.53), calls=%async_computation.4 | async-start | bytes 6291456
  539.0 121.2 %copy-start.16 = (f32[896]{0:T(1024)S(1)}, f32[896]{0:T(1024)}, u32[]{:S(2)}) copy-start(f32[896]{0:T(1024)} %copy-done.15) | copy-start | bytes 10756
  655.7 4.5 copy-start.3
  655.7 4.5 copy-start.7
  655.7 5.4 copy-start.11
  655.7 5.4 dynamic-slice-start
  661.1 3.9 copy-start.5
  661.1 3.9 copy-start.8
  661.1 3.9 copy-start.9
  661.1 4.7 copy-start.10
  (1 other events, 2.8 us)
Sparse Core Ops, SparseCore 0:
  115.3 171.2 all-gather.1
  470.2 84.6 reduce-scatter.1

commit v7 on v6

--- a/solution.py
+++ b/solution.py
@@ -177,7 +177,7 @@
 
 def scan_backward_kernel(
     pre_ref, states_ref, gated_ref, inverse_ref, mean_ref, bound_ref, gain_ref,
-    grad_ref, out_ref, gain_grad_ref, dot_ref,
+    grad_ref, gain_grad_ref, dot_ref,
 ):
     length, width = states_ref.shape[1], states_ref.shape[2]
     bound = bound_ref[...]
@@ -199,7 +199,6 @@
         unit = states * inverse
         gate_sig = jax.nn.sigmoid(pre_gate)
         gate = pre_gate * gate_sig
-        out_ref[0, rows, :] = (unit * gain * gate).astype(out_ref.dtype)
         gain_sum = gain_sum + grad_gated * unit * gate
         scaled = grad_gated * gain
         grad_gate = (scaled * unit * (gate_sig * (1.0 + pre_gate * (1.0 - gate_sig)))).astype(BF)
@@ -260,13 +259,11 @@
         in_specs=[three, whole, whole, column, column, line, line],
         out_specs=[
             three,
-            whole,
             pl.BlockSpec((1, 1, block), lambda b, c: (b, 0, c)),
             column,
         ],
         out_shape=[
             jax.ShapeDtypeStruct((3, batches, length, width), BF),
-            jax.ShapeDtypeStruct((batches, length, width), BF),
             jax.ShapeDtypeStruct((batches, 1, width), F32),
             jax.ShapeDtypeStruct((batches, length, 1), F32),
         ],
@@ -297,15 +294,17 @@
     return (z * 4 + x * 2 + core, lax.axis_index("mp"))
 
 
-def scatter_barrier(z, x, core, with_mp=False):
+def greet(z, x, core):
     barrier = pltpu.get_barrier_semaphore()
     targets = [device_at(z, x, 1 - core), device_at(z, 1 - x, core)]
     targets += [device_at(lax.rem(z + hop, DEPTH), x, core) for hop in range(1, DEPTH)]
-    if with_mp:
-        targets.append((lax.axis_index("dp"), 1 - lax.axis_index("mp")))
+    targets.append((lax.axis_index("dp"), 1 - lax.axis_index("mp")))
     for target in targets:
         pl.semaphore_signal(barrier, 1, device_id=target, device_id_type=MESH_ID)
-    pl.semaphore_wait(barrier, len(targets))
+
+
+def await_partners():
+    pl.semaphore_wait(pltpu.get_barrier_semaphore(), DEPTH + 2)
 
 
 def scatter_step(step, chunks, compute, finish, scratch, small_last=False):
@@ -503,9 +502,9 @@
 
     @pl.when(step == 0)
     def _():
+        greet(z, x, core)
         for one in (load_in(0), *left_loads, load_back(0)):
             one.start()
-        scatter_barrier(z, x, core, with_mp=True)
 
     @pl.when((step < spread) & ((step == 0) | (unit_block > first_tasks(step - 1))))
     def _():
@@ -532,6 +531,10 @@
         def _():
             load_in(unit_block + 1).start()
 
+    @pl.when(step == 0)
+    def _():
+        await_partners()
+
     @pl.when(has_second(second - 1))
     def _():
         index = second_task(second - 1)
@@ -601,9 +604,11 @@
         return pltpu.make_async_copy(
             tail_stage.at[lax.rem(index, 2)], spot, tail_sem.at[lax.rem(index, 2)])
 
-    @pl.when((step >= chunks) & (step < chunks + 3 * TAIL))
-    def _():
-        index = step - chunks
+    tail_start = chunks + Z_LAG - 3 * TAIL
+
+    @pl.when(step >= tail_start)
+    def _():
+        index = step - tail_start
 
         @pl.when(index >= 2)
         def _():
@@ -613,7 +618,7 @@
             def to_stage(value):
                 tail_stage[lax.rem(index, 2), :, :, side] = value.astype(BF)
 
-            compute(step, side, to_stage)
+            compute(chunks + index, side, to_stage)
         tail_copy(index).start()
 
     @pl.when(step == chunks + Z_LAG - 1)
@@ -665,7 +670,7 @@
         cost_estimate=pl.CostEstimate(
             flops=18 * rows * full * hidden, bytes_accessed=6 * full * hidden * 2,
             transcendentals=rows * hidden),
-    )(normed, back_low, normed.T.reshape(left_shape), left_back.reshape(left_shape), glu)
+    )(normed, back_low, owner_rows(normed), left_back, glu)
     return out, tail.reshape(3, full, TAIL * LANES), sum_own, sum_came, half_own, half_send
 
 
@@ -721,11 +726,12 @@
 
     @pl.when(step == 0)
     def _():
+        greet(z, x, core)
         for one in (*big_loads, *loads(0)):
             one.start()
         gain_chunk[...] = jnp.zeros_like(gain_chunk)
         gain_sum[...] = jnp.zeros_like(gain_sum)
-        scatter_barrier(z, x, core, with_mp=True)
+        await_partners()
         dot_copy.start()
 
     @pl.when(step == 1)
@@ -866,7 +872,7 @@
     left_in, grad_pre, left_out, right_out, gain_parts, tokens, inverse, weights, dots, collective
 ):
     _, rows, channels = grad_pre.shape
-    full = left_in.shape[0]
+    full = right_out.shape[1]
     block, half = full // 16, channels // 16
     full_blocks, across = full // LANES, channels // LANES
     outer, inner = full_blocks // 2, 3 * across
@@ -918,10 +924,28 @@
         cost_estimate=pl.CostEstimate(
             flops=14 * full * rows * channels, bytes_accessed=16 * full * channels, transcendentals=0),
     )(
-        left_in.reshape(DEPTH, 2, 2, block, rows), grad_pre,
-        left_out.reshape(DEPTH, 2, 2, half, rows), right_out, gain_parts, tokens, inverse, weights, dots,
+        left_in, grad_pre, left_out, right_out, gain_parts, tokens, inverse, weights, dots,
     )
     return out, gains, half_own.astype(F32) + half_came.astype(F32), dot_came
+
+
+def transpose_kernel(in_ref, out_ref):
+    turned = in_ref[...].T
+    out_ref[...] = turned.reshape(out_ref.shape)
+
+
+def owner_rows(value, owners=2):
+    rows, width = value.shape
+    block = width // 16
+    return pl.pallas_call(
+        transpose_kernel,
+        grid=(2 * DEPTH,),
+        in_specs=[pl.BlockSpec((rows, owners * block), lambda q: (0, q))],
+        out_specs=pl.BlockSpec((1, 1, owners, block, rows), lambda q: (q // 2, lax.rem(q, 2), 0, 0, 0)),
+        out_shape=jax.ShapeDtypeStruct((DEPTH, 2, owners, block, rows), value.dtype),
+        compiler_params=pltpu.CompilerParams(vmem_limit_bytes=VMEM_LIMIT),
+        cost_estimate=pl.CostEstimate(flops=0, bytes_accessed=4 * rows * width, transcendentals=0),
+    )(value)
 
 
 def middle_back_kernel(
@@ -1027,6 +1051,13 @@
     z, x, core = device_place()
     mp = lax.axis_index("mp")
     barrier = pltpu.get_barrier_semaphore()
+    right, left = lax.rem(z + 1, DEPTH), lax.rem(z + DEPTH - 1, DEPTH)
+    dp = lax.axis_index("dp")
+    for target in (
+        device_at(right, x, core), device_at(left, x, core), device_at(z, 1 - x, core),
+        device_at(z, x, 1 - core), (dp, 1 - mp),
+    ):
+        pl.semaphore_signal(barrier, 1, device_id=target, device_id_type=MESH_ID)
     for kind in range(3):
         for tile in range(in_ref.shape[3] // 128):
             first = mixer_ref[kind, :, 256 * tile : 256 * tile + 128]
@@ -1042,13 +1073,6 @@
     small_ref[...] = jnp.zeros_like(small_ref)
     small_ref[0:3, 0:64] = gain_ref[...].astype(BF).astype(F32)
     small_ref[3:4, :] = live
-    right, left = lax.rem(z + 1, DEPTH), lax.rem(z + DEPTH - 1, DEPTH)
-    dp = lax.axis_index("dp")
-    for target in (
-        device_at(right, x, core), device_at(left, x, core), device_at(z, 1 - x, core),
-        device_at(z, x, 1 - core), (dp, 1 - mp),
-    ):
-        pl.semaphore_signal(barrier, 1, device_id=target, device_id_type=MESH_ID)
     pl.semaphore_wait(barrier, 5)
 
     def spot(item, zs, xs, cs, side=None):
@@ -1310,10 +1334,14 @@
     inverse_state = lax.rsqrt(square / full + EPSILON)
     mixed = jnp.dot(raw.reshape(rows, channels), mixer_out, preferred_element_type=F32)
     back_low = (cot_full.astype(F32) * token_weight).astype(BF)
+    gated_out = (raw.reshape(rows, channels).astype(F32) * inverse_state).astype(BF)
     if quick:
         mixed = mixed.astype(BF)
-        came, left_back, left_in = lax.optimization_barrier(
-            (partner_swap(mixed), back_low.T, normed_in.T)
+        came, left_back, left_in, left_out, token_weight, inverse_in = lax.optimization_barrier(
+            (
+                partner_swap(mixed), owner_rows(back_low), owner_rows(normed_in), owner_rows(gated_out),
+                token_weight, inverse_in,
+            )
         )
         mixed = mixed.astype(F32) + came.astype(F32)
     else:
@@ -1366,7 +1394,7 @@
         state_mean = jnp.mean(middle_low.astype(F32) * branch_mix, axis=-1, keepdims=True)
         grad_gated = dot(middle_low, mixer_out, across)
     by_batch = lambda v: v.reshape(batches, length, v.shape[-1])
-    grad_pre, gated_out, gain_state, pre_dot = scan_backward(
+    grad_pre, gain_state, pre_dot = scan_backward(
         pre, states, by_batch(grad_gated), by_batch(inverse_state), by_batch(state_mean), bound, state_gain
     )
     if quick:
@@ -1376,10 +1404,10 @@
         glu_new = glu_update(
             glu_sums, lambda kind, q: (3 * q + kind, 0, 0), 0, scattered, glu_ins, glu_downs, scale
         )
-        half_came, grad_pre, glu_new = lax.optimization_barrier((half_came, grad_pre, glu_new))
         branch = half_own.astype(F32) + half_came.astype(F32)
+        layer_out = (own_features(middle) + branch).astype(BF)
+        layer_out, grad_pre, glu_new = lax.optimization_barrier((layer_out, grad_pre, glu_new))
     grad_pre = grad_pre.reshape(3, rows, channels)
-    gated_out = gated_out.reshape(rows, channels)
     gain_state = jnp.sum(gain_state, axis=0).reshape(groups, 1, own_rows)
     gain_state = lax.dynamic_update_slice_in_dim(
         jnp.zeros((groups, narrow, own_rows), F32), gain_state, place, 1
@@ -1397,7 +1425,7 @@
         gain_parts = jnp.pad(gain_parts, ((0, 0), (0, 5), (0, 0)))
         pre_dot = pre_dot.reshape(-1, 128)
         mixer_own, gain_own, grad_normed_in, dot_came = mixer_call(
-            left_in, grad_pre, gated_out.T, middle_low, gain_parts, token_rows, inverse_in, mixer_in, pre_dot, 1
+            left_in, grad_pre, left_out, middle_low, gain_parts, token_rows, inverse_in, mixer_in, pre_dot, 1
         )
         in_mean = (pre_dot + dot_came).reshape(rows, 1) / full
         gain_own = lax.dynamic_slice_in_dim(gain_own[:3], place * own_rows, own_rows, 1)
@@ -1422,7 +1450,8 @@
         grad_normed_in * own_features(gain_full[0]) - unit_in_own * in_mean
     )
     grad_tokens = grad_seq.astype(BF)
-    layer_out = (own_features(middle) + branch).astype(BF)
+    if not quick:
+        layer_out = (own_features(middle) + branch).astype(BF)
 
     update = functools.partial(adamw_update, count=STEP_NUMBER)
     mixer_new = update(

time: 685 us -> 670 us (0.978)
  Pallas kernels: 468 us -> 494 us
  local copies, waits for them, and re-layouts: 39.9 us -> 16.8 us
  waiting for transfers between devices: 85.1 us -> 77.7 us
  other arithmetic: 46.1 us -> 39 us
    pallas_call x0 -> x4, Pallas kernels: none -> 27.3 us  [owner_rows(): pl.pallas_call(transpose_kernel, grid=(2 * DEPTH,), in_specs=[pl.BlockSpe...]
    reshape x3 -> x0, local copies, waits for them, and re-layouts: 16.4 us -> none  [the longest x1 6.26 us: mixer_call(): left_in.reshape(DEPTH, 2, 2, block, rows)]
    ppermute x3, waiting for transfers between devices: 67.4 us -> 55.6 us  [partner_swap(): return lax.ppermute(value, 'mp', [(0, 1), (1, 0)])]
    transpose x3 -> x0, other arithmetic: 10 us -> none  [the longest x2 7.46 us: shards(): came, left_back, left_in = lax.optimization_barrier((partner_swap(mixed),...]
  transfers between devices with their start and end apart: 5 -> 5, of which waited for: 2 -> 2; matrix products, arithmetic and copies ran while one was open for 15% -> 11% of each run, Pallas kernels for 26% -> 31%
where the time goes in v7:
time: 670 us; the launch traced here: 669 us
  Pallas kernels  494 us (74%)
  waiting for transfers between devices  77.7 us (12%)
  other arithmetic  39 us (6%)
  matrix products  23.1 us (3%)
  local copies, waits for them, and re-layouts  16.8 us (3%)
  between operations  14.4 us (2%)
    pallas_call x1, Pallas kernels, glu_call(): pl.pallas_call(functools.partial(glu_kernel, hidden_blocks, full_blocks),...  182 us
    pallas_call x1, Pallas kernels, mixer_call(): pl.pallas_call(functools.partial(mixer_kernel, full_blocks), grid=(chunks...  116 us
    pallas_call x1, Pallas kernels, gather_call(): pl.pallas_call(gather_kernel, in_specs=[in_vmem] * 6 + [any_space], out_s...  105 us
    ppermute x3, waiting for transfers between devices, partner_swap(): return lax.ppermute(value, 'mp', [(0, 1), (1, 0)])  55.6 us
    pallas_call x4, Pallas kernels, owner_rows(): pl.pallas_call(transpose_kernel, grid=(2 * DEPTH,), in_specs=[pl.BlockSpe...  27.3 us
    all_gather x1, waiting for transfers between devices, shards(): glu = lax.all_gather(glu_low, 'dp', axis=1, tiled=True)  22.1 us
    pallas_call x1, Pallas kernels, middle_back(): pl.pallas_call(middle_back_kernel, grid=(rows // step,), in_specs=[line(f...  19.7 us
    pallas_call x2, Pallas kernels, glu_update(): pl.pallas_call(functools.partial(glu_update_kernel, scale), grid=(blocks,...  17 us
  transfers between devices with their start and end apart: 5, of which 2 were waited for; matrix products, arithmetic and copies ran while one was open for 11% of the time, Pallas kernels for 31%

profile of v7, /device:TPU:0, one launch (start us, length us, event | category | flops | bytes accessed | tf_op | source)
XLA Modules:
  0.0 669.0 jit_solution(7358115693090554535)
XLA Ops:
  7.2 1.3 copy.51.lengths_ref
  8.5 1.3 copy.52.domains_ref
  9.8 104.9 %shard_map.272 = (bf16[3,4,2,2,2,64,1024]{6,5,4,3,2,1,0:T(8,128)(2,1)}, bf16[4,2,2,64,2048]{4,3,2,1,0:T(8,128)(2,1)}, f32[4,2,2,2,8,128]{5,4,3,2,1,0:T(8,128)}, ...) custom-call(f32[4,64,2048]{2,1,0:T(8,128)} %mixer_ref.1, f32[3,64]{1,0:T(4,128)} %gain_ref.1, s32[2,1]{1,0:T(2,128)} %copy.51.lengths_ref, ...), custom_call_target="tpu_custom_call" | custom-call | bytes 300000000 | tf_op jit(solution)/shard_map/pallas_call | solution.py:1234
  117.4 3.0 fusion.2
  122.2 16.1 %fusion.7 = f32[3,1024,896]{1,2,0:T(8,128)} fusion(bf16[896,2048,1]{1,0,2:T(8,128)(2,1)S(1)} %bitcast.51, bf16[3,2048,1024]{2,1,0:T(8,128)(2,1)} %bitcast.62), kind=kOutput, calls=%fused_computation.38 | convolution fusion | flops 11274289152 | bytes 27262976 | tf_op jit(solution)/shard_map/td,kde->kte/dot_general | solution.py:1330
  138.3 10.8 %shard_map.273 = (f32[2,448,1024]{2,1,0:T(8,128)}, bf16[2,448,1024]{2,1,0:T(8,128)(2,1)}, f32[2,448,1]{2,1,0:T(8,128)}) custom-call(f32[3,2,448,1024]{3,2,1,0:T(8,128)} %bitcast.46, f32[1,1024]{1,0:T(1,128)} %broadcast_in_dim_reshape.8.bound_ref, f32[1,1024]{1,0:T(1,128)} %broadcast_in_dim_reshape.9.gain_ref), custom_call_target="tpu_custom_call" | custom-call | flops 36700160 | bytes 16515072 | tf_op jit(solution)/shard_map/pallas_call | solution.py:151
  149.1 7.0 %convolution_convert_fusion = bf16[896,2048]{1,0:T(8,128)(2,1)} fusion(bf16[896,1024]{1,0:T(8,128)(2,1)} %bitcast.55, bf16[1024,2048]{1,0:T(8,128)(2,1)S(1)} %bitcast.50), kind=kOutput, calls=%fused_computation.15 | convolution fusion | flops 3759931392 | bytes 9699328 | tf_op jit(solution)/shard_map/dot_general | solution.py:1335
  156.2 1.2 collective-permute-start.1
  158.6 1.5 slice_reduce_fusion.1
  161.0 4.9 fusion.1.in_ref
  165.9 2.6 multiply_convert_fusion.1.in_ref.back_ref
  168.7 7.1 %shard_map.274.left_back_ref = bf16[4,2,2,128,896]{4,3,2,1,0:T(8,128)(2,1)} custom-call(bf16[896,2048]{1,0:T(8,128)(2,1)} %multiply_convert_fusion.1.in_ref.back_ref), custom_call_target="tpu_custom_call" | custom-call | bytes 7340032 | tf_op jit(solution)/shard_map/pallas_call | solution.py:940
  175.8 7.1 %shard_map.275.left_hbm = bf16[4,2,2,128,896]{4,3,2,1,0:T(8,128)(2,1)} custom-call(bf16[896,2048]{1,0:T(8,128)(2,1)} %fusion.1.in_ref), custom_call_target="tpu_custom_call" | custom-call | bytes 7340032 | tf_op jit(solution)/shard_map/pallas_call | solution.py:940
  183.0 55.6 %collective-permute-done = f32[896,1]{0,1:T(1,128)S(1)} collective-permute-done((f32[896,1]{0,1:T(1,128)S(1)}, f32[896,1]{0,1:T(1,128)S(1)}, u32[]{:S(2)}, u32[]{:S(2)}) %collective-permute-start) | collective-permute-done | bytes 3616 | tf_op jit(solution)/shard_map/ppermute | solution.py:47
  238.7 1.6 multiply_convert_fusion.2.in_ref
  240.3 6.2 shard_map.276.left_out_ref
  246.5 5.2 multiply_reduce_fusion
  251.7 3.0 copy-done.3
  254.7 2.5 multiply_convert_fusion.in_ref.normed_ref
  257.2 6.9 %shard_map.277.left_ref = bf16[4,2,2,128,896]{4,3,2,1,0:T(8,128)(2,1)} custom-call(bf16[896,2048]{1,0:T(8,128)(2,1)} %multiply_convert_fusion.in_ref.normed_ref), custom_call_target="tpu_custom_call" | custom-call | bytes 7340032 | tf_op jit(solution)/shard_map/pallas_call | solution.py:940
  264.1 22.1 %all-gather.2.cloned.1.call-done.glu_ref = bf16[3,2048,2816]{2,1,0:T(8,128)(2,1)} async-done(((bf16[3,128,2816]{2,1,0:T(8,128)(2,1)}), bf16[3,2048,2816]{2,1,0:T(8,128)(2,1)}) %all-gather.2.cloned.1.call-update) | async-done | bytes 34603024 | tf_op jit(solution)/shard_map/all_gather | solution.py:1312
  286.2 182.0 %shard_map.278 = (f32[27,128,256]{2,1,0:T(8,128)}, bf16[896,2048]{1,0:T(8,128)(2,1)}, bf16[896,2048]{1,0:T(8,128)(2,1)}, bf16[896,1024]{1,0:T(8,128)(2,1)}, bf16...) custom-call(bf16[896,2048]{1,0:T(8,128)(2,1)} %multiply_convert_fusion.in_ref.normed_ref, ...), custom_call_target="tpu_custom_call" | custom-call | flops 93012885504 | bytes 69206016 | tf_op jit(solution)/shard_map/pallas_call | solution.py:644
  468.2 1.6 collective-permute-start.2
  473.6 19.7 %shard_map.279 = (f32[896,1024]{1,0:T(8,128)}, bf16[896,2048]{1,0:T(8,128)(2,1)}, f32[896,1]{1,0:T(8,128)}, f32[896,1024]{1,0:T(8,128)}, f32[1,2048]{1,0:T(1,128)}) custom-call(bf16[896,2048]{1,0:T(8,128)(2,1)} %get-tuple-element.79.sum_own_ref, bf16[896,2048]{1,0:T(8,128)(2,1)} %get-tuple-element.80.sum_came_ref, f32[896,2048]{1,0:T(8,128)} %copy-done.3, ...), custom_call_target="tpu_custom_call" | custom-call | flops 3758096384 | bytes 36700160 | tf_op jit(solution)/shard_map/pallas_call | solution.py:983
  493.3 17.0 %shard_map.280 = (bf16[3,2,448,1024]{3,2,1,0:T(8,128)(2,1)}, f32[2,1,1024]{2,1,0:T(1,128)}, f32[2,448,1]{2,1,0:T(8,128)}) custom-call(f32[3,2,448,1024]{3,2,1,0:T(8,128)} %bitcast.47, f32[2,448,1024]{2,1,0:T(8,128)} %get-tuple-element.78.states_ref, f32[2,448,1024]{2,1,0:T(8,128)} %bitcast.52, f32[2,448,1]{2,1,0:T(8,128)} %reshape.309.inverse_ref, ...), custom_call_target="tpu_custom_call" | custom-call | flops 73400320 | bytes 25690112 | tf_op jit(solution)/shard_map/pallas_call | solution.py:256
  512.0 1.2 reduce.13
  513.9 13.8 %shard_map.281 = (f32[2,128,2816]{2,1,0:T(8,128)}, f32[2,128,2816]{2,1,0:T(8,128)}, f32[2,128,2816]{2,1,0:T(8,128)}, f32[2816,128]{1,0:T(8,128)}, f32[2816,128]{1,0:T(8,128)}, /*index=5*/f32[2816,128]{1,0:T(8,128)}) custom-call(f32[27,128,256]{2,1,0:T(8,128)} %get-tuple-element.85.act_ref.up_ref.out_ref, ...), custom_call_target="tpu_custom_call" | custom-call | flops 17694720 | bytes 24772608 | tf_op jit(solution)/shard_map/pallas_call | solution.py:1020
  527.7 4.3 add_convert_fusion.1
  532.1 115.6 %shard_map.282 = (f32[4,64,2048]{2,1,0:T(8,128)}, f32[8,128]{1,0:T(8,128)}, bf16[896,1024]{1,0:T(8,128)(2,1)}, bf16[896,1024]{1,0:T(8,128)(2,1)}, bf16[896,1024]{1,0:T(8,128)(2,1)}, /*index=5*/f32[7,128]{1,0:T(8,128)}) custom-call(bf16[4,2,2,128,896]{4,3,2,1,0:T(8,128)(2,1)} %shard_map.275.left_hbm, bf16[3,896,1024]{2,1,0:T(8,128)(2,1)} %bitcast.64, ...), custom_call_target="tpu_custom_call" | custom-call | flops 26306674688 | bytes 33554432 | tf_op jit(solution)/shard_map/pallas_call | solution.py:890
  649.7 4.0 add_convert_fusion
  654.9 4.0 multiply_subtract_fusion
  658.9 3.2 shard_map.283
  (99 shorter events, 16.4 us)
Async XLA Ops:
  7.2 279.0 %all-gather.2.cloned.1.call-start = ((), (), s32[]{:S(2)}) async-start(), calls=%async_computation.1 | async-start | bytes 36765696 | tf_op jit(solution)/shard_map/all_gather | solution.py:1312
  9.8 106.8 %copy-start.16 = (f32[2048]{0:T(1024)S(1)}, f32[2048]{0:T(1024)}, u32[]{:S(2)}) copy-start(f32[2048]{0:T(1024)} %param.21) | copy-start | bytes 24580
  114.8 544.2 %reduce-scatter.2.cloned.1.call-start = ((), (), s32[]{:S(2)}) async-start(), calls=%async_computation.2 | async-start | bytes 6684672 | tf_op jit(solution)/shard_map/reduce_scatter | solution.py:1361
  116.6 353.9 %copy-start.13 = (f32[2048]{0:T(1024)}, f32[2048]{0:T(1024)S(1)}, u32[]{:S(2)}) copy-start(f32[2048]{0:T(1024)S(1)} %mul.240) | copy-start | bytes 24580
  117.4 3.9 copy-start
  138.3 10.8 %copy-start.6 = (bf16[4,2,2,64,2048]{4,3,2,1,0:T(8,128)(2,1)S(1)}, bf16[4,2,2,64,2048]{4,3,2,1,0:T(8,128)(2,1)}, u32[]{:S(2)}) copy-start(bf16[4,2,2,64,2048]{4,3,2,1,0:T(8,128)(2,1)} %get-tuple-element.71) | copy-start | bytes 12582916
  149.1 8.2 %copy-start.12 = (f32[2,448,1]{2,1,0:T(8,128)S(1)}, f32[2,448,1]{2,1,0:T(8,128)}, u32[]{:S(2)}) copy-start(f32[2,448,1]{2,1,0:T(8,128)} %get-tuple-element.69) | copy-start | bytes 10756
  149.1 10.9 %copy-start.21 = (s32[2,1,1]{0,2,1:T(1,128)S(1)}, s32[2,1,1]{0,2,1:T(1,128)}, u32[]{:S(2)}) copy-start(s32[2,1,1]{0,2,1:T(1,128)} %param.20) | copy-start | bytes 28
  149.1 11.7 %copy-start.20 = (s32[2,1]{0,1:T(1,128)S(1)}, s32[2,1]{0,1:T(1,128)}, u32[]{:S(2)}) copy-start(s32[2,1]{0,1:T(1,128)} %param.19) | copy-start | bytes 28
  156.2 90.3 %collective-permute-start.1 = (bf16[896,2048]{1,0:T(8,128)(2,1)}, bf16[896,2048]{1,0:T(8,128)(2,1)}, u32[]{:S(2)}, u32[]{:S(2)}) collective-permute-start(bf16[896,2048]{1,0:T(8,128)(2,1)} %convolution_convert_fusion), channel_id=1, source_target_pairs={{0,1},{1,0},{2,3},{3,2},{4,5},{5,4},{6,7},{7,6},{8,9},{9,8},{10,11... | collective-permute-start | bytes 11010056 | tf_op jit(solution)/shard_map/ppermute | solution.py:47
  157.7 80.9 %collective-permute-start = (f32[896,1]{0,1:T(1,128)S(1)}, f32[896,1]{0,1:T(1,128)S(1)}, u32[]{:S(2)}, u32[]{:S(2)}) collective-permute-start(f32[896,1]{0,1:T(1,128)S(1)} %reshape.296), channel_id=1, source_target_pairs={{0,1},{1,0},{2,3},{3,2},{4,5},{5,4},{6,7},{7,6},{8,9},{9,8},{10,11... | collective-permute-start | bytes 10760 | tf_op jit(solution)/shard_map/ppermute | solution.py:47
  161.0 4.9 copy-start.4
  175.8 62.8 %copy-start.11 = (bf16[2,448,1024]{2,1,0:T(8,128)(2,1)S(1)}, bf16[2,448,1024]{2,1,0:T(8,128)(2,1)}, u32[]{:S(2)}) copy-start(bf16[2,448,1024]{2,1,0:T(8,128)(2,1)} %get-tuple-element.70) | copy-start | bytes 5505028
  238.6 7.8 %copy-start.1 = (bf16[2,1,448,2048]{3,2,1,0:T(8,128)(2,1)S(1)}, bf16[2,1,448,2048]{3,2,1,0:T(8,128)(2,1)}, u32[]{:S(2)}) copy-start(bf16[2,1,448,2048]{3,2,1,0:T(8,128)(2,1)} %param.17) | copy-start | bytes 11010052
  251.7 3.0 copy-start.3
  468.2 59.5 %collective-permute-start.2 = (bf16[896,1024]{1,0:T(8,128)(2,1)}, bf16[896,1024]{1,0:T(8,128)(2,1)}, u32[]{:S(2)}, u32[]{:S(2)}) collective-permute-start(bf16[896,1024]{1,0:T(8,128)(2,1)} %get-tuple-element.77), channel_id=1, source_target_pairs={{0,1},{1,0},{2,3},{3,2},{4,5},{5,4},{6,7},{7,6},{8,9},{9,8},{10,11... | collective-permute-start | bytes 5505032 | tf_op jit(solution)/shard_map/ppermute | solution.py:47
  493.3 17.9 %copy-start.17 = (f32[1,2048]{1,0:T(1,128)S(1)}, f32[1,2048]{1,0:T(1,128)}, u32[]{:S(2)}) copy-start(f32[1,2048]{1,0:T(1,128)} %get-tuple-element.100) | copy-start | bytes 24580
  493.3 34.4 %slice-start = ((s8[7340032]{0:T(1024)(128)(4,1)}), s8[3145728]{0:T(1024)(128)(4,1)S(1)}, s32[]{:S(2)}) async-start(s8[7340032]{0:T(1024)(128)(4,1)} %bitcast.44), calls=%async_computation.3 | async-start | bytes 6291456
  513.9 13.8 %slice-start.1 = ((s8[7340032]{0:T(1024)(128)(4,1)}), s8[4194304]{0:T(1024)(128)(4,1)S(1)}, s32[]{:S(2)}) async-start(s8[7340032]{0:T(1024)(128)(4,1)} %bitcast.44), calls=%async_computation.4 | async-start | bytes 8388608
  532.0 116.3 %copy-start.14 = (f32[7,128]{1,0:T(8,128)S(1)}, f32[7,128]{1,0:T(8,128)}, u32[]{:S(2)}) copy-start(f32[7,128]{1,0:T(8,128)} %reshape.305.dot_ref) | copy-start | bytes 10756
  532.0 117.0 %copy-start.15 = (f32[3,64]{1,0:T(4,128)S(1)}, f32[3,64]{1,0:T(4,128)}, u32[]{:S(2)}) copy-start(f32[3,64]{1,0:T(4,128)} %gain_ref.1) | copy-start | bytes 2308
  532.0 117.0 %copy-start.18 = (f32[3,64]{1,0:T(4,128)S(1)}, f32[3,64]{1,0:T(4,128)}, u32[]{:S(2)}) copy-start(f32[3,64]{1,0:T(4,128)} %param.32) | copy-start | bytes 2308
  532.0 117.0 %copy-start.19 = (f32[3,64]{1,0:T(4,128)S(1)}, f32[3,64]{1,0:T(4,128)}, u32[]{:S(2)}) copy-start(f32[3,64]{1,0:T(4,128)} %param.33) | copy-start | bytes 2308
  532.0 117.6 %copy-start.2 = (bf16[2,1,448,2048]{3,2,1,0:T(8,128)(2,1)S(1)}, bf16[2,1,448,2048]{3,2,1,0:T(8,128)(2,1)}, u32[]{:S(2)}) copy-start(bf16[2,1,448,2048]{3,2,1,0:T(8,128)(2,1)} %param.17) | copy-start | bytes 11010052
  532.0 117.6 %copy-start.7 = (f32[896,1024]{1,0:T(8,128)S(1)}, f32[896,1024]{1,0:T(8,128)}, u32[]{:S(2)}) copy-start(f32[896,1024]{1,0:T(8,128)} %get-tuple-element.93) | copy-start | bytes 11010052
  532.0 117.6 %dynamic-slice-start = ((f32[2048]{0:T(1024)}, s32[]{:T(128)}), f32[1024]{0:T(1024)S(1)}, s32[]{:S(2)}) async-start(f32[2048]{0:T(1024)} %copy-done.13, s32[]{:T(128)} %select_n.36), calls=%async_computation.5 | async-start | bytes 8704 | tf_op jit(solution)/shard_map/dynamic_slice | solution.py:1377
  649.7 4.0 copy-start.5
  649.7 4.0 copy-start.8
  649.7 4.6 copy-start.9
  649.7 5.2 copy-start.10
Sparse Core Ops, SparseCore 0:
  114.9 171.2 all-gather.1
  468.4 85.0 reduce-scatter.1

commit v8 on v7

--- a/solution.py
+++ b/solution.py
@@ -1033,7 +1033,8 @@
     return tuple(new)
 
 
-ITEMS = 4
+ITEMS = 6
+ALONG_Z = (0, 5, 2, 3)
 
 
 def split_lanes(first, second):
@@ -1078,8 +1079,9 @@
     def spot(item, zs, xs, cs, side=None):
         if item == 0:
             return all_in.at[:, zs, xs, cs, mp if side is None else side]
-        if item == 1:
-            return all_out.at[zs, xs, cs]
+        if item in (1, 4, 5):
+            rows = out_ref.shape[0] // 2
+            return all_out.at[zs, xs, cs, slice(rows, None) if item == 5 else slice(0, rows)]
         if item == 2:
             return all_in.at[:, zs, xs, cs, 1 - mp]
         return all_small.at[zs, xs, cs]
@@ -1087,8 +1089,9 @@
     def own(item):
         if item == 0:
             return in_ref.at[mp]
-        if item == 1:
-            return out_ref
+        if item in (1, 5):
+            rows = out_ref.shape[0] // 2
+            return out_ref.at[slice(rows, None) if item == 5 else slice(0, rows)]
         return spot(item, z, x, core)
 
     def copy(item, zs, xs, target, send, recv, source=None):
@@ -1096,11 +1099,14 @@
             spot(item, zs, xs, core) if source is None else source, spot(item, zs, xs, core),
             send, recv, device_id=target, device_id_type=MESH_ID)
 
+    def column(item):
+        return 1 - x if item == 4 else x
+
     def right_copy(item, zs, source=None):
-        return copy(item, zs, x, device_at(right, x, core), right_send.at[zs, item], z_recv.at[zs, item], source)
+        return copy(item, zs, column(item), device_at(right, x, core), right_send.at[zs, item], z_recv.at[zs, item], source)
 
     def left_copy(item, zs, source=None):
-        return copy(item, zs, x, device_at(left, x, core), left_send.at[zs, item], z_recv.at[zs, item], source)
+        return copy(item, zs, column(item), device_at(left, x, core), left_send.at[zs, item], z_recv.at[zs, item], source)
 
     def x_copy(item, zs, source=None):
         return copy(item, zs, x, device_at(z, 1 - x, core), x_send.at[zs, item], x_recv.at[zs, item], source)
@@ -1118,7 +1124,7 @@
     ]
     locals_ = [
         pltpu.make_async_copy(in_ref.at[mp], spot(0, z, x, core), local_sem.at[0]),
-        pltpu.make_async_copy(out_ref, spot(1, z, x, core), local_sem.at[1]),
+        pltpu.make_async_copy(out_ref, all_out.at[z, x, core], local_sem.at[1]),
         pltpu.make_async_copy(small_ref, all_small.at[z, x, core, mp], local_sem.at[2]),
     ]
     cot_lanes = pl.ds(pl.multiple_of(mp * cot_ref.shape[1], 128), cot_ref.shape[1])
@@ -1130,22 +1136,23 @@
         one.start()
     locals_[2].start()
 
-    for item in range(ITEMS):
+    def both_ways(item, source=None):
+        @pl.when(z < DEPTH - 1)
+        def _():
+            right_copy(item, z, source).start()
+
+        @pl.when(z > 0)
+        def _():
+            left_copy(item, z, source).start()
+
+    for item in (1, *ALONG_Z):
         if item == 2:
             y_copies[0].wait_recv()
         if item == 3:
             y_copies[1].wait_recv()
             locals_[2].wait()
         source = own(item)
-
-        @pl.when(z < DEPTH - 1)
-        def _():
-            right_copy(item, z, source).start()
-
-        @pl.when(z > 0)
-        def _():
-            left_copy(item, z, source).start()
-
+        both_ways(item, source)
         x_copy(item, z, source).start()
         core_copy(item, z, x, source).start()
     locals_[0].start()
@@ -1163,32 +1170,44 @@
             x_recv.at[zs, item], device_id=device_at(z, 1 - x, core), device_id_type=MESH_ID).wait_recv()
         core_copy(item, zs, 1 - x).start()
 
+    def arrived(item, hop):
+        sent = 1 if item == 4 else item
+
+        @pl.when(z >= hop)
+        def _():
+            zs = z - hop
+            right_copy(item, zs).wait_recv()
+
+            @pl.when(z < DEPTH - 1)
+            def _():
+                right_copy(item, zs).start()
+
+            if item in ALONG_Z:
+                x_copy(item, zs).start()
+            core_copy(sent, zs, column(item)).start()
+
+        @pl.when(z + hop < DEPTH)
+        def _():
+            zs = z + hop
+            left_copy(item, zs).wait_recv()
+
+            @pl.when(z > 0)
+            def _():
+                left_copy(item, zs).start()
+
+            if item in ALONG_Z:
+                x_copy(item, zs).start()
+            core_copy(sent, zs, column(item)).start()
+
     for hop in range(1, DEPTH + 1):
-        for item in range(ITEMS):
+        if hop == 1:
+            from_x(1, z)
+            both_ways(4)
+        if hop < DEPTH:
+            arrived(1, hop)
+        for item in ALONG_Z:
             if hop < DEPTH:
-                @pl.when(z >= hop)
-                def _():
-                    zs = z - hop
-                    right_copy(item, zs).wait_recv()
-
-                    @pl.when(z < DEPTH - 1)
-                    def _():
-                        right_copy(item, zs).start()
-
-                    x_copy(item, zs).start()
-                    core_copy(item, zs, x).start()
-
-                @pl.when(z + hop < DEPTH)
-                def _():
-                    zs = z + hop
-                    left_copy(item, zs).wait_recv()
-
-                    @pl.when(z > 0)
-                    def _():
-                        left_copy(item, zs).start()
-
-                    x_copy(item, zs).start()
-                    core_copy(item, zs, x).start()
+                arrived(item, hop)
             if hop == 1:
                 from_x(item, z)
             else:
@@ -1199,6 +1218,8 @@
                 @pl.when(z + hop - 1 < DEPTH)
                 def _():
                     from_x(item, z + (hop - 1))
+        if hop < DEPTH:
+            arrived(4, hop)
 
     for item in range(ITEMS):
         for zs in range(DEPTH):
@@ -1210,9 +1231,13 @@
             def _():
                 left_copy(item, zs).wait_send()
 
-            x_copy(item, zs).wait_send()
+            if item in ALONG_Z:
+                x_copy(item, zs).wait_send()
+            if item == 4:
+                continue
             for xs in range(2):
                 core_copy(item, zs, xs).wait()
+    x_copy(1, z).wait_send()
     for one in y_copies:
         one.wait_send()
     locals_[0].wait()

time: 670 us -> 668 us (level)
  Pallas kernels: 494 us -> 487 us
    pallas_call x1, Pallas kernels: 105 us -> 97.2 us  [gather_call(): pl.pallas_call(gather_kernel, in_specs=[in_vmem] * 6 + [any_space], out_s...]
where the time goes in v8:
time: 668 us; the launch traced here: 662 us
  Pallas kernels  487 us (73%)
  waiting for transfers between devices  78.6 us (12%)
  other arithmetic  39.1 us (6%)
  matrix products  23.2 us (3%)
  local copies, waits for them, and re-layouts  16.2 us (2%)
  between operations  14.8 us (2%)
    pallas_call x1, Pallas kernels, glu_call(): pl.pallas_call(functools.partial(glu_kernel, hidden_blocks, full_blocks),...  182 us
    pallas_call x1, Pallas kernels, mixer_call(): pl.pallas_call(functools.partial(mixer_kernel, full_blocks), grid=(chunks...  116 us
    pallas_call x1, Pallas kernels, gather_call(): pl.pallas_call(gather_kernel, in_specs=[in_vmem] * 6 + [any_space], out_s...  97.2 us
    ppermute x3, waiting for transfers between devices, partner_swap(): return lax.ppermute(value, 'mp', [(0, 1), (1, 0)])  55.3 us
    pallas_call x4, Pallas kernels, owner_rows(): pl.pallas_call(transpose_kernel, grid=(2 * DEPTH,), in_specs=[pl.BlockSpe...  27.2 us
    all_gather x1, waiting for transfers between devices, shards(): glu = lax.all_gather(glu_low, 'dp', axis=1, tiled=True)  23.3 us
    pallas_call x1, Pallas kernels, middle_back(): pl.pallas_call(middle_back_kernel, grid=(rows // step,), in_specs=[line(f...  19.7 us
    pallas_call x2, Pallas kernels, glu_update(): pl.pallas_call(functools.partial(glu_update_kernel, scale), grid=(blocks,...  17 us
  transfers between devices with their start and end apart: 5, of which 2 were waited for; matrix products, arithmetic and copies ran while one was open for 11% of the time, Pallas kernels for 31%

profile of v8, /device:TPU:0, one launch (start us, length us, event | category | flops | bytes accessed | tf_op | source)
XLA Modules:
  0.0 662.4 jit_solution(15465449649230251530)
XLA Ops:
  7.2 1.3 copy.51.lengths_ref
  8.5 1.3 copy.52.domains_ref
  9.8 97.2 %shard_map.272 = (bf16[3,4,2,2,2,64,1024]{6,5,4,3,2,1,0:T(8,128)(2,1)}, bf16[4,2,2,64,2048]{4,3,2,1,0:T(8,128)(2,1)}, f32[4,2,2,2,8,128]{5,4,3,2,1,0:T(8,128)}, ...) custom-call(f32[4,64,2048]{2,1,0:T(8,128)} %mixer_ref.1, f32[3,64]{1,0:T(4,128)} %gain_ref.1, s32[2,1]{1,0:T(2,128)} %copy.51.lengths_ref, ...), custom_call_target="tpu_custom_call" | custom-call | bytes 300000000 | tf_op jit(solution)/shard_map/pallas_call | solution.py:1259
  109.6 3.0 fusion.2
  113.9 16.2 %fusion.7 = f32[3,1024,896]{1,2,0:T(8,128)} fusion(bf16[896,2048,1]{1,0,2:T(8,128)(2,1)S(1)} %bitcast.51, bf16[3,2048,1024]{2,1,0:T(8,128)(2,1)} %bitcast.62), kind=kOutput, calls=%fused_computation.38 | convolution fusion | flops 11274289152 | bytes 27262976 | tf_op jit(solution)/shard_map/td,kde->kte/dot_general | solution.py:1355
  130.2 10.8 %shard_map.273 = (f32[2,448,1024]{2,1,0:T(8,128)}, bf16[2,448,1024]{2,1,0:T(8,128)(2,1)}, f32[2,448,1]{2,1,0:T(8,128)}) custom-call(f32[3,2,448,1024]{3,2,1,0:T(8,128)} %bitcast.46, f32[1,1024]{1,0:T(1,128)} %broadcast_in_dim_reshape.8.bound_ref, f32[1,1024]{1,0:T(1,128)} %broadcast_in_dim_reshape.9.gain_ref), custom_call_target="tpu_custom_call" | custom-call | flops 36700160 | bytes 16515072 | tf_op jit(solution)/shard_map/pallas_call | solution.py:151
  141.0 7.0 %convolution_convert_fusion = bf16[896,2048]{1,0:T(8,128)(2,1)} fusion(bf16[896,1024]{1,0:T(8,128)(2,1)} %bitcast.55, bf16[1024,2048]{1,0:T(8,128)(2,1)S(1)} %bitcast.50), kind=kOutput, calls=%fused_computation.15 | convolution fusion | flops 3759931392 | bytes 9699328 | tf_op jit(solution)/shard_map/dot_general | solution.py:1360
  148.0 1.4 collective-permute-start.1
  150.4 1.5 slice_reduce_fusion.1
  152.9 4.9 fusion.1.in_ref
  157.8 2.6 multiply_convert_fusion.1.in_ref.back_ref
  160.6 7.0 %shard_map.274.left_back_ref = bf16[4,2,2,128,896]{4,3,2,1,0:T(8,128)(2,1)} custom-call(bf16[896,2048]{1,0:T(8,128)(2,1)} %multiply_convert_fusion.1.in_ref.back_ref), custom_call_target="tpu_custom_call" | custom-call | bytes 7340032 | tf_op jit(solution)/shard_map/pallas_call | solution.py:940
  167.5 7.1 %shard_map.275.left_hbm = bf16[4,2,2,128,896]{4,3,2,1,0:T(8,128)(2,1)} custom-call(bf16[896,2048]{1,0:T(8,128)(2,1)} %fusion.1.in_ref), custom_call_target="tpu_custom_call" | custom-call | bytes 7340032 | tf_op jit(solution)/shard_map/pallas_call | solution.py:940
  174.7 55.3 %collective-permute-done = f32[896,1]{0,1:T(1,128)S(1)} collective-permute-done((f32[896,1]{0,1:T(1,128)S(1)}, f32[896,1]{0,1:T(1,128)S(1)}, u32[]{:S(2)}, u32[]{:S(2)}) %collective-permute-start) | collective-permute-done | bytes 3616 | tf_op jit(solution)/shard_map/ppermute | solution.py:47
  230.0 1.6 multiply_convert_fusion.2.in_ref
  231.7 6.2 shard_map.276.left_out_ref
  237.8 5.3 multiply_reduce_fusion
  243.1 3.0 copy-done.3
  246.1 2.5 multiply_convert_fusion.in_ref.normed_ref
  248.6 7.0 %shard_map.277.left_ref = bf16[4,2,2,128,896]{4,3,2,1,0:T(8,128)(2,1)} custom-call(bf16[896,2048]{1,0:T(8,128)(2,1)} %multiply_convert_fusion.in_ref.normed_ref), custom_call_target="tpu_custom_call" | custom-call | bytes 7340032 | tf_op jit(solution)/shard_map/pallas_call | solution.py:940
  255.6 23.3 %all-gather.2.cloned.1.call-done.glu_ref = bf16[3,2048,2816]{2,1,0:T(8,128)(2,1)} async-done(((bf16[3,128,2816]{2,1,0:T(8,128)(2,1)}), bf16[3,2048,2816]{2,1,0:T(8,128)(2,1)}) %all-gather.2.cloned.1.call-update) | async-done | bytes 34603024 | tf_op jit(solution)/shard_map/all_gather | solution.py:1337
  279.0 182.2 %shard_map.278 = (f32[27,128,256]{2,1,0:T(8,128)}, bf16[896,2048]{1,0:T(8,128)(2,1)}, bf16[896,2048]{1,0:T(8,128)(2,1)}, bf16[896,1024]{1,0:T(8,128)(2,1)}, bf16...) custom-call(bf16[896,2048]{1,0:T(8,128)(2,1)} %multiply_convert_fusion.in_ref.normed_ref, ...), custom_call_target="tpu_custom_call" | custom-call | flops 93012885504 | bytes 69206016 | tf_op jit(solution)/shard_map/pallas_call | solution.py:644
  461.2 1.5 collective-permute-start.2
  466.5 19.7 %shard_map.279 = (f32[896,1024]{1,0:T(8,128)}, bf16[896,2048]{1,0:T(8,128)(2,1)}, f32[896,1]{1,0:T(8,128)}, f32[896,1024]{1,0:T(8,128)}, f32[1,2048]{1,0:T(1,128)}) custom-call(bf16[896,2048]{1,0:T(8,128)(2,1)} %get-tuple-element.79.sum_own_ref, bf16[896,2048]{1,0:T(8,128)(2,1)} %get-tuple-element.80.sum_came_ref, f32[896,2048]{1,0:T(8,128)} %copy-done.3, ...), custom_call_target="tpu_custom_call" | custom-call | flops 3758096384 | bytes 36700160 | tf_op jit(solution)/shard_map/pallas_call | solution.py:983
  486.3 17.0 %shard_map.280 = (bf16[3,2,448,1024]{3,2,1,0:T(8,128)(2,1)}, f32[2,1,1024]{2,1,0:T(1,128)}, f32[2,448,1]{2,1,0:T(8,128)}) custom-call(f32[3,2,448,1024]{3,2,1,0:T(8,128)} %bitcast.47, f32[2,448,1024]{2,1,0:T(8,128)} %get-tuple-element.78.states_ref, f32[2,448,1024]{2,1,0:T(8,128)} %bitcast.52, f32[2,448,1]{2,1,0:T(8,128)} %reshape.309.inverse_ref, ...), custom_call_target="tpu_custom_call" | custom-call | flops 73400320 | bytes 25690112 | tf_op jit(solution)/shard_map/pallas_call | solution.py:256
  504.9 1.2 reduce.13
  506.8 13.8 %shard_map.281 = (f32[2,128,2816]{2,1,0:T(8,128)}, f32[2,128,2816]{2,1,0:T(8,128)}, f32[2,128,2816]{2,1,0:T(8,128)}, f32[2816,128]{1,0:T(8,128)}, f32[2816,128]{1,0:T(8,128)}, /*index=5*/f32[2816,128]{1,0:T(8,128)}) custom-call(f32[27,128,256]{2,1,0:T(8,128)} %get-tuple-element.85.act_ref.up_ref.out_ref, ...), custom_call_target="tpu_custom_call" | custom-call | flops 17694720 | bytes 24772608 | tf_op jit(solution)/shard_map/pallas_call | solution.py:1020
  520.7 4.3 add_convert_fusion.1
  525.0 115.6 %shard_map.282 = (f32[4,64,2048]{2,1,0:T(8,128)}, f32[8,128]{1,0:T(8,128)}, bf16[896,1024]{1,0:T(8,128)(2,1)}, bf16[896,1024]{1,0:T(8,128)(2,1)}, bf16[896,1024]{1,0:T(8,128)(2,1)}, /*index=5*/f32[7,128]{1,0:T(8,128)}) custom-call(bf16[4,2,2,128,896]{4,3,2,1,0:T(8,128)(2,1)} %shard_map.275.left_hbm, bf16[3,896,1024]{2,1,0:T(8,128)(2,1)} %bitcast.64, ...), custom_call_target="tpu_custom_call" | custom-call | flops 26306674688 | bytes 33554432 | tf_op jit(solution)/shard_map/pallas_call | solution.py:890
  642.7 4.0 add_convert_fusion
  647.9 4.0 multiply_subtract_fusion
  651.9 3.2 shard_map.283
  (99 shorter events, 15.6 us)
Async XLA Ops:
  7.2 271.8 %all-gather.2.cloned.1.call-start = ((), (), s32[]{:S(2)}) async-start(), calls=%async_computation.1 | async-start | bytes 36765696 | tf_op jit(solution)/shard_map/all_gather | solution.py:1337
  9.8 99.0 %copy-start.16 = (f32[2048]{0:T(1024)S(1)}, f32[2048]{0:T(1024)}, u32[]{:S(2)}) copy-start(f32[2048]{0:T(1024)} %param.21) | copy-start | bytes 24580
  107.0 544.9 %reduce-scatter.2.cloned.1.call-start = ((), (), s32[]{:S(2)}) async-start(), calls=%async_computation.2 | async-start | bytes 6684672 | tf_op jit(solution)/shard_map/reduce_scatter | solution.py:1386
  108.9 354.6 %copy-start.13 = (f32[2048]{0:T(1024)}, f32[2048]{0:T(1024)S(1)}, u32[]{:S(2)}) copy-start(f32[2048]{0:T(1024)S(1)} %mul.240) | copy-start | bytes 24580
  109.6 3.4 copy-start
  130.2 10.8 %copy-start.6 = (bf16[4,2,2,64,2048]{4,3,2,1,0:T(8,128)(2,1)S(1)}, bf16[4,2,2,64,2048]{4,3,2,1,0:T(8,128)(2,1)}, u32[]{:S(2)}) copy-start(bf16[4,2,2,64,2048]{4,3,2,1,0:T(8,128)(2,1)} %get-tuple-element.71) | copy-start | bytes 12582916
  141.0 8.5 %copy-start.12 = (f32[2,448,1]{2,1,0:T(8,128)S(1)}, f32[2,448,1]{2,1,0:T(8,128)}, u32[]{:S(2)}) copy-start(f32[2,448,1]{2,1,0:T(8,128)} %get-tuple-element.69) | copy-start | bytes 10756
  141.0 10.9 %copy-start.21 = (s32[2,1,1]{0,2,1:T(1,128)S(1)}, s32[2,1,1]{0,2,1:T(1,128)}, u32[]{:S(2)}) copy-start(s32[2,1,1]{0,2,1:T(1,128)} %param.20) | copy-start | bytes 28
  141.0 11.8 %copy-start.20 = (s32[2,1]{0,1:T(1,128)S(1)}, s32[2,1]{0,1:T(1,128)}, u32[]{:S(2)}) copy-start(s32[2,1]{0,1:T(1,128)} %param.19) | copy-start | bytes 28
  148.0 89.8 %collective-permute-start.1 = (bf16[896,2048]{1,0:T(8,128)(2,1)}, bf16[896,2048]{1,0:T(8,128)(2,1)}, u32[]{:S(2)}, u32[]{:S(2)}) collective-permute-start(bf16[896,2048]{1,0:T(8,128)(2,1)} %convolution_convert_fusion), channel_id=1, source_target_pairs={{0,1},{1,0},{2,3},{3,2},{4,5},{5,4},{6,7},{7,6},{8,9},{9,8},{10,11... | collective-permute-start | bytes 11010056 | tf_op jit(solution)/shard_map/ppermute | solution.py:47
  149.8 80.2 %collective-permute-start = (f32[896,1]{0,1:T(1,128)S(1)}, f32[896,1]{0,1:T(1,128)S(1)}, u32[]{:S(2)}, u32[]{:S(2)}) collective-permute-start(f32[896,1]{0,1:T(1,128)S(1)} %reshape.296), channel_id=1, source_target_pairs={{0,1},{1,0},{2,3},{3,2},{4,5},{5,4},{6,7},{7,6},{8,9},{9,8},{10,11... | collective-permute-start | bytes 10760 | tf_op jit(solution)/shard_map/ppermute | solution.py:47
  152.9 4.9 copy-start.4
  167.5 62.5 %copy-start.11 = (bf16[2,448,1024]{2,1,0:T(8,128)(2,1)S(1)}, bf16[2,448,1024]{2,1,0:T(8,128)(2,1)}, u32[]{:S(2)}) copy-start(bf16[2,448,1024]{2,1,0:T(8,128)(2,1)} %get-tuple-element.70) | copy-start | bytes 5505028
  230.0 7.8 %copy-start.1 = (bf16[2,1,448,2048]{3,2,1,0:T(8,128)(2,1)S(1)}, bf16[2,1,448,2048]{3,2,1,0:T(8,128)(2,1)}, u32[]{:S(2)}) copy-start(bf16[2,1,448,2048]{3,2,1,0:T(8,128)(2,1)} %param.17) | copy-start | bytes 11010052
  243.1 3.0 copy-start.3
  461.2 59.4 %collective-permute-start.2 = (bf16[896,1024]{1,0:T(8,128)(2,1)}, bf16[896,1024]{1,0:T(8,128)(2,1)}, u32[]{:S(2)}, u32[]{:S(2)}) collective-permute-start(bf16[896,1024]{1,0:T(8,128)(2,1)} %get-tuple-element.77), channel_id=1, source_target_pairs={{0,1},{1,0},{2,3},{3,2},{4,5},{5,4},{6,7},{7,6},{8,9},{9,8},{10,11... | collective-permute-start | bytes 5505032 | tf_op jit(solution)/shard_map/ppermute | solution.py:47
  486.3 17.9 %copy-start.17 = (f32[1,2048]{1,0:T(1,128)S(1)}, f32[1,2048]{1,0:T(1,128)}, u32[]{:S(2)}) copy-start(f32[1,2048]{1,0:T(1,128)} %get-tuple-element.100) | copy-start | bytes 24580
  486.3 34.4 %slice-start = ((s8[7340032]{0:T(1024)(128)(4,1)}), s8[3145728]{0:T(1024)(128)(4,1)S(1)}, s32[]{:S(2)}) async-start(s8[7340032]{0:T(1024)(128)(4,1)} %bitcast.44), calls=%async_computation.3 | async-start | bytes 6291456
  506.8 13.9 %slice-start.1 = ((s8[7340032]{0:T(1024)(128)(4,1)}), s8[4194304]{0:T(1024)(128)(4,1)S(1)}, s32[]{:S(2)}) async-start(s8[7340032]{0:T(1024)(128)(4,1)} %bitcast.44), calls=%async_computation.4 | async-start | bytes 8388608
  525.0 116.3 %copy-start.14 = (f32[7,128]{1,0:T(8,128)S(1)}, f32[7,128]{1,0:T(8,128)}, u32[]{:S(2)}) copy-start(f32[7,128]{1,0:T(8,128)} %reshape.305.dot_ref) | copy-start | bytes 10756
  525.0 117.0 %copy-start.15 = (f32[3,64]{1,0:T(4,128)S(1)}, f32[3,64]{1,0:T(4,128)}, u32[]{:S(2)}) copy-start(f32[3,64]{1,0:T(4,128)} %gain_ref.1) | copy-start | bytes 2308
  525.0 117.0 %copy-start.18 = (f32[3,64]{1,0:T(4,128)S(1)}, f32[3,64]{1,0:T(4,128)}, u32[]{:S(2)}) copy-start(f32[3,64]{1,0:T(4,128)} %param.32) | copy-start | bytes 2308
  525.0 117.0 %copy-start.19 = (f32[3,64]{1,0:T(4,128)S(1)}, f32[3,64]{1,0:T(4,128)}, u32[]{:S(2)}) copy-start(f32[3,64]{1,0:T(4,128)} %param.33) | copy-start | bytes 2308
  525.0 117.7 %copy-start.2 = (bf16[2,1,448,2048]{3,2,1,0:T(8,128)(2,1)S(1)}, bf16[2,1,448,2048]{3,2,1,0:T(8,128)(2,1)}, u32[]{:S(2)}) copy-start(bf16[2,1,448,2048]{3,2,1,0:T(8,128)(2,1)} %param.17) | copy-start | bytes 11010052
  525.0 117.7 %copy-start.7 = (f32[896,1024]{1,0:T(8,128)S(1)}, f32[896,1024]{1,0:T(8,128)}, u32[]{:S(2)}) copy-start(f32[896,1024]{1,0:T(8,128)} %get-tuple-element.93) | copy-start | bytes 11010052
  525.0 117.6 %dynamic-slice-start = ((f32[2048]{0:T(1024)}, s32[]{:T(128)}), f32[1024]{0:T(1024)S(1)}, s32[]{:S(2)}) async-start(f32[2048]{0:T(1024)} %copy-done.13, s32[]{:T(128)} %select_n.36), calls=%async_computation.5 | async-start | bytes 8704 | tf_op jit(solution)/shard_map/dynamic_slice | solution.py:1402
  642.7 4.0 copy-start.5
  642.7 4.0 copy-start.8
  642.7 4.6 copy-start.9
  642.7 5.2 copy-start.10
Sparse Core Ops, SparseCore 0:
  107.2 171.7 all-gather.1
  461.4 85.0 reduce-scatter.1

commit v9 on v8

--- a/solution.py
+++ b/solution.py
@@ -1045,12 +1045,18 @@
     )
 
 
-def gather_kernel(mixer_ref, gain_ref, lengths_ref, domains_ref, glu_in_ref, glu_out_ref, cot_ref,
+def gather_kernel(mixer_ref, gain_ref, lengths_ref, domains_ref, glu_in_hbm, glu_out_hbm, cot_ref,
                   all_in, all_out, all_small, cot_full, glu_low,
-                  in_ref, out_ref, small_ref, right_send, left_send,
+                  glu_in_ref, glu_out_ref, glu_sem, in_ref, out_ref, small_ref, right_send, left_send,
                   z_recv, x_send, x_recv, core_send, core_recv, y_send, y_recv, local_sem):
     z, x, core = device_place()
     mp = lax.axis_index("mp")
+    glu_loads = (
+        pltpu.make_async_copy(glu_in_hbm, glu_in_ref, glu_sem.at[0]),
+        pltpu.make_async_copy(glu_out_hbm, glu_out_ref, glu_sem.at[1]),
+    )
+    for one in glu_loads:
+        one.start()
     barrier = pltpu.get_barrier_semaphore()
     right, left = lax.rem(z + 1, DEPTH), lax.rem(z + DEPTH - 1, DEPTH)
     dp = lax.axis_index("dp")
@@ -1159,6 +1165,8 @@
     locals_[1].start()
     cot_copy.start()
     cot_local.start()
+    for one in glu_loads:
+        one.wait()
     glu_low[0:2] = glu_in_ref[...].astype(BF)
     for tile in range(glu_out_ref.shape[0] // 128):
         lanes = slice(128 * tile, 128 * tile + 128)
@@ -1258,7 +1266,7 @@
     _, glu_rows, hidden = glu_in.shape
     return pl.pallas_call(
         gather_kernel,
-        in_specs=[in_vmem] * 6 + [any_space],
+        in_specs=[in_vmem] * 4 + [any_space] * 3,
         out_specs=[any_space] * 4 + [in_vmem],
         out_shape=[
             jax.ShapeDtypeStruct((3, DEPTH, 2, 2, 2, own_rows, channels), BF),
@@ -1268,6 +1276,9 @@
             jax.ShapeDtypeStruct((3, glu_rows, hidden), BF),
         ],
         scratch_shapes=[
+            pltpu.VMEM(glu_in.shape, F32),
+            pltpu.VMEM(glu_out.shape, F32),
+            dma((2,)),
             pltpu.VMEM((2, 3, own_rows, channels), BF),
             pltpu.VMEM((own_rows, full), BF),
             pltpu.VMEM((8, 128), F32),

time: 668 us -> 667 us (level)
  no operation moved by 1% of the time
where the time goes in v9:
time: 667 us; the launch traced here: 661 us
  Pallas kernels  485 us (73%)
  waiting for transfers between devices  78.6 us (12%)
  other arithmetic  39.1 us (6%)
  matrix products  23.2 us (3%)
  local copies, waits for them, and re-layouts  16.2 us (2%)
  between operations  14.8 us (2%)
    pallas_call x1, Pallas kernels, glu_call(): pl.pallas_call(functools.partial(glu_kernel, hidden_blocks, full_blocks),...  182 us
    pallas_call x1, Pallas kernels, mixer_call(): pl.pallas_call(functools.partial(mixer_kernel, full_blocks), grid=(chunks...  116 us
    pallas_call x1, Pallas kernels, gather_call(): pl.pallas_call(gather_kernel, in_specs=[in_vmem] * 4 + [any_space] * 3, o...  95.9 us
    ppermute x3, waiting for transfers between devices, partner_swap(): return lax.ppermute(value, 'mp', [(0, 1), (1, 0)])  55.3 us
    pallas_call x4, Pallas kernels, owner_rows(): pl.pallas_call(transpose_kernel, grid=(2 * DEPTH,), in_specs=[pl.BlockSpe...  27.2 us
    all_gather x1, waiting for transfers between devices, shards(): glu = lax.all_gather(glu_low, 'dp', axis=1, tiled=True)  23.3 us
    pallas_call x1, Pallas kernels, middle_back(): pl.pallas_call(middle_back_kernel, grid=(rows // step,), in_specs=[line(f...  19.7 us
    pallas_call x2, Pallas kernels, glu_update(): pl.pallas_call(functools.partial(glu_update_kernel, scale), grid=(blocks,...  17 us
  transfers between devices with their start and end apart: 5, of which 2 were waited for; matrix products, arithmetic and copies ran while one was open for 11% of the time, Pallas kernels for 31%

profile of v9, /device:TPU:0, one launch (start us, length us, event | category | flops | bytes accessed | tf_op | source)
XLA Modules:
  0.0 661.2 jit_solution(6387933050821239690)
XLA Ops:
  7.2 1.3 copy.51.lengths_ref
  8.5 1.3 copy.52.domains_ref
  9.8 95.9 %shard_map.272 = (bf16[3,4,2,2,2,64,1024]{6,5,4,3,2,1,0:T(8,128)(2,1)}, bf16[4,2,2,64,2048]{4,3,2,1,0:T(8,128)(2,1)}, f32[4,2,2,2,8,128]{5,4,3,2,1,0:T(8,128)}, ...) custom-call(f32[4,64,2048]{2,1,0:T(8,128)} %mixer_ref.1, f32[3,64]{1,0:T(4,128)} %gain_ref.1, s32[2,1]{1,0:T(2,128)} %copy.51.lengths_ref, ...), custom_call_target="tpu_custom_call" | custom-call | bytes 300000000 | tf_op jit(solution)/shard_map/pallas_call | solution.py:1267
  108.4 3.0 fusion.2
  112.7 16.2 %fusion.7 = f32[3,1024,896]{1,2,0:T(8,128)} fusion(bf16[896,2048,1]{1,0,2:T(8,128)(2,1)S(1)} %bitcast.51, bf16[3,2048,1024]{2,1,0:T(8,128)(2,1)} %bitcast.62), kind=kOutput, calls=%fused_computation.38 | convolution fusion | flops 11274289152 | bytes 27262976 | tf_op jit(solution)/shard_map/td,kde->kte/dot_general | solution.py:1366
  128.9 10.8 %shard_map.273 = (f32[2,448,1024]{2,1,0:T(8,128)}, bf16[2,448,1024]{2,1,0:T(8,128)(2,1)}, f32[2,448,1]{2,1,0:T(8,128)}) custom-call(f32[3,2,448,1024]{3,2,1,0:T(8,128)} %bitcast.46, f32[1,1024]{1,0:T(1,128)} %broadcast_in_dim_reshape.8.bound_ref, f32[1,1024]{1,0:T(1,128)} %broadcast_in_dim_reshape.9.gain_ref), custom_call_target="tpu_custom_call" | custom-call | flops 36700160 | bytes 16515072 | tf_op jit(solution)/shard_map/pallas_call | solution.py:151
  139.7 7.0 %convolution_convert_fusion = bf16[896,2048]{1,0:T(8,128)(2,1)} fusion(bf16[896,1024]{1,0:T(8,128)(2,1)} %bitcast.55, bf16[1024,2048]{1,0:T(8,128)(2,1)S(1)} %bitcast.50), kind=kOutput, calls=%fused_computation.15 | convolution fusion | flops 3759931392 | bytes 9699328 | tf_op jit(solution)/shard_map/dot_general | solution.py:1371
  146.7 1.4 collective-permute-start.1
  149.2 1.5 slice_reduce_fusion.1
  151.6 4.9 fusion.1.in_ref
  156.5 2.6 multiply_convert_fusion.1.in_ref.back_ref
  159.3 7.0 %shard_map.274.left_back_ref = bf16[4,2,2,128,896]{4,3,2,1,0:T(8,128)(2,1)} custom-call(bf16[896,2048]{1,0:T(8,128)(2,1)} %multiply_convert_fusion.1.in_ref.back_ref), custom_call_target="tpu_custom_call" | custom-call | bytes 7340032 | tf_op jit(solution)/shard_map/pallas_call | solution.py:940
  166.3 7.1 %shard_map.275.left_hbm = bf16[4,2,2,128,896]{4,3,2,1,0:T(8,128)(2,1)} custom-call(bf16[896,2048]{1,0:T(8,128)(2,1)} %fusion.1.in_ref), custom_call_target="tpu_custom_call" | custom-call | bytes 7340032 | tf_op jit(solution)/shard_map/pallas_call | solution.py:940
  173.4 55.3 %collective-permute-done = f32[896,1]{0,1:T(1,128)S(1)} collective-permute-done((f32[896,1]{0,1:T(1,128)S(1)}, f32[896,1]{0,1:T(1,128)S(1)}, u32[]{:S(2)}, u32[]{:S(2)}) %collective-permute-start) | collective-permute-done | bytes 3616 | tf_op jit(solution)/shard_map/ppermute | solution.py:47
  228.8 1.6 multiply_convert_fusion.2.in_ref
  230.4 6.2 shard_map.276.left_out_ref
  236.6 5.3 multiply_reduce_fusion
  241.9 3.0 copy-done.3
  244.9 2.5 multiply_convert_fusion.in_ref.normed_ref
  247.4 7.0 %shard_map.277.left_ref = bf16[4,2,2,128,896]{4,3,2,1,0:T(8,128)(2,1)} custom-call(bf16[896,2048]{1,0:T(8,128)(2,1)} %multiply_convert_fusion.in_ref.normed_ref), custom_call_target="tpu_custom_call" | custom-call | bytes 7340032 | tf_op jit(solution)/shard_map/pallas_call | solution.py:940
  254.4 23.3 %all-gather.2.cloned.1.call-done.glu_ref = bf16[3,2048,2816]{2,1,0:T(8,128)(2,1)} async-done(((bf16[3,128,2816]{2,1,0:T(8,128)(2,1)}), bf16[3,2048,2816]{2,1,0:T(8,128)(2,1)}) %all-gather.2.cloned.1.call-update) | async-done | bytes 34603024 | tf_op jit(solution)/shard_map/all_gather | solution.py:1348
  277.7 182.2 %shard_map.278 = (f32[27,128,256]{2,1,0:T(8,128)}, bf16[896,2048]{1,0:T(8,128)(2,1)}, bf16[896,2048]{1,0:T(8,128)(2,1)}, bf16[896,1024]{1,0:T(8,128)(2,1)}, bf16...) custom-call(bf16[896,2048]{1,0:T(8,128)(2,1)} %multiply_convert_fusion.in_ref.normed_ref, ...), custom_call_target="tpu_custom_call" | custom-call | flops 93012885504 | bytes 69206016 | tf_op jit(solution)/shard_map/pallas_call | solution.py:644
  460.0 1.5 collective-permute-start.2
  465.3 19.7 %shard_map.279 = (f32[896,1024]{1,0:T(8,128)}, bf16[896,2048]{1,0:T(8,128)(2,1)}, f32[896,1]{1,0:T(8,128)}, f32[896,1024]{1,0:T(8,128)}, f32[1,2048]{1,0:T(1,128)}) custom-call(bf16[896,2048]{1,0:T(8,128)(2,1)} %get-tuple-element.79.sum_own_ref, bf16[896,2048]{1,0:T(8,128)(2,1)} %get-tuple-element.80.sum_came_ref, f32[896,2048]{1,0:T(8,128)} %copy-done.3, ...), custom_call_target="tpu_custom_call" | custom-call | flops 3758096384 | bytes 36700160 | tf_op jit(solution)/shard_map/pallas_call | solution.py:983
  485.0 17.0 %shard_map.280 = (bf16[3,2,448,1024]{3,2,1,0:T(8,128)(2,1)}, f32[2,1,1024]{2,1,0:T(1,128)}, f32[2,448,1]{2,1,0:T(8,128)}) custom-call(f32[3,2,448,1024]{3,2,1,0:T(8,128)} %bitcast.47, f32[2,448,1024]{2,1,0:T(8,128)} %get-tuple-element.78.states_ref, f32[2,448,1024]{2,1,0:T(8,128)} %bitcast.52, f32[2,448,1]{2,1,0:T(8,128)} %reshape.309.inverse_ref, ...), custom_call_target="tpu_custom_call" | custom-call | flops 73400320 | bytes 25690112 | tf_op jit(solution)/shard_map/pallas_call | solution.py:256
  503.6 1.2 reduce.13
  505.6 13.8 %shard_map.281 = (f32[2,128,2816]{2,1,0:T(8,128)}, f32[2,128,2816]{2,1,0:T(8,128)}, f32[2,128,2816]{2,1,0:T(8,128)}, f32[2816,128]{1,0:T(8,128)}, f32[2816,128]{1,0:T(8,128)}, /*index=5*/f32[2816,128]{1,0:T(8,128)}) custom-call(f32[27,128,256]{2,1,0:T(8,128)} %get-tuple-element.85.act_ref.up_ref.out_ref, ...), custom_call_target="tpu_custom_call" | custom-call | flops 17694720 | bytes 24772608 | tf_op jit(solution)/shard_map/pallas_call | solution.py:1020
  519.4 4.3 add_convert_fusion.1
  523.7 115.6 %shard_map.282 = (f32[4,64,2048]{2,1,0:T(8,128)}, f32[8,128]{1,0:T(8,128)}, bf16[896,1024]{1,0:T(8,128)(2,1)}, bf16[896,1024]{1,0:T(8,128)(2,1)}, bf16[896,1024]{1,0:T(8,128)(2,1)}, /*index=5*/f32[7,128]{1,0:T(8,128)}) custom-call(bf16[4,2,2,128,896]{4,3,2,1,0:T(8,128)(2,1)} %shard_map.275.left_hbm, bf16[3,896,1024]{2,1,0:T(8,128)(2,1)} %bitcast.64, ...), custom_call_target="tpu_custom_call" | custom-call | flops 26306674688 | bytes 33554432 | tf_op jit(solution)/shard_map/pallas_call | solution.py:890
  641.5 4.0 add_convert_fusion
  646.7 4.0 multiply_subtract_fusion
  650.7 3.2 shard_map.283
  (99 shorter events, 15.6 us)
Async XLA Ops:
  7.2 270.5 %all-gather.2.cloned.1.call-start = ((), (), s32[]{:S(2)}) async-start(), calls=%async_computation.1 | async-start | bytes 36765696 | tf_op jit(solution)/shard_map/all_gather | solution.py:1348
  9.8 97.8 %copy-start.16 = (f32[2048]{0:T(1024)S(1)}, f32[2048]{0:T(1024)}, u32[]{:S(2)}) copy-start(f32[2048]{0:T(1024)} %param.21) | copy-start | bytes 24580
  105.8 544.9 %reduce-scatter.2.cloned.1.call-start = ((), (), s32[]{:S(2)}) async-start(), calls=%async_computation.2 | async-start | bytes 6684672 | tf_op jit(solution)/shard_map/reduce_scatter | solution.py:1397
  107.6 354.6 %copy-start.13 = (f32[2048]{0:T(1024)}, f32[2048]{0:T(1024)S(1)}, u32[]{:S(2)}) copy-start(f32[2048]{0:T(1024)S(1)} %mul.240) | copy-start | bytes 24580
  108.4 3.4 copy-start
  128.9 10.8 %copy-start.6 = (bf16[4,2,2,64,2048]{4,3,2,1,0:T(8,128)(2,1)S(1)}, bf16[4,2,2,64,2048]{4,3,2,1,0:T(8,128)(2,1)}, u32[]{:S(2)}) copy-start(bf16[4,2,2,64,2048]{4,3,2,1,0:T(8,128)(2,1)} %get-tuple-element.71) | copy-start | bytes 12582916
  139.7 8.5 %copy-start.12 = (f32[2,448,1]{2,1,0:T(8,128)S(1)}, f32[2,448,1]{2,1,0:T(8,128)}, u32[]{:S(2)}) copy-start(f32[2,448,1]{2,1,0:T(8,128)} %get-tuple-element.69) | copy-start | bytes 10756
  139.7 10.9 %copy-start.21 = (s32[2,1,1]{0,2,1:T(1,128)S(1)}, s32[2,1,1]{0,2,1:T(1,128)}, u32[]{:S(2)}) copy-start(s32[2,1,1]{0,2,1:T(1,128)} %param.20) | copy-start | bytes 28
  139.7 11.8 %copy-start.20 = (s32[2,1]{0,1:T(1,128)S(1)}, s32[2,1]{0,1:T(1,128)}, u32[]{:S(2)}) copy-start(s32[2,1]{0,1:T(1,128)} %param.19) | copy-start | bytes 28
  146.7 89.8 %collective-permute-start.1 = (bf16[896,2048]{1,0:T(8,128)(2,1)}, bf16[896,2048]{1,0:T(8,128)(2,1)}, u32[]{:S(2)}, u32[]{:S(2)}) collective-permute-start(bf16[896,2048]{1,0:T(8,128)(2,1)} %convolution_convert_fusion), channel_id=1, source_target_pairs={{0,1},{1,0},{2,3},{3,2},{4,5},{5,4},{6,7},{7,6},{8,9},{9,8},{10,11... | collective-permute-start | bytes 11010056 | tf_op jit(solution)/shard_map/ppermute | solution.py:47
  148.5 80.2 %collective-permute-start = (f32[896,1]{0,1:T(1,128)S(1)}, f32[896,1]{0,1:T(1,128)S(1)}, u32[]{:S(2)}, u32[]{:S(2)}) collective-permute-start(f32[896,1]{0,1:T(1,128)S(1)} %reshape.296), channel_id=1, source_target_pairs={{0,1},{1,0},{2,3},{3,2},{4,5},{5,4},{6,7},{7,6},{8,9},{9,8},{10,11... | collective-permute-start | bytes 10760 | tf_op jit(solution)/shard_map/ppermute | solution.py:47
  151.6 4.9 copy-start.4
  166.3 62.5 %copy-start.11 = (bf16[2,448,1024]{2,1,0:T(8,128)(2,1)S(1)}, bf16[2,448,1024]{2,1,0:T(8,128)(2,1)}, u32[]{:S(2)}) copy-start(bf16[2,448,1024]{2,1,0:T(8,128)(2,1)} %get-tuple-element.70) | copy-start | bytes 5505028
  228.7 7.8 %copy-start.1 = (bf16[2,1,448,2048]{3,2,1,0:T(8,128)(2,1)S(1)}, bf16[2,1,448,2048]{3,2,1,0:T(8,128)(2,1)}, u32[]{:S(2)}) copy-start(bf16[2,1,448,2048]{3,2,1,0:T(8,128)(2,1)} %param.17) | copy-start | bytes 11010052
  241.8 3.0 copy-start.3
  460.0 59.4 %collective-permute-start.2 = (bf16[896,1024]{1,0:T(8,128)(2,1)}, bf16[896,1024]{1,0:T(8,128)(2,1)}, u32[]{:S(2)}, u32[]{:S(2)}) collective-permute-start(bf16[896,1024]{1,0:T(8,128)(2,1)} %get-tuple-element.77), channel_id=1, source_target_pairs={{0,1},{1,0},{2,3},{3,2},{4,5},{5,4},{6,7},{7,6},{8,9},{9,8},{10,11... | collective-permute-start | bytes 5505032 | tf_op jit(solution)/shard_map/ppermute | solution.py:47
  485.0 17.9 %copy-start.17 = (f32[1,2048]{1,0:T(1,128)S(1)}, f32[1,2048]{1,0:T(1,128)}, u32[]{:S(2)}) copy-start(f32[1,2048]{1,0:T(1,128)} %get-tuple-element.100) | copy-start | bytes 24580
  485.0 34.4 %slice-start = ((s8[7340032]{0:T(1024)(128)(4,1)}), s8[3145728]{0:T(1024)(128)(4,1)S(1)}, s32[]{:S(2)}) async-start(s8[7340032]{0:T(1024)(128)(4,1)} %bitcast.44), calls=%async_computation.3 | async-start | bytes 6291456
  505.6 13.8 %slice-start.1 = ((s8[7340032]{0:T(1024)(128)(4,1)}), s8[4194304]{0:T(1024)(128)(4,1)S(1)}, s32[]{:S(2)}) async-start(s8[7340032]{0:T(1024)(128)(4,1)} %bitcast.44), calls=%async_computation.4 | async-start | bytes 8388608
  523.7 116.3 %copy-start.14 = (f32[7,128]{1,0:T(8,128)S(1)}, f32[7,128]{1,0:T(8,128)}, u32[]{:S(2)}) copy-start(f32[7,128]{1,0:T(8,128)} %reshape.305.dot_ref) | copy-start | bytes 10756
  523.7 117.0 %copy-start.15 = (f32[3,64]{1,0:T(4,128)S(1)}, f32[3,64]{1,0:T(4,128)}, u32[]{:S(2)}) copy-start(f32[3,64]{1,0:T(4,128)} %gain_ref.1) | copy-start | bytes 2308
  523.7 117.0 %copy-start.18 = (f32[3,64]{1,0:T(4,128)S(1)}, f32[3,64]{1,0:T(4,128)}, u32[]{:S(2)}) copy-start(f32[3,64]{1,0:T(4,128)} %param.32) | copy-start | bytes 2308
  523.7 117.0 %copy-start.19 = (f32[3,64]{1,0:T(4,128)S(1)}, f32[3,64]{1,0:T(4,128)}, u32[]{:S(2)}) copy-start(f32[3,64]{1,0:T(4,128)} %param.33) | copy-start | bytes 2308
  523.7 117.7 %copy-start.2 = (bf16[2,1,448,2048]{3,2,1,0:T(8,128)(2,1)S(1)}, bf16[2,1,448,2048]{3,2,1,0:T(8,128)(2,1)}, u32[]{:S(2)}) copy-start(bf16[2,1,448,2048]{3,2,1,0:T(8,128)(2,1)} %param.17) | copy-start | bytes 11010052
  523.7 117.7 %copy-start.7 = (f32[896,1024]{1,0:T(8,128)S(1)}, f32[896,1024]{1,0:T(8,128)}, u32[]{:S(2)}) copy-start(f32[896,1024]{1,0:T(8,128)} %get-tuple-element.93) | copy-start | bytes 11010052
  523.7 117.7 %dynamic-slice-start = ((f32[2048]{0:T(1024)}, s32[]{:T(128)}), f32[1024]{0:T(1024)S(1)}, s32[]{:S(2)}) async-start(f32[2048]{0:T(1024)} %copy-done.13, s32[]{:T(128)} %select_n.36), calls=%async_computation.5 | async-start | bytes 8704 | tf_op jit(solution)/shard_map/dynamic_slice | solution.py:1413
  641.4 4.0 copy-start.5
  641.4 4.0 copy-start.8
  641.4 4.6 copy-start.9
  641.5 5.2 copy-start.10
Sparse Core Ops, SparseCore 0:
  105.9 171.7 all-gather.1
  460.1 85.0 reduce-scatter.1
